TPU v7x, 32 devices: a whole 2x2x4 slice. The times are simulated.
32 devices in a mesh: dom: 16 (over z, x, core), sub: 2 (over y).
Axes of the slice: x: 2, y: 2, z: 4, core: 2. Of those that a mesh axis runs over, the one named last changes fastest.
Arguments:
- element_load: float32 [16, 8, 16, 8, 128], P('dom', None, 'sub'), may hold values from -48 to 48
- mobility: float32 [16, 8, 16, 8, 128], P('dom', None, 'sub'), may hold values from 0.5 to 4
- metric: float32 [3, 16, 16, 16], P(None, 'dom', 'sub'), may hold values from 0.5 to 2
Outputs:
- pressure: float32 [16, 8, 16, 8, 128], P('dom', None, 'sub')
- coarse_residual: float32 [16, 16, 17], P('dom', 'sub')
All inputs are finite; a program needn't handle non-finite values.
Results may differ from a plain program's by a relative error of at most 0.00008.
Values sent between devices are 32-bit elements; how exact they have to be, the bound alone decides.
No kernel may reach another device: no remote copies, remote signals or barrier semaphores. Data moves between devices by JAX's collectives and lax.ppermute only.
A program may use at most 64 MiB of HBM per device.

v0:
```python
import jax
import jax.numpy as jnp
import numpy as np
from jax import lax
from jax.sharding import PartitionSpec as P

GLL_NODES = np.array(
    [
        -1.0,
        -0.8717401485096066,
        -0.5917001814331423,
        -0.2092992179024789,
        0.2092992179024789,
        0.5917001814331423,
        0.8717401485096066,
        1.0,
    ]
)
GLL_WEIGHTS = np.array(
    [
        0.03571428571428571,
        0.2107042271435061,
        0.3411226924835044,
        0.4124587946587038,
        0.4124587946587038,
        0.3411226924835044,
        0.2107042271435061,
        0.03571428571428571,
    ]
)
THETA = 1.65
DELTA = 1.35
RHO_FIRST = DELTA / THETA
RHO_SECOND = 1.0 / (2.0 * THETA / DELTA - RHO_FIRST)
EXACT = lax.Precision.HIGHEST


def passed_along(array, axis, by):
    size = lax.axis_size(axis)
    return lax.ppermute(array, axis, [(i, (i + by) % size) for i in range(size)])


def derivative_table():
    identity = np.eye(8)
    differences = GLL_NODES[:, None] - GLL_NODES[None, :] + identity
    barycentric = 1.0 / np.prod(differences, axis=1)
    matrix = barycentric[None, :] / barycentric[:, None] / differences
    matrix = matrix * (1.0 - identity)
    row_sums = np.sum(matrix, axis=1)
    return matrix - identity * row_sums[:, None]


def make_tables():
    derivative = jnp.asarray(derivative_table(), jnp.float32)
    weights = jnp.asarray(GLL_WEIGHTS, jnp.float32)
    coarse_basis = jnp.asarray(
        np.stack([(1.0 - GLL_NODES) / 8.0, (1.0 + GLL_NODES) / 8.0], axis=1), jnp.float32
    )
    return (derivative, weights, coarse_basis)


def kron_tables(derivative, coarse_basis, width):
    layers_z = width // 8
    identity = jnp.eye(layers_z, dtype=jnp.float32)
    deriv_z = jnp.kron(identity, derivative)
    squared_z = jnp.kron(identity, derivative * derivative)
    column = jnp.arange(width)
    source_cell = column[:, None]
    target_cell = column[None, :]
    joins = (
        (source_cell == target_cell)
        | (source_cell % 8 == 7) & (target_cell == source_cell + 1)
        | (source_cell % 8 == 0) & (target_cell == source_cell - 1)
    )
    face_sum_z = jnp.where(joins, 1.0, 0.0).astype(jnp.float32)
    vertex = jnp.arange(layers_z + 1)[None, :]
    cell_of = (column // 8)[:, None]
    lower_weight = jnp.tile(coarse_basis[:, 0], layers_z)[:, None]
    upper_weight = jnp.tile(coarse_basis[:, 1], layers_z)[:, None]
    restrict_z = jnp.where(vertex == cell_of, lower_weight, 0.0) + jnp.where(
        vertex == cell_of + 1, upper_weight, 0.0
    )
    return (deriv_z, squared_z, face_sum_z, restrict_z)


def point_factors(mobility, metric, weights):
    spread = jnp.repeat(metric, 8, axis=3)[:, :, None, :, None, :]
    layers_z = mobility.shape[-1] // 8
    z_weights = jnp.tile(weights, layers_z)
    quadrature = weights[:, None, None, None] * weights[None, None, :, None] * z_weights
    return spread * (mobility * quadrature)


def apply_local(values, factors, derivative, deriv_z):
    grad_x = jnp.einsum("ai,xiyjc->xayjc", derivative, values, precision=EXACT)
    grad_y = jnp.einsum("bj,xiyjc->xiybc", derivative, values, precision=EXACT)
    grad_z = jnp.dot(values, deriv_z.T, precision=EXACT)
    back_x = jnp.einsum("ai,xayjc->xiyjc", derivative, factors[0] * grad_x, precision=EXACT)
    back_y = jnp.einsum("bj,xiybc->xiyjc", derivative, factors[1] * grad_y, precision=EXACT)
    back_z = jnp.dot(factors[2] * grad_z, deriv_z, precision=EXACT)
    return back_x + back_y + back_z


def diagonal_of(factors, derivative, squared_z):
    squared = derivative * derivative
    part_x = jnp.einsum("ai,xayjc->xiyjc", squared, factors[0], precision=EXACT)
    part_y = jnp.einsum("bj,xiybc->xiyjc", squared, factors[1], precision=EXACT)
    part_z = jnp.dot(factors[2], squared_z, precision=EXACT)
    return part_x + part_y + part_z


def assemble(fields, face_sum_z):
    upper = fields[:, :, 7]
    bottom = fields[:, :, 0]
    from_before = passed_along(upper[:, -1], "dom", 1)
    from_after = passed_along(bottom[:, 0], "dom", -1)
    after_bottom = jnp.concatenate([bottom[:, 1:], from_after[:, None]], axis=1)
    before_upper = jnp.concatenate([from_before[:, None], upper[:, :-1]], axis=1)
    new_upper = upper + after_bottom
    new_bottom = bottom + before_upper
    fields = jnp.concatenate(
        [new_bottom[:, :, None], fields[:, :, 1:7], new_upper[:, :, None]], axis=2
    )
    upper = fields[:, :, :, :, 7]
    bottom = fields[:, :, :, :, 0]
    from_before = passed_along(upper[:, :, :, -1], "sub", 1)
    from_after = passed_along(bottom[:, :, :, 0], "sub", -1)
    after_bottom = jnp.concatenate([bottom[:, :, :, 1:], from_after[:, :, :, None]], axis=3)
    before_upper = jnp.concatenate([from_before[:, :, :, None], upper[:, :, :, :-1]], axis=3)
    new_upper = upper + after_bottom
    new_bottom = bottom + before_upper
    fields = jnp.concatenate(
        [new_bottom[:, :, :, :, None], fields[:, :, :, :, 1:7], new_upper[:, :, :, :, None]], axis=4
    )
    return jnp.dot(fields, face_sum_z, precision=EXACT)


def coarse_gather(source, coarse_basis, restrict_z):
    along_z = jnp.dot(source, restrict_z, precision=EXACT)
    corners = jnp.einsum("ip,jq,xiyjv->xpyqv", coarse_basis, coarse_basis, along_z, precision=EXACT)
    plane_pad = jnp.zeros_like(corners[:1, 0])
    planes = jnp.concatenate([corners[:, 0], plane_pad], axis=0) + jnp.concatenate(
        [plane_pad, corners[:, 1]], axis=0
    )
    arriving = passed_along(planes[-1], "dom", 1)
    planes = jnp.concatenate([planes[:1] + arriving[None], planes[1:-1]], axis=0)
    row_pad = jnp.zeros_like(planes[:, :1, 0])
    lines = jnp.concatenate([planes[:, :, 0], row_pad], axis=1) + jnp.concatenate(
        [row_pad, planes[:, :, 1]], axis=1
    )
    arriving_y = passed_along(lines[:, -1], "sub", 1)
    return jnp.concatenate([lines[:, :1] + arriving_y[:, None], lines[:, 1:-1]], axis=1)


def shards(element_load, mobility, metric):
    derivative, weights, coarse_basis = make_tables()
    width = element_load.shape[-1]
    deriv_z, squared_z, face_sum_z, restrict_z = kron_tables(derivative, coarse_basis, width)
    factors = point_factors(mobility, metric, weights)
    diag_local = diagonal_of(factors, derivative, squared_z)
    assembled = assemble(jnp.stack([element_load, diag_local]), face_sum_z)
    right_side = assembled[0]
    inverse = 1.0 / assembled[1]
    first_step = inverse * right_side / THETA
    resid_first = (
        right_side
        - assemble(apply_local(first_step, factors, derivative, deriv_z)[None], face_sum_z)[0]
    )
    pressure = first_step + (
        RHO_SECOND * RHO_FIRST * first_step + 2.0 * RHO_SECOND / DELTA * (inverse * resid_first)
    )
    final_local = element_load - apply_local(pressure, factors, derivative, deriv_z)
    return (pressure, coarse_gather(final_local, coarse_basis, restrict_z))


def solution(mesh):
    in_specs = (
        P("dom", None, "sub", None, None),
        P("dom", None, "sub", None, None),
        P(None, "dom", "sub", None),
    )
    out_specs = (P("dom", None, "sub", None, None), P("dom", "sub", None))
    return jax.shard_map(shards, mesh=mesh, in_specs=in_specs, out_specs=out_specs, check_vma=False)
```

profile of v0, /device:TPU:0, one launch (start us, length us, event | category | flops | bytes accessed | tf_op | source)
XLA Modules:
  0.0 61.6 jit_solution(12305634196738631202)
XLA Ops:
  0.7 0.6 %copy-done.5 = f32[8]{0:T(128)S(1)} copy-done((f32[8]{0:T(128)S(1)}, f32[8]{0:T(128)}, u32[]{:S(2)}) %copy-start.5) | copy-done | bytes 56
  1.5 1.0 %multiply_bitcast_fusion = f32[8,8,8,128]{3,2,1,0:T(8,128)S(1)} fusion(f32[1,8,8,8,128]{4,3,2,1,0:T(8,128)} %param.7, f32[8,8,128]{2,1,0:T(8,128)S(1)} %broadcast_multiply_fusion.3), kind=kLoop, calls=%fused_computation.68 | loop fusion | flops 65536 | bytes 557056 | tf_op jit(solution)/shard_map/mul | solution.py:91
  2.7 0.5 copy-done.4
  3.5 0.5 copy-done.6
  4.0 0.2 broadcast_multiply_fusion
  4.2 0.5 reshape.323
  4.9 0.4 convolution_bitcast_fusion.7
  5.2 0.6 copy-done.1
  6.0 0.5 copy-done.3
  6.5 0.4 fusion.39
  6.9 0.5 fusion.2
  7.4 5.5 %collective-permute-start.1 = (f32[2,8,8,128]{3,2,1,0:T(8,128)S(1)}, f32[2,8,8,128]{3,2,1,0:T(8,128)S(1)}, u32[]{:S(2)}, u32[]{:S(2)}) collective-permute-start(f32[2,8,8,128]{3,2,1,0:T(8,128)S(1)} %bitcast.297), channel_id=1, source_target_pairs={{0,30},{2,0},{4,2},{6,4},{8,6},{10,8},{12,10},{14,12},{16,14},{18,... | collective-permute-start | bytes 196616 | tf_op jit(solution)/shard_map/ppermute | solution.py:40
  12.9 1.9 %collective-permute-done.1 = f32[2,8,8,128]{3,2,1,0:T(8,128)S(1)} collective-permute-done((f32[2,8,8,128]{3,2,1,0:T(8,128)S(1)}, f32[2,8,8,128]{3,2,1,0:T(8,128)S(1)}, u32[]{:S(2)}, u32[]{:S(2)}) %collective-permute-start.1) | collective-permute-done | bytes 65568 | tf_op jit(solution)/shard_map/ppermute | solution.py:40
  14.8 4.5 %collective-permute-done = f32[2,8,8,128]{3,2,1,0:T(8,128)S(1)} collective-permute-done((f32[2,8,8,128]{3,2,1,0:T(8,128)S(1)}, f32[2,8,8,128]{3,2,1,0:T(8,128)S(1)}, u32[]{:S(2)}, u32[]{:S(2)}) %collective-permute-start) | collective-permute-done | bytes 65568 | tf_op jit(solution)/shard_map/ppermute | solution.py:40
  19.5 1.6 %collective-permute-start.3 = (f32[2,1,8,128]{3,2,0,1:T(8,128)S(1)}, f32[2,1,8,128]{3,2,0,1:T(8,128)S(1)}, u32[]{:S(2)}, u32[]{:S(2)}) collective-permute-start(f32[2,1,8,128]{3,2,0,1:T(8,128)S(1)} %slice_bitcast_fusion.9), channel_id=1, source_target_pairs={{0,1},{1,0},{2,3},{3,2},{4,5},{5,4},{6,7},{7,6},{8,9},{9,8},{10,11... | collective-permute-start | bytes 24584 | tf_op jit(solution)/shard_map/ppermute | solution.py:40
  21.1 0.5 reshape.328
  21.6 1.6 %collective-permute-done.3 = f32[2,1,8,128]{3,2,0,1:T(8,128)S(1)} collective-permute-done((f32[2,1,8,128]{3,2,0,1:T(8,128)S(1)}, f32[2,1,8,128]{3,2,0,1:T(8,128)S(1)}, u32[]{:S(2)}, u32[]{:S(2)}) %collective-permute-start.3) | collective-permute-done | bytes 8224 | tf_op jit(solution)/shard_map/ppermute | solution.py:40
  23.2 1.6 %collective-permute-start.2 = (f32[2,1,8,128]{3,2,0,1:T(8,128)S(1)}, f32[2,1,8,128]{3,2,0,1:T(8,128)S(1)}, u32[]{:S(2)}, u32[]{:S(2)}) collective-permute-start(f32[2,1,8,128]{3,2,0,1:T(8,128)S(1)} %slice_bitcast_fusion.10), channel_id=1, source_target_pairs={{0,1},{1,0},{2,3},{3,2},{4,5},{5,4},{6,7},{7,6},{8,9},{9,8},{10,11... | collective-permute-start | bytes 24584 | tf_op jit(solution)/shard_map/ppermute | solution.py:40
  24.8 2.1 %collective-permute-done.2 = f32[2,1,8,128]{3,2,0,1:T(8,128)S(1)} collective-permute-done((f32[2,1,8,128]{3,2,0,1:T(8,128)S(1)}, f32[2,1,8,128]{3,2,0,1:T(8,128)S(1)}, u32[]{:S(2)}, u32[]{:S(2)}) %collective-permute-start.2) | collective-permute-done | bytes 8224 | tf_op jit(solution)/shard_map/ppermute | solution.py:40
  27.0 0.7 %fusion.21 = f32[2,8,8,8,128]{4,3,2,1,0:T(8,128)S(1)} fusion(f32[2,8,8,8,128]{4,1,3,2,0:T(8,128)S(1)} %maximum_bitcast_fusion, s32[128]{0:T(128)S(1)} %get-tuple-element.16, s32[128]{0:T(128)S(1)} %get-tuple-element.17, pred[128]{0:T(512)(128)(4,1)S(1)} %get-tuple-element.18, pred[128]{0:T(512)(128)(4,1)S(1)} %get-tuple-element.19), kind=kOutput, calls=%fused_computation.37 | convolution fusion | flops 201457664 | bytes 1049856 | tf_op jit(solution)/shard_map/dot_general | solution.py:135
  27.8 0.6 %copy-done.2 = f32[8,8,1,1]{1,0,3,2:T(8,128)S(1)} copy-done((f32[8,8,1,1]{1,0,3,2:T(8,128)S(1)}, f32[8,8,1,1]{1,0,3,2:T(8,128)}, u32[]{:S(2)}) %copy-start.2) | copy-done | bytes 280
  28.4 0.5 fusion.4
  28.9 0.3 fusion.87
  29.3 0.5 convolution_multiply_fusion.1
  29.8 0.4 convolution_bitcast_fusion.4
  30.3 0.4 fusion.37
  30.7 0.5 fusion.7
  31.3 1.6 %collective-permute-done.5 = f32[1,8,8,128]{3,2,1,0:T(8,128)S(1)} collective-permute-done((f32[1,8,8,128]{3,2,1,0:T(8,128)S(1)}, f32[1,8,8,128]{3,2,1,0:T(8,128)S(1)}, u32[]{:S(2)}, u32[]{:S(2)}) %collective-permute-start.5) | collective-permute-done | bytes 32800 | tf_op jit(solution)/shard_map/ppermute | solution.py:40
  33.1 0.6 copy-done.10
  33.7 0.6 copy-done.9
  34.4 4.7 %collective-permute-done.4 = f32[1,8,8,128]{3,2,1,0:T(8,128)S(1)} collective-permute-done((f32[1,8,8,128]{3,2,1,0:T(8,128)S(1)}, f32[1,8,8,128]{3,2,1,0:T(8,128)S(1)}, u32[]{:S(2)}, u32[]{:S(2)}) %collective-permute-start.4) | collective-permute-done | bytes 32800 | tf_op jit(solution)/shard_map/ppermute | solution.py:40
  39.1 1.6 %collective-permute-start.6 = (f32[1,1,8,128]{3,2,1,0:T(8,128)S(1)}, f32[1,1,8,128]{3,2,1,0:T(8,128)S(1)}, u32[]{:S(2)}, u32[]{:S(2)}) collective-permute-start(f32[1,1,8,128]{3,2,1,0:T(8,128)S(1)} %slice_bitcast_fusion.12), channel_id=1, source_target_pairs={{0,1},{1,0},{2,3},{3,2},{4,5},{5,4},{6,7},{7,6},{8,9},{9,8},{10,11... | collective-permute-start | bytes 12296 | tf_op jit(solution)/shard_map/ppermute | solution.py:40
  40.7 2.1 %collective-permute-done.6 = f32[1,1,8,128]{3,2,1,0:T(8,128)S(1)} collective-permute-done((f32[1,1,8,128]{3,2,1,0:T(8,128)S(1)}, f32[1,1,8,128]{3,2,1,0:T(8,128)S(1)}, u32[]{:S(2)}, u32[]{:S(2)}) %collective-permute-start.6) | collective-permute-done | bytes 4128 | tf_op jit(solution)/shard_map/ppermute | solution.py:40
  42.8 1.6 %collective-permute-start.7 = (f32[1,1,8,128]{3,2,1,0:T(8,128)S(1)}, f32[1,1,8,128]{3,2,1,0:T(8,128)S(1)}, u32[]{:S(2)}, u32[]{:S(2)}) collective-permute-start(f32[1,1,8,128]{3,2,1,0:T(8,128)S(1)} %slice_bitcast_fusion.11), channel_id=1, source_target_pairs={{0,1},{1,0},{2,3},{3,2},{4,5},{5,4},{6,7},{7,6},{8,9},{9,8},{10,11... | collective-permute-start | bytes 12296 | tf_op jit(solution)/shard_map/ppermute | solution.py:40
  44.4 2.1 %collective-permute-done.7 = f32[1,1,8,128]{3,2,1,0:T(8,128)S(1)} collective-permute-done((f32[1,1,8,128]{3,2,1,0:T(8,128)S(1)}, f32[1,1,8,128]{3,2,1,0:T(8,128)S(1)}, u32[]{:S(2)}, u32[]{:S(2)}) %collective-permute-start.7) | collective-permute-done | bytes 4128 | tf_op jit(solution)/shard_map/ppermute | solution.py:40
  46.6 0.5 fusion.12
  47.1 0.5 convolution_multiply_fusion
  47.6 0.5 fusion.14
  48.1 0.3 fusion.77
  48.5 0.4 convolution_bitcast_fusion
  49.0 0.4 fusion.34
  49.5 0.6 %fusion.18 = f32[8,8,8,128]{3,0,2,1:T(8,128)S(1)} fusion(f32[1,8,8,8,128]{4,1,3,2,0:T(8,128)S(1)} %convolution_bitcast_fusion, f32[8,8,8,128]{3,0,2,1:T(8,128)S(1)} %fusion.14, f32[8,8,1,1]{1,0,3,2:T(8,128)S(1)} %copy-done.2, f32[8,8,128,8]{2,3,1,0:T(8,128)S(1)} %fusion.34, f32[1,8,8,8,128]{4,3,2,1,0:T(8,128)S(1)} %copy-done.1), kind=kOutput, calls=%fused_computation.29 | convolution fusion | flops 6488064 | bytes 1310976 | tf_op jit(solution)/shard_map/ai,xayjc->xiyjc/dot_general | solution.py:98
  50.1 0.5 fusion.32
  50.8 0.5 fusion.30
  51.6 5.8 %collective-permute-done.8 = f32[8,2,17]{2,1,0:T(2,128)S(1)} collective-permute-done((f32[8,2,17]{2,1,0:T(2,128)S(1)}, f32[8,2,17]{2,1,0:T(2,128)S(1)}, u32[]{:S(2)}, u32[]{:S(2)}) %collective-permute-start.8) | collective-permute-done | bytes 1120 | tf_op jit(solution)/shard_map/ppermute | solution.py:40
  57.4 1.6 %collective-permute-start.9 = (f32[1,17]{1,0:T(1,128)S(1)}, f32[1,17]{1,0:T(1,128)S(1)}, u32[]{:S(2)}, u32[]{:S(2)}) collective-permute-start(f32[1,17]{1,0:T(1,128)S(1)} %add_bitcast_fusion), channel_id=1, source_target_pairs={{0,1},{1,0},{2,3},{3,2},{4,5},{5,4},{6,7},{7,6},{8,9},{9,8},{10,11... | collective-permute-start | bytes 212 | tf_op jit(solution)/shard_map/ppermute | solution.py:40
  59.0 2.0 %collective-permute-done.9 = f32[1,17]{1,0:T(1,128)S(1)} collective-permute-done((f32[1,17]{1,0:T(1,128)S(1)}, f32[1,17]{1,0:T(1,128)S(1)}, u32[]{:S(2)}, u32[]{:S(2)}) %collective-permute-start.9) | collective-permute-done | bytes 100 | tf_op jit(solution)/shard_map/ppermute | solution.py:40
  61.0 0.6 pad_maximum_fusion.4
  (72 shorter events, 2.7 us)
Async XLA Ops:
  0.6 0.7 %copy-start.5 = (f32[8]{0:T(128)S(1)}, f32[8]{0:T(128)}, u32[]{:S(2)}) copy-start(f32[8]{0:T(128)} %constant.62.clone) | copy-start | bytes 100
  2.5 0.7 %copy-start.4 = (f32[3,1,8,16]{3,2,1,0:T(8,128)S(1)}, f32[3,1,8,16]{3,2,1,0:T(8,128)}, u32[]{:S(2)}) copy-start(f32[3,1,8,16]{3,2,1,0:T(8,128)} %param.8) | copy-start | bytes 4612
  3.3 0.7 %copy-start.6 = (f32[8,8]{1,0:T(8,128)S(1)}, f32[8,8]{1,0:T(8,128)}, u32[]{:S(2)}) copy-start(f32[8,8]{1,0:T(8,128)} %constant.61.clone) | copy-start | bytes 772
  3.3 0.7 %copy-start.7 = (f32[8,8]{1,0:T(8,128)S(1)}, f32[8,8]{1,0:T(8,128)}, u32[]{:S(2)}) copy-start(f32[8,8]{1,0:T(8,128)} %constant.81) | copy-start | bytes 772
  4.9 1.0 %copy-start.1 = (f32[1,8,8,8,128]{4,3,2,1,0:T(8,128)S(1)}, f32[1,8,8,8,128]{4,3,2,1,0:T(8,128)}, u32[]{:S(2)}) copy-start(f32[1,8,8,8,128]{4,3,2,1,0:T(8,128)} %param.6) | copy-start | bytes 786436
  5.8 0.7 %copy-start.3 = (f32[8,8,1,1]{0,1,3,2:T(8,128)S(1)}, f32[8,8,1,1]{0,1,3,2:T(8,128)}, u32[]{:S(2)}) copy-start(f32[8,8,1,1]{0,1,3,2:T(8,128)} %constant.80) | copy-start | bytes 772
  7.4 7.4 %collective-permute-start.1 = (f32[2,8,8,128]{3,2,1,0:T(8,128)S(1)}, f32[2,8,8,128]{3,2,1,0:T(8,128)S(1)}, u32[]{:S(2)}, u32[]{:S(2)}) collective-permute-start(f32[2,8,8,128]{3,2,1,0:T(8,128)S(1)} %bitcast.297), channel_id=1, source_target_pairs={{0,30},{2,0},{4,2},{6,4},{8,6},{10,8},{12,10},{14,12},{16,14},{18,... | collective-permute-start | bytes 196616 | tf_op jit(solution)/shard_map/ppermute | solution.py:40
  12.9 6.4 %collective-permute-start = (f32[2,8,8,128]{3,2,1,0:T(8,128)S(1)}, f32[2,8,8,128]{3,2,1,0:T(8,128)S(1)}, u32[]{:S(2)}, u32[]{:S(2)}) collective-permute-start(f32[2,8,8,128]{3,2,1,0:T(8,128)S(1)} %bitcast.299), channel_id=1, source_target_pairs={{0,2},{2,4},{4,6},{6,8},{8,10},{10,12},{12,14},{14,16},{16,18},{18... | collective-permute-start | bytes 196616 | tf_op jit(solution)/shard_map/ppermute | solution.py:40
  19.5 3.7 %collective-permute-start.3 = (f32[2,1,8,128]{3,2,0,1:T(8,128)S(1)}, f32[2,1,8,128]{3,2,0,1:T(8,128)S(1)}, u32[]{:S(2)}, u32[]{:S(2)}) collective-permute-start(f32[2,1,8,128]{3,2,0,1:T(8,128)S(1)} %slice_bitcast_fusion.9), channel_id=1, source_target_pairs={{0,1},{1,0},{2,3},{3,2},{4,5},{5,4},{6,7},{7,6},{8,9},{9,8},{10,11... | collective-permute-start | bytes 24584 | tf_op jit(solution)/shard_map/ppermute | solution.py:40
  23.2 3.7 %collective-permute-start.2 = (f32[2,1,8,128]{3,2,0,1:T(8,128)S(1)}, f32[2,1,8,128]{3,2,0,1:T(8,128)S(1)}, u32[]{:S(2)}, u32[]{:S(2)}) collective-permute-start(f32[2,1,8,128]{3,2,0,1:T(8,128)S(1)} %slice_bitcast_fusion.10), channel_id=1, source_target_pairs={{0,1},{1,0},{2,3},{3,2},{4,5},{5,4},{6,7},{7,6},{8,9},{9,8},{10,11... | collective-permute-start | bytes 24584 | tf_op jit(solution)/shard_map/ppermute | solution.py:40
  27.7 0.7 %copy-start.2 = (f32[8,8,1,1]{1,0,3,2:T(8,128)S(1)}, f32[8,8,1,1]{1,0,3,2:T(8,128)}, u32[]{:S(2)}) copy-start(f32[8,8,1,1]{1,0,3,2:T(8,128)} %constant.82) | copy-start | bytes 772
  31.3 1.7 %collective-permute-start.5 = (f32[1,8,8,128]{3,2,1,0:T(8,128)S(1)}, f32[1,8,8,128]{3,2,1,0:T(8,128)S(1)}, u32[]{:S(2)}, u32[]{:S(2)}) collective-permute-start(f32[1,8,8,128]{3,2,1,0:T(8,128)S(1)} %bitcast.305), channel_id=1, source_target_pairs={{0,30},{2,0},{4,2},{6,4},{8,6},{10,8},{12,10},{14,12},{16,14},{18,... | collective-permute-start | bytes 98312 | tf_op jit(solution)/shard_map/ppermute | solution.py:40
  33.0 0.7 %copy-start.10 = (f32[8]{0:T(128)S(1)}, f32[8]{0:T(128)}, u32[]{:S(2)}) copy-start(f32[8]{0:T(128)} %constant.79) | copy-start | bytes 100
  33.0 6.1 %collective-permute-start.4 = (f32[1,8,8,128]{3,2,1,0:T(8,128)S(1)}, f32[1,8,8,128]{3,2,1,0:T(8,128)S(1)}, u32[]{:S(2)}, u32[]{:S(2)}) collective-permute-start(f32[1,8,8,128]{3,2,1,0:T(8,128)S(1)} %bitcast.315), channel_id=1, source_target_pairs={{0,2},{2,4},{4,6},{6,8},{8,10},{10,12},{12,14},{14,16},{16,18},{18... | collective-permute-start | bytes 98312 | tf_op jit(solution)/shard_map/ppermute | solution.py:40
  33.7 0.7 %copy-start.9 = (f32[8]{0:T(128)S(1)}, f32[8]{0:T(128)}, u32[]{:S(2)}) copy-start(f32[8]{0:T(128)} %constant.77) | copy-start | bytes 100
  39.1 3.7 %collective-permute-start.6 = (f32[1,1,8,128]{3,2,1,0:T(8,128)S(1)}, f32[1,1,8,128]{3,2,1,0:T(8,128)S(1)}, u32[]{:S(2)}, u32[]{:S(2)}) collective-permute-start(f32[1,1,8,128]{3,2,1,0:T(8,128)S(1)} %slice_bitcast_fusion.12), channel_id=1, source_target_pairs={{0,1},{1,0},{2,3},{3,2},{4,5},{5,4},{6,7},{7,6},{8,9},{9,8},{10,11... | collective-permute-start | bytes 12296 | tf_op jit(solution)/shard_map/ppermute | solution.py:40
  42.8 3.7 %collective-permute-start.7 = (f32[1,1,8,128]{3,2,1,0:T(8,128)S(1)}, f32[1,1,8,128]{3,2,1,0:T(8,128)S(1)}, u32[]{:S(2)}, u32[]{:S(2)}) collective-permute-start(f32[1,1,8,128]{3,2,1,0:T(8,128)S(1)} %slice_bitcast_fusion.11), channel_id=1, source_target_pairs={{0,1},{1,0},{2,3},{3,2},{4,5},{5,4},{6,7},{7,6},{8,9},{9,8},{10,11... | collective-permute-start | bytes 12296 | tf_op jit(solution)/shard_map/ppermute | solution.py:40
  47.1 1.0 %copy-start = (f32[1,8,8,8,128]{4,3,2,1,0:T(8,128)}, f32[1,8,8,8,128]{4,3,2,1,0:T(8,128)S(1)}, u32[]{:S(2)}) copy-start(f32[1,8,8,8,128]{4,3,2,1,0:T(8,128)S(1)} %fusion.12) | copy-start | bytes 786436
  50.1 0.7 %copy-start.8 = (f32[8,2,1,1]{0,1,3,2:T(2,128)S(1)}, f32[8,2,1,1]{0,1,3,2:T(2,128)}, u32[]{:S(2)}) copy-start(f32[8,2,1,1]{0,1,3,2:T(2,128)} %constant.83) | copy-start | bytes 196
  51.5 5.8 %collective-permute-start.8 = (f32[8,2,17]{2,1,0:T(2,128)S(1)}, f32[8,2,17]{2,1,0:T(2,128)S(1)}, u32[]{:S(2)}, u32[]{:S(2)}) collective-permute-start(f32[8,2,17]{2,1,0:T(2,128)S(1)} %fusion.75), channel_id=1, source_target_pairs={{0,2},{2,4},{4,6},{6,8},{8,10},{10,12},{12,14},{14,16},{16,18},{18... | collective-permute-start | bytes 3272 | tf_op jit(solution)/shard_map/ppermute | solution.py:40
  57.4 3.6 %collective-permute-start.9 = (f32[1,17]{1,0:T(1,128)S(1)}, f32[1,17]{1,0:T(1,128)S(1)}, u32[]{:S(2)}, u32[]{:S(2)}) collective-permute-start(f32[1,17]{1,0:T(1,128)S(1)} %add_bitcast_fusion), channel_id=1, source_target_pairs={{0,1},{1,0},{2,3},{3,2},{4,5},{5,4},{6,7},{7,6},{8,9},{9,8},{10,11... | collective-permute-start | bytes 212 | tf_op jit(solution)/shard_map/ppermute | solution.py:40
where the time goes:
time: 62 us; the launch traced here: 61.6 us
  waiting for transfers between devices  28.3 us (46%)
  starting transfers between devices  13.6 us (22%)
  matrix products  8.94 us (14%)
  local copies, waits for them, and re-layouts  6.76 us (11%)
  other arithmetic  2.92 us (5%)
  between operations  1.13 us (2%)
    ppermute x10, waiting for transfers between devices, passed_along(): lax.ppermute(array, axis, [(i, (i + by) % size) for i in range(size)])  28.3 us
    ppermute x10, starting transfers between devices, passed_along(): lax.ppermute(array, axis, [(i, (i + by) % size) for i in range(size)])  13.6 us
    unnamed x24, local copies, waits for them, and re-layouts  4.97 us
  transfers between devices with their start and end apart: 10, of which 10 were waited for; matrix products, arithmetic and copies ran while one was open for 1% of the time, Pallas kernels for 0%

commit v1 on v0

v1 whole, which is shorter than its diff:
```python
import functools

import jax
import jax.numpy as jnp
import numpy as np
from jax import lax
from jax.experimental import pallas as pl
from jax.experimental.pallas import tpu as pltpu
from jax.sharding import PartitionSpec as P

GLL_NODES = np.array(
    [
        -1.0,
        -0.8717401485096066,
        -0.5917001814331423,
        -0.2092992179024789,
        0.2092992179024789,
        0.5917001814331423,
        0.8717401485096066,
        1.0,
    ]
)
GLL_WEIGHTS = np.array(
    [
        0.03571428571428571,
        0.2107042271435061,
        0.3411226924835044,
        0.4124587946587038,
        0.4124587946587038,
        0.3411226924835044,
        0.2107042271435061,
        0.03571428571428571,
    ]
)
THETA = 1.65
DELTA = 1.35
RHO_FIRST = DELTA / THETA
RHO_SECOND = 1.0 / (2.0 * THETA / DELTA - RHO_FIRST)
KEEP = 1.0 + RHO_SECOND * RHO_FIRST
GAIN = 2.0 * RHO_SECOND / DELTA
EXACT = lax.Precision.HIGHEST
PTS = 8
F32 = jnp.float32


def derivative_table():
    identity = np.eye(8)
    differences = GLL_NODES[:, None] - GLL_NODES[None, :] + identity
    barycentric = 1.0 / np.prod(differences, axis=1)
    matrix = barycentric[None, :] / barycentric[:, None] / differences
    matrix = matrix * (1.0 - identity)
    row_sums = np.sum(matrix, axis=1)
    return matrix - identity * row_sums[:, None]


D = derivative_table()
W = GLL_WEIGHTS
HAT = np.stack([(1.0 - GLL_NODES) / 8.0, (1.0 + GLL_NODES) / 8.0], axis=1)
SLOPE = (-0.125, 0.125)


def small_tables(width):
    cells = width // PTS
    grad = np.tile(D.T, (1, cells))
    back = np.tile(D, (1, cells))
    square = np.tile(D * D, (1, cells))
    weight = np.tile(W[None], (PTS, cells))
    return jnp.asarray(np.stack([grad, back, square, weight]), F32)


def restrict_tables(width):
    cells = width // PTS
    hat = np.zeros((width, 128))
    slope = np.zeros((width, 128))
    for c in range(cells):
        rows = slice(c * PTS, (c + 1) * PTS)
        hat[rows, c], hat[rows, c + 1] = HAT[:, 0], HAT[:, 1]
        slope[rows, c], slope[rows, c + 1] = SLOPE
    return jnp.asarray(np.stack([hat, slope]), F32)


def dot(a, b):
    return jnp.dot(a, b, precision=EXACT, preferred_element_type=F32)


def cell_blocks(rows):
    width = rows.shape[1]
    cell = lax.broadcasted_iota(jnp.int32, rows.shape, 1) // PTS
    return jnp.concatenate(
        [jnp.where(cell == g, rows, 0.0) for g in range(width // PTS)], axis=0
    )


def contract(matrix, lines, parity):
    n = len(lines)
    half = n // 2
    plus = [lines[c] + lines[n - 1 - c] for c in range(half)]
    minus = [lines[c] - lines[n - 1 - c] for c in range(half)]
    top, low = [], []
    for r in range(half):
        even = sum(float(0.5 * (matrix[r, c] + matrix[r, n - 1 - c])) * plus[c] for c in range(half))
        odd = sum(float(0.5 * (matrix[r, c] - matrix[r, n - 1 - c])) * minus[c] for c in range(half))
        top.append(even + odd)
        low.append(even - odd if parity > 0 else odd - even)
    return top + low[::-1]


def spread_metric(metric, weight_row):
    cells = metric.shape[2]
    width = weight_row.shape[1]
    cell = lax.broadcasted_iota(jnp.int32, (cells, width), 1) // PTS
    row = lax.broadcasted_iota(jnp.int32, (cells, width), 0)
    pick = jnp.where(cell == row, 1.0, 0.0).astype(F32)
    return [dot(metric[d], pick) * weight_row for d in range(3)]


def column_masks(shape):
    lane = lax.broadcasted_iota(jnp.int32, shape, len(shape) - 1)
    up = (lane % PTS == PTS - 1) & (lane != shape[-1] - 1)
    down = (lane % PTS == 0) & (lane != 0)
    return up, down


def sum_z(v, masks):
    width = v.shape[-1]
    axis = v.ndim - 1
    up = pltpu.roll(v, width - 1, axis)
    down = pltpu.roll(v, 1, axis)
    return v + jnp.where(masks[0], up, jnp.where(masks[1], down, 0.0))


def sum_y_local(ref, ny):
    for i in range(PTS):
        low, high = ref[i, 0], ref[i, PTS - 1]
        row = lax.broadcasted_iota(jnp.int32, low.shape, 0)
        ref[i, PTS - 1] = high + jnp.where(row == ny - 1, 0.0, pltpu.roll(low, ny - 1, 0))
        ref[i, 0] = low + jnp.where(row == 0, 0.0, pltpu.roll(high, 1, 0))


def edge_planes(ref, ny):
    low = jnp.concatenate([ref[i, 0, 0:1] for i in range(PTS)], axis=0)
    high = jnp.concatenate([ref[i, PTS - 1, ny - 1 : ny] for i in range(PTS)], axis=0)
    return low, high


def stiffness(v_ref, mob, spread, out_ref, work_ref, tables):
    grad = cell_blocks(tables[0])
    back = cell_blocks(tables[1])
    _, _, ny, width = v_ref.shape
    for j in range(PTS):
        flux = contract(D, [v_ref[i, j] for i in range(PTS)], -1)
        flux = [flux[i] * (mob(i, j) * (float(W[i] * W[j]) * spread[0])) for i in range(PTS)]
        for i, value in enumerate(contract(D.T, flux, -1)):
            out_ref[i, j] = value
    for i in range(PTS):
        flux = contract(D, [v_ref[i, j] for j in range(PTS)], -1)
        flux = [flux[j] * (mob(i, j) * (float(W[i] * W[j]) * spread[1])) for j in range(PTS)]
        for j, value in enumerate(contract(D.T, flux, -1)):
            out_ref[i, j] += value
    for i in range(PTS):
        work_ref[i] = dot(v_ref[i].reshape(PTS * ny, width), grad).reshape(PTS, ny, width)
        for j in range(PTS):
            work_ref[i, j] *= mob(i, j) * (float(W[i] * W[j]) * spread[2])
        out_ref[i] += dot(work_ref[i].reshape(PTS * ny, width), back).reshape(PTS, ny, width)


def plane(ref, ny):
    return lambda i, j: ref[i, pl.ds(j, ny, stride=PTS)]


def diag_kernel(load_ref, mob_ref, metric_ref, tab_ref, fields_ref, xface_ref, yface_ref):
    tables = tab_ref[...]
    ny, width = fields_ref.shape[3:]
    spread = spread_metric(metric_ref[...], tables[3])
    squared = cell_blocks(tables[2])
    square = D * D
    mob, load = plane(mob_ref, ny), plane(load_ref, ny)
    diag_ref = fields_ref.at[1]
    for j in range(PTS):
        factor = [mob(i, j) * (float(W[i] * W[j]) * spread[0]) for i in range(PTS)]
        for i, value in enumerate(contract(square.T, factor, 1)):
            diag_ref[i, j] = value
    for i in range(PTS):
        factor = [mob(i, j) * (float(W[i] * W[j]) * spread[1]) for j in range(PTS)]
        for j, value in enumerate(contract(square.T, factor, 1)):
            diag_ref[i, j] += value
    for i in range(PTS):
        factor = jnp.concatenate(
            [mob(i, j) * (float(W[i] * W[j]) * spread[2]) for j in range(PTS)], axis=0
        )
        diag_ref[i] += dot(factor, squared).reshape(PTS, ny, width)
        fields_ref[0, i] = jnp.stack([load(i, j) for j in range(PTS)], axis=0)
    masks = column_masks((PTS, ny, width))
    for f in range(2):
        for i in range(PTS):
            fields_ref[f, i] = sum_z(fields_ref[f, i], masks)
        sum_y_local(fields_ref.at[f], ny)
        xface_ref[f, 0] = fields_ref[f, 0]
        xface_ref[f, 1] = fields_ref[f, PTS - 1]
        yface_ref[0, f], yface_ref[1, f] = edge_planes(fields_ref.at[f], ny)


def merge_kernel(side_ref, xface_ref, below_ref, above_ref, first_ref, second_ref):
    even = side_ref[0] == 0
    fields, _, _, ny, width = xface_ref.shape
    row = lax.broadcasted_iota(jnp.int32, (ny, width), 0)
    for f in range(fields):
        for j in range(PTS):
            low, high = xface_ref[f, 0, j], xface_ref[f, 1, j]
            if j == 0:
                low = low + jnp.where(row == 0, below_ref[f, 0:1], 0.0)
                high = high + jnp.where(row == 0, below_ref[f, PTS - 1 : PTS], 0.0)
            if j == PTS - 1:
                low = low + jnp.where(row == ny - 1, above_ref[f, 0:1], 0.0)
                high = high + jnp.where(row == ny - 1, above_ref[f, PTS - 1 : PTS], 0.0)
            first_ref[f, j] = jnp.where(even, high, low)
            second_ref[f, j] = jnp.where(even, low, high)


def add_arrivals(get, put, f, even, below_ref, above_ref, first_ref, second_ref, ny, width):
    row = lax.broadcasted_iota(jnp.int32, (ny, width), 0)
    for i in range(PTS):
        put(i, 0, get(i, 0) + jnp.where(row == 0, below_ref[f, i : i + 1], 0.0))
        put(
            i,
            PTS - 1,
            get(i, PTS - 1) + jnp.where(row == ny - 1, above_ref[f, i : i + 1], 0.0),
        )
    for j in range(PTS):
        first, second = first_ref[f, j], second_ref[f, j]
        put(0, j, get(0, j) + jnp.where(even, second, first))
        put(PTS - 1, j, get(PTS - 1, j) + jnp.where(even, first, second))


def smooth_kernel(
    side_ref, fields_ref, mob_ref, metric_ref, tab_ref, below_ref, above_ref, first_ref, second_ref,
    partial_ref, gain_ref, xface_ref, yface_ref, value_ref, out_ref, work_ref,
):
    tables = tab_ref[...]
    ny, width = out_ref.shape[2:]
    spread = spread_metric(metric_ref[...], tables[3])
    even = side_ref[0] == 0
    mob = plane(mob_ref, ny)
    for f, ref in ((0, partial_ref), (1, gain_ref)):
        for i in range(PTS):
            ref[i] = fields_ref[f, i]

        def put(i, j, value, ref=ref):
            ref[i, j] = value

        add_arrivals(
            lambda i, j, ref=ref: ref[i, j], put, f, even,
            below_ref, above_ref, first_ref, second_ref, ny, width,
        )
    for i in range(PTS):
        inverse = 1.0 / gain_ref[i]
        right = partial_ref[i]
        value = inverse * right * (1.0 / THETA)
        value_ref[i] = value
        partial_ref[i] = KEEP * value + GAIN * (inverse * right)
        gain_ref[i] = GAIN * inverse
    stiffness(value_ref, mob, spread, out_ref, work_ref, tables)
    masks = column_masks((PTS, ny, width))
    for i in range(PTS):
        out_ref[i] = sum_z(out_ref[i], masks)
    sum_y_local(out_ref, ny)
    xface_ref[0, 0] = out_ref[0]
    xface_ref[0, 1] = out_ref[PTS - 1]
    yface_ref[0, 0], yface_ref[1, 0] = edge_planes(out_ref, ny)
    for i in range(PTS):
        partial_ref[i] -= gain_ref[i] * out_ref[i]


def coarse_kernel(
    side_ref, load_ref, partial_ref, gain_ref, mob_ref, metric_ref, tab_ref, restrict_ref,
    below_ref, above_ref, first_ref, second_ref,
    pressure_ref, planes_ref, tops_ref, value_ref, work_ref,
):
    tables = tab_ref[...]
    ny, width = value_ref.shape[2:]
    spread = spread_metric(metric_ref[...], tables[3])
    even = side_ref[0] == 0
    mob, load = plane(mob_ref, ny), plane(load_ref, ny)
    row = lax.broadcasted_iota(jnp.int32, (ny, width), 0)
    for i in range(PTS):
        value_ref[i] = partial_ref[i]
    for i in range(PTS):
        value_ref[i, 0] -= gain_ref[i, 0] * jnp.where(row == 0, below_ref[0, i : i + 1], 0.0)
        value_ref[i, PTS - 1] -= gain_ref[i, PTS - 1] * jnp.where(
            row == ny - 1, above_ref[0, i : i + 1], 0.0
        )
    for j in range(PTS):
        first, second = first_ref[0, j], second_ref[0, j]
        value_ref[0, j] -= gain_ref[0, j] * jnp.where(even, second, first)
        value_ref[PTS - 1, j] -= gain_ref[PTS - 1, j] * jnp.where(even, first, second)
    for i in range(PTS):
        for j in range(PTS):
            pressure_ref[i, pl.ds(j, ny, stride=PTS)] = value_ref[i, j]
    grad = cell_blocks(tables[0])
    zero = jnp.zeros((ny, width), F32)
    smooth = {(p, q): zero for p in range(2) for q in range(2)}
    slope = {(p, q): zero for p in range(2) for q in range(2)}
    for j in range(PTS):
        flux = contract(D, [value_ref[i, j] for i in range(PTS)], -1)
        total = sum(flux[i] * mob(i, j) * float(W[i] * W[j]) for i in range(PTS)) * spread[0]
        for p in range(2):
            for q in range(2):
                smooth[p, q] -= float(SLOPE[p] * HAT[j, q]) * total
    for i in range(PTS):
        flux = contract(D, [value_ref[i, j] for j in range(PTS)], -1)
        total = sum(flux[j] * mob(i, j) * float(W[i] * W[j]) for j in range(PTS)) * spread[1]
        for p in range(2):
            for q in range(2):
                smooth[p, q] -= float(HAT[i, p] * SLOPE[q]) * total
    for i in range(PTS):
        work_ref[i] = dot(value_ref[i].reshape(PTS * ny, width), grad).reshape(PTS, ny, width)
        flux = [work_ref[i, j] * mob(i, j) for j in range(PTS)]
        for q in range(2):
            total = sum(float(W[i] * W[j] * HAT[j, q]) * flux[j] for j in range(PTS))
            from_load = sum(float(HAT[j, q]) * load(i, j) for j in range(PTS))
            for p in range(2):
                slope[p, q] += float(HAT[i, p]) * total
                smooth[p, q] += float(HAT[i, p]) * from_load
    keys = [(p, q) for p in range(2) for q in range(2)]
    corners = dot(jnp.concatenate([smooth[k] for k in keys], axis=0), restrict_ref[0]) - dot(
        jnp.concatenate([slope[k] * spread[2] for k in keys], axis=0), restrict_ref[1]
    )
    row = lax.broadcasted_iota(jnp.int32, (ny, corners.shape[1]), 0)
    for p in range(2):
        lower = corners[(2 * p) * ny : (2 * p + 1) * ny]
        upper = corners[(2 * p + 1) * ny : (2 * p + 2) * ny]
        planes_ref[p] = lower + jnp.where(row == 0, 0.0, pltpu.roll(upper, 1, 0))
        tops_ref[p : p + 1] = upper[ny - 1 : ny]


def call(body, outs, scratch, *args):
    specs = [
        pl.BlockSpec(memory_space=pltpu.SMEM if a.dtype == jnp.int32 else pltpu.VMEM) for a in args
    ]
    return pl.pallas_call(
        body,
        out_shape=[jax.ShapeDtypeStruct(s, F32) for s in outs],
        in_specs=specs,
        out_specs=[pl.BlockSpec(memory_space=pltpu.VMEM) for _ in outs],
        scratch_shapes=[pltpu.VMEM(s, F32) for s in scratch],
        compiler_params=pltpu.CompilerParams(vmem_limit_bytes=16 * 1024 * 1024),
    )(*args)


def from_y(faces):
    size = lax.axis_size("sub")
    if size == 2:
        got = lax.ppermute(faces, "sub", [(0, 1), (1, 0)])
        return got[1], got[0]
    below = lax.ppermute(faces[1], "sub", [(i, (i + 1) % size) for i in range(size)])
    above = lax.ppermute(faces[0], "sub", [(i, (i - 1) % size) for i in range(size)])
    return below, above


def inner_pairs(size):
    return [(i, i ^ 1) for i in range(size)]


def outer_pairs(size):
    return [(i, (i + 1) % size if i % 2 else (i - 1) % size) for i in range(size)]


def exchange(side, xface, yface):
    size = lax.axis_size("dom")
    below, above = from_y(yface)
    face = (xface.shape[0],) + xface.shape[2:]
    first, second = call(merge_kernel, [face, face], [], side, xface, below, above)
    second = lax.ppermute(second, "dom", outer_pairs(size))
    first = lax.ppermute(first, "dom", inner_pairs(size))
    return below, above, first, second


def shards(element_load, mobility, metric):
    _, _, ny, _, width = element_load.shape
    load = element_load.reshape(PTS, ny * PTS, width)
    mob = mobility.reshape(PTS, ny * PTS, width)
    metric = metric[:, 0]
    side = (lax.axis_index("dom") % 2).astype(jnp.int32).reshape(1)
    tables = small_tables(width)
    restrict = restrict_tables(width)
    field = (PTS, PTS, ny, width)
    face = (PTS, ny, width)
    fields, xface, yface = call(
        diag_kernel,
        [(2,) + field, (2, 2) + face, (2, 2, PTS, width)],
        [],
        load, mob, metric, tables,
    )
    arrivals = exchange(side, xface, yface)
    partial, gain, xface, yface = call(
        smooth_kernel,
        [field, field, (1, 2) + face, (2, 1, PTS, width)],
        [field, field, field],
        side, fields, mob, metric, tables, *arrivals,
    )
    arrivals = exchange(side, xface, yface)
    pressure, planes, tops = call(
        coarse_kernel,
        [(PTS, ny * PTS, width), (2, ny, 128), (2, 128)],
        [field, field],
        side, load, partial, gain, mob, metric, tables, restrict, *arrivals,
    )
    size = lax.axis_size("sub")
    below = lax.ppermute(tops, "sub", [(i, (i + 1) % size) for i in range(size)])
    planes = planes.at[:, 0].add(below)
    size = lax.axis_size("dom")
    upper = planes[1]
    outer = lax.ppermute(upper, "dom", [p for p in outer_pairs(size) if p[0] % 2 == 1])
    inner = lax.ppermute(upper, "dom", [p for p in inner_pairs(size) if p[0] % 2 == 0])
    coarse = planes[0] + (inner + outer)
    coarse = coarse[None, :, : width // PTS + 1]
    return pressure.reshape(element_load.shape), coarse


def solution(mesh):
    in_specs = (
        P("dom", None, "sub", None, None),
        P("dom", None, "sub", None, None),
        P(None, "dom", "sub", None),
    )
    out_specs = (P("dom", None, "sub", None, None), P("dom", "sub", None))
    return jax.shard_map(shards, mesh=mesh, in_specs=in_specs, out_specs=out_specs, check_vma=False)
```

time: 62 us -> 41.8 us (0.67)
  waiting for transfers between devices: 28.3 us -> 15.6 us
  matrix products: 8.94 us -> 0 us
  Pallas kernels: 0 us -> 3.77 us
  starting transfers between devices: 13.6 us -> 17.3 us
  other arithmetic: 2.92 us -> 0.01 us
  local copies, waits for them, and re-layouts: 6.76 us -> 3.97 us
    ppermute x10 -> x9, waiting for transfers between devices: 28.3 us -> 15.6 us  [the longest x1 5.03 us: shards(): lax.ppermute(upper, 'dom', [p for p in outer_pairs(size) if p[0] % 2 == 1])]
    dot_general x20 -> x0, matrix products: 8.94 us -> none  [the longest x2 1.23 us: assemble(): return jnp.dot(fields, face_sum_z, precision=EXACT)]
    ppermute x10 -> x9, starting transfers between devices: 13.6 us -> 17.3 us  [the longest x2 8.49 us: exchange(): second = lax.ppermute(second, 'dom', outer_pairs(size))]
    pallas_call x0 -> x5, Pallas kernels: none -> 3.77 us  [call(): pl.pallas_call(body, out_shape=[jax.ShapeDtypeStruct(s, F32) for s in out...]
    unnamed x24 -> x16, local copies, waits for them, and re-layouts: 4.97 us -> 3.33 us
    mul x5 -> x0, other arithmetic: 1.4 us -> none  [the longest x2 1.06 us: point_factors(): return spread * (mobility * quadrature)]
    mul x4 -> x0, local copies, waits for them, and re-layouts: 1.24 us -> none  [the longest x1 0.5 us: kron_tables(): squared_z = jnp.kron(identity, derivative * derivative)]
    concatenate x2 -> x0, other arithmetic: 0.75 us -> none  [the longest x1 0.6 us: coarse_gather(): jnp.concatenate([lines[:, :1] + arriving_y[:, None], lines[:, 1:-1]], axi...]
  transfers between devices with their start and end apart: 10 -> 9, of which waited for: 10 -> 6; matrix products, arithmetic and copies ran while one was open for 1% -> 0% of each run, Pallas kernels for 0% -> 0%
where the time goes in v1:
time: 41.8 us; the launch traced here: 41.4 us
  starting transfers between devices  17.3 us (41%)
  waiting for transfers between devices  15.6 us (37%)
  local copies, waits for them, and re-layouts  3.97 us (9%)
  Pallas kernels  3.77 us (9%)
  between operations  0.71 us (2%)
    ppermute x2, starting transfers between devices, exchange(): second = lax.ppermute(second, 'dom', outer_pairs(size))  8.49 us
    ppermute x1, waiting for transfers between devices, shards(): lax.ppermute(upper, 'dom', [p for p in outer_pairs(size) if p[0] % 2 == 1])  5.03 us
    ppermute x2, waiting for transfers between devices, exchange(): second = lax.ppermute(second, 'dom', outer_pairs(size))  4.69 us
    ppermute x2, starting transfers between devices, from_y(): got = lax.ppermute(faces, 'sub', [(0, 1), (1, 0)])  4.62 us
    ppermute x2, waiting for transfers between devices, from_y(): got = lax.ppermute(faces, 'sub', [(0, 1), (1, 0)])  3.85 us
    pallas_call x5, Pallas kernels, call(): pl.pallas_call(body, out_shape=[jax.ShapeDtypeStruct(s, F32) for s in out...  3.77 us
    unnamed x16, local copies, waits for them, and re-layouts  3.33 us
    ppermute x1, waiting for transfers between devices, shards(): lax.ppermute(tops, 'sub', [(i, (i + 1) % size) for i in range(size)])  2.04 us
  transfers between devices with their start and end apart: 9, of which 6 were waited for; matrix products, arithmetic and copies ran while one was open for 0% of the time, Pallas kernels for 0%

profile of v1, /device:TPU:0, one launch (start us, length us, event | category | flops | bytes accessed | tf_op | source)
XLA Modules:
  0.0 41.4 jit_solution(6565494431840756475)
XLA Ops:
  0.6 0.0 copy-start.4
  0.6 0.7 %copy-done.4 = f32[4,8,128]{2,1,0:T(8,128)S(1)} copy-done((f32[4,8,128]{2,1,0:T(8,128)S(1)}, f32[4,8,128]{2,1,0:T(8,128)}, u32[]{:S(2)}) %copy-start.4) | copy-done | bytes 16408
  1.4 0.0 copy-start
  1.4 0.9 %copy-done = f32[1,8,8,8,128]{4,3,2,1,0:T(8,128)S(1)} copy-done((f32[1,8,8,8,128]{4,3,2,1,0:T(8,128)S(1)}, f32[1,8,8,8,128]{4,3,2,1,0:T(8,128)}, u32[]{:S(2)}) %copy-start) | copy-done | bytes 262168
  2.3 0.0 copy-start.2
  2.3 0.9 %copy-done.2 = f32[1,8,8,8,128]{4,3,2,1,0:T(8,128)S(1)} copy-done((f32[1,8,8,8,128]{4,3,2,1,0:T(8,128)S(1)}, f32[1,8,8,8,128]{4,3,2,1,0:T(8,128)}, u32[]{:S(2)}) %copy-start.2) | copy-done | bytes 262168
  3.3 0.0 copy-start.6
  3.3 0.7 %copy-done.6 = f32[3,1,8,16]{3,2,1,0:T(8,128)S(1)} copy-done((f32[3,1,8,16]{3,2,1,0:T(8,128)S(1)}, f32[3,1,8,16]{3,2,1,0:T(8,128)}, u32[]{:S(2)}) %copy-start.6) | copy-done | bytes 1560
  4.0 0.0 copy-start.1
  4.0 0.9 %shard_map.68 = (f32[2,8,8,8,128]{4,3,2,1,0:T(8,128)S(1)}, f32[2,2,8,8,128]{4,3,2,1,0:T(8,128)S(1)}, f32[2,2,8,128]{3,2,1,0:T(8,128)S(1)}) custom-call(f32[8,64,128]{2,1,0:T(8,128)S(1)} %bitcast.27, f32[8,64,128]{2,1,0:T(8,128)S(1)} %bitcast.24, f32[3,8,16]{2,1,0:T(8,128)S(1)} %bitcast.29, f32[4,8,128]{2,1,0:T(8,128)S(1)} %copy-done.4), custom_call_target="tpu_custom_call" | custom-call | tf_op jit(solution)/shard_map/pallas_call | solution.py:340
  4.9 3.0 %collective-permute-start = (f32[2,2,8,128]{3,2,1,0:T(8,128)S(1)}, f32[2,2,8,128]{3,2,1,0:T(8,128)S(1)}, u32[]{:S(2)}, u32[]{:S(2)}) collective-permute-start(f32[2,2,8,128]{3,2,1,0:T(8,128)S(1)} %get-tuple-element.29), channel_id=1, source_target_pairs={{0,1},{1,0},{2,3},{3,2},{4,5},{5,4},{6,7},{7,6},{8,9},{9,8},{10,11... | collective-permute-start | bytes 49160 | tf_op jit(solution)/shard_map/ppermute | solution.py:353
  7.9 1.7 %collective-permute-done = f32[2,2,8,128]{3,2,1,0:T(8,128)S(1)} collective-permute-done((f32[2,2,8,128]{3,2,1,0:T(8,128)S(1)}, f32[2,2,8,128]{3,2,1,0:T(8,128)S(1)}, u32[]{:S(2)}, u32[]{:S(2)}) %collective-permute-start) | collective-permute-done | bytes 16416 | tf_op jit(solution)/shard_map/ppermute | solution.py:353
  9.6 0.0 copy-start.7
  9.7 0.1 collective-permute-start.1
  9.7 5.1 %collective-permute-start.2 = (f32[2,8,8,128]{3,2,1,0:T(8,128)S(1)}, f32[2,8,8,128]{3,2,1,0:T(8,128)S(1)}, u32[]{:S(2)}, u32[]{:S(2)}) collective-permute-start(f32[2,8,8,128]{3,2,1,0:T(8,128)S(1)} %get-tuple-element.32), channel_id=1, source_target_pairs={{0,30},{2,4},{4,2},{6,8},{8,6},{10,12},{12,10},{14,16},{16,14},{18... | collective-permute-start | bytes 196616 | tf_op jit(solution)/shard_map/ppermute | solution.py:373
  14.9 0.0 collective-permute-done.1.first_ref
  14.9 1.9 %collective-permute-done.2.second_ref = f32[2,8,8,128]{3,2,1,0:T(8,128)S(1)} collective-permute-done((f32[2,8,8,128]{3,2,1,0:T(8,128)S(1)}, f32[2,8,8,128]{3,2,1,0:T(8,128)S(1)}, u32[]{:S(2)}, u32[]{:S(2)}) %collective-permute-start.2) | collective-permute-done | bytes 65568 | tf_op jit(solution)/shard_map/ppermute | solution.py:373
  16.8 0.0 copy-done.1
  16.8 0.0 copy-done.7
  16.8 0.0 copy-start.3
  16.8 0.0 copy-start.5
  16.8 1.4 %shard_map.70 = (f32[8,8,8,128]{3,2,1,0:T(8,128)S(1)}, f32[8,8,8,128]{3,2,1,0:T(8,128)S(1)}, f32[1,2,8,8,128]{4,3,2,1,0:T(8,128)S(1)}, f32[2,1,8,128]{3,2,1,0:T(8,128)S(1)}) custom-call(s32[1]{0:T(128)} %bitcast.side_ref, f32[2,8,8,8,128]{4,3,2,1,0:T(8,128)S(1)} %get-tuple-element.28.fields_ref, f32[8,64,128]{2,1,0:T(8,128)S(1)} %bitcast.25, ...), custom_call_target="tpu_custom_call" | custom-call | tf_op jit(solution)/shard_map/pallas_call | solution.py:340
  18.2 1.6 %collective-permute-start.3 = (f32[2,1,8,128]{3,2,1,0:T(8,128)S(1)}, f32[2,1,8,128]{3,2,1,0:T(8,128)S(1)}, u32[]{:S(2)}, u32[]{:S(2)}) collective-permute-start(f32[2,1,8,128]{3,2,1,0:T(8,128)S(1)} %get-tuple-element.35), channel_id=1, source_target_pairs={{0,1},{1,0},{2,3},{3,2},{4,5},{5,4},{6,7},{7,6},{8,9},{9,8},{10,11... | collective-permute-start | bytes 24584 | tf_op jit(solution)/shard_map/ppermute | solution.py:353
  19.8 2.1 %collective-permute-done.3 = f32[2,1,8,128]{3,2,1,0:T(8,128)S(1)} collective-permute-done((f32[2,1,8,128]{3,2,1,0:T(8,128)S(1)}, f32[2,1,8,128]{3,2,1,0:T(8,128)S(1)}, u32[]{:S(2)}, u32[]{:S(2)}) %collective-permute-start.3) | collective-permute-done | bytes 8224 | tf_op jit(solution)/shard_map/ppermute | solution.py:353
  22.0 0.1 collective-permute-start.4
  22.1 3.4 %collective-permute-start.5 = (f32[1,8,8,128]{3,2,1,0:T(8,128)S(1)}, f32[1,8,8,128]{3,2,1,0:T(8,128)S(1)}, u32[]{:S(2)}, u32[]{:S(2)}) collective-permute-start(f32[1,8,8,128]{3,2,1,0:T(8,128)S(1)} %get-tuple-element.38), channel_id=1, source_target_pairs={{0,30},{2,4},{4,2},{6,8},{8,6},{10,12},{12,10},{14,16},{16,14},{18... | collective-permute-start | bytes 98312 | tf_op jit(solution)/shard_map/ppermute | solution.py:373
  25.4 0.0 collective-permute-done.4.first_ref
  25.4 2.7 %collective-permute-done.5.second_ref = f32[1,8,8,128]{3,2,1,0:T(8,128)S(1)} collective-permute-done((f32[1,8,8,128]{3,2,1,0:T(8,128)S(1)}, f32[1,8,8,128]{3,2,1,0:T(8,128)S(1)}, u32[]{:S(2)}, u32[]{:S(2)}) %collective-permute-start.5) | collective-permute-done | bytes 32800 | tf_op jit(solution)/shard_map/ppermute | solution.py:373
  28.2 0.0 copy-done.3
  28.2 0.0 copy-done.5
  28.2 1.4 %shard_map.72 = (f32[8,64,128]{2,1,0:T(8,128)}, f32[2,8,128]{2,1,0:T(8,128)S(1)}, f32[2,128]{1,0:T(2,128)S(1)}) custom-call(s32[1]{0:T(128)} %bitcast.side_ref, f32[8,64,128]{2,1,0:T(8,128)S(1)} %bitcast.28, f32[8,8,8,128]{3,2,1,0:T(8,128)S(1)} %get-tuple-element.33.partial_ref, f32[8,8,8,128]{3,2,1,0:T(8,128)S(1)} %get-tuple-element.34.gain_ref, ...), custom_call_target="tpu_custom_call" | custom-call | tf_op jit(solution)/shard_map/pallas_call | solution.py:340
  29.6 1.5 %collective-permute-start.6 = (f32[2,128]{1,0:T(2,128)S(1)}, f32[2,128]{1,0:T(2,128)S(1)}, u32[]{:S(2)}, u32[]{:S(2)}) collective-permute-start(f32[2,128]{1,0:T(2,128)S(1)} %get-tuple-element.41), channel_id=1, source_target_pairs={{0,1},{1,0},{2,3},{3,2},{4,5},{5,4},{6,7},{7,6},{8,9},{9,8},{10,11... | collective-permute-start | bytes 3080 | tf_op jit(solution)/shard_map/ppermute | solution.py:409
  31.1 2.0 %collective-permute-done.6 = f32[2,128]{1,0:T(2,128)S(1)} collective-permute-done((f32[2,128]{1,0:T(2,128)S(1)}, f32[2,128]{1,0:T(2,128)S(1)}, u32[]{:S(2)}, u32[]{:S(2)}) %collective-permute-start.6) | collective-permute-done | bytes 1056 | tf_op jit(solution)/shard_map/ppermute | solution.py:409
  33.2 1.3 %collective-permute-start.8 = (f32[8,128]{1,0:T(8,128)S(1)}, f32[8,128]{1,0:T(8,128)S(1)}, u32[]{:S(2)}, u32[]{:S(2)}) collective-permute-start(f32[8,128]{1,0:T(8,128)S(1)} %slice_bitcast_fusion.2), channel_id=1, source_target_pairs={{2,4},{6,8},{10,12},{14,16},{18,20},{22,24},{26,28},{30,0},{3,5},{... | collective-permute-start | bytes 12296 | tf_op jit(solution)/shard_map/ppermute | solution.py:413
  34.5 1.3 %collective-permute-start.7 = (f32[8,128]{1,0:T(8,128)S(1)}, f32[8,128]{1,0:T(8,128)S(1)}, u32[]{:S(2)}, u32[]{:S(2)}) collective-permute-start(f32[8,128]{1,0:T(8,128)S(1)} %slice_bitcast_fusion.2), channel_id=1, source_target_pairs={{0,2},{4,6},{8,10},{12,14},{16,18},{20,22},{24,26},{28,30},{1,3},{... | collective-permute-start | bytes 12296 | tf_op jit(solution)/shard_map/ppermute | solution.py:414
  35.8 5.0 %collective-permute-done.8 = f32[8,128]{1,0:T(8,128)S(1)} collective-permute-done((f32[8,128]{1,0:T(8,128)S(1)}, f32[8,128]{1,0:T(8,128)S(1)}, u32[]{:S(2)}, u32[]{:S(2)}) %collective-permute-start.8) | collective-permute-done | bytes 4128 | tf_op jit(solution)/shard_map/ppermute | solution.py:413
  40.8 0.0 collective-permute-done.7
  40.8 0.6 %slice_bitcast_fusion.6 = f32[1,8,17]{2,1,0:T(8,128)} fusion(f32[8,128]{1,0:T(8,128)S(1)} %fusion), kind=kLoop, calls=%fused_computation.7 | loop fusion | bytes 1088 | tf_op jit(solution)/shard_map/broadcast_in_dim | solution.py:416
  (9 shorter events, 0.1 us)
Async XLA Ops:
  0.6 0.7 %copy-start.4 = (f32[4,8,128]{2,1,0:T(8,128)S(1)}, f32[4,8,128]{2,1,0:T(8,128)}, u32[]{:S(2)}) copy-start(f32[4,8,128]{2,1,0:T(8,128)} %constant.49.clone.tab_ref) | copy-start | bytes 49156
  1.4 0.9 %copy-start = (f32[1,8,8,8,128]{4,3,2,1,0:T(8,128)S(1)}, f32[1,8,8,8,128]{4,3,2,1,0:T(8,128)}, u32[]{:S(2)}) copy-start(f32[1,8,8,8,128]{4,3,2,1,0:T(8,128)} %param.8) | copy-start | bytes 786436
  2.3 0.9 %copy-start.2 = (f32[1,8,8,8,128]{4,3,2,1,0:T(8,128)S(1)}, f32[1,8,8,8,128]{4,3,2,1,0:T(8,128)}, u32[]{:S(2)}) copy-start(f32[1,8,8,8,128]{4,3,2,1,0:T(8,128)} %param.7) | copy-start | bytes 786436
  3.3 0.7 %copy-start.6 = (f32[3,1,8,16]{3,2,1,0:T(8,128)S(1)}, f32[3,1,8,16]{3,2,1,0:T(8,128)}, u32[]{:S(2)}) copy-start(f32[3,1,8,16]{3,2,1,0:T(8,128)} %param.9) | copy-start | bytes 4612
  4.0 12.9 %copy-start.1 = (f32[1,8,8,8,128]{4,3,2,1,0:T(8,128)S(1)}, f32[1,8,8,8,128]{4,3,2,1,0:T(8,128)}, u32[]{:S(2)}) copy-start(f32[1,8,8,8,128]{4,3,2,1,0:T(8,128)} %param.8) | copy-start | bytes 786436
  4.9 4.8 %collective-permute-start = (f32[2,2,8,128]{3,2,1,0:T(8,128)S(1)}, f32[2,2,8,128]{3,2,1,0:T(8,128)S(1)}, u32[]{:S(2)}, u32[]{:S(2)}) collective-permute-start(f32[2,2,8,128]{3,2,1,0:T(8,128)S(1)} %get-tuple-element.29), channel_id=1, source_target_pairs={{0,1},{1,0},{2,3},{3,2},{4,5},{5,4},{6,7},{7,6},{8,9},{9,8},{10,11... | collective-permute-start | bytes 49160 | tf_op jit(solution)/shard_map/ppermute | solution.py:353
  9.6 7.2 %copy-start.7 = (f32[3,1,8,16]{3,2,1,0:T(8,128)S(1)}, f32[3,1,8,16]{3,2,1,0:T(8,128)}, u32[]{:S(2)}) copy-start(f32[3,1,8,16]{3,2,1,0:T(8,128)} %param.9) | copy-start | bytes 4612
  9.7 5.2 %collective-permute-start.1 = (f32[2,8,8,128]{3,2,1,0:T(8,128)S(1)}, f32[2,8,8,128]{3,2,1,0:T(8,128)S(1)}, u32[]{:S(2)}, u32[]{:S(2)}) collective-permute-start(f32[2,8,8,128]{3,2,1,0:T(8,128)S(1)} %get-tuple-element.31), channel_id=1, source_target_pairs={{0,2},{2,0},{4,6},{6,4},{8,10},{10,8},{12,14},{14,12},{16,18},{18,... | collective-permute-start | bytes 196616 | tf_op jit(solution)/shard_map/ppermute | solution.py:374
  9.7 7.1 %collective-permute-start.2 = (f32[2,8,8,128]{3,2,1,0:T(8,128)S(1)}, f32[2,8,8,128]{3,2,1,0:T(8,128)S(1)}, u32[]{:S(2)}, u32[]{:S(2)}) collective-permute-start(f32[2,8,8,128]{3,2,1,0:T(8,128)S(1)} %get-tuple-element.32), channel_id=1, source_target_pairs={{0,30},{2,4},{4,2},{6,8},{8,6},{10,12},{12,10},{14,16},{16,14},{18... | collective-permute-start | bytes 196616 | tf_op jit(solution)/shard_map/ppermute | solution.py:373
  16.8 11.3 %copy-start.3 = (f32[1,8,8,8,128]{4,3,2,1,0:T(8,128)S(1)}, f32[1,8,8,8,128]{4,3,2,1,0:T(8,128)}, u32[]{:S(2)}) copy-start(f32[1,8,8,8,128]{4,3,2,1,0:T(8,128)} %param.7) | copy-start | bytes 786436
  16.8 11.3 %copy-start.5 = (f32[2,128,128]{2,1,0:T(8,128)S(1)}, f32[2,128,128]{2,1,0:T(8,128)}, u32[]{:S(2)}) copy-start(f32[2,128,128]{2,1,0:T(8,128)} %constant.50.clone.restrict_ref) | copy-start | bytes 393220
  18.2 3.7 %collective-permute-start.3 = (f32[2,1,8,128]{3,2,1,0:T(8,128)S(1)}, f32[2,1,8,128]{3,2,1,0:T(8,128)S(1)}, u32[]{:S(2)}, u32[]{:S(2)}) collective-permute-start(f32[2,1,8,128]{3,2,1,0:T(8,128)S(1)} %get-tuple-element.35), channel_id=1, source_target_pairs={{0,1},{1,0},{2,3},{3,2},{4,5},{5,4},{6,7},{7,6},{8,9},{9,8},{10,11... | collective-permute-start | bytes 24584 | tf_op jit(solution)/shard_map/ppermute | solution.py:353
  22.0 3.4 %collective-permute-start.4 = (f32[1,8,8,128]{3,2,1,0:T(8,128)S(1)}, f32[1,8,8,128]{3,2,1,0:T(8,128)S(1)}, u32[]{:S(2)}, u32[]{:S(2)}) collective-permute-start(f32[1,8,8,128]{3,2,1,0:T(8,128)S(1)} %get-tuple-element.37), channel_id=1, source_target_pairs={{0,2},{2,0},{4,6},{6,4},{8,10},{10,8},{12,14},{14,12},{16,18},{18,... | collective-permute-start | bytes 98312 | tf_op jit(solution)/shard_map/ppermute | solution.py:374
  22.1 6.1 %collective-permute-start.5 = (f32[1,8,8,128]{3,2,1,0:T(8,128)S(1)}, f32[1,8,8,128]{3,2,1,0:T(8,128)S(1)}, u32[]{:S(2)}, u32[]{:S(2)}) collective-permute-start(f32[1,8,8,128]{3,2,1,0:T(8,128)S(1)} %get-tuple-element.38), channel_id=1, source_target_pairs={{0,30},{2,4},{4,2},{6,8},{8,6},{10,12},{12,10},{14,16},{16,14},{18... | collective-permute-start | bytes 98312 | tf_op jit(solution)/shard_map/ppermute | solution.py:373
  29.6 3.6 %collective-permute-start.6 = (f32[2,128]{1,0:T(2,128)S(1)}, f32[2,128]{1,0:T(2,128)S(1)}, u32[]{:S(2)}, u32[]{:S(2)}) collective-permute-start(f32[2,128]{1,0:T(2,128)S(1)} %get-tuple-element.41), channel_id=1, source_target_pairs={{0,1},{1,0},{2,3},{3,2},{4,5},{5,4},{6,7},{7,6},{8,9},{9,8},{10,11... | collective-permute-start | bytes 3080 | tf_op jit(solution)/shard_map/ppermute | solution.py:409
  33.2 7.6 %collective-permute-start.8 = (f32[8,128]{1,0:T(8,128)S(1)}, f32[8,128]{1,0:T(8,128)S(1)}, u32[]{:S(2)}, u32[]{:S(2)}) collective-permute-start(f32[8,128]{1,0:T(8,128)S(1)} %slice_bitcast_fusion.2), channel_id=1, source_target_pairs={{2,4},{6,8},{10,12},{14,16},{18,20},{22,24},{26,28},{30,0},{3,5},{... | collective-permute-start | bytes 12296 | tf_op jit(solution)/shard_map/ppermute | solution.py:413
  34.5 6.3 %collective-permute-start.7 = (f32[8,128]{1,0:T(8,128)S(1)}, f32[8,128]{1,0:T(8,128)S(1)}, u32[]{:S(2)}, u32[]{:S(2)}) collective-permute-start(f32[8,128]{1,0:T(8,128)S(1)} %slice_bitcast_fusion.2), channel_id=1, source_target_pairs={{0,2},{4,6},{8,10},{12,14},{16,18},{20,22},{24,26},{28,30},{1,3},{... | collective-permute-start | bytes 12296 | tf_op jit(solution)/shard_map/ppermute | solution.py:414

commit v2 on v1

--- a/solution.py
+++ b/solution.py
@@ -1,5 +1,3 @@
-import functools
-
 import jax
 import jax.numpy as jnp
 import numpy as np
@@ -83,6 +81,30 @@
     return jnp.dot(a, b, precision=EXACT, preferred_element_type=F32)
 
 
+def halves(a):
+    high = a.astype(jnp.bfloat16)
+    return high, (a - high.astype(F32)).astype(jnp.bfloat16)
+
+
+def paired(b):
+    high, low = halves(b)
+    return jnp.concatenate(
+        [
+            jnp.concatenate([high, low], axis=1),
+            jnp.concatenate([high, jnp.zeros_like(low)], axis=1),
+        ],
+        axis=0,
+    )
+
+
+def dot_split(a, b_pair):
+    both = jnp.dot(
+        jnp.concatenate(halves(a), axis=1), b_pair, preferred_element_type=F32
+    )
+    n = both.shape[1] // 2
+    return both[:, :n] + both[:, n:]
+
+
 def cell_blocks(rows):
     width = rows.shape[1]
     cell = lax.broadcasted_iota(jnp.int32, rows.shape, 1) // PTS
@@ -144,8 +166,8 @@
 
 
 def stiffness(v_ref, mob, spread, out_ref, work_ref, tables):
-    grad = cell_blocks(tables[0])
-    back = cell_blocks(tables[1])
+    grad = paired(cell_blocks(tables[0]))
+    back = paired(cell_blocks(tables[1]))
     _, _, ny, width = v_ref.shape
     for j in range(PTS):
         flux = contract(D, [v_ref[i, j] for i in range(PTS)], -1)
@@ -158,21 +180,77 @@
         for j, value in enumerate(contract(D.T, flux, -1)):
             out_ref[i, j] += value
     for i in range(PTS):
-        work_ref[i] = dot(v_ref[i].reshape(PTS * ny, width), grad).reshape(PTS, ny, width)
+        work_ref[i] = dot_split(v_ref[i].reshape(PTS * ny, width), grad).reshape(PTS, ny, width)
         for j in range(PTS):
             work_ref[i, j] *= mob(i, j) * (float(W[i] * W[j]) * spread[2])
-        out_ref[i] += dot(work_ref[i].reshape(PTS * ny, width), back).reshape(PTS, ny, width)
+        out_ref[i] += dot_split(work_ref[i].reshape(PTS * ny, width), back).reshape(PTS, ny, width)
 
 
 def plane(ref, ny):
     return lambda i, j: ref[i, pl.ds(j, ny, stride=PTS)]
 
 
-def diag_kernel(load_ref, mob_ref, metric_ref, tab_ref, fields_ref, xface_ref, yface_ref):
+def edge_kernel(
+    load_in, mob_in, metric_in, tab_in, restrict_in,
+    load_ref, mob_ref, spread_ref, tab_ref, restrict_ref, yface_ref, metric_ref, sems,
+):
+    copies = [
+        pltpu.make_async_copy(source, target, sems.at[n])
+        for n, (source, target) in enumerate(
+            [
+                (tab_in, tab_ref),
+                (metric_in, metric_ref),
+                (mob_in, mob_ref),
+                (load_in, load_ref),
+                (restrict_in, restrict_ref),
+            ]
+        )
+    ]
+    for copy in copies:
+        copy.start()
+    copies[0].wait()
+    copies[1].wait()
+    ny, width = spread_ref.shape[1:]
+    tables = tab_ref[...]
+    spread = spread_metric(metric_ref[...], tables[3])
+    for d in range(3):
+        spread_ref[d] = spread[d]
+    squared = paired(cell_blocks(tables[2]))
+    square = D * D
+    mob, load = plane(mob_ref, ny), plane(load_ref, ny)
+    masks = column_masks((PTS * ny, width))
+    copies[2].wait()
+    ends = (0, PTS - 1)
+    sums = [[], []]
+    for i in range(PTS):
+        factor = [mob(i, j) * (float(W[i]) * spread[1]) for j in range(PTS)]
+        for s in range(2):
+            sums[s].append(sum(float(square[j, ends[s]] * W[j]) * factor[j] for j in range(PTS)))
+    for s in range(2):
+        j = ends[s]
+        points = [mob(i, j) * float(W[i] * W[j]) for i in range(PTS)]
+        along = contract(square.T, [p * spread[0] for p in points], 1)
+        column = dot_split(jnp.concatenate([p * spread[2] for p in points], axis=0), squared)
+        total = column + jnp.concatenate([along[i] + sums[s][i] for i in range(PTS)], axis=0)
+        total = sum_z(total, masks)
+        e = 0 if s == 0 else ny - 1
+        yface_ref[s, 1] = jnp.concatenate(
+            [total[i * ny + e : i * ny + e + 1] for i in range(PTS)], axis=0
+        )
+    copies[3].wait()
+    for s in range(2):
+        e = 0 if s == 0 else ny - 1
+        row = e * PTS + ends[s]
+        value = jnp.concatenate([load_ref[i, row : row + 1] for i in range(PTS)], axis=0)
+        yface_ref[s, 0] = sum_z(value, column_masks((PTS, width)))
+    copies[4].wait()
+
+
+def diag_kernel(load_ref, mob_ref, spread_ref, tab_ref, fields_ref, xface_ref):
     tables = tab_ref[...]
     ny, width = fields_ref.shape[3:]
-    spread = spread_metric(metric_ref[...], tables[3])
-    squared = cell_blocks(tables[2])
+    spread = [spread_ref[d] for d in range(3)]
+    squared = paired(cell_blocks(tables[2]))
     square = D * D
     mob, load = plane(mob_ref, ny), plane(load_ref, ny)
     diag_ref = fields_ref.at[1]
@@ -188,7 +266,7 @@
         factor = jnp.concatenate(
             [mob(i, j) * (float(W[i] * W[j]) * spread[2]) for j in range(PTS)], axis=0
         )
-        diag_ref[i] += dot(factor, squared).reshape(PTS, ny, width)
+        diag_ref[i] += dot_split(factor, squared).reshape(PTS, ny, width)
         fields_ref[0, i] = jnp.stack([load(i, j) for j in range(PTS)], axis=0)
     masks = column_masks((PTS, ny, width))
     for f in range(2):
@@ -197,10 +275,9 @@
         sum_y_local(fields_ref.at[f], ny)
         xface_ref[f, 0] = fields_ref[f, 0]
         xface_ref[f, 1] = fields_ref[f, PTS - 1]
-        yface_ref[0, f], yface_ref[1, f] = edge_planes(fields_ref.at[f], ny)
-
-
-def merge_kernel(side_ref, xface_ref, below_ref, above_ref, first_ref, second_ref):
+
+
+def merge_kernel(side_ref, xface_ref, below_ref, above_ref, outer_ref, inner_ref):
     even = side_ref[0] == 0
     fields, _, _, ny, width = xface_ref.shape
     row = lax.broadcasted_iota(jnp.int32, (ny, width), 0)
@@ -213,11 +290,11 @@
             if j == PTS - 1:
                 low = low + jnp.where(row == ny - 1, above_ref[f, 0:1], 0.0)
                 high = high + jnp.where(row == ny - 1, above_ref[f, PTS - 1 : PTS], 0.0)
-            first_ref[f, j] = jnp.where(even, high, low)
-            second_ref[f, j] = jnp.where(even, low, high)
-
-
-def add_arrivals(get, put, f, even, below_ref, above_ref, first_ref, second_ref, ny, width):
+            inner_ref[f, j] = jnp.where(even, high, low)
+            outer_ref[f, j] = jnp.where(even, low, high)
+
+
+def add_arrivals(get, put, f, even, below_ref, above_ref, outer_ref, inner_ref, ny, width):
     row = lax.broadcasted_iota(jnp.int32, (ny, width), 0)
     for i in range(PTS):
         put(i, 0, get(i, 0) + jnp.where(row == 0, below_ref[f, i : i + 1], 0.0))
@@ -227,18 +304,18 @@
             get(i, PTS - 1) + jnp.where(row == ny - 1, above_ref[f, i : i + 1], 0.0),
         )
     for j in range(PTS):
-        first, second = first_ref[f, j], second_ref[f, j]
-        put(0, j, get(0, j) + jnp.where(even, second, first))
-        put(PTS - 1, j, get(PTS - 1, j) + jnp.where(even, first, second))
+        inner, outer = inner_ref[f, j], outer_ref[f, j]
+        put(0, j, get(0, j) + jnp.where(even, outer, inner))
+        put(PTS - 1, j, get(PTS - 1, j) + jnp.where(even, inner, outer))
 
 
 def smooth_kernel(
-    side_ref, fields_ref, mob_ref, metric_ref, tab_ref, below_ref, above_ref, first_ref, second_ref,
+    side_ref, fields_ref, mob_ref, spread_ref, tab_ref, below_ref, above_ref, outer_ref, inner_ref,
     partial_ref, gain_ref, xface_ref, yface_ref, value_ref, out_ref, work_ref,
 ):
     tables = tab_ref[...]
     ny, width = out_ref.shape[2:]
-    spread = spread_metric(metric_ref[...], tables[3])
+    spread = [spread_ref[d] for d in range(3)]
     even = side_ref[0] == 0
     mob = plane(mob_ref, ny)
     for f, ref in ((0, partial_ref), (1, gain_ref)):
@@ -250,7 +327,7 @@
 
         add_arrivals(
             lambda i, j, ref=ref: ref[i, j], put, f, even,
-            below_ref, above_ref, first_ref, second_ref, ny, width,
+            below_ref, above_ref, outer_ref, inner_ref, ny, width,
         )
     for i in range(PTS):
         inverse = 1.0 / gain_ref[i]
@@ -272,13 +349,13 @@
 
 
 def coarse_kernel(
-    side_ref, load_ref, partial_ref, gain_ref, mob_ref, metric_ref, tab_ref, restrict_ref,
-    below_ref, above_ref, first_ref, second_ref,
-    pressure_ref, planes_ref, tops_ref, value_ref, work_ref,
+    side_ref, load_ref, partial_ref, gain_ref, mob_ref, spread_ref, tab_ref, restrict_ref,
+    below_ref, above_ref, outer_ref, inner_ref,
+    pressure_out, planes_ref, tops_ref, value_ref, work_ref, pressure_ref, sem,
 ):
     tables = tab_ref[...]
     ny, width = value_ref.shape[2:]
-    spread = spread_metric(metric_ref[...], tables[3])
+    spread = [spread_ref[d] for d in range(3)]
     even = side_ref[0] == 0
     mob, load = plane(mob_ref, ny), plane(load_ref, ny)
     row = lax.broadcasted_iota(jnp.int32, (ny, width), 0)
@@ -290,13 +367,15 @@
             row == ny - 1, above_ref[0, i : i + 1], 0.0
         )
     for j in range(PTS):
-        first, second = first_ref[0, j], second_ref[0, j]
-        value_ref[0, j] -= gain_ref[0, j] * jnp.where(even, second, first)
-        value_ref[PTS - 1, j] -= gain_ref[PTS - 1, j] * jnp.where(even, first, second)
+        inner, outer = inner_ref[0, j], outer_ref[0, j]
+        value_ref[0, j] -= gain_ref[0, j] * jnp.where(even, outer, inner)
+        value_ref[PTS - 1, j] -= gain_ref[PTS - 1, j] * jnp.where(even, inner, outer)
     for i in range(PTS):
         for j in range(PTS):
             pressure_ref[i, pl.ds(j, ny, stride=PTS)] = value_ref[i, j]
-    grad = cell_blocks(tables[0])
+    copy = pltpu.make_async_copy(pressure_ref, pressure_out, sem)
+    copy.start()
+    grad = paired(cell_blocks(tables[0]))
     zero = jnp.zeros((ny, width), F32)
     smooth = {(p, q): zero for p in range(2) for q in range(2)}
     slope = {(p, q): zero for p in range(2) for q in range(2)}
@@ -313,7 +392,7 @@
             for q in range(2):
                 smooth[p, q] -= float(HAT[i, p] * SLOPE[q]) * total
     for i in range(PTS):
-        work_ref[i] = dot(value_ref[i].reshape(PTS * ny, width), grad).reshape(PTS, ny, width)
+        work_ref[i] = dot_split(value_ref[i].reshape(PTS * ny, width), grad).reshape(PTS, ny, width)
         flux = [work_ref[i, j] * mob(i, j) for j in range(PTS)]
         for q in range(2):
             total = sum(float(W[i] * W[j] * HAT[j, q]) * flux[j] for j in range(PTS))
@@ -331,18 +410,17 @@
         upper = corners[(2 * p + 1) * ny : (2 * p + 2) * ny]
         planes_ref[p] = lower + jnp.where(row == 0, 0.0, pltpu.roll(upper, 1, 0))
         tops_ref[p : p + 1] = upper[ny - 1 : ny]
-
-
-def call(body, outs, scratch, *args):
-    specs = [
-        pl.BlockSpec(memory_space=pltpu.SMEM if a.dtype == jnp.int32 else pltpu.VMEM) for a in args
-    ]
+    copy.wait()
+
+
+def call(body, outs, scratch, *args, spaces=None, out_spaces=None):
+    spaces = spaces or [pltpu.SMEM if a.dtype == jnp.int32 else pltpu.VMEM for a in args]
     return pl.pallas_call(
         body,
         out_shape=[jax.ShapeDtypeStruct(s, F32) for s in outs],
-        in_specs=specs,
-        out_specs=[pl.BlockSpec(memory_space=pltpu.VMEM) for _ in outs],
-        scratch_shapes=[pltpu.VMEM(s, F32) for s in scratch],
+        in_specs=[pl.BlockSpec(memory_space=m) for m in spaces],
+        out_specs=[pl.BlockSpec(memory_space=m) for m in out_spaces or [pltpu.VMEM] * len(outs)],
+        scratch_shapes=[pltpu.VMEM(s, F32) if isinstance(s, tuple) else s for s in scratch],
         compiler_params=pltpu.CompilerParams(vmem_limit_bytes=16 * 1024 * 1024),
     )(*args)
 
@@ -365,14 +443,13 @@
     return [(i, (i + 1) % size if i % 2 else (i - 1) % size) for i in range(size)]
 
 
-def exchange(side, xface, yface):
+def exchange_x(side, xface, below, above):
     size = lax.axis_size("dom")
-    below, above = from_y(yface)
     face = (xface.shape[0],) + xface.shape[2:]
-    first, second = call(merge_kernel, [face, face], [], side, xface, below, above)
-    second = lax.ppermute(second, "dom", outer_pairs(size))
-    first = lax.ppermute(first, "dom", inner_pairs(size))
-    return below, above, first, second
+    outer, inner = call(merge_kernel, [face, face], [], side, xface, below, above)
+    outer = lax.ppermute(outer, "dom", outer_pairs(size))
+    inner = lax.ppermute(inner, "dom", inner_pairs(size))
+    return below, above, outer, inner
 
 
 def shards(element_load, mobility, metric):
@@ -385,34 +462,39 @@
     restrict = restrict_tables(width)
     field = (PTS, PTS, ny, width)
     face = (PTS, ny, width)
-    fields, xface, yface = call(
-        diag_kernel,
-        [(2,) + field, (2, 2) + face, (2, 2, PTS, width)],
-        [],
-        load, mob, metric, tables,
-    )
-    arrivals = exchange(side, xface, yface)
+    load, mob, spread, tables, restrict, yface = call(
+        edge_kernel,
+        [load.shape, mob.shape, (3, ny, width), tables.shape, restrict.shape, (2, 2, PTS, width)],
+        [metric.shape, pltpu.SemaphoreType.DMA((5,))],
+        *(pltpu.with_memory_space_constraint(a, pltpu.HBM) for a in (load, mob, metric, tables, restrict)),
+        spaces=[pltpu.HBM] * 5,
+    )
+    arrivals = from_y(yface)
+    fields, xface = call(
+        diag_kernel, [(2,) + field, (2, 2) + face], [], load, mob, spread, tables
+    )
+    arrivals = exchange_x(side, xface, *arrivals)
     partial, gain, xface, yface = call(
         smooth_kernel,
         [field, field, (1, 2) + face, (2, 1, PTS, width)],
         [field, field, field],
-        side, fields, mob, metric, tables, *arrivals,
-    )
-    arrivals = exchange(side, xface, yface)
+        side, fields, mob, spread, tables, *arrivals,
+    )
+    arrivals = exchange_x(side, xface, *from_y(yface))
     pressure, planes, tops = call(
         coarse_kernel,
         [(PTS, ny * PTS, width), (2, ny, 128), (2, 128)],
-        [field, field],
-        side, load, partial, gain, mob, metric, tables, restrict, *arrivals,
+        [field, field, (PTS, ny * PTS, width), pltpu.SemaphoreType.DMA(())],
+        side, load, partial, gain, mob, spread, tables, restrict, *arrivals,
+        out_spaces=[pltpu.HBM, pltpu.VMEM, pltpu.VMEM],
     )
     size = lax.axis_size("sub")
     below = lax.ppermute(tops, "sub", [(i, (i + 1) % size) for i in range(size)])
     planes = planes.at[:, 0].add(below)
     size = lax.axis_size("dom")
-    upper = planes[1]
-    outer = lax.ppermute(upper, "dom", [p for p in outer_pairs(size) if p[0] % 2 == 1])
-    inner = lax.ppermute(upper, "dom", [p for p in inner_pairs(size) if p[0] % 2 == 0])
-    coarse = planes[0] + (inner + outer)
+    inner = lax.ppermute(planes[1], "dom", inner_pairs(size))
+    outer = lax.ppermute(planes[1], "dom", outer_pairs(size))
+    coarse = planes[0] + jnp.where(side == 0, outer, inner)
     coarse = coarse[None, :, : width // PTS + 1]
     return pressure.reshape(element_load.shape), coarse
 

time: 41.8 us -> 35.6 us (0.85)
  starting transfers between devices: 17.3 us -> 13.9 us
  local copies, waits for them, and re-layouts: 3.97 us -> 0.63 us
    ppermute x6, starting transfers between devices: 11.2 us -> 6.7 us  [the longest x2 5.61 us: exchange_x(): outer = lax.ppermute(outer, 'dom', outer_pairs(size))]
    unnamed x16 -> x0, local copies, waits for them, and re-layouts: 3.33 us -> none
    ppermute x6, waiting for transfers between devices: 9.72 us -> 11.7 us  [the longest x2 6.94 us: exchange_x(): outer = lax.ppermute(outer, 'dom', outer_pairs(size))]
    ppermute x2, waiting for transfers between devices: 3.85 us -> 2.79 us  [from_y(): got = lax.ppermute(faces, 'sub', [(0, 1), (1, 0)])]
    ppermute x1, starting transfers between devices: 1.52 us -> 2.08 us  [shards(): lax.ppermute(tops, 'sub', [(i, (i + 1) % size) for i in range(size)])]
    ppermute x2, starting transfers between devices: 4.62 us -> 5.12 us  [from_y(): got = lax.ppermute(faces, 'sub', [(0, 1), (1, 0)])]
    ppermute x1, waiting for transfers between devices: 2.04 us -> 1.54 us  [shards(): lax.ppermute(tops, 'sub', [(i, (i + 1) % size) for i in range(size)])]
    pallas_call x5 -> x6, Pallas kernels: 3.77 us -> 4.12 us  [call(): pl.pallas_call(body, out_shape=[jax.ShapeDtypeStruct(s, F32) for s in out...]
  transfers between devices with their start and end apart: 9 -> 9, of which waited for: 6 -> 6; matrix products, arithmetic and copies ran while one was open for 0% -> 0% of each run, Pallas kernels for 0% -> 2%
where the time goes in v2:
time: 35.6 us; the launch traced here: 35.3 us
  waiting for transfers between devices  16 us (45%)
  starting transfers between devices  13.9 us (39%)
  Pallas kernels  4.12 us (12%)
  between operations  0.68 us (2%)
  local copies, waits for them, and re-layouts  0.63 us (2%)
    ppermute x2, waiting for transfers between devices, exchange_x(): outer = lax.ppermute(outer, 'dom', outer_pairs(size))  6.94 us
    ppermute x2, starting transfers between devices, exchange_x(): outer = lax.ppermute(outer, 'dom', outer_pairs(size))  5.61 us
    ppermute x2, starting transfers between devices, from_y(): got = lax.ppermute(faces, 'sub', [(0, 1), (1, 0)])  5.12 us
    ppermute x1, waiting for transfers between devices, shards(): outer = lax.ppermute(planes[1], 'dom', outer_pairs(size))  4.71 us
    pallas_call x6, Pallas kernels, call(): pl.pallas_call(body, out_shape=[jax.ShapeDtypeStruct(s, F32) for s in out...  4.12 us
    ppermute x2, waiting for transfers between devices, from_y(): got = lax.ppermute(faces, 'sub', [(0, 1), (1, 0)])  2.79 us
    ppermute x1, starting transfers between devices, shards(): lax.ppermute(tops, 'sub', [(i, (i + 1) % size) for i in range(size)])  2.08 us
    ppermute x1, waiting for transfers between devices, shards(): lax.ppermute(tops, 'sub', [(i, (i + 1) % size) for i in range(size)])  1.54 us
  transfers between devices with their start and end apart: 9, of which 6 were waited for; matrix products, arithmetic and copies ran while one was open for 0% of the time, Pallas kernels for 2%

profile of v2, /device:TPU:0, one launch (start us, length us, event | category | flops | bytes accessed | tf_op | source)
XLA Modules:
  0.0 35.3 jit_solution(1817531875229009732)
XLA Ops:
  0.6 1.4 %shard_map.68 = (f32[8,64,128]{2,1,0:T(8,128)S(1)}, f32[8,64,128]{2,1,0:T(8,128)S(1)}, f32[3,8,128]{2,1,0:T(8,128)S(1)}, f32[4,8,128]{2,1,0:T(8,128)S(1)}, f32[2...) custom-call(f32[8,64,128]{2,1,0:T(8,128)} %bitcast.25, f32[8,64,128]{2,1,0:T(8,128)} %bitcast.26, ...), custom_call_target="tpu_custom_call" | custom-call | tf_op jit(solution)/shard_map/pallas_call | solution.py:418
  2.0 3.0 %collective-permute-start = (f32[2,2,8,128]{3,2,1,0:T(8,128)S(1)}, f32[2,2,8,128]{3,2,1,0:T(8,128)S(1)}, u32[]{:S(2)}, u32[]{:S(2)}) collective-permute-start(f32[2,2,8,128]{3,2,1,0:T(8,128)S(1)} %get-tuple-element.38), channel_id=1, source_target_pairs={{0,1},{1,0},{2,3},{3,2},{4,5},{5,4},{6,7},{7,6},{8,9},{9,8},{10,11... | collective-permute-start | bytes 49160 | tf_op jit(solution)/shard_map/ppermute | solution.py:431
  5.0 0.6 %shard_map.69 = (f32[2,8,8,8,128]{4,3,2,1,0:T(8,128)S(1)}, f32[2,2,8,8,128]{4,3,2,1,0:T(8,128)S(1)}) custom-call(f32[8,64,128]{2,1,0:T(8,128)S(1)} %get-tuple-element.33.load_ref, f32[8,64,128]{2,1,0:T(8,128)S(1)} %get-tuple-element.34.mob_ref, f32[3,8,128]{2,1,0:T(8,128)S(1)} %get-tuple-element.35.spread_ref, f32[4,8,128]{2,1,0:T(8,128)S(1)} %get-tuple-element.36.tab_ref), custom_call_target="tpu_custom_call" | custom-call | tf_op jit(solution)/shard_map/pallas_call | solution.py:418
  5.6 1.2 %collective-permute-done = f32[2,2,8,128]{3,2,1,0:T(8,128)S(1)} collective-permute-done((f32[2,2,8,128]{3,2,1,0:T(8,128)S(1)}, f32[2,2,8,128]{3,2,1,0:T(8,128)S(1)}, u32[]{:S(2)}, u32[]{:S(2)}) %collective-permute-start) | collective-permute-done | bytes 16416 | tf_op jit(solution)/shard_map/ppermute | solution.py:431
  6.8 3.4 %collective-permute-start.1 = (f32[2,8,8,128]{3,2,1,0:T(8,128)S(1)}, f32[2,8,8,128]{3,2,1,0:T(8,128)S(1)}, u32[]{:S(2)}, u32[]{:S(2)}) collective-permute-start(f32[2,8,8,128]{3,2,1,0:T(8,128)S(1)} %get-tuple-element.40), channel_id=1, source_target_pairs={{0,30},{2,4},{4,2},{6,8},{8,6},{10,12},{12,10},{14,16},{16,14},{18... | collective-permute-start | bytes 196616 | tf_op jit(solution)/shard_map/ppermute | solution.py:450
  10.2 0.0 collective-permute-start.2
  10.2 3.1 %collective-permute-done.1.outer_ref = f32[2,8,8,128]{3,2,1,0:T(8,128)S(1)} collective-permute-done((f32[2,8,8,128]{3,2,1,0:T(8,128)S(1)}, f32[2,8,8,128]{3,2,1,0:T(8,128)S(1)}, u32[]{:S(2)}, u32[]{:S(2)}) %collective-permute-start.1) | collective-permute-done | bytes 65568 | tf_op jit(solution)/shard_map/ppermute | solution.py:450
  13.2 0.0 collective-permute-done.2.inner_ref
  13.2 0.9 %shard_map.71 = (f32[8,8,8,128]{3,2,1,0:T(8,128)S(1)}, f32[8,8,8,128]{3,2,1,0:T(8,128)S(1)}, f32[1,2,8,8,128]{4,3,2,1,0:T(8,128)S(1)}, f32[2,1,8,128]{3,2,1,0:T(8,128)S(1)}) custom-call(s32[1]{0:T(128)} %bitcast.side_ref, f32[2,8,8,8,128]{4,3,2,1,0:T(8,128)S(1)} %get-tuple-element.37.fields_ref, f32[8,64,128]{2,1,0:T(8,128)S(1)} %get-tuple-element.34.mob_ref, ...), custom_call_target="tpu_custom_call" | custom-call | tf_op jit(solution)/shard_map/pallas_call | solution.py:418
  14.1 2.1 %collective-permute-start.3 = (f32[2,1,8,128]{3,2,1,0:T(8,128)S(1)}, f32[2,1,8,128]{3,2,1,0:T(8,128)S(1)}, u32[]{:S(2)}, u32[]{:S(2)}) collective-permute-start(f32[2,1,8,128]{3,2,1,0:T(8,128)S(1)} %get-tuple-element.45), channel_id=1, source_target_pairs={{0,1},{1,0},{2,3},{3,2},{4,5},{5,4},{6,7},{7,6},{8,9},{9,8},{10,11... | collective-permute-start | bytes 24584 | tf_op jit(solution)/shard_map/ppermute | solution.py:431
  16.2 1.6 %collective-permute-done.3 = f32[2,1,8,128]{3,2,1,0:T(8,128)S(1)} collective-permute-done((f32[2,1,8,128]{3,2,1,0:T(8,128)S(1)}, f32[2,1,8,128]{3,2,1,0:T(8,128)S(1)}, u32[]{:S(2)}, u32[]{:S(2)}) %collective-permute-start.3) | collective-permute-done | bytes 8224 | tf_op jit(solution)/shard_map/ppermute | solution.py:431
  17.9 2.2 %collective-permute-start.4 = (f32[1,8,8,128]{3,2,1,0:T(8,128)S(1)}, f32[1,8,8,128]{3,2,1,0:T(8,128)S(1)}, u32[]{:S(2)}, u32[]{:S(2)}) collective-permute-start(f32[1,8,8,128]{3,2,1,0:T(8,128)S(1)} %get-tuple-element.47), channel_id=1, source_target_pairs={{0,30},{2,4},{4,2},{6,8},{8,6},{10,12},{12,10},{14,16},{16,14},{18... | collective-permute-start | bytes 98312 | tf_op jit(solution)/shard_map/ppermute | solution.py:450
  20.1 0.0 collective-permute-start.5
  20.1 3.9 %collective-permute-done.4.outer_ref = f32[1,8,8,128]{3,2,1,0:T(8,128)S(1)} collective-permute-done((f32[1,8,8,128]{3,2,1,0:T(8,128)S(1)}, f32[1,8,8,128]{3,2,1,0:T(8,128)S(1)}, u32[]{:S(2)}, u32[]{:S(2)}) %collective-permute-start.4) | collective-permute-done | bytes 32800 | tf_op jit(solution)/shard_map/ppermute | solution.py:450
  24.0 0.0 collective-permute-done.5.inner_ref
  24.0 1.3 %shard_map.73 = (f32[8,64,128]{2,1,0:T(8,128)}, f32[2,8,128]{2,1,0:T(8,128)S(1)}, f32[2,128]{1,0:T(2,128)S(1)}) custom-call(s32[1]{0:T(128)} %bitcast.side_ref, f32[8,64,128]{2,1,0:T(8,128)S(1)} %get-tuple-element.33.load_ref, f32[8,8,8,128]{3,2,1,0:T(8,128)S(1)} %get-tuple-element.42.partial_ref, f32[8,8,8,128]{3,2,1,0:T(8,128)S(1)} %get-tuple-element.43.gain_ref, ...), custom_call_target="tpu_custom_call" | custom-call | tf_op jit(solution)/shard_map/pallas_call | solution.py:418
  25.3 2.1 %collective-permute-start.6 = (f32[2,128]{1,0:T(2,128)S(1)}, f32[2,128]{1,0:T(2,128)S(1)}, u32[]{:S(2)}, u32[]{:S(2)}) collective-permute-start(f32[2,128]{1,0:T(2,128)S(1)} %get-tuple-element.51), channel_id=1, source_target_pairs={{0,1},{1,0},{2,3},{3,2},{4,5},{5,4},{6,7},{7,6},{8,9},{9,8},{10,11... | collective-permute-start | bytes 3080 | tf_op jit(solution)/shard_map/ppermute | solution.py:492
  27.3 1.5 %collective-permute-done.6 = f32[2,128]{1,0:T(2,128)S(1)} collective-permute-done((f32[2,128]{1,0:T(2,128)S(1)}, f32[2,128]{1,0:T(2,128)S(1)}, u32[]{:S(2)}, u32[]{:S(2)}) %collective-permute-start.6) | collective-permute-done | bytes 1056 | tf_op jit(solution)/shard_map/ppermute | solution.py:492
  28.9 1.1 %collective-permute-start.7 = (f32[8,128]{1,0:T(8,128)S(1)}, f32[8,128]{1,0:T(8,128)S(1)}, u32[]{:S(2)}, u32[]{:S(2)}) collective-permute-start(f32[8,128]{1,0:T(8,128)S(1)} %slice_bitcast_fusion.2), channel_id=1, source_target_pairs={{0,30},{2,4},{4,2},{6,8},{8,6},{10,12},{12,10},{14,16},{16,14},{18... | collective-permute-start | bytes 12296 | tf_op jit(solution)/shard_map/ppermute | solution.py:496
  30.0 0.0 collective-permute-start.8
  30.0 4.7 %collective-permute-done.7 = f32[8,128]{1,0:T(8,128)S(1)} collective-permute-done((f32[8,128]{1,0:T(8,128)S(1)}, f32[8,128]{1,0:T(8,128)S(1)}, u32[]{:S(2)}, u32[]{:S(2)}) %collective-permute-start.7) | collective-permute-done | bytes 4128 | tf_op jit(solution)/shard_map/ppermute | solution.py:496
  34.7 0.0 collective-permute-done.8
  34.7 0.6 %slice_bitcast_fusion.6 = f32[1,8,17]{2,1,0:T(8,128)} fusion(f32[8,128]{1,0:T(8,128)S(1)} %fusion), kind=kLoop, calls=%fused_computation.7 | loop fusion | bytes 1088 | tf_op jit(solution)/shard_map/broadcast_in_dim | solution.py:498
  (9 shorter events, 0.1 us)
Async XLA Ops:
  2.0 4.8 %collective-permute-start = (f32[2,2,8,128]{3,2,1,0:T(8,128)S(1)}, f32[2,2,8,128]{3,2,1,0:T(8,128)S(1)}, u32[]{:S(2)}, u32[]{:S(2)}) collective-permute-start(f32[2,2,8,128]{3,2,1,0:T(8,128)S(1)} %get-tuple-element.38), channel_id=1, source_target_pairs={{0,1},{1,0},{2,3},{3,2},{4,5},{5,4},{6,7},{7,6},{8,9},{9,8},{10,11... | collective-permute-start | bytes 49160 | tf_op jit(solution)/shard_map/ppermute | solution.py:431
  6.8 6.5 %collective-permute-start.1 = (f32[2,8,8,128]{3,2,1,0:T(8,128)S(1)}, f32[2,8,8,128]{3,2,1,0:T(8,128)S(1)}, u32[]{:S(2)}, u32[]{:S(2)}) collective-permute-start(f32[2,8,8,128]{3,2,1,0:T(8,128)S(1)} %get-tuple-element.40), channel_id=1, source_target_pairs={{0,30},{2,4},{4,2},{6,8},{8,6},{10,12},{12,10},{14,16},{16,14},{18... | collective-permute-start | bytes 196616 | tf_op jit(solution)/shard_map/ppermute | solution.py:450
  10.2 3.1 %collective-permute-start.2 = (f32[2,8,8,128]{3,2,1,0:T(8,128)S(1)}, f32[2,8,8,128]{3,2,1,0:T(8,128)S(1)}, u32[]{:S(2)}, u32[]{:S(2)}) collective-permute-start(f32[2,8,8,128]{3,2,1,0:T(8,128)S(1)} %get-tuple-element.41), channel_id=1, source_target_pairs={{0,2},{2,0},{4,6},{6,4},{8,10},{10,8},{12,14},{14,12},{16,18},{18,... | collective-permute-start | bytes 196616 | tf_op jit(solution)/shard_map/ppermute | solution.py:451
  14.1 3.7 %collective-permute-start.3 = (f32[2,1,8,128]{3,2,1,0:T(8,128)S(1)}, f32[2,1,8,128]{3,2,1,0:T(8,128)S(1)}, u32[]{:S(2)}, u32[]{:S(2)}) collective-permute-start(f32[2,1,8,128]{3,2,1,0:T(8,128)S(1)} %get-tuple-element.45), channel_id=1, source_target_pairs={{0,1},{1,0},{2,3},{3,2},{4,5},{5,4},{6,7},{7,6},{8,9},{9,8},{10,11... | collective-permute-start | bytes 24584 | tf_op jit(solution)/shard_map/ppermute | solution.py:431
  17.9 6.1 %collective-permute-start.4 = (f32[1,8,8,128]{3,2,1,0:T(8,128)S(1)}, f32[1,8,8,128]{3,2,1,0:T(8,128)S(1)}, u32[]{:S(2)}, u32[]{:S(2)}) collective-permute-start(f32[1,8,8,128]{3,2,1,0:T(8,128)S(1)} %get-tuple-element.47), channel_id=1, source_target_pairs={{0,30},{2,4},{4,2},{6,8},{8,6},{10,12},{12,10},{14,16},{16,14},{18... | collective-permute-start | bytes 98312 | tf_op jit(solution)/shard_map/ppermute | solution.py:450
  20.1 3.9 %collective-permute-start.5 = (f32[1,8,8,128]{3,2,1,0:T(8,128)S(1)}, f32[1,8,8,128]{3,2,1,0:T(8,128)S(1)}, u32[]{:S(2)}, u32[]{:S(2)}) collective-permute-start(f32[1,8,8,128]{3,2,1,0:T(8,128)S(1)} %get-tuple-element.48), channel_id=1, source_target_pairs={{0,2},{2,0},{4,6},{6,4},{8,10},{10,8},{12,14},{14,12},{16,18},{18,... | collective-permute-start | bytes 98312 | tf_op jit(solution)/shard_map/ppermute | solution.py:451
  25.3 3.6 %collective-permute-start.6 = (f32[2,128]{1,0:T(2,128)S(1)}, f32[2,128]{1,0:T(2,128)S(1)}, u32[]{:S(2)}, u32[]{:S(2)}) collective-permute-start(f32[2,128]{1,0:T(2,128)S(1)} %get-tuple-element.51), channel_id=1, source_target_pairs={{0,1},{1,0},{2,3},{3,2},{4,5},{5,4},{6,7},{7,6},{8,9},{9,8},{10,11... | collective-permute-start | bytes 3080 | tf_op jit(solution)/shard_map/ppermute | solution.py:492
  28.9 5.8 %collective-permute-start.7 = (f32[8,128]{1,0:T(8,128)S(1)}, f32[8,128]{1,0:T(8,128)S(1)}, u32[]{:S(2)}, u32[]{:S(2)}) collective-permute-start(f32[8,128]{1,0:T(8,128)S(1)} %slice_bitcast_fusion.2), channel_id=1, source_target_pairs={{0,30},{2,4},{4,2},{6,8},{8,6},{10,12},{12,10},{14,16},{16,14},{18... | collective-permute-start | bytes 12296 | tf_op jit(solution)/shard_map/ppermute | solution.py:496
  30.0 4.7 %collective-permute-start.8 = (f32[8,128]{1,0:T(8,128)S(1)}, f32[8,128]{1,0:T(8,128)S(1)}, u32[]{:S(2)}, u32[]{:S(2)}) collective-permute-start(f32[8,128]{1,0:T(8,128)S(1)} %slice_bitcast_fusion.2), channel_id=1, source_target_pairs={{0,2},{2,0},{4,6},{6,4},{8,10},{10,8},{12,14},{14,12},{16,18},{18,... | collective-permute-start | bytes 12296 | tf_op jit(solution)/shard_map/ppermute | solution.py:495

commit v3 on v2

--- a/solution.py
+++ b/solution.py
@@ -63,7 +63,8 @@
     back = np.tile(D, (1, cells))
     square = np.tile(D * D, (1, cells))
     weight = np.tile(W[None], (PTS, cells))
-    return jnp.asarray(np.stack([grad, back, square, weight]), F32)
+    row_weight = np.tile(W[:, None], (1, width))
+    return jnp.asarray(np.stack([grad, back, square, weight, row_weight]), F32)
 
 
 def restrict_tables(width):
@@ -243,10 +244,14 @@
         row = e * PTS + ends[s]
         value = jnp.concatenate([load_ref[i, row : row + 1] for i in range(PTS)], axis=0)
         yface_ref[s, 0] = sum_z(value, column_masks((PTS, width)))
+        points = jnp.concatenate([mob_ref[i, row : row + 1] for i in range(PTS)], axis=0)
+        points = points * (float(W[ends[s]]) * tables[4])
+        yface_ref[s, 2] = points * spread[0][e : e + 1]
+        yface_ref[s, 3] = points * spread[2][e : e + 1]
     copies[4].wait()
 
 
-def diag_kernel(load_ref, mob_ref, spread_ref, tab_ref, fields_ref, xface_ref):
+def diag_kernel(load_ref, mob_ref, spread_ref, tab_ref, fields_ref, xface_ref, factor_ref):
     tables = tab_ref[...]
     ny, width = fields_ref.shape[3:]
     spread = [spread_ref[d] for d in range(3)]
@@ -275,9 +280,14 @@
         sum_y_local(fields_ref.at[f], ny)
         xface_ref[f, 0] = fields_ref[f, 0]
         xface_ref[f, 1] = fields_ref[f, PTS - 1]
-
-
-def merge_kernel(side_ref, xface_ref, below_ref, above_ref, outer_ref, inner_ref):
+    for s, i in enumerate((0, PTS - 1)):
+        for n, e in enumerate((0, ny - 1)):
+            points = mob_ref[i, e * PTS : (e + 1) * PTS] * (float(W[i]) * tables[4])
+            factor_ref[s, n] = points * spread[1][e : e + 1]
+
+
+def merge_kernel(side_ref, xface_ref, factor_ref, below_ref, above_ref, outer_ref, inner_ref):
+    below_ref, above_ref = below_ref.at[1], above_ref.at[0]
     even = side_ref[0] == 0
     fields, _, _, ny, width = xface_ref.shape
     row = lax.broadcasted_iota(jnp.int32, (ny, width), 0)
@@ -290,8 +300,14 @@
             if j == PTS - 1:
                 low = low + jnp.where(row == ny - 1, above_ref[f, 0:1], 0.0)
                 high = high + jnp.where(row == ny - 1, above_ref[f, PTS - 1 : PTS], 0.0)
-            inner_ref[f, j] = jnp.where(even, high, low)
-            outer_ref[f, j] = jnp.where(even, low, high)
+            at = (f * PTS + j) * ny
+            inner_ref[at : at + ny] = jnp.where(even, high, low)
+            outer_ref[at : at + ny] = jnp.where(even, low, high)
+    for n in range(2):
+        at = fields * PTS * ny + n * PTS
+        low, high = factor_ref[0, n], factor_ref[1, n]
+        inner_ref[at : at + PTS] = jnp.where(even, high, low)
+        outer_ref[at : at + PTS] = jnp.where(even, low, high)
 
 
 def add_arrivals(get, put, f, even, below_ref, above_ref, outer_ref, inner_ref, ny, width):
@@ -304,18 +320,53 @@
             get(i, PTS - 1) + jnp.where(row == ny - 1, above_ref[f, i : i + 1], 0.0),
         )
     for j in range(PTS):
-        inner, outer = inner_ref[f, j], outer_ref[f, j]
+        at = (f * PTS + j) * ny
+        inner, outer = inner_ref[at : at + ny], outer_ref[at : at + ny]
         put(0, j, get(0, j) + jnp.where(even, outer, inner))
         put(PTS - 1, j, get(PTS - 1, j) + jnp.where(even, inner, outer))
 
 
+def corner_sums(even, value_ref, tables, below_ref, above_ref, outer_ref, inner_ref, masks):
+    ny, width = value_ref.shape[2:]
+    ends = (0, PTS - 1)
+    grad = paired(cell_blocks(tables[0]))
+    back = paired(cell_blocks(tables[1]))
+    along_xz = [[None, None], [None, None]]
+    lines, line_factors = [], []
+    for t, ref in enumerate((below_ref, above_ref)):
+        flux = contract(D, [value_ref[i, ends[t]] for i in range(PTS)], -1)
+        flux = contract(D.T, [flux[i] * ref[2, i : i + 1] for i in range(PTS)], -1)
+        for s in range(2):
+            along_xz[s][t] = flux[ends[s]]
+            lines.append(value_ref[ends[s], ends[t]])
+            line_factors.append(jnp.broadcast_to(ref[3, ends[s] : ends[s] + 1], (ny, width)))
+    flux = dot_split(jnp.concatenate(lines, axis=0), grad) * jnp.concatenate(line_factors, axis=0)
+    flux = dot_split(flux, back)
+    along_y = [[None, None], [None, None]]
+    base = 2 * PTS * ny
+    for s in range(2):
+        gradient = contract(D, [value_ref[ends[s], j] for j in range(PTS)], -1)
+        for t in range(2):
+            at = base + t * PTS
+            inner, outer = inner_ref[at : at + PTS], outer_ref[at : at + PTS]
+            own = even if s == 0 else jnp.logical_not(even)
+            factor = jnp.where(own, outer, inner)
+            total = [gradient[j] * factor[j : j + 1] for j in range(PTS)]
+            along_y[s][t] = sum(float(D[j, ends[t]]) * total[j] for j in range(PTS))
+            n = (t * 2 + s) * ny
+            along_xz[s][t] = sum_z(along_xz[s][t] + flux[n : n + ny], masks)
+            along_y[s][t] = sum_z(along_y[s][t], masks)
+    return along_xz, along_y
+
+
 def smooth_kernel(
     side_ref, fields_ref, mob_ref, spread_ref, tab_ref, below_ref, above_ref, outer_ref, inner_ref,
-    partial_ref, gain_ref, xface_ref, yface_ref, value_ref, out_ref, work_ref,
+    partial_ref, gain_ref, to_outer_ref, to_inner_ref, yface_ref, value_ref, out_ref, work_ref,
 ):
     tables = tab_ref[...]
     ny, width = out_ref.shape[2:]
     spread = [spread_ref[d] for d in range(3)]
+    below_ref, above_ref = below_ref.at[1], above_ref.at[0]
     even = side_ref[0] == 0
     mob = plane(mob_ref, ny)
     for f, ref in ((0, partial_ref), (1, gain_ref)):
@@ -341,21 +392,36 @@
     for i in range(PTS):
         out_ref[i] = sum_z(out_ref[i], masks)
     sum_y_local(out_ref, ny)
-    xface_ref[0, 0] = out_ref[0]
-    xface_ref[0, 1] = out_ref[PTS - 1]
-    yface_ref[0, 0], yface_ref[1, 0] = edge_planes(out_ref, ny)
+    along_xz, along_y = corner_sums(
+        even, value_ref, tables, below_ref, above_ref, outer_ref, inner_ref, column_masks((ny, width))
+    )
+    row = lax.broadcasted_iota(jnp.int32, (ny, width), 0)
+    end_rows = (row == 0, row == ny - 1)
+    for j in range(PTS):
+        low, high = out_ref[0, j], out_ref[PTS - 1, j]
+        if j in (0, PTS - 1):
+            t = 0 if j == 0 else 1
+            low = low + jnp.where(end_rows[t], along_xz[0][t], 0.0)
+            high = high + jnp.where(end_rows[t], along_xz[1][t], 0.0)
+        to_inner_ref[j * ny : (j + 1) * ny] = jnp.where(even, high, low)
+        to_outer_ref[j * ny : (j + 1) * ny] = jnp.where(even, low, high)
+    for t, (e, edge) in enumerate(zip((0, ny - 1), edge_planes(out_ref, ny))):
+        at = lax.broadcasted_iota(jnp.int32, edge.shape, 0)
+        edge = edge + jnp.where(at == 0, along_y[0][t][e : e + 1], 0.0)
+        yface_ref[t, 0] = edge + jnp.where(at == PTS - 1, along_y[1][t][e : e + 1], 0.0)
     for i in range(PTS):
         partial_ref[i] -= gain_ref[i] * out_ref[i]
 
 
 def coarse_kernel(
     side_ref, load_ref, partial_ref, gain_ref, mob_ref, spread_ref, tab_ref, restrict_ref,
-    below_ref, above_ref, outer_ref, inner_ref,
+    outer_ref, below_ref, above_ref, inner_ref,
     pressure_out, planes_ref, tops_ref, value_ref, work_ref, pressure_ref, sem,
 ):
     tables = tab_ref[...]
     ny, width = value_ref.shape[2:]
     spread = [spread_ref[d] for d in range(3)]
+    below_ref, above_ref = below_ref.at[1], above_ref.at[0]
     even = side_ref[0] == 0
     mob, load = plane(mob_ref, ny), plane(load_ref, ny)
     row = lax.broadcasted_iota(jnp.int32, (ny, width), 0)
@@ -367,7 +433,7 @@
             row == ny - 1, above_ref[0, i : i + 1], 0.0
         )
     for j in range(PTS):
-        inner, outer = inner_ref[0, j], outer_ref[0, j]
+        inner, outer = inner_ref[j * ny : (j + 1) * ny], outer_ref[j * ny : (j + 1) * ny]
         value_ref[0, j] -= gain_ref[0, j] * jnp.where(even, outer, inner)
         value_ref[PTS - 1, j] -= gain_ref[PTS - 1, j] * jnp.where(even, inner, outer)
     for i in range(PTS):
@@ -427,12 +493,10 @@
 
 def from_y(faces):
     size = lax.axis_size("sub")
+    up = lax.ppermute(faces, "sub", [(i, (i + 1) % size) for i in range(size)])
     if size == 2:
-        got = lax.ppermute(faces, "sub", [(0, 1), (1, 0)])
-        return got[1], got[0]
-    below = lax.ppermute(faces[1], "sub", [(i, (i + 1) % size) for i in range(size)])
-    above = lax.ppermute(faces[0], "sub", [(i, (i - 1) % size) for i in range(size)])
-    return below, above
+        return up, up
+    return up, lax.ppermute(faces, "sub", [(i, (i - 1) % size) for i in range(size)])
 
 
 def inner_pairs(size):
@@ -443,13 +507,11 @@
     return [(i, (i + 1) % size if i % 2 else (i - 1) % size) for i in range(size)]
 
 
-def exchange_x(side, xface, below, above):
+def to_x(outer, inner):
     size = lax.axis_size("dom")
-    face = (xface.shape[0],) + xface.shape[2:]
-    outer, inner = call(merge_kernel, [face, face], [], side, xface, below, above)
     outer = lax.ppermute(outer, "dom", outer_pairs(size))
     inner = lax.ppermute(inner, "dom", inner_pairs(size))
-    return below, above, outer, inner
+    return outer, inner
 
 
 def shards(element_load, mobility, metric):
@@ -464,28 +526,30 @@
     face = (PTS, ny, width)
     load, mob, spread, tables, restrict, yface = call(
         edge_kernel,
-        [load.shape, mob.shape, (3, ny, width), tables.shape, restrict.shape, (2, 2, PTS, width)],
+        [load.shape, mob.shape, (3, ny, width), tables.shape, restrict.shape, (2, 4, PTS, width)],
         [metric.shape, pltpu.SemaphoreType.DMA((5,))],
         *(pltpu.with_memory_space_constraint(a, pltpu.HBM) for a in (load, mob, metric, tables, restrict)),
         spaces=[pltpu.HBM] * 5,
     )
-    arrivals = from_y(yface)
-    fields, xface = call(
-        diag_kernel, [(2,) + field, (2, 2) + face], [], load, mob, spread, tables
-    )
-    arrivals = exchange_x(side, xface, *arrivals)
-    partial, gain, xface, yface = call(
+    below, above = from_y(yface)
+    fields, xface, factor = call(
+        diag_kernel, [(2,) + field, (2, 2) + face, (2, 2, PTS, width)], [], load, mob, spread, tables
+    )
+    rows = (2 * PTS * ny + 2 * PTS, width)
+    outer, inner = to_x(*call(merge_kernel, [rows, rows], [], side, xface, factor, below, above))
+    partial, gain, outer, inner, yface = call(
         smooth_kernel,
-        [field, field, (1, 2) + face, (2, 1, PTS, width)],
+        [field, field, (PTS * ny, width), (PTS * ny, width), (2, 1, PTS, width)],
         [field, field, field],
-        side, fields, mob, spread, tables, *arrivals,
-    )
-    arrivals = exchange_x(side, xface, *from_y(yface))
+        side, fields, mob, spread, tables, below, above, outer, inner,
+    )
+    outer, inner = to_x(outer, inner)
+    below, above = from_y(yface)
     pressure, planes, tops = call(
         coarse_kernel,
         [(PTS, ny * PTS, width), (2, ny, 128), (2, 128)],
         [field, field, (PTS, ny * PTS, width), pltpu.SemaphoreType.DMA(())],
-        side, load, partial, gain, mob, spread, tables, restrict, *arrivals,
+        side, load, partial, gain, mob, spread, tables, restrict, outer, below, above, inner,
         out_spaces=[pltpu.HBM, pltpu.VMEM, pltpu.VMEM],
     )
     size = lax.axis_size("sub")

time: 35.6 us -> 33 us (0.927)
  waiting for transfers between devices: 16 us -> 13.2 us
    ppermute x6, waiting for transfers between devices: 9.73 us -> 6.63 us  [the longest x2 3.47 us: from_y(): up = lax.ppermute(faces, 'sub', [(i, (i + 1) % size) for i in range(size)])]
    ppermute x6, starting transfers between devices: 10.7 us -> 11.3 us  [the longest x2 6.78 us: to_x(): outer = lax.ppermute(outer, 'dom', outer_pairs(size))]
    ppermute x1, waiting for transfers between devices: 1.54 us -> 2.04 us  [shards(): lax.ppermute(tops, 'sub', [(i, (i + 1) % size) for i in range(size)])]
    ppermute x1, starting transfers between devices: 2.08 us -> 1.58 us  [shards(): lax.ppermute(tops, 'sub', [(i, (i + 1) % size) for i in range(size)])]
    pallas_call x6 -> x5, Pallas kernels: 4.12 us -> 4.15 us  [call(): pl.pallas_call(body, out_shape=[jax.ShapeDtypeStruct(s, F32) for s in out...]
  transfers between devices with their start and end apart: 9 -> 9, of which waited for: 6 -> 5; matrix products, arithmetic and copies ran while one was open for 0% -> 0% of each run, Pallas kernels for 2% -> 2%
where the time goes in v3:
time: 33 us; the launch traced here: 32.8 us
  starting transfers between devices  14.2 us (43%)
  waiting for transfers between devices  13.2 us (40%)
  Pallas kernels  4.15 us (13%)
  between operations  0.68 us (2%)
  local copies, waits for them, and re-layouts  0.63 us (2%)
    ppermute x2, starting transfers between devices, to_x(): outer = lax.ppermute(outer, 'dom', outer_pairs(size))  6.78 us
    ppermute x2, starting transfers between devices, from_y(): up = lax.ppermute(faces, 'sub', [(i, (i + 1) % size) for i in range(size)])  4.55 us
    ppermute x1, waiting for transfers between devices, shards(): outer = lax.ppermute(planes[1], 'dom', outer_pairs(size))  4.49 us
    pallas_call x5, Pallas kernels, call(): pl.pallas_call(body, out_shape=[jax.ShapeDtypeStruct(s, F32) for s in out...  4.15 us
    ppermute x2, waiting for transfers between devices, from_y(): up = lax.ppermute(faces, 'sub', [(i, (i + 1) % size) for i in range(size)])  3.47 us
    ppermute x2, waiting for transfers between devices, to_x(): outer = lax.ppermute(outer, 'dom', outer_pairs(size))  3.15 us
    ppermute x1, waiting for transfers between devices, shards(): lax.ppermute(tops, 'sub', [(i, (i + 1) % size) for i in range(size)])  2.04 us
    ppermute x1, starting transfers between devices, shards(): lax.ppermute(tops, 'sub', [(i, (i + 1) % size) for i in range(size)])  1.58 us
  transfers between devices with their start and end apart: 9, of which 5 were waited for; matrix products, arithmetic and copies ran while one was open for 0% of the time, Pallas kernels for 2%

profile of v3, /device:TPU:0, one launch (start us, length us, event | category | flops | bytes accessed | tf_op | source)
XLA Modules:
  0.0 32.8 jit_solution(10711992070382475411)
XLA Ops:
  0.6 1.4 %shard_map.68 = (f32[8,64,128]{2,1,0:T(8,128)S(1)}, f32[8,64,128]{2,1,0:T(8,128)S(1)}, f32[3,8,128]{2,1,0:T(8,128)S(1)}, f32[5,8,128]{2,1,0:T(8,128)S(1)}, f32[2...) custom-call(f32[8,64,128]{2,1,0:T(8,128)} %bitcast.17, f32[8,64,128]{2,1,0:T(8,128)} %bitcast.18, ...), custom_call_target="tpu_custom_call" | custom-call | tf_op jit(solution)/shard_map/pallas_call | solution.py:484
  2.0 3.0 %collective-permute-start = (f32[2,4,8,128]{3,2,1,0:T(8,128)S(1)}, f32[2,4,8,128]{3,2,1,0:T(8,128)S(1)}, u32[]{:S(2)}, u32[]{:S(2)}) collective-permute-start(f32[2,4,8,128]{3,2,1,0:T(8,128)S(1)} %get-tuple-element.38), channel_id=1, source_target_pairs={{0,1},{1,0},{2,3},{3,2},{4,5},{5,4},{6,7},{7,6},{8,9},{9,8},{10,11... | collective-permute-start | bytes 98312 | tf_op jit(solution)/shard_map/ppermute | solution.py:496
  5.0 0.5 %shard_map.69 = (f32[2,8,8,8,128]{4,3,2,1,0:T(8,128)S(1)}, f32[2,2,8,8,128]{4,3,2,1,0:T(8,128)S(1)}, f32[2,2,8,128]{3,2,1,0:T(8,128)S(1)}) custom-call(f32[8,64,128]{2,1,0:T(8,128)S(1)} %get-tuple-element.33.load_ref, f32[8,64,128]{2,1,0:T(8,128)S(1)} %get-tuple-element.34.mob_ref, f32[3,8,128]{2,1,0:T(8,128)S(1)} %get-tuple-element.35.spread_ref, ...), custom_call_target="tpu_custom_call" | custom-call | tf_op jit(solution)/shard_map/pallas_call | solution.py:484
  5.6 1.3 %collective-permute-done.below_ref.above_ref = f32[2,4,8,128]{3,2,1,0:T(8,128)S(1)} collective-permute-done((f32[2,4,8,128]{3,2,1,0:T(8,128)S(1)}, f32[2,4,8,128]{3,2,1,0:T(8,128)S(1)}, u32[]{:S(2)}, u32[]{:S(2)}) %collective-permute-start) | collective-permute-done | bytes 32800 | tf_op jit(solution)/shard_map/ppermute | solution.py:496
  7.0 3.4 %collective-permute-start.1 = (f32[144,128]{1,0:T(8,128)S(1)}, f32[144,128]{1,0:T(8,128)S(1)}, u32[]{:S(2)}, u32[]{:S(2)}) collective-permute-start(f32[144,128]{1,0:T(8,128)S(1)} %get-tuple-element.41), channel_id=1, source_target_pairs={{0,30},{2,4},{4,2},{6,8},{8,6},{10,12},{12,10},{14,16},{16,14},{18... | collective-permute-start | bytes 221192 | tf_op jit(solution)/shard_map/ppermute | solution.py:512
  10.3 0.0 collective-permute-start.2
  10.3 3.1 %collective-permute-done.1.outer_ref = f32[144,128]{1,0:T(8,128)S(1)} collective-permute-done((f32[144,128]{1,0:T(8,128)S(1)}, f32[144,128]{1,0:T(8,128)S(1)}, u32[]{:S(2)}, u32[]{:S(2)}) %collective-permute-start.1) | collective-permute-done | bytes 73760 | tf_op jit(solution)/shard_map/ppermute | solution.py:512
  13.5 0.0 collective-permute-done.2.inner_ref
  13.5 0.9 %shard_map.71 = (f32[8,8,8,128]{3,2,1,0:T(8,128)S(1)}, f32[8,8,8,128]{3,2,1,0:T(8,128)S(1)}, f32[64,128]{1,0:T(8,128)S(1)}, f32[64,128]{1,0:T(8,128)S(1)}, f32[2,1,8,128]{3,2,1,0:T(8,128)S(1)}) custom-call(s32[1]{0:T(128)} %bitcast.side_ref, f32[2,8,8,8,128]{4,3,2,1,0:T(8,128)S(1)} %get-tuple-element.37.fields_ref, ...), custom_call_target="tpu_custom_call" | custom-call | tf_op jit(solution)/shard_map/pallas_call | solution.py:484
  14.4 3.4 %collective-permute-start.3 = (f32[64,128]{1,0:T(8,128)S(1)}, f32[64,128]{1,0:T(8,128)S(1)}, u32[]{:S(2)}, u32[]{:S(2)}) collective-permute-start(f32[64,128]{1,0:T(8,128)S(1)} %get-tuple-element.46), channel_id=1, source_target_pairs={{0,30},{2,4},{4,2},{6,8},{8,6},{10,12},{12,10},{14,16},{16,14},{18... | collective-permute-start | bytes 98312 | tf_op jit(solution)/shard_map/ppermute | solution.py:512
  17.8 0.0 collective-permute-start.5
  17.8 1.5 %collective-permute-start.4 = (f32[2,1,8,128]{3,2,1,0:T(8,128)S(1)}, f32[2,1,8,128]{3,2,1,0:T(8,128)S(1)}, u32[]{:S(2)}, u32[]{:S(2)}) collective-permute-start(f32[2,1,8,128]{3,2,1,0:T(8,128)S(1)} %get-tuple-element.47), channel_id=1, source_target_pairs={{0,1},{1,0},{2,3},{3,2},{4,5},{5,4},{6,7},{7,6},{8,9},{9,8},{10,11... | collective-permute-start | bytes 24584 | tf_op jit(solution)/shard_map/ppermute | solution.py:496
  19.4 2.1 %collective-permute-done.4.below_ref.above_ref = f32[2,1,8,128]{3,2,1,0:T(8,128)S(1)} collective-permute-done((f32[2,1,8,128]{3,2,1,0:T(8,128)S(1)}, f32[2,1,8,128]{3,2,1,0:T(8,128)S(1)}, u32[]{:S(2)}, u32[]{:S(2)}) %collective-permute-start.4) | collective-permute-done | bytes 8224 | tf_op jit(solution)/shard_map/ppermute | solution.py:496
  21.5 0.0 collective-permute-done.3.outer_ref
  21.5 0.0 collective-permute-done.5.inner_ref
  21.5 1.3 %shard_map.72 = (f32[8,64,128]{2,1,0:T(8,128)}, f32[2,8,128]{2,1,0:T(8,128)S(1)}, f32[2,128]{1,0:T(2,128)S(1)}) custom-call(s32[1]{0:T(128)} %bitcast.side_ref, f32[8,64,128]{2,1,0:T(8,128)S(1)} %get-tuple-element.33.load_ref, f32[8,8,8,128]{3,2,1,0:T(8,128)S(1)} %get-tuple-element.43.partial_ref, f32[8,8,8,128]{3,2,1,0:T(8,128)S(1)} %get-tuple-element.44.gain_ref, ...), custom_call_target="tpu_custom_call" | custom-call | tf_op jit(solution)/shard_map/pallas_call | solution.py:484
  22.8 1.6 %collective-permute-start.6 = (f32[2,128]{1,0:T(2,128)S(1)}, f32[2,128]{1,0:T(2,128)S(1)}, u32[]{:S(2)}, u32[]{:S(2)}) collective-permute-start(f32[2,128]{1,0:T(2,128)S(1)} %get-tuple-element.51), channel_id=1, source_target_pairs={{0,1},{1,0},{2,3},{3,2},{4,5},{5,4},{6,7},{7,6},{8,9},{9,8},{10,11... | collective-permute-start | bytes 3080 | tf_op jit(solution)/shard_map/ppermute | solution.py:556
  24.4 2.0 %collective-permute-done.6 = f32[2,128]{1,0:T(2,128)S(1)} collective-permute-done((f32[2,128]{1,0:T(2,128)S(1)}, f32[2,128]{1,0:T(2,128)S(1)}, u32[]{:S(2)}, u32[]{:S(2)}) %collective-permute-start.6) | collective-permute-done | bytes 1056 | tf_op jit(solution)/shard_map/ppermute | solution.py:556
  26.4 1.3 %collective-permute-start.7 = (f32[8,128]{1,0:T(8,128)S(1)}, f32[8,128]{1,0:T(8,128)S(1)}, u32[]{:S(2)}, u32[]{:S(2)}) collective-permute-start(f32[8,128]{1,0:T(8,128)S(1)} %slice_bitcast_fusion), channel_id=1, source_target_pairs={{0,30},{2,4},{4,2},{6,8},{8,6},{10,12},{12,10},{14,16},{16,14},{18... | collective-permute-start | bytes 12296 | tf_op jit(solution)/shard_map/ppermute | solution.py:560
  27.7 0.0 collective-permute-start.8
  27.7 4.5 %collective-permute-done.7 = f32[8,128]{1,0:T(8,128)S(1)} collective-permute-done((f32[8,128]{1,0:T(8,128)S(1)}, f32[8,128]{1,0:T(8,128)S(1)}, u32[]{:S(2)}, u32[]{:S(2)}) %collective-permute-start.7) | collective-permute-done | bytes 4128 | tf_op jit(solution)/shard_map/ppermute | solution.py:560
  32.2 0.0 collective-permute-done.8
  32.3 0.6 %slice_bitcast_fusion.2 = f32[1,8,17]{2,1,0:T(8,128)} fusion(f32[8,128]{1,0:T(8,128)S(1)} %fusion), kind=kLoop, calls=%fused_computation.3 | loop fusion | bytes 1088 | tf_op jit(solution)/shard_map/broadcast_in_dim | solution.py:562
  (6 shorter events, 0.1 us)
Async XLA Ops:
  2.0 4.9 %collective-permute-start = (f32[2,4,8,128]{3,2,1,0:T(8,128)S(1)}, f32[2,4,8,128]{3,2,1,0:T(8,128)S(1)}, u32[]{:S(2)}, u32[]{:S(2)}) collective-permute-start(f32[2,4,8,128]{3,2,1,0:T(8,128)S(1)} %get-tuple-element.38), channel_id=1, source_target_pairs={{0,1},{1,0},{2,3},{3,2},{4,5},{5,4},{6,7},{7,6},{8,9},{9,8},{10,11... | collective-permute-start | bytes 98312 | tf_op jit(solution)/shard_map/ppermute | solution.py:496
  7.0 6.5 %collective-permute-start.1 = (f32[144,128]{1,0:T(8,128)S(1)}, f32[144,128]{1,0:T(8,128)S(1)}, u32[]{:S(2)}, u32[]{:S(2)}) collective-permute-start(f32[144,128]{1,0:T(8,128)S(1)} %get-tuple-element.41), channel_id=1, source_target_pairs={{0,30},{2,4},{4,2},{6,8},{8,6},{10,12},{12,10},{14,16},{16,14},{18... | collective-permute-start | bytes 221192 | tf_op jit(solution)/shard_map/ppermute | solution.py:512
  10.3 3.2 %collective-permute-start.2 = (f32[144,128]{1,0:T(8,128)S(1)}, f32[144,128]{1,0:T(8,128)S(1)}, u32[]{:S(2)}, u32[]{:S(2)}) collective-permute-start(f32[144,128]{1,0:T(8,128)S(1)} %get-tuple-element.42), channel_id=1, source_target_pairs={{0,2},{2,0},{4,6},{6,4},{8,10},{10,8},{12,14},{14,12},{16,18},{18,... | collective-permute-start | bytes 221192 | tf_op jit(solution)/shard_map/ppermute | solution.py:513
  14.4 7.0 %collective-permute-start.3 = (f32[64,128]{1,0:T(8,128)S(1)}, f32[64,128]{1,0:T(8,128)S(1)}, u32[]{:S(2)}, u32[]{:S(2)}) collective-permute-start(f32[64,128]{1,0:T(8,128)S(1)} %get-tuple-element.46), channel_id=1, source_target_pairs={{0,30},{2,4},{4,2},{6,8},{8,6},{10,12},{12,10},{14,16},{16,14},{18... | collective-permute-start | bytes 98312 | tf_op jit(solution)/shard_map/ppermute | solution.py:512
  17.8 3.7 %collective-permute-start.5 = (f32[64,128]{1,0:T(8,128)S(1)}, f32[64,128]{1,0:T(8,128)S(1)}, u32[]{:S(2)}, u32[]{:S(2)}) collective-permute-start(f32[64,128]{1,0:T(8,128)S(1)} %get-tuple-element.48), channel_id=1, source_target_pairs={{0,2},{2,0},{4,6},{6,4},{8,10},{10,8},{12,14},{14,12},{16,18},{18,... | collective-permute-start | bytes 98312 | tf_op jit(solution)/shard_map/ppermute | solution.py:513
  17.8 3.7 %collective-permute-start.4 = (f32[2,1,8,128]{3,2,1,0:T(8,128)S(1)}, f32[2,1,8,128]{3,2,1,0:T(8,128)S(1)}, u32[]{:S(2)}, u32[]{:S(2)}) collective-permute-start(f32[2,1,8,128]{3,2,1,0:T(8,128)S(1)} %get-tuple-element.47), channel_id=1, source_target_pairs={{0,1},{1,0},{2,3},{3,2},{4,5},{5,4},{6,7},{7,6},{8,9},{9,8},{10,11... | collective-permute-start | bytes 24584 | tf_op jit(solution)/shard_map/ppermute | solution.py:496
  22.8 3.6 %collective-permute-start.6 = (f32[2,128]{1,0:T(2,128)S(1)}, f32[2,128]{1,0:T(2,128)S(1)}, u32[]{:S(2)}, u32[]{:S(2)}) collective-permute-start(f32[2,128]{1,0:T(2,128)S(1)} %get-tuple-element.51), channel_id=1, source_target_pairs={{0,1},{1,0},{2,3},{3,2},{4,5},{5,4},{6,7},{7,6},{8,9},{9,8},{10,11... | collective-permute-start | bytes 3080 | tf_op jit(solution)/shard_map/ppermute | solution.py:556
  26.4 5.8 %collective-permute-start.7 = (f32[8,128]{1,0:T(8,128)S(1)}, f32[8,128]{1,0:T(8,128)S(1)}, u32[]{:S(2)}, u32[]{:S(2)}) collective-permute-start(f32[8,128]{1,0:T(8,128)S(1)} %slice_bitcast_fusion), channel_id=1, source_target_pairs={{0,30},{2,4},{4,2},{6,8},{8,6},{10,12},{12,10},{14,16},{16,14},{18... | collective-permute-start | bytes 12296 | tf_op jit(solution)/shard_map/ppermute | solution.py:560
  27.7 4.5 %collective-permute-start.8 = (f32[8,128]{1,0:T(8,128)S(1)}, f32[8,128]{1,0:T(8,128)S(1)}, u32[]{:S(2)}, u32[]{:S(2)}) collective-permute-start(f32[8,128]{1,0:T(8,128)S(1)} %slice_bitcast_fusion), channel_id=1, source_target_pairs={{0,2},{2,0},{4,6},{6,4},{8,10},{10,8},{12,14},{14,12},{16,18},{18,... | collective-permute-start | bytes 12296 | tf_op jit(solution)/shard_map/ppermute | solution.py:559

commit v4 on v3

--- a/solution.py
+++ b/solution.py
@@ -75,7 +75,7 @@
         rows = slice(c * PTS, (c + 1) * PTS)
         hat[rows, c], hat[rows, c + 1] = HAT[:, 0], HAT[:, 1]
         slope[rows, c], slope[rows, c + 1] = SLOPE
-    return jnp.asarray(np.stack([hat, slope]), F32)
+    return jnp.asarray(np.concatenate([hat, slope]), F32)
 
 
 def dot(a, b):
@@ -164,27 +164,6 @@
     low = jnp.concatenate([ref[i, 0, 0:1] for i in range(PTS)], axis=0)
     high = jnp.concatenate([ref[i, PTS - 1, ny - 1 : ny] for i in range(PTS)], axis=0)
     return low, high
-
-
-def stiffness(v_ref, mob, spread, out_ref, work_ref, tables):
-    grad = paired(cell_blocks(tables[0]))
-    back = paired(cell_blocks(tables[1]))
-    _, _, ny, width = v_ref.shape
-    for j in range(PTS):
-        flux = contract(D, [v_ref[i, j] for i in range(PTS)], -1)
-        flux = [flux[i] * (mob(i, j) * (float(W[i] * W[j]) * spread[0])) for i in range(PTS)]
-        for i, value in enumerate(contract(D.T, flux, -1)):
-            out_ref[i, j] = value
-    for i in range(PTS):
-        flux = contract(D, [v_ref[i, j] for j in range(PTS)], -1)
-        flux = [flux[j] * (mob(i, j) * (float(W[i] * W[j]) * spread[1])) for j in range(PTS)]
-        for j, value in enumerate(contract(D.T, flux, -1)):
-            out_ref[i, j] += value
-    for i in range(PTS):
-        work_ref[i] = dot_split(v_ref[i].reshape(PTS * ny, width), grad).reshape(PTS, ny, width)
-        for j in range(PTS):
-            work_ref[i, j] *= mob(i, j) * (float(W[i] * W[j]) * spread[2])
-        out_ref[i] += dot_split(work_ref[i].reshape(PTS * ny, width), back).reshape(PTS, ny, width)
 
 
 def plane(ref, ny):
@@ -310,172 +289,314 @@
         outer_ref[at : at + PTS] = jnp.where(even, low, high)
 
 
-def add_arrivals(get, put, f, even, below_ref, above_ref, outer_ref, inner_ref, ny, width):
-    row = lax.broadcasted_iota(jnp.int32, (ny, width), 0)
-    for i in range(PTS):
-        put(i, 0, get(i, 0) + jnp.where(row == 0, below_ref[f, i : i + 1], 0.0))
-        put(
-            i,
-            PTS - 1,
-            get(i, PTS - 1) + jnp.where(row == ny - 1, above_ref[f, i : i + 1], 0.0),
-        )
-    for j in range(PTS):
-        at = (f * PTS + j) * ny
-        inner, outer = inner_ref[at : at + ny], outer_ref[at : at + ny]
-        put(0, j, get(0, j) + jnp.where(even, outer, inner))
-        put(PTS - 1, j, get(PTS - 1, j) + jnp.where(even, inner, outer))
-
-
-def corner_sums(even, value_ref, tables, below_ref, above_ref, outer_ref, inner_ref, masks):
-    ny, width = value_ref.shape[2:]
-    ends = (0, PTS - 1)
-    grad = paired(cell_blocks(tables[0]))
-    back = paired(cell_blocks(tables[1]))
-    along_xz = [[None, None], [None, None]]
-    lines, line_factors = [], []
-    for t, ref in enumerate((below_ref, above_ref)):
-        flux = contract(D, [value_ref[i, ends[t]] for i in range(PTS)], -1)
-        flux = contract(D.T, [flux[i] * ref[2, i : i + 1] for i in range(PTS)], -1)
-        for s in range(2):
-            along_xz[s][t] = flux[ends[s]]
-            lines.append(value_ref[ends[s], ends[t]])
-            line_factors.append(jnp.broadcast_to(ref[3, ends[s] : ends[s] + 1], (ny, width)))
-    flux = dot_split(jnp.concatenate(lines, axis=0), grad) * jnp.concatenate(line_factors, axis=0)
-    flux = dot_split(flux, back)
-    along_y = [[None, None], [None, None]]
-    base = 2 * PTS * ny
-    for s in range(2):
-        gradient = contract(D, [value_ref[ends[s], j] for j in range(PTS)], -1)
-        for t in range(2):
-            at = base + t * PTS
-            inner, outer = inner_ref[at : at + PTS], outer_ref[at : at + PTS]
-            own = even if s == 0 else jnp.logical_not(even)
-            factor = jnp.where(own, outer, inner)
-            total = [gradient[j] * factor[j : j + 1] for j in range(PTS)]
-            along_y[s][t] = sum(float(D[j, ends[t]]) * total[j] for j in range(PTS))
-            n = (t * 2 + s) * ny
-            along_xz[s][t] = sum_z(along_xz[s][t] + flux[n : n + ny], masks)
-            along_y[s][t] = sum_z(along_y[s][t], masks)
-    return along_xz, along_y
-
-
-def smooth_kernel(
-    side_ref, fields_ref, mob_ref, spread_ref, tab_ref, below_ref, above_ref, outer_ref, inner_ref,
-    partial_ref, gain_ref, to_outer_ref, to_inner_ref, yface_ref, value_ref, out_ref, work_ref,
+def inside_kernel(
+    fields_ref, mob_ref, spread_ref, tab_ref, below_ref, above_ref,
+    rough_ref, value_ref, partial_ref, gain_ref, out_ref, pair_ref, work_ref,
 ):
+    below_ref, above_ref = below_ref.at[1], above_ref.at[0]
     tables = tab_ref[...]
     ny, width = out_ref.shape[2:]
     spread = [spread_ref[d] for d in range(3)]
+    mob = plane(mob_ref, ny)
+    row = lax.broadcasted_iota(jnp.int32, (ny, width), 0)
+    zero = jnp.zeros((ny, width), F32)
+    for i in range(PTS):
+        for j in range(PTS):
+            sums = [fields_ref[f, i, j] for f in range(2)]
+            for f in range(2):
+                if j == 0:
+                    sums[f] += jnp.where(row == 0, below_ref[f, i : i + 1], 0.0)
+                if j == PTS - 1:
+                    sums[f] += jnp.where(row == ny - 1, above_ref[f, i : i + 1], 0.0)
+            if i in (0, PTS - 1):
+                for f in range(2):
+                    rough_ref[f, 0 if i == 0 else 1, j] = sums[f]
+                value_ref[i, j] = partial_ref[i, j] = gain_ref[i, j] = zero
+            else:
+                value_ref[i, j], partial_ref[i, j], gain_ref[i, j] = first_step(*sums)
+    grad = paired(cell_blocks(tables[0]))
+    back = paired(cell_blocks(tables[1]))
+    for j in range(PTS):
+        factor = [mob(i, j) * (float(W[i] * W[j]) * spread[0]) for i in range(PTS)]
+        for n, (p, q) in enumerate(((0, 0), (0, PTS - 1), (PTS - 1, PTS - 1))):
+            pair_ref[n, j] = sum(float(D[a, p] * D[a, q]) * factor[a] for a in range(PTS))
+        flux = contract(D, [value_ref[i, j] for i in range(PTS)], -1)
+        flux = [flux[i] * factor[i] for i in range(PTS)]
+        for i, value in enumerate(contract(D.T, flux, -1)):
+            out_ref[i, j] = value
+    for i in range(1, PTS - 1):
+        flux = contract(D, [value_ref[i, j] for j in range(PTS)], -1)
+        flux = [flux[j] * (mob(i, j) * (float(W[i] * W[j]) * spread[1])) for j in range(PTS)]
+        for j, value in enumerate(contract(D.T, flux, -1)):
+            out_ref[i, j] += value
+        work_ref[...] = dot_split(value_ref[i].reshape(PTS * ny, width), grad).reshape(PTS, ny, width)
+        for j in range(PTS):
+            work_ref[j] *= mob(i, j) * (float(W[i] * W[j]) * spread[2])
+        out_ref[i] += dot_split(work_ref[...].reshape(PTS * ny, width), back).reshape(PTS, ny, width)
+
+
+def first_step(right, diagonal):
+    inverse = 1.0 / diagonal
+    scaled = inverse * right
+    value = scaled * (1.0 / THETA)
+    return value, KEEP * value + GAIN * scaled, GAIN * inverse
+
+
+def faces_kernel(
+    side_ref, rough_ref, value_ref, out_ref, pair_ref, mob_ref, spread_ref, tab_ref,
+    below_ref, above_ref, outer_ref, inner_ref,
+    to_outer_ref, to_inner_ref, yface_ref, vface_ref, fface_ref, pface_ref, gface_ref, line_ref,
+):
     below_ref, above_ref = below_ref.at[1], above_ref.at[0]
     even = side_ref[0] == 0
+    tables = tab_ref[...]
+    ny, width = out_ref.shape[2:]
+    spread = [spread_ref[d] for d in range(3)]
     mob = plane(mob_ref, ny)
-    for f, ref in ((0, partial_ref), (1, gain_ref)):
-        for i in range(PTS):
-            ref[i] = fields_ref[f, i]
-
-        def put(i, j, value, ref=ref):
-            ref[i, j] = value
-
-        add_arrivals(
-            lambda i, j, ref=ref: ref[i, j], put, f, even,
-            below_ref, above_ref, outer_ref, inner_ref, ny, width,
-        )
-    for i in range(PTS):
-        inverse = 1.0 / gain_ref[i]
-        right = partial_ref[i]
-        value = inverse * right * (1.0 / THETA)
-        value_ref[i] = value
-        partial_ref[i] = KEEP * value + GAIN * (inverse * right)
-        gain_ref[i] = GAIN * inverse
-    stiffness(value_ref, mob, spread, out_ref, work_ref, tables)
-    masks = column_masks((PTS, ny, width))
-    for i in range(PTS):
-        out_ref[i] = sum_z(out_ref[i], masks)
-    sum_y_local(out_ref, ny)
-    along_xz, along_y = corner_sums(
-        even, value_ref, tables, below_ref, above_ref, outer_ref, inner_ref, column_masks((ny, width))
-    )
+    ends = (0, PTS - 1)
+    rows = (0, ny - 1)
     row = lax.broadcasted_iota(jnp.int32, (ny, width), 0)
-    end_rows = (row == 0, row == ny - 1)
+    masks = column_masks((ny, width))
+
+    def arrived(at, count):
+        inner, outer = inner_ref[at : at + count], outer_ref[at : at + count]
+        return jnp.where(even, outer, inner), jnp.where(even, inner, outer)
+
+    value = [[None] * PTS, [None] * PTS]
     for j in range(PTS):
-        low, high = out_ref[0, j], out_ref[PTS - 1, j]
-        if j in (0, PTS - 1):
-            t = 0 if j == 0 else 1
-            low = low + jnp.where(end_rows[t], along_xz[0][t], 0.0)
-            high = high + jnp.where(end_rows[t], along_xz[1][t], 0.0)
+        load = arrived(j * ny, ny)
+        diagonal = arrived((PTS + j) * ny, ny)
+        for s in range(2):
+            value[s][j], pface_ref[s, j], gface_ref[s, j] = first_step(
+                rough_ref[0, s, j] + load[s], rough_ref[1, s, j] + diagonal[s]
+            )
+            vface_ref[s, j] = value[s][j]
+    lines = [value[s][j] for s in range(2) for j in range(PTS)]
+    factors = [
+        mob(ends[s], j) * (float(W[ends[s]] * W[j]) * spread[2]) for s in range(2) for j in range(PTS)
+    ]
+    for s in range(2):
+        for t, ref in enumerate((below_ref, above_ref)):
+            lines.append(value[s][ends[t]])
+            factors.append(jnp.broadcast_to(ref[3, ends[s] : ends[s] + 1], (ny, width)))
+    grad = paired(cell_blocks(tables[0]))
+    back = paired(cell_blocks(tables[1]))
+    flux = dot_split(jnp.concatenate(lines, axis=0), grad) * jnp.concatenate(factors, axis=0)
+    line_ref[...] = dot_split(flux, back)
+    edge_y = [[None, None], [None, None]]
+    total = [[None] * PTS, [None] * PTS]
+    for s in range(2):
+        gradient = contract(D, value[s], -1)
+        flux = [
+            gradient[j] * (mob(ends[s], j) * (float(W[ends[s]] * W[j]) * spread[1])) for j in range(PTS)
+        ]
+        total[s] = contract(D.T, flux, -1)
+        for t in range(2):
+            factor = arrived(2 * PTS * ny + t * PTS, PTS)[s]
+            edge_y[s][t] = sum(
+                float(D[j, ends[t]]) * (gradient[j] * factor[j : j + 1]) for j in range(PTS)
+            )[rows[t] : rows[t] + 1]
+    for j in range(PTS):
+        total[0][j] += out_ref[0, j] + pair_ref[0, j] * value[0][j] + pair_ref[1, j] * value[1][j]
+        total[1][j] += out_ref[PTS - 1, j] + pair_ref[1, j] * value[0][j] + pair_ref[2, j] * value[1][j]
+    for s in range(2):
+        for j in range(PTS):
+            at = (s * PTS + j) * ny
+            total[s][j] += line_ref[at : at + ny]
+    for t in range(2):
+        j = ends[t]
+        flux = [
+            mob(a, j)
+            * (float(W[a] * W[j]) * spread[0])
+            * (float(D[a, 0]) * value[0][j] + float(D[a, PTS - 1]) * value[1][j])
+            for a in range(PTS)
+        ]
+        flux = contract(D.T, flux, -1)
+        edge = [total[0][j]] + [out_ref[i, j] + flux[i] for i in range(1, PTS - 1)] + [total[1][j]]
+        edge = [v[rows[t] : rows[t] + 1] for v in edge]
+        edge[0] += edge_y[0][t]
+        edge[PTS - 1] += edge_y[1][t]
+        yface_ref[t, 0] = sum_z(jnp.concatenate(edge, axis=0), column_masks((PTS, width)))
+    extra = [[None, None], [None, None]]
+    for t, ref in enumerate((below_ref, above_ref)):
+        j = ends[t]
+        points = [value[0][j]] + [value_ref[i, j] for i in range(1, PTS - 1)] + [value[1][j]]
+        flux = contract(D, points, -1)
+        flux = contract(D.T, [flux[i] * ref[2, i : i + 1] for i in range(PTS)], -1)
+        for s in range(2):
+            at = (2 * PTS + 2 * s + t) * ny
+            extra[s][t] = sum_z(flux[ends[s]] + line_ref[at : at + ny], masks)
+            extra[s][t] = jnp.where(row == rows[t], extra[s][t], 0.0)
+    for s in range(2):
+        for j in range(PTS):
+            total[s][j] = sum_z(total[s][j], masks)
+        low, high = total[s][0], total[s][PTS - 1]
+        total[s][PTS - 1] = high + jnp.where(row == ny - 1, 0.0, pltpu.roll(low, ny - 1, 0))
+        total[s][0] = low + jnp.where(row == 0, 0.0, pltpu.roll(high, 1, 0))
+    for j in range(PTS):
+        fface_ref[0, j], fface_ref[1, j] = total[0][j], total[1][j]
+        low, high = total[0][j], total[1][j]
+        if j in ends:
+            t = ends.index(j)
+            low, high = low + extra[0][t], high + extra[1][t]
         to_inner_ref[j * ny : (j + 1) * ny] = jnp.where(even, high, low)
         to_outer_ref[j * ny : (j + 1) * ny] = jnp.where(even, low, high)
-    for t, (e, edge) in enumerate(zip((0, ny - 1), edge_planes(out_ref, ny))):
-        at = lax.broadcasted_iota(jnp.int32, edge.shape, 0)
-        edge = edge + jnp.where(at == 0, along_y[0][t][e : e + 1], 0.0)
-        yface_ref[t, 0] = edge + jnp.where(at == PTS - 1, along_y[1][t][e : e + 1], 0.0)
-    for i in range(PTS):
-        partial_ref[i] -= gain_ref[i] * out_ref[i]
-
-
-def coarse_kernel(
-    side_ref, load_ref, partial_ref, gain_ref, mob_ref, spread_ref, tab_ref, restrict_ref,
-    outer_ref, below_ref, above_ref, inner_ref,
-    pressure_out, planes_ref, tops_ref, value_ref, work_ref, pressure_ref, sem,
+
+
+def partial_kernel(
+    load_ref, mob_ref, spread_ref, tab_ref, out_ref, partial_ref, gain_ref,
+    vface_ref, fface_ref, pface_ref, gface_ref,
+    sofar_ref, sums_ref, face_weights_ref, plane_weights_ref, weights_ref, work_ref,
 ):
     tables = tab_ref[...]
-    ny, width = value_ref.shape[2:]
+    ny, width = sofar_ref.shape[2:]
     spread = [spread_ref[d] for d in range(3)]
-    below_ref, above_ref = below_ref.at[1], above_ref.at[0]
-    even = side_ref[0] == 0
     mob, load = plane(mob_ref, ny), plane(load_ref, ny)
+    masks = column_masks((PTS, ny, width))
+    back = paired(cell_blocks(tables[1]))
+    ends = (0, PTS - 1)
+    for j in range(PTS):
+        factor = [mob(a, j) * (float(W[a] * W[j]) * spread[0]) for a in range(PTS)]
+        for i, value in enumerate(contract(D.T, factor, -1)):
+            weights_ref[0, i, j] = value
+        low, high = vface_ref[0, j], vface_ref[1, j]
+        flux = [
+            factor[a] * (float(D[a, 0]) * low + float(D[a, PTS - 1]) * high) for a in range(PTS)
+        ]
+        flux = contract(D.T, flux, -1)
+        for i in range(1, PTS - 1):
+            work_ref[i, j] = out_ref[i, j] + flux[i]
+    for i in range(1, PTS - 1):
+        work_ref[i] = sum_z(work_ref[i], masks)
+        low, high = work_ref[i, 0], work_ref[i, PTS - 1]
+        row = lax.broadcasted_iota(jnp.int32, low.shape, 0)
+        work_ref[i, PTS - 1] = high + jnp.where(row == ny - 1, 0.0, pltpu.roll(low, ny - 1, 0))
+        work_ref[i, 0] = low + jnp.where(row == 0, 0.0, pltpu.roll(high, 1, 0))
+        sofar_ref[i] = partial_ref[i] - gain_ref[i] * work_ref[i]
+    for s in range(2):
+        sofar_ref[ends[s]] = pface_ref[s] - gface_ref[s] * fface_ref[s]
+    for i in range(PTS):
+        factor = [mob(i, j) * (float(W[i] * W[j]) * spread[1]) for j in range(PTS)]
+        for j, value in enumerate(contract(D.T, factor, -1)):
+            weights_ref[1, i, j] = value
+        factor = jnp.concatenate(
+            [mob(i, j) * (float(W[i] * W[j]) * spread[2]) for j in range(PTS)], axis=0
+        )
+        weights_ref[2, i] = dot_split(factor, back).reshape(PTS, ny, width)
+    for s in range(2):
+        for d in range(3):
+            face_weights_ref[d, s] = weights_ref[d, ends[s]]
+            for i in range(PTS):
+                plane_weights_ref[d, s, i] = weights_ref[d, i, ends[s]]
+    points = [(i, j) for i in range(PTS) for j in range(PTS)]
+    sums = restricted(
+        points,
+        lambda i, j: sofar_ref[i, j],
+        lambda d, i, j: weights_ref[d, i, j],
+        jnp.zeros((ny, width), F32),
+    )
+    for i in range(PTS):
+        for q in range(2):
+            from_load = sum(float(HAT[j, q]) * load(i, j) for j in range(PTS))
+            for p in range(2):
+                if HAT[i, p]:
+                    sums[2 * p + q] = sums[2 * p + q] + float(HAT[i, p]) * from_load
+    for n in range(8):
+        sums_ref[n] = sums[n]
+
+
+def restricted(points, value, weight, zero):
+    sums = [zero] * 8
+    along_x = {}
+    along_y = {}
+    along_z = {}
+    for i, j in points:
+        v = value(i, j)
+        along_x[j] = along_x.get(j, 0.0) + weight(0, i, j) * v
+        along_y[i] = along_y.get(i, 0.0) + weight(1, i, j) * v
+        product = weight(2, i, j) * v
+        for q in range(2):
+            if HAT[j, q]:
+                along_z[i, q] = along_z.get((i, q), 0.0) + float(HAT[j, q]) * product
+    x_sums = [
+        sum(float(HAT[j, q]) * total for j, total in along_x.items() if HAT[j, q]) for q in range(2)
+    ]
+    y_sums = [
+        sum(float(HAT[i, p]) * total for i, total in along_y.items() if HAT[i, p]) for p in range(2)
+    ]
+    for p in range(2):
+        for q in range(2):
+            sums[2 * p + q] = -(SLOPE[p] * x_sums[q] + SLOPE[q] * y_sums[p])
+            sums[4 + 2 * p + q] = -sum(
+                float(HAT[i, p]) * total for (i, r), total in along_z.items() if r == q and HAT[i, p]
+            )
+    return sums
+
+
+def corrections(even, gain_ref, gface_ref, outer_ref, below_ref, above_ref, inner_ref):
+    ny, width = gain_ref.shape[2:]
     row = lax.broadcasted_iota(jnp.int32, (ny, width), 0)
-    for i in range(PTS):
-        value_ref[i] = partial_ref[i]
-    for i in range(PTS):
-        value_ref[i, 0] -= gain_ref[i, 0] * jnp.where(row == 0, below_ref[0, i : i + 1], 0.0)
-        value_ref[i, PTS - 1] -= gain_ref[i, PTS - 1] * jnp.where(
-            row == ny - 1, above_ref[0, i : i + 1], 0.0
-        )
+    change = {}
     for j in range(PTS):
         inner, outer = inner_ref[j * ny : (j + 1) * ny], outer_ref[j * ny : (j + 1) * ny]
-        value_ref[0, j] -= gain_ref[0, j] * jnp.where(even, outer, inner)
-        value_ref[PTS - 1, j] -= gain_ref[PTS - 1, j] * jnp.where(even, inner, outer)
-    for i in range(PTS):
-        for j in range(PTS):
-            pressure_ref[i, pl.ds(j, ny, stride=PTS)] = value_ref[i, j]
-    copy = pltpu.make_async_copy(pressure_ref, pressure_out, sem)
-    copy.start()
-    grad = paired(cell_blocks(tables[0]))
-    zero = jnp.zeros((ny, width), F32)
-    smooth = {(p, q): zero for p in range(2) for q in range(2)}
-    slope = {(p, q): zero for p in range(2) for q in range(2)}
-    for j in range(PTS):
-        flux = contract(D, [value_ref[i, j] for i in range(PTS)], -1)
-        total = sum(flux[i] * mob(i, j) * float(W[i] * W[j]) for i in range(PTS)) * spread[0]
-        for p in range(2):
-            for q in range(2):
-                smooth[p, q] -= float(SLOPE[p] * HAT[j, q]) * total
-    for i in range(PTS):
-        flux = contract(D, [value_ref[i, j] for j in range(PTS)], -1)
-        total = sum(flux[j] * mob(i, j) * float(W[i] * W[j]) for j in range(PTS)) * spread[1]
-        for p in range(2):
-            for q in range(2):
-                smooth[p, q] -= float(HAT[i, p] * SLOPE[q]) * total
-    for i in range(PTS):
-        work_ref[i] = dot_split(value_ref[i].reshape(PTS * ny, width), grad).reshape(PTS, ny, width)
-        flux = [work_ref[i, j] * mob(i, j) for j in range(PTS)]
-        for q in range(2):
-            total = sum(float(W[i] * W[j] * HAT[j, q]) * flux[j] for j in range(PTS))
-            from_load = sum(float(HAT[j, q]) * load(i, j) for j in range(PTS))
-            for p in range(2):
-                slope[p, q] += float(HAT[i, p]) * total
-                smooth[p, q] += float(HAT[i, p]) * from_load
-    keys = [(p, q) for p in range(2) for q in range(2)]
-    corners = dot(jnp.concatenate([smooth[k] for k in keys], axis=0), restrict_ref[0]) - dot(
-        jnp.concatenate([slope[k] * spread[2] for k in keys], axis=0), restrict_ref[1]
-    )
+        change[0, j] = jnp.where(even, outer, inner)
+        change[PTS - 1, j] = jnp.where(even, inner, outer)
+    for i in range(PTS):
+        low = jnp.where(row == 0, below_ref[0, i : i + 1], 0.0)
+        high = jnp.where(row == ny - 1, above_ref[0, i : i + 1], 0.0)
+        change[i, 0] = change[i, 0] + low if (i, 0) in change else low
+        change[i, PTS - 1] = change[i, PTS - 1] + high if (i, PTS - 1) in change else high
+    faces = {0: 0, PTS - 1: 1}
+    for i, j in change:
+        gain = gface_ref[faces[i], j] if i in faces else gain_ref[i, j]
+        change[i, j] = -(gain * change[i, j])
+    return change
+
+
+def coarse_kernel(
+    side_ref, gain_ref, gface_ref, sums_ref, face_weights_ref, plane_weights_ref, restrict_ref,
+    outer_ref, below_ref, above_ref, inner_ref,
+    planes_ref, tops_ref,
+):
+    below_ref, above_ref = below_ref.at[1], above_ref.at[0]
+    ny, width = gain_ref.shape[2:]
+    even = side_ref[0] == 0
+    change = corrections(even, gain_ref, gface_ref, outer_ref, below_ref, above_ref, inner_ref)
+    faces = {0: 0, PTS - 1: 1}
+
+    def weight(d, i, j):
+        return face_weights_ref[d, faces[i], j] if i in faces else plane_weights_ref[d, faces[j], i]
+
+    sums = restricted(list(change), lambda i, j: change[i, j], weight, jnp.zeros((ny, width), F32))
+    sums = [sums_ref[n] + sums[n] for n in range(8)]
+    both = jnp.concatenate(
+        [jnp.concatenate(sums[:4], axis=0), jnp.concatenate(sums[4:], axis=0)], axis=1
+    )
+    corners = dot_split(both, paired(restrict_ref[...]))
     row = lax.broadcasted_iota(jnp.int32, (ny, corners.shape[1]), 0)
     for p in range(2):
         lower = corners[(2 * p) * ny : (2 * p + 1) * ny]
         upper = corners[(2 * p + 1) * ny : (2 * p + 2) * ny]
         planes_ref[p] = lower + jnp.where(row == 0, 0.0, pltpu.roll(upper, 1, 0))
         tops_ref[p : p + 1] = upper[ny - 1 : ny]
+
+
+def pressure_kernel(
+    side_ref, sofar_ref, gain_ref, gface_ref, outer_ref, below_ref, above_ref, inner_ref,
+    pressure_out, pressure_ref, sem,
+):
+    below_ref, above_ref = below_ref.at[1], above_ref.at[0]
+    ny = sofar_ref.shape[2]
+    even = side_ref[0] == 0
+    change = corrections(even, gain_ref, gface_ref, outer_ref, below_ref, above_ref, inner_ref)
+    for i in range(PTS):
+        for j in range(PTS):
+            value = sofar_ref[i, j]
+            if (i, j) in change:
+                value = value + change[i, j]
+            pressure_ref[i, pl.ds(j, ny, stride=PTS)] = value
+    copy = pltpu.make_async_copy(pressure_ref, pressure_out, sem)
+    copy.start()
     copy.wait()
 
 
@@ -537,20 +658,39 @@
     )
     rows = (2 * PTS * ny + 2 * PTS, width)
     outer, inner = to_x(*call(merge_kernel, [rows, rows], [], side, xface, factor, below, above))
-    partial, gain, outer, inner, yface = call(
-        smooth_kernel,
-        [field, field, (PTS * ny, width), (PTS * ny, width), (2, 1, PTS, width)],
-        [field, field, field],
-        side, fields, mob, spread, tables, below, above, outer, inner,
+    faces = (2,) + face
+    rough, value, partial, gain, out, pair = call(
+        inside_kernel,
+        [(2,) + faces, field, field, field, field, (3,) + face],
+        [face],
+        fields, mob, spread, tables, below, above,
+    )
+    outer, inner, yface, vface, fface, pface, gface = call(
+        faces_kernel,
+        [(PTS * ny, width), (PTS * ny, width), (2, 1, PTS, width), faces, faces, faces, faces],
+        [((2 * PTS + 4) * ny, width)],
+        side, rough, value, out, pair, mob, spread, tables, below, above, outer, inner,
     )
     outer, inner = to_x(outer, inner)
     below, above = from_y(yface)
-    pressure, planes, tops = call(
+    sofar, sums, face_weights, plane_weights = call(
+        partial_kernel,
+        [field, (8, ny, width), (3,) + faces, (3,) + faces],
+        [(3,) + field, field],
+        load, mob, spread, tables, out, partial, gain, vface, fface, pface, gface,
+    )
+    planes, tops = call(
         coarse_kernel,
-        [(PTS, ny * PTS, width), (2, ny, 128), (2, 128)],
-        [field, field, (PTS, ny * PTS, width), pltpu.SemaphoreType.DMA(())],
-        side, load, partial, gain, mob, spread, tables, restrict, outer, below, above, inner,
-        out_spaces=[pltpu.HBM, pltpu.VMEM, pltpu.VMEM],
+        [(2, ny, 128), (2, 128)],
+        [],
+        side, gain, gface, sums, face_weights, plane_weights, restrict, outer, below, above, inner,
+    )
+    (pressure,) = call(
+        pressure_kernel,
+        [(PTS, ny * PTS, width)],
+        [(PTS, ny * PTS, width), pltpu.SemaphoreType.DMA(())],
+        side, sofar, gain, gface, outer, below, above, inner,
+        out_spaces=[pltpu.HBM],
     )
     size = lax.axis_size("sub")
     below = lax.ppermute(tops, "sub", [(i, (i + 1) % size) for i in range(size)])

time: 33 us -> 31.4 us (0.952)
  waiting for transfers between devices: 13.2 us -> 11 us
  Pallas kernels: 4.15 us -> 4.68 us
    ppermute x1, waiting for transfers between devices: 4.49 us -> 3.71 us  [shards(): outer = lax.ppermute(planes[1], 'dom', outer_pairs(size))]
    ppermute x2, waiting for transfers between devices: 3.15 us -> 2.47 us  [to_x(): outer = lax.ppermute(outer, 'dom', outer_pairs(size))]
    ppermute x2, waiting for transfers between devices: 3.47 us -> 2.8 us  [from_y(): up = lax.ppermute(faces, 'sub', [(i, (i + 1) % size) for i in range(size)])]
    pallas_call x5 -> x8, Pallas kernels: 4.15 us -> 4.68 us  [call(): pl.pallas_call(body, out_shape=[jax.ShapeDtypeStruct(s, F32) for s in out...]
  transfers between devices with their start and end apart: 9 -> 9, of which waited for: 5 -> 5; matrix products, arithmetic and copies ran while one was open for 0% -> 0% of each run, Pallas kernels for 2% -> 9%
where the time goes in v4:
time: 31.4 us; the launch traced here: 31.3 us
  starting transfers between devices  14.2 us (45%)
  waiting for transfers between devices  11 us (35%)
  Pallas kernels  4.68 us (15%)
  between operations  0.69 us (2%)
  local copies, waits for them, and re-layouts  0.63 us (2%)
    ppermute x2, starting transfers between devices, to_x(): outer = lax.ppermute(outer, 'dom', outer_pairs(size))  6.78 us
    pallas_call x8, Pallas kernels, call(): pl.pallas_call(body, out_shape=[jax.ShapeDtypeStruct(s, F32) for s in out...  4.68 us
    ppermute x2, starting transfers between devices, from_y(): up = lax.ppermute(faces, 'sub', [(i, (i + 1) % size) for i in range(size)])  4.55 us
    ppermute x1, waiting for transfers between devices, shards(): outer = lax.ppermute(planes[1], 'dom', outer_pairs(size))  3.71 us
    ppermute x2, waiting for transfers between devices, from_y(): up = lax.ppermute(faces, 'sub', [(i, (i + 1) % size) for i in range(size)])  2.8 us
    ppermute x2, waiting for transfers between devices, to_x(): outer = lax.ppermute(outer, 'dom', outer_pairs(size))  2.47 us
    ppermute x1, waiting for transfers between devices, shards(): lax.ppermute(tops, 'sub', [(i, (i + 1) % size) for i in range(size)])  2.04 us
    ppermute x1, starting transfers between devices, shards(): lax.ppermute(tops, 'sub', [(i, (i + 1) % size) for i in range(size)])  1.58 us
  transfers between devices with their start and end apart: 9, of which 5 were waited for; matrix products, arithmetic and copies ran while one was open for 0% of the time, Pallas kernels for 9%

profile of v4, /device:TPU:0, one launch (start us, length us, event | category | flops | bytes accessed | tf_op | source)
XLA Modules:
  0.0 31.3 jit_solution(7136448835441840804)
XLA Ops:
  0.6 1.4 %shard_map.68 = (f32[8,64,128]{2,1,0:T(8,128)S(1)}, f32[8,64,128]{2,1,0:T(8,128)S(1)}, f32[3,8,128]{2,1,0:T(8,128)S(1)}, f32[5,8,128]{2,1,0:T(8,128)S(1)}, f32[2...) custom-call(f32[8,64,128]{2,1,0:T(8,128)} %bitcast.18, f32[8,64,128]{2,1,0:T(8,128)} %bitcast.19, f32[3,8,16]{2,1,0:T(8,128)} %bitcast.20, ...), custom_call_target="tpu_custom_call" | custom-call | tf_op jit(solution)/shard_map/pallas_call | solution.py:605
  2.0 3.0 %collective-permute-start = (f32[2,4,8,128]{3,2,1,0:T(8,128)S(1)}, f32[2,4,8,128]{3,2,1,0:T(8,128)S(1)}, u32[]{:S(2)}, u32[]{:S(2)}) collective-permute-start(f32[2,4,8,128]{3,2,1,0:T(8,128)S(1)} %get-tuple-element.49), channel_id=1, source_target_pairs={{0,1},{1,0},{2,3},{3,2},{4,5},{5,4},{6,7},{7,6},{8,9},{9,8},{10,11... | collective-permute-start | bytes 98312 | tf_op jit(solution)/shard_map/ppermute | solution.py:617
  5.0 0.5 %shard_map.69 = (f32[2,8,8,8,128]{4,3,2,1,0:T(8,128)S(1)}, f32[2,2,8,8,128]{4,3,2,1,0:T(8,128)S(1)}, f32[2,2,8,128]{3,2,1,0:T(8,128)S(1)}) custom-call(f32[8,64,128]{2,1,0:T(8,128)S(1)} %get-tuple-element.44.load_ref, f32[8,64,128]{2,1,0:T(8,128)S(1)} %get-tuple-element.45.mob_ref, f32[3,8,128]{2,1,0:T(8,128)S(1)} %get-tuple-element.46.spread_ref, ...), custom_call_target="tpu_custom_call" | custom-call | tf_op jit(solution)/shard_map/pallas_call | solution.py:605
  5.6 1.3 %collective-permute-done.below_ref.above_ref = f32[2,4,8,128]{3,2,1,0:T(8,128)S(1)} collective-permute-done((f32[2,4,8,128]{3,2,1,0:T(8,128)S(1)}, f32[2,4,8,128]{3,2,1,0:T(8,128)S(1)}, u32[]{:S(2)}, u32[]{:S(2)}) %collective-permute-start) | collective-permute-done | bytes 32800 | tf_op jit(solution)/shard_map/ppermute | solution.py:617
  7.0 3.4 %collective-permute-start.1 = (f32[144,128]{1,0:T(8,128)S(1)}, f32[144,128]{1,0:T(8,128)S(1)}, u32[]{:S(2)}, u32[]{:S(2)}) collective-permute-start(f32[144,128]{1,0:T(8,128)S(1)} %get-tuple-element.58), channel_id=1, source_target_pairs={{0,30},{2,4},{4,2},{6,8},{8,6},{10,12},{12,10},{14,16},{16,14},{18... | collective-permute-start | bytes 221192 | tf_op jit(solution)/shard_map/ppermute | solution.py:633
  10.3 0.0 collective-permute-start.2
  10.3 0.7 %shard_map.70 = (f32[2,2,8,8,128]{4,3,2,1,0:T(8,128)S(1)}, f32[8,8,8,128]{3,2,1,0:T(8,128)S(1)}, f32[8,8,8,128]{3,2,1,0:T(8,128)S(1)}, f32[8,8,8,128]{3,2,1,0:T(...) custom-call(f32[2,8,8,8,128]{4,3,2,1,0:T(8,128)S(1)} %get-tuple-element.48.fields_ref, ...), custom_call_target="tpu_custom_call" | custom-call | tf_op jit(solution)/shard_map/pallas_call | solution.py:605
  11.0 2.5 %collective-permute-done.1.outer_ref = f32[144,128]{1,0:T(8,128)S(1)} collective-permute-done((f32[144,128]{1,0:T(8,128)S(1)}, f32[144,128]{1,0:T(8,128)S(1)}, u32[]{:S(2)}, u32[]{:S(2)}) %collective-permute-start.1) | collective-permute-done | bytes 73760 | tf_op jit(solution)/shard_map/ppermute | solution.py:633
  13.5 0.0 collective-permute-done.2.inner_ref
  13.5 0.4 %shard_map.72 = (f32[64,128]{1,0:T(8,128)S(1)}, f32[64,128]{1,0:T(8,128)S(1)}, f32[2,1,8,128]{3,2,1,0:T(8,128)S(1)}, f32[2,8,8,128]{3,2,1,0:T(8,128)S(1)}, f32[2...) custom-call(s32[1]{0:T(128)} %bitcast.side_ref, ...), custom_call_target="tpu_custom_call" | custom-call | tf_op jit(solution)/shard_map/pallas_call | solution.py:605
  13.9 3.4 %collective-permute-start.3 = (f32[64,128]{1,0:T(8,128)S(1)}, f32[64,128]{1,0:T(8,128)S(1)}, u32[]{:S(2)}, u32[]{:S(2)}) collective-permute-start(f32[64,128]{1,0:T(8,128)S(1)} %get-tuple-element.65), channel_id=1, source_target_pairs={{0,30},{2,4},{4,2},{6,8},{8,6},{10,12},{12,10},{14,16},{16,14},{18... | collective-permute-start | bytes 98312 | tf_op jit(solution)/shard_map/ppermute | solution.py:633
  17.3 0.0 collective-permute-start.5
  17.3 1.5 %collective-permute-start.4 = (f32[2,1,8,128]{3,2,1,0:T(8,128)S(1)}, f32[2,1,8,128]{3,2,1,0:T(8,128)S(1)}, u32[]{:S(2)}, u32[]{:S(2)}) collective-permute-start(f32[2,1,8,128]{3,2,1,0:T(8,128)S(1)} %get-tuple-element.66), channel_id=1, source_target_pairs={{0,1},{1,0},{2,3},{3,2},{4,5},{5,4},{6,7},{7,6},{8,9},{9,8},{10,11... | collective-permute-start | bytes 24584 | tf_op jit(solution)/shard_map/ppermute | solution.py:617
  18.8 0.7 %shard_map.73 = (f32[8,8,8,128]{3,2,1,0:T(8,128)S(1)}, f32[8,8,128]{2,1,0:T(8,128)S(1)}, f32[3,2,8,8,128]{4,3,2,1,0:T(8,128)S(1)}, f32[3,2,8,8,128]{4,3,2,1,0:T(8,128)S(1)}) custom-call(f32[8,64,128]{2,1,0:T(8,128)S(1)} %get-tuple-element.44.load_ref, f32[8,64,128]{2,1,0:T(8,128)S(1)} %get-tuple-element.45.mob_ref, ...), custom_call_target="tpu_custom_call" | custom-call | tf_op jit(solution)/shard_map/pallas_call | solution.py:605
  19.5 1.5 %collective-permute-done.4.below_ref.above_ref = f32[2,1,8,128]{3,2,1,0:T(8,128)S(1)} collective-permute-done((f32[2,1,8,128]{3,2,1,0:T(8,128)S(1)}, f32[2,1,8,128]{3,2,1,0:T(8,128)S(1)}, u32[]{:S(2)}, u32[]{:S(2)}) %collective-permute-start.4) | collective-permute-done | bytes 8224 | tf_op jit(solution)/shard_map/ppermute | solution.py:617
  21.0 0.0 collective-permute-done.3.outer_ref
  21.0 0.0 collective-permute-done.5.inner_ref
  21.0 0.2 shard_map.75
  21.2 1.6 %collective-permute-start.6 = (f32[2,128]{1,0:T(2,128)S(1)}, f32[2,128]{1,0:T(2,128)S(1)}, u32[]{:S(2)}, u32[]{:S(2)}) collective-permute-start(f32[2,128]{1,0:T(2,128)S(1)} %get-tuple-element.73), channel_id=1, source_target_pairs={{0,1},{1,0},{2,3},{3,2},{4,5},{5,4},{6,7},{7,6},{8,9},{9,8},{10,11... | collective-permute-start | bytes 3080 | tf_op jit(solution)/shard_map/ppermute | solution.py:696
  22.8 2.0 %collective-permute-done.6 = f32[2,128]{1,0:T(2,128)S(1)} collective-permute-done((f32[2,128]{1,0:T(2,128)S(1)}, f32[2,128]{1,0:T(2,128)S(1)}, u32[]{:S(2)}, u32[]{:S(2)}) %collective-permute-start.6) | collective-permute-done | bytes 1056 | tf_op jit(solution)/shard_map/ppermute | solution.py:696
  24.9 1.3 %collective-permute-start.7 = (f32[8,128]{1,0:T(8,128)S(1)}, f32[8,128]{1,0:T(8,128)S(1)}, u32[]{:S(2)}, u32[]{:S(2)}) collective-permute-start(f32[8,128]{1,0:T(8,128)S(1)} %slice_bitcast_fusion), channel_id=1, source_target_pairs={{0,30},{2,4},{4,2},{6,8},{8,6},{10,12},{12,10},{14,16},{16,14},{18... | collective-permute-start | bytes 12296 | tf_op jit(solution)/shard_map/ppermute | solution.py:700
  26.2 0.0 collective-permute-start.8
  26.2 0.8 %shard_map.74 = f32[8,64,128]{2,1,0:T(8,128)} custom-call(s32[1]{0:T(128)} %bitcast.side_ref, f32[8,8,8,128]{3,2,1,0:T(8,128)S(1)} %get-tuple-element.64.sofar_ref, f32[8,8,8,128]{3,2,1,0:T(8,128)S(1)} %get-tuple-element.52.gain_ref, f32[2,8,8,128]{3,2,1,0:T(8,128)S(1)} %get-tuple-element.63.gface_ref, f32[64,128]{1,0:T(8,128)S(1)} %collective-permute-done.3.outer_ref, ...), custom_call_target="tpu_custom_call" | custom-call | tf_op jit(solution)/shard_map/pallas_call | solution.py:605
  26.9 3.7 %collective-permute-done.7 = f32[8,128]{1,0:T(8,128)S(1)} collective-permute-done((f32[8,128]{1,0:T(8,128)S(1)}, f32[8,128]{1,0:T(8,128)S(1)}, u32[]{:S(2)}, u32[]{:S(2)}) %collective-permute-start.7) | collective-permute-done | bytes 4128 | tf_op jit(solution)/shard_map/ppermute | solution.py:700
  30.7 0.0 collective-permute-done.8
  30.7 0.6 %slice_bitcast_fusion.2 = f32[1,8,17]{2,1,0:T(8,128)} fusion(f32[8,128]{1,0:T(8,128)S(1)} %fusion), kind=kLoop, calls=%fused_computation.3 | loop fusion | bytes 1088 | tf_op jit(solution)/shard_map/broadcast_in_dim | solution.py:702
  (6 shorter events, 0.1 us)
Async XLA Ops:
  2.0 4.9 %collective-permute-start = (f32[2,4,8,128]{3,2,1,0:T(8,128)S(1)}, f32[2,4,8,128]{3,2,1,0:T(8,128)S(1)}, u32[]{:S(2)}, u32[]{:S(2)}) collective-permute-start(f32[2,4,8,128]{3,2,1,0:T(8,128)S(1)} %get-tuple-element.49), channel_id=1, source_target_pairs={{0,1},{1,0},{2,3},{3,2},{4,5},{5,4},{6,7},{7,6},{8,9},{9,8},{10,11... | collective-permute-start | bytes 98312 | tf_op jit(solution)/shard_map/ppermute | solution.py:617
  7.0 6.5 %collective-permute-start.1 = (f32[144,128]{1,0:T(8,128)S(1)}, f32[144,128]{1,0:T(8,128)S(1)}, u32[]{:S(2)}, u32[]{:S(2)}) collective-permute-start(f32[144,128]{1,0:T(8,128)S(1)} %get-tuple-element.58), channel_id=1, source_target_pairs={{0,30},{2,4},{4,2},{6,8},{8,6},{10,12},{12,10},{14,16},{16,14},{18... | collective-permute-start | bytes 221192 | tf_op jit(solution)/shard_map/ppermute | solution.py:633
  10.3 3.2 %collective-permute-start.2 = (f32[144,128]{1,0:T(8,128)S(1)}, f32[144,128]{1,0:T(8,128)S(1)}, u32[]{:S(2)}, u32[]{:S(2)}) collective-permute-start(f32[144,128]{1,0:T(8,128)S(1)} %get-tuple-element.59), channel_id=1, source_target_pairs={{0,2},{2,0},{4,6},{6,4},{8,10},{10,8},{12,14},{14,12},{16,18},{18,... | collective-permute-start | bytes 221192 | tf_op jit(solution)/shard_map/ppermute | solution.py:634
  13.9 7.0 %collective-permute-start.3 = (f32[64,128]{1,0:T(8,128)S(1)}, f32[64,128]{1,0:T(8,128)S(1)}, u32[]{:S(2)}, u32[]{:S(2)}) collective-permute-start(f32[64,128]{1,0:T(8,128)S(1)} %get-tuple-element.65), channel_id=1, source_target_pairs={{0,30},{2,4},{4,2},{6,8},{8,6},{10,12},{12,10},{14,16},{16,14},{18... | collective-permute-start | bytes 98312 | tf_op jit(solution)/shard_map/ppermute | solution.py:633
  17.3 3.7 %collective-permute-start.5 = (f32[64,128]{1,0:T(8,128)S(1)}, f32[64,128]{1,0:T(8,128)S(1)}, u32[]{:S(2)}, u32[]{:S(2)}) collective-permute-start(f32[64,128]{1,0:T(8,128)S(1)} %get-tuple-element.67), channel_id=1, source_target_pairs={{0,2},{2,0},{4,6},{6,4},{8,10},{10,8},{12,14},{14,12},{16,18},{18,... | collective-permute-start | bytes 98312 | tf_op jit(solution)/shard_map/ppermute | solution.py:634
  17.3 3.7 %collective-permute-start.4 = (f32[2,1,8,128]{3,2,1,0:T(8,128)S(1)}, f32[2,1,8,128]{3,2,1,0:T(8,128)S(1)}, u32[]{:S(2)}, u32[]{:S(2)}) collective-permute-start(f32[2,1,8,128]{3,2,1,0:T(8,128)S(1)} %get-tuple-element.66), channel_id=1, source_target_pairs={{0,1},{1,0},{2,3},{3,2},{4,5},{5,4},{6,7},{7,6},{8,9},{9,8},{10,11... | collective-permute-start | bytes 24584 | tf_op jit(solution)/shard_map/ppermute | solution.py:617
  21.2 3.6 %collective-permute-start.6 = (f32[2,128]{1,0:T(2,128)S(1)}, f32[2,128]{1,0:T(2,128)S(1)}, u32[]{:S(2)}, u32[]{:S(2)}) collective-permute-start(f32[2,128]{1,0:T(2,128)S(1)} %get-tuple-element.73), channel_id=1, source_target_pairs={{0,1},{1,0},{2,3},{3,2},{4,5},{5,4},{6,7},{7,6},{8,9},{9,8},{10,11... | collective-permute-start | bytes 3080 | tf_op jit(solution)/shard_map/ppermute | solution.py:696
  24.9 5.8 %collective-permute-start.7 = (f32[8,128]{1,0:T(8,128)S(1)}, f32[8,128]{1,0:T(8,128)S(1)}, u32[]{:S(2)}, u32[]{:S(2)}) collective-permute-start(f32[8,128]{1,0:T(8,128)S(1)} %slice_bitcast_fusion), channel_id=1, source_target_pairs={{0,30},{2,4},{4,2},{6,8},{8,6},{10,12},{12,10},{14,16},{16,14},{18... | collective-permute-start | bytes 12296 | tf_op jit(solution)/shard_map/ppermute | solution.py:700
  26.2 4.5 %collective-permute-start.8 = (f32[8,128]{1,0:T(8,128)S(1)}, f32[8,128]{1,0:T(8,128)S(1)}, u32[]{:S(2)}, u32[]{:S(2)}) collective-permute-start(f32[8,128]{1,0:T(8,128)S(1)} %slice_bitcast_fusion), channel_id=1, source_target_pairs={{0,2},{2,0},{4,6},{6,4},{8,10},{10,8},{12,14},{14,12},{16,18},{18,... | collective-permute-start | bytes 12296 | tf_op jit(solution)/shard_map/ppermute | solution.py:699

commit v5 on v4

--- a/solution.py
+++ b/solution.py
@@ -39,6 +39,7 @@
 EXACT = lax.Precision.HIGHEST
 PTS = 8
 F32 = jnp.float32
+FLOPS_JOIN = 5_000_000_000
 
 
 def derivative_table():
@@ -201,11 +202,15 @@
     masks = column_masks((PTS * ny, width))
     copies[2].wait()
     ends = (0, PTS - 1)
-    sums = [[], []]
+    sums, weights = [[], []], [[], []]
     for i in range(PTS):
         factor = [mob(i, j) * (float(W[i]) * spread[1]) for j in range(PTS)]
         for s in range(2):
+            e = 0 if s == 0 else ny - 1
             sums[s].append(sum(float(square[j, ends[s]] * W[j]) * factor[j] for j in range(PTS)))
+            weights[s].append(
+                sum(float(D[j, ends[s]] * W[j]) * factor[j] for j in range(PTS))[e : e + 1]
+            )
     for s in range(2):
         j = ends[s]
         points = [mob(i, j) * float(W[i] * W[j]) for i in range(PTS)]
@@ -227,10 +232,14 @@
         points = points * (float(W[ends[s]]) * tables[4])
         yface_ref[s, 2] = points * spread[0][e : e + 1]
         yface_ref[s, 3] = points * spread[2][e : e + 1]
+        yface_ref[s, 4] = jnp.concatenate(weights[s], axis=0)
     copies[4].wait()
 
 
-def diag_kernel(load_ref, mob_ref, spread_ref, tab_ref, fields_ref, xface_ref, factor_ref):
+def diag_kernel(
+    side_ref, load_ref, mob_ref, spread_ref, tab_ref,
+    fields_ref, xface_ref, factor_ref, to_outer_ref, to_inner_ref,
+):
     tables = tab_ref[...]
     ny, width = fields_ref.shape[3:]
     spread = [spread_ref[d] for d in range(3)]
@@ -238,8 +247,18 @@
     square = D * D
     mob, load = plane(mob_ref, ny), plane(load_ref, ny)
     diag_ref = fields_ref.at[1]
+    even = side_ref[0] == 0
+
+    def post(at, low, high):
+        to_inner_ref[at : at + ny] = jnp.where(even, high, low)
+        to_outer_ref[at : at + ny] = jnp.where(even, low, high)
+
+    for d in (1, 2):
+        post((2 * PTS + d - 1) * ny, spread[d], spread[d])
     for j in range(PTS):
         factor = [mob(i, j) * (float(W[i] * W[j]) * spread[0]) for i in range(PTS)]
+        post(j * ny, *(sum(float(D[a, i]) * factor[a] for a in range(PTS)) for i in (0, PTS - 1)))
+        post((PTS + j) * ny, *(float(W[i] * W[j]) * mob(i, j) for i in (0, PTS - 1)))
         for i, value in enumerate(contract(square.T, factor, 1)):
             diag_ref[i, j] = value
     for i in range(PTS):
@@ -290,14 +309,15 @@
 
 
 def inside_kernel(
-    fields_ref, mob_ref, spread_ref, tab_ref, below_ref, above_ref,
-    rough_ref, value_ref, partial_ref, gain_ref, out_ref, pair_ref, work_ref,
+    fields_ref, load_ref, mob_ref, spread_ref, tab_ref, below_ref, above_ref,
+    rough_ref, value_ref, partial_ref, gain_ref, out_ref, pair_ref, weights_ref, sums_ref, edge_weights_ref,
+    work_ref,
 ):
     below_ref, above_ref = below_ref.at[1], above_ref.at[0]
     tables = tab_ref[...]
     ny, width = out_ref.shape[2:]
     spread = [spread_ref[d] for d in range(3)]
-    mob = plane(mob_ref, ny)
+    mob, load = plane(mob_ref, ny), plane(load_ref, ny)
     row = lax.broadcasted_iota(jnp.int32, (ny, width), 0)
     zero = jnp.zeros((ny, width), F32)
     for i in range(PTS):
@@ -324,6 +344,8 @@
         flux = [flux[i] * factor[i] for i in range(PTS)]
         for i, value in enumerate(contract(D.T, flux, -1)):
             out_ref[i, j] = value
+        for i, value in enumerate(contract(D.T, factor, -1)):
+            weights_ref[0, i, j] = value
     for i in range(1, PTS - 1):
         flux = contract(D, [value_ref[i, j] for j in range(PTS)], -1)
         flux = [flux[j] * (mob(i, j) * (float(W[i] * W[j]) * spread[1])) for j in range(PTS)]
@@ -333,6 +355,27 @@
         for j in range(PTS):
             work_ref[j] *= mob(i, j) * (float(W[i] * W[j]) * spread[2])
         out_ref[i] += dot_split(work_ref[...].reshape(PTS * ny, width), back).reshape(PTS, ny, width)
+    for i in range(PTS):
+        factor = [mob(i, j) * (float(W[i] * W[j]) * spread[1]) for j in range(PTS)]
+        for j, value in enumerate(contract(D.T, factor, -1)):
+            weights_ref[1, i, j] = value
+        factor = jnp.concatenate(
+            [mob(i, j) * (float(W[i] * W[j]) * spread[2]) for j in range(PTS)], axis=0
+        )
+        weights_ref[2, i] = dot_split(factor, back).reshape(PTS, ny, width)
+    sums = [zero] * 4
+    for i in range(PTS):
+        for q in range(2):
+            from_load = sum(float(HAT[j, q]) * load(i, j) for j in range(PTS))
+            for p in range(2):
+                if HAT[i, p]:
+                    sums[2 * p + q] = sums[2 * p + q] + float(HAT[i, p]) * from_load
+    for n in range(4):
+        sums_ref[n] = sums[n]
+    for t, ref in enumerate((below_ref, above_ref)):
+        edge_weights_ref[t, 0] = dot(tables[0][:, :PTS], ref[2])
+        edge_weights_ref[t, 1] = ref[4]
+        edge_weights_ref[t, 2] = dot_split(ref[3], back)
 
 
 def first_step(right, diagonal):
@@ -344,8 +387,9 @@
 
 def faces_kernel(
     side_ref, rough_ref, value_ref, out_ref, pair_ref, mob_ref, spread_ref, tab_ref,
-    below_ref, above_ref, outer_ref, inner_ref,
-    to_outer_ref, to_inner_ref, yface_ref, vface_ref, fface_ref, pface_ref, gface_ref, line_ref,
+    below_ref, above_ref, partial_ref, gain_ref, weights_ref, load_sums_ref, edge_weights_ref,
+    outer_ref, inner_ref,
+    to_outer_ref, to_inner_ref, yface_ref, gface_ref, sofar_ref, sums_ref, line_ref, work_ref,
 ):
     below_ref, above_ref = below_ref.at[1], above_ref.at[0]
     even = side_ref[0] == 0
@@ -363,14 +407,16 @@
         return jnp.where(even, outer, inner), jnp.where(even, inner, outer)
 
     value = [[None] * PTS, [None] * PTS]
+    pface = [[None] * PTS, [None] * PTS]
+    gface = [[None] * PTS, [None] * PTS]
     for j in range(PTS):
         load = arrived(j * ny, ny)
         diagonal = arrived((PTS + j) * ny, ny)
         for s in range(2):
-            value[s][j], pface_ref[s, j], gface_ref[s, j] = first_step(
+            value[s][j], pface[s][j], gface[s][j] = first_step(
                 rough_ref[0, s, j] + load[s], rough_ref[1, s, j] + diagonal[s]
             )
-            vface_ref[s, j] = value[s][j]
+            gface_ref[s, j] = gface[s][j]
     lines = [value[s][j] for s in range(2) for j in range(PTS)]
     factors = [
         mob(ends[s], j) * (float(W[ends[s]] * W[j]) * spread[2]) for s in range(2) for j in range(PTS)
@@ -403,8 +449,7 @@
         for j in range(PTS):
             at = (s * PTS + j) * ny
             total[s][j] += line_ref[at : at + ny]
-    for t in range(2):
-        j = ends[t]
+    for j in range(PTS):
         flux = [
             mob(a, j)
             * (float(W[a] * W[j]) * spread[0])
@@ -412,11 +457,17 @@
             for a in range(PTS)
         ]
         flux = contract(D.T, flux, -1)
-        edge = [total[0][j]] + [out_ref[i, j] + flux[i] for i in range(1, PTS - 1)] + [total[1][j]]
+        for i in range(1, PTS - 1):
+            work_ref[i, j] = out_ref[i, j] + flux[i]
+    ymessage = []
+    for t in range(2):
+        j = ends[t]
+        edge = [total[0][j]] + [work_ref[i, j] for i in range(1, PTS - 1)] + [total[1][j]]
         edge = [v[rows[t] : rows[t] + 1] for v in edge]
         edge[0] += edge_y[0][t]
         edge[PTS - 1] += edge_y[1][t]
-        yface_ref[t, 0] = sum_z(jnp.concatenate(edge, axis=0), column_masks((PTS, width)))
+        ymessage.append(sum_z(jnp.concatenate(edge, axis=0), column_masks((PTS, width))))
+        yface_ref[t, 0] = ymessage[t]
     extra = [[None, None], [None, None]]
     for t, ref in enumerate((below_ref, above_ref)):
         j = ends[t]
@@ -434,75 +485,56 @@
         total[s][PTS - 1] = high + jnp.where(row == ny - 1, 0.0, pltpu.roll(low, ny - 1, 0))
         total[s][0] = low + jnp.where(row == 0, 0.0, pltpu.roll(high, 1, 0))
     for j in range(PTS):
-        fface_ref[0, j], fface_ref[1, j] = total[0][j], total[1][j]
         low, high = total[0][j], total[1][j]
         if j in ends:
             t = ends.index(j)
             low, high = low + extra[0][t], high + extra[1][t]
         to_inner_ref[j * ny : (j + 1) * ny] = jnp.where(even, high, low)
         to_outer_ref[j * ny : (j + 1) * ny] = jnp.where(even, low, high)
-
-
-def partial_kernel(
-    load_ref, mob_ref, spread_ref, tab_ref, out_ref, partial_ref, gain_ref,
-    vface_ref, fface_ref, pface_ref, gface_ref,
-    sofar_ref, sums_ref, face_weights_ref, plane_weights_ref, weights_ref, work_ref,
-):
-    tables = tab_ref[...]
-    ny, width = sofar_ref.shape[2:]
-    spread = [spread_ref[d] for d in range(3)]
-    mob, load = plane(mob_ref, ny), plane(load_ref, ny)
-    masks = column_masks((PTS, ny, width))
-    back = paired(cell_blocks(tables[1]))
-    ends = (0, PTS - 1)
-    for j in range(PTS):
-        factor = [mob(a, j) * (float(W[a] * W[j]) * spread[0]) for a in range(PTS)]
-        for i, value in enumerate(contract(D.T, factor, -1)):
-            weights_ref[0, i, j] = value
-        low, high = vface_ref[0, j], vface_ref[1, j]
-        flux = [
-            factor[a] * (float(D[a, 0]) * low + float(D[a, PTS - 1]) * high) for a in range(PTS)
-        ]
-        flux = contract(D.T, flux, -1)
-        for i in range(1, PTS - 1):
-            work_ref[i, j] = out_ref[i, j] + flux[i]
+        for s in range(2):
+            sofar_ref[ends[s], j] = pface[s][j] - gface[s][j] * total[s][j]
     for i in range(1, PTS - 1):
-        work_ref[i] = sum_z(work_ref[i], masks)
-        low, high = work_ref[i, 0], work_ref[i, PTS - 1]
-        row = lax.broadcasted_iota(jnp.int32, low.shape, 0)
-        work_ref[i, PTS - 1] = high + jnp.where(row == ny - 1, 0.0, pltpu.roll(low, ny - 1, 0))
-        work_ref[i, 0] = low + jnp.where(row == 0, 0.0, pltpu.roll(high, 1, 0))
-        sofar_ref[i] = partial_ref[i] - gain_ref[i] * work_ref[i]
-    for s in range(2):
-        sofar_ref[ends[s]] = pface_ref[s] - gface_ref[s] * fface_ref[s]
-    for i in range(PTS):
-        factor = [mob(i, j) * (float(W[i] * W[j]) * spread[1]) for j in range(PTS)]
-        for j, value in enumerate(contract(D.T, factor, -1)):
-            weights_ref[1, i, j] = value
-        factor = jnp.concatenate(
-            [mob(i, j) * (float(W[i] * W[j]) * spread[2]) for j in range(PTS)], axis=0
-        )
-        weights_ref[2, i] = dot_split(factor, back).reshape(PTS, ny, width)
-    for s in range(2):
-        for d in range(3):
-            face_weights_ref[d, s] = weights_ref[d, ends[s]]
-            for i in range(PTS):
-                plane_weights_ref[d, s, i] = weights_ref[d, i, ends[s]]
-    points = [(i, j) for i in range(PTS) for j in range(PTS)]
+        lines = [sum_z(work_ref[i, j], masks) for j in range(PTS)]
+        low, high = lines[0], lines[PTS - 1]
+        lines[PTS - 1] = high + jnp.where(row == ny - 1, 0.0, pltpu.roll(low, ny - 1, 0))
+        lines[0] = low + jnp.where(row == 0, 0.0, pltpu.roll(high, 1, 0))
+        for j in range(PTS):
+            sofar_ref[i, j] = partial_ref[i, j] - gain_ref[i, j] * lines[j]
     sums = restricted(
-        points,
+        [(i, j) for i in range(PTS) for j in range(PTS)],
         lambda i, j: sofar_ref[i, j],
         lambda d, i, j: weights_ref[d, i, j],
         jnp.zeros((ny, width), F32),
     )
-    for i in range(PTS):
-        for q in range(2):
-            from_load = sum(float(HAT[j, q]) * load(i, j) for j in range(PTS))
-            for p in range(2):
-                if HAT[i, p]:
-                    sums[2 * p + q] = sums[2 * p + q] + float(HAT[i, p]) * from_load
-    for n in range(8):
-        sums_ref[n] = sums[n]
+    for q in range(2):
+        sums_ref[q] = sums[q] + load_sums_ref[q]
+        sums_ref[2 + q] = sums[4 + q]
+        sums[2 + q] = sums[2 + q] + load_sums_ref[2 + q]
+    base = PTS * ny
+    changes = []
+    for t in range(2):
+        j = ends[t]
+        gain = [gface[0][j]] + [gain_ref[i, j] for i in range(1, PTS - 1)] + [gface[1][j]]
+        gain = jnp.concatenate([g[rows[t] : rows[t] + 1] for g in gain], axis=0)
+        changes += edge_change(-(gain * ymessage[t]), edge_weights_ref.at[t], ends[1 - t])
+    changes = jnp.concatenate(changes, axis=0)
+    for ref in (to_outer_ref, to_inner_ref):
+        for n, k in enumerate((2, 3, 6, 7)):
+            ref[base + n * ny : base + (n + 1) * ny] = sums[k]
+        ref[base + 4 * ny : base + 4 * ny + PTS] = changes
+
+
+def edge_change(change, weight_ref, j):
+    upper = lax.broadcasted_iota(jnp.int32, change.shape, 0)
+    hat = jnp.zeros_like(change)
+    for i in range(PTS):
+        hat = jnp.where(upper == i, float(HAT[i, 1]), hat)
+    along_x, along_y, along_z = (
+        jnp.sum(v, axis=0, keepdims=True)
+        for v in (weight_ref[0] * change, hat * weight_ref[1] * change, hat * weight_ref[2] * change)
+    )
+    smooth = [-(SLOPE[1] * float(HAT[j, q]) * along_x + SLOPE[q] * along_y) for q in range(2)]
+    return smooth + [-float(HAT[j, q]) * along_z for q in range(2)]
 
 
 def restricted(points, value, weight, zero):
@@ -553,38 +585,97 @@
     return change
 
 
+def face_change(change, weight, i, p, q):
+    along_x = sum(float(HAT[j, q]) * (weight[0][j] * change[j]) for j in range(PTS) if HAT[j, q])
+    smooth = SLOPE[p] * along_x
+    slope = 0.0
+    if HAT[i, p]:
+        along_y = sum(weight[1][j] * change[j] for j in range(PTS))
+        smooth = smooth + float(HAT[i, p]) * SLOPE[q] * along_y
+        along_z = sum(float(HAT[j, q]) * (weight[2][j] * change[j]) for j in range(PTS) if HAT[j, q])
+        slope = float(HAT[i, p]) * along_z
+    return -smooth, -slope
+
+
+def to_vertices(smooth, slope, restrict):
+    return dot_split(jnp.concatenate([smooth, slope], axis=1), restrict)
+
+
+def ahead_kernel(
+    side_ref, sent_outer_ref, sent_inner_ref, gface_ref, tab_ref, restrict_ref, outer_ref, inner_ref, yface_ref,
+    own_ref, next_ref, top_ref, to_y_ref,
+):
+    ny, width = gface_ref.shape[2:]
+    to_y_ref[...] = yface_ref[...]
+    even = side_ref[0] == 0
+    back = paired(cell_blocks(tab_ref[1]))
+
+    def rows(at, first, second):
+        return jnp.where(even, first[at : at + ny], second[at : at + ny])
+
+    change = [-(gface_ref[0, j] * rows(j * ny, sent_outer_ref, sent_inner_ref)) for j in range(PTS)]
+    spread = [rows((2 * PTS + d) * ny, outer_ref, inner_ref) for d in range(2)]
+    points = [rows((PTS + j) * ny, outer_ref, inner_ref) for j in range(PTS)]
+    column = dot_split(jnp.concatenate([p * spread[1] for p in points], axis=0), back)
+    weight = [
+        [rows(j * ny, outer_ref, inner_ref) for j in range(PTS)],
+        contract(D.T, [p * spread[0] for p in points], -1),
+        [column[j * ny : (j + 1) * ny] for j in range(PTS)],
+    ]
+    for q in range(2):
+        own_ref[q], own_ref[2 + q] = face_change(change, weight, PTS - 1, 1, q)
+    change = [-(gface_ref[1, j] * rows(j * ny, sent_inner_ref, sent_outer_ref)) for j in range(PTS)]
+    weight = [[rows(j * ny, inner_ref, outer_ref) for j in range(PTS)]]
+    smooth = jnp.concatenate([face_change(change, weight, 0, 1, q)[0] for q in range(2)], axis=0)
+    corners = to_vertices(smooth, jnp.zeros_like(smooth), paired(restrict_ref[...]))
+    lower, upper = corners[:ny], corners[ny:]
+    row = lax.broadcasted_iota(jnp.int32, lower.shape, 0)
+    next_ref[...] = lower + jnp.where(row == 0, 0.0, pltpu.roll(upper, 1, 0))
+    top_ref[...] = upper[ny - 1 : ny]
+
+
 def coarse_kernel(
-    side_ref, gain_ref, gface_ref, sums_ref, face_weights_ref, plane_weights_ref, restrict_ref,
+    side_ref, gain_ref, gface_ref, sums_ref, own_ref, weights_ref, restrict_ref,
     outer_ref, below_ref, above_ref, inner_ref,
-    planes_ref, tops_ref,
+    plane_ref, edge_ref,
 ):
     below_ref, above_ref = below_ref.at[1], above_ref.at[0]
     ny, width = gain_ref.shape[2:]
     even = side_ref[0] == 0
     change = corrections(even, gain_ref, gface_ref, outer_ref, below_ref, above_ref, inner_ref)
-    faces = {0: 0, PTS - 1: 1}
-
-    def weight(d, i, j):
-        return face_weights_ref[d, faces[i], j] if i in faces else plane_weights_ref[d, faces[j], i]
-
-    sums = restricted(list(change), lambda i, j: change[i, j], weight, jnp.zeros((ny, width), F32))
-    sums = [sums_ref[n] + sums[n] for n in range(8)]
-    both = jnp.concatenate(
-        [jnp.concatenate(sums[:4], axis=0), jnp.concatenate(sums[4:], axis=0)], axis=1
-    )
-    corners = dot_split(both, paired(restrict_ref[...]))
-    row = lax.broadcasted_iota(jnp.int32, (ny, corners.shape[1]), 0)
-    for p in range(2):
-        lower = corners[(2 * p) * ny : (2 * p + 1) * ny]
-        upper = corners[(2 * p + 1) * ny : (2 * p + 2) * ny]
-        planes_ref[p] = lower + jnp.where(row == 0, 0.0, pltpu.roll(upper, 1, 0))
-        tops_ref[p : p + 1] = upper[ny - 1 : ny]
+    sums = restricted(
+        list(change),
+        lambda i, j: change[i, j],
+        lambda d, i, j: weights_ref[d, i, j],
+        jnp.zeros((ny, width), F32),
+    )
+    base = PTS * ny
+
+    def before(at, count):
+        return jnp.where(even, outer_ref[at : at + count], inner_ref[at : at + count])
+
+    total = [
+        sums[(0, 1, 4, 5)[n]] + sums_ref[n] + own_ref[n] + before(base + n * ny, ny) for n in range(4)
+    ]
+    extra = before(base + 4 * ny, PTS)
+    smooth = jnp.concatenate(total[:2] + [extra], axis=0)
+    slope = jnp.concatenate(total[2:] + [pltpu.roll(extra, PTS - 2, 0)], axis=0)
+    corners = to_vertices(smooth, slope, paired(restrict_ref[...]))
+    lower, upper = corners[:ny], corners[ny : 2 * ny]
+    extra = corners[2 * ny :]
+    row = lax.broadcasted_iota(jnp.int32, lower.shape, 0)
+    shifted = jnp.where(row == 0, extra[1:2], pltpu.roll(upper, 1, 0))
+    plane_ref[...] = lower + shifted
+    edge_ref[0:1] = upper[ny - 1 : ny] + extra[4:5]
+    edge_ref[1:2] = extra[5:6]
+    edge_ref[2:3] = extra[0:1]
 
 
 def pressure_kernel(
     side_ref, sofar_ref, gain_ref, gface_ref, outer_ref, below_ref, above_ref, inner_ref,
-    pressure_out, pressure_ref, sem,
+    pressure_out, token_ref, pressure_ref, sem,
 ):
+    token_ref[...] = jnp.zeros_like(token_ref)
     below_ref, above_ref = below_ref.at[1], above_ref.at[0]
     ny = sofar_ref.shape[2]
     even = side_ref[0] == 0
@@ -600,7 +691,21 @@
     copy.wait()
 
 
-def call(body, outs, scratch, *args, spaces=None, out_spaces=None):
+def join_kernel(next_ref, top_ref, token_ref, joined_ref):
+    row = lax.broadcasted_iota(jnp.int32, next_ref.shape, 0)
+    joined_ref[...] = next_ref[...] + jnp.where(row == 0, top_ref[...], 0.0) + token_ref[...]
+
+
+def last_kernel(plane_ref, joined_ref, below_ref, above_ref, coarse_ref):
+    total = plane_ref[...] + joined_ref[...]
+    ny = total.shape[0]
+    row = lax.broadcasted_iota(jnp.int32, total.shape, 0)
+    total = total + jnp.where(row == 0, below_ref[0:1], jnp.where(row == 1, below_ref[1:2], 0.0))
+    total = total + jnp.where(row == ny - 1, above_ref[2:3], 0.0)
+    coarse_ref[...] = total[:, : coarse_ref.shape[1]]
+
+
+def call(body, outs, scratch, *args, spaces=None, out_spaces=None, flops=None):
     spaces = spaces or [pltpu.SMEM if a.dtype == jnp.int32 else pltpu.VMEM for a in args]
     return pl.pallas_call(
         body,
@@ -609,6 +714,7 @@
         out_specs=[pl.BlockSpec(memory_space=m) for m in out_spaces or [pltpu.VMEM] * len(outs)],
         scratch_shapes=[pltpu.VMEM(s, F32) if isinstance(s, tuple) else s for s in scratch],
         compiler_params=pltpu.CompilerParams(vmem_limit_bytes=16 * 1024 * 1024),
+        cost_estimate=flops and pl.CostEstimate(flops=flops, bytes_accessed=0, transcendentals=0),
     )(*args)
 
 
@@ -633,6 +739,15 @@
     outer = lax.ppermute(outer, "dom", outer_pairs(size))
     inner = lax.ppermute(inner, "dom", inner_pairs(size))
     return outer, inner
+
+
+def two_on(rows, top):
+    size, rest = lax.axis_size("dom"), lax.axis_size("sub")
+    rows = lax.ppermute(rows, "dom", [(i, (i + 2) % size) for i in range(size)])
+    pairs = [
+        (i * rest + k, (i + 2) % size * rest + (k + 1) % rest) for i in range(size) for k in range(rest)
+    ]
+    return rows, lax.ppermute(top, ("dom", "sub"), pairs)
 
 
 def shards(element_load, mobility, metric):
@@ -647,60 +762,66 @@
     face = (PTS, ny, width)
     load, mob, spread, tables, restrict, yface = call(
         edge_kernel,
-        [load.shape, mob.shape, (3, ny, width), tables.shape, restrict.shape, (2, 4, PTS, width)],
+        [load.shape, mob.shape, (3, ny, width), tables.shape, restrict.shape, (2, 5, PTS, width)],
         [metric.shape, pltpu.SemaphoreType.DMA((5,))],
         *(pltpu.with_memory_space_constraint(a, pltpu.HBM) for a in (load, mob, metric, tables, restrict)),
         spaces=[pltpu.HBM] * 5,
     )
     below, above = from_y(yface)
-    fields, xface, factor = call(
-        diag_kernel, [(2,) + field, (2, 2) + face, (2, 2, PTS, width)], [], load, mob, spread, tables
+    still = (2 * (PTS + 1) * ny, width)
+    fields, xface, factor, still_outer, still_inner = call(
+        diag_kernel,
+        [(2,) + field, (2, 2) + face, (2, 2, PTS, width), still, still],
+        [],
+        side, load, mob, spread, tables,
     )
     rows = (2 * PTS * ny + 2 * PTS, width)
     outer, inner = to_x(*call(merge_kernel, [rows, rows], [], side, xface, factor, below, above))
+    still_outer, still_inner = to_x(still_outer, still_inner)
     faces = (2,) + face
-    rough, value, partial, gain, out, pair = call(
+    rough, value, partial, gain, out, pair, weights, load_sums, edge_weights = call(
         inside_kernel,
-        [(2,) + faces, field, field, field, field, (3,) + face],
+        [
+            (2,) + faces, field, field, field, field, (3,) + face,
+            (3,) + field, (4, ny, width), (2, 3, PTS, width),
+        ],
         [face],
-        fields, mob, spread, tables, below, above,
-    )
-    outer, inner, yface, vface, fface, pface, gface = call(
+        fields, load, mob, spread, tables, below, above,
+    )
+    rows = ((PTS + 4) * ny + PTS, width)
+    sent_outer, sent_inner, yface, gface, sofar, sums = call(
         faces_kernel,
-        [(PTS * ny, width), (PTS * ny, width), (2, 1, PTS, width), faces, faces, faces, faces],
-        [((2 * PTS + 4) * ny, width)],
-        side, rough, value, out, pair, mob, spread, tables, below, above, outer, inner,
-    )
-    outer, inner = to_x(outer, inner)
+        [rows, rows, (2, 1, PTS, width), faces, field, (4, ny, width)],
+        [((2 * PTS + 4) * ny, width), field],
+        side, rough, value, out, pair, mob, spread, tables, below, above,
+        partial, gain, weights, load_sums, edge_weights, outer, inner,
+    )
+    outer, inner = to_x(sent_outer, sent_inner)
+    own, onward, top, yface = call(
+        ahead_kernel,
+        [(4, ny, width), (ny, 128), (1, 128), yface.shape],
+        [],
+        side, sent_outer, sent_inner, gface, tables, restrict, still_outer, still_inner, yface,
+    )
+    onward, top = two_on(onward, top)
     below, above = from_y(yface)
-    sofar, sums, face_weights, plane_weights = call(
-        partial_kernel,
-        [field, (8, ny, width), (3,) + faces, (3,) + faces],
-        [(3,) + field, field],
-        load, mob, spread, tables, out, partial, gain, vface, fface, pface, gface,
-    )
-    planes, tops = call(
+    plane, edge = call(
         coarse_kernel,
-        [(2, ny, 128), (2, 128)],
+        [(ny, 128), (3, 128)],
         [],
-        side, gain, gface, sums, face_weights, plane_weights, restrict, outer, below, above, inner,
-    )
-    (pressure,) = call(
+        side, gain, gface, sums, own, weights, restrict, outer, below, above, inner,
+    )
+    pressure, token = call(
         pressure_kernel,
-        [(PTS, ny * PTS, width)],
+        [(PTS, ny * PTS, width), (1, 128)],
         [(PTS, ny * PTS, width), pltpu.SemaphoreType.DMA(())],
         side, sofar, gain, gface, outer, below, above, inner,
-        out_spaces=[pltpu.HBM],
-    )
-    size = lax.axis_size("sub")
-    below = lax.ppermute(tops, "sub", [(i, (i + 1) % size) for i in range(size)])
-    planes = planes.at[:, 0].add(below)
-    size = lax.axis_size("dom")
-    inner = lax.ppermute(planes[1], "dom", inner_pairs(size))
-    outer = lax.ppermute(planes[1], "dom", outer_pairs(size))
-    coarse = planes[0] + jnp.where(side == 0, outer, inner)
-    coarse = coarse[None, :, : width // PTS + 1]
-    return pressure.reshape(element_load.shape), coarse
+        out_spaces=[pltpu.HBM, pltpu.VMEM],
+    )
+    (onward,) = call(join_kernel, [(ny, 128)], [], onward, top, token, flops=FLOPS_JOIN)
+    below, above = from_y(edge)
+    (coarse,) = call(last_kernel, [(ny, width // PTS + 1)], [], plane, onward, below, above)
+    return pressure.reshape(element_load.shape), coarse[None]
 
 
 def solution(mesh):

time: 31.4 us -> 27.3 us (0.87)
  waiting for transfers between devices: 11 us -> 6.02 us
  Pallas kernels: 4.68 us -> 5.5 us
  starting transfers between devices: 14.2 us -> 14.9 us
  local copies, waits for them, and re-layouts: 0.63 us -> 0 us
    ppermute x3 -> x2, waiting for transfers between devices: 5.76 us -> 2.43 us  [the longest x1 2.43 us: two_on(): return (rows, lax.ppermute(top, ('dom', 'sub'), pairs))]
    ppermute x3 -> x2, starting transfers between devices: 2.88 us -> 0.01 us  [the longest x1 0.01 us: two_on(): rows = lax.ppermute(rows, 'dom', [(i, (i + 2) % size) for i in range(size)])]
    ppermute x2 -> x3, waiting for transfers between devices: 2.47 us -> 0.08 us  [to_x(): outer = lax.ppermute(outer, 'dom', outer_pairs(size))]
    ppermute x2 -> x3, starting transfers between devices: 6.78 us -> 8.69 us  [to_x(): outer = lax.ppermute(outer, 'dom', outer_pairs(size))]
    ppermute x2 -> x3, starting transfers between devices: 4.55 us -> 6.2 us  [from_y(): up = lax.ppermute(faces, 'sub', [(i, (i + 1) % size) for i in range(size)])]
    pallas_call x8 -> x10, Pallas kernels: 4.68 us -> 5.5 us  [call(): pl.pallas_call(body, out_shape=[jax.ShapeDtypeStruct(s, F32) for s in out...]
    ppermute x2 -> x3, waiting for transfers between devices: 2.8 us -> 3.5 us  [from_y(): up = lax.ppermute(faces, 'sub', [(i, (i + 1) % size) for i in range(size)])]
    broadcast_in_dim x1 -> x0, local copies, waits for them, and re-layouts: 0.6 us -> none  [shards(): coarse = coarse[None, :, :width // PTS + 1]]
  transfers between devices with their start and end apart: 9 -> 11, of which waited for: 5 -> 4; matrix products, arithmetic and copies ran while one was open for 0% -> 0% of each run, Pallas kernels for 9% -> 13%
where the time goes in v5:
time: 27.3 us; the launch traced here: 27.1 us
  starting transfers between devices  14.9 us (55%)
  waiting for transfers between devices  6.02 us (22%)
  Pallas kernels  5.5 us (20%)
  between operations  0.7 us (3%)
    ppermute x3, starting transfers between devices, to_x(): outer = lax.ppermute(outer, 'dom', outer_pairs(size))  8.69 us
    ppermute x3, starting transfers between devices, from_y(): up = lax.ppermute(faces, 'sub', [(i, (i + 1) % size) for i in range(size)])  6.2 us
    pallas_call x10, Pallas kernels, call(): pl.pallas_call(body, out_shape=[jax.ShapeDtypeStruct(s, F32) for s in out...  5.5 us
    ppermute x3, waiting for transfers between devices, from_y(): up = lax.ppermute(faces, 'sub', [(i, (i + 1) % size) for i in range(size)])  3.5 us
    ppermute x1, waiting for transfers between devices, two_on(): return (rows, lax.ppermute(top, ('dom', 'sub'), pairs))  2.43 us
  transfers between devices with their start and end apart: 11, of which 4 were waited for; matrix products, arithmetic and copies ran while one was open for 0% of the time, Pallas kernels for 13%

profile of v5, /device:TPU:0, one launch (start us, length us, event | category | flops | bytes accessed | tf_op | source)
XLA Modules:
  0.0 27.1 jit_solution(4321544081421154469)
XLA Ops:
  0.6 1.4 %shard_map.68 = (f32[8,64,128]{2,1,0:T(8,128)S(1)}, f32[8,64,128]{2,1,0:T(8,128)S(1)}, f32[3,8,128]{2,1,0:T(8,128)S(1)}, f32[5,8,128]{2,1,0:T(8,128)S(1)}, f32[2...) custom-call(f32[8,64,128]{2,1,0:T(8,128)} %bitcast.6, f32[8,64,128]{2,1,0:T(8,128)} %bitcast.7, f32[3,8,16]{2,1,0:T(8,128)} %bitcast.8, ...), custom_call_target="tpu_custom_call" | custom-call | tf_op jit(solution)/shard_map/pallas_call | solution.py:710
  2.0 3.0 %collective-permute-start = (f32[2,5,8,128]{3,2,1,0:T(8,128)S(1)}, f32[2,5,8,128]{3,2,1,0:T(8,128)S(1)}, u32[]{:S(2)}, u32[]{:S(2)}) collective-permute-start(f32[2,5,8,128]{3,2,1,0:T(8,128)S(1)} %get-tuple-element.43), channel_id=1, source_target_pairs={{0,1},{1,0},{2,3},{3,2},{4,5},{5,4},{6,7},{7,6},{8,9},{9,8},{10,11... | collective-permute-start | bytes 122888 | tf_op jit(solution)/shard_map/ppermute | solution.py:723
  5.1 0.6 %shard_map.69 = (f32[2,8,8,8,128]{4,3,2,1,0:T(8,128)S(1)}, f32[2,2,8,8,128]{4,3,2,1,0:T(8,128)S(1)}, f32[2,2,8,128]{3,2,1,0:T(8,128)S(1)}, f32[144,128]{1,0:T(8,128)S(1)}, f32[144,128]{1,0:T(8,128)S(1)}) custom-call(s32[1]{0:T(128)} %bitcast.side_ref, f32[8,64,128]{2,1,0:T(8,128)S(1)} %get-tuple-element.38.load_ref, ...), custom_call_target="tpu_custom_call" | custom-call | tf_op jit(solution)/shard_map/pallas_call | solution.py:710
  5.7 1.4 %collective-permute-done.below_ref.above_ref = f32[2,5,8,128]{3,2,1,0:T(8,128)S(1)} collective-permute-done((f32[2,5,8,128]{3,2,1,0:T(8,128)S(1)}, f32[2,5,8,128]{3,2,1,0:T(8,128)S(1)}, u32[]{:S(2)}, u32[]{:S(2)}) %collective-permute-start) | collective-permute-done | bytes 40992 | tf_op jit(solution)/shard_map/ppermute | solution.py:723
  7.1 3.4 %collective-permute-start.1 = (f32[144,128]{1,0:T(8,128)S(1)}, f32[144,128]{1,0:T(8,128)S(1)}, u32[]{:S(2)}, u32[]{:S(2)}) collective-permute-start(f32[144,128]{1,0:T(8,128)S(1)} %get-tuple-element.55), channel_id=1, source_target_pairs={{0,30},{2,4},{4,2},{6,8},{8,6},{10,12},{12,10},{14,16},{16,14},{18... | collective-permute-start | bytes 221192 | tf_op jit(solution)/shard_map/ppermute | solution.py:739
  10.4 0.0 collective-permute-start.2
  10.4 1.9 %collective-permute-start.4 = (f32[144,128]{1,0:T(8,128)S(1)}, f32[144,128]{1,0:T(8,128)S(1)}, u32[]{:S(2)}, u32[]{:S(2)}) collective-permute-start(f32[144,128]{1,0:T(8,128)S(1)} %get-tuple-element.62), channel_id=1, source_target_pairs={{0,30},{2,4},{4,2},{6,8},{8,6},{10,12},{12,10},{14,16},{16,14},{18... | collective-permute-start | bytes 221192 | tf_op jit(solution)/shard_map/ppermute | solution.py:739
  12.3 0.0 collective-permute-start.5
  12.3 1.2 %shard_map.70 = (f32[2,2,8,8,128]{4,3,2,1,0:T(8,128)S(1)}, f32[8,8,8,128]{3,2,1,0:T(8,128)S(1)}, f32[8,8,8,128]{3,2,1,0:T(8,128)S(1)}, f32[8,8,8,128]{3,2,1,0:T(...) custom-call(f32[2,8,8,8,128]{4,3,2,1,0:T(8,128)S(1)} %get-tuple-elem, ...), custom_call_target="tpu_custom_call" | custom-call | tf_op jit(solution)/shard_map/pallas_call | solution.py:710
  13.5 0.1 collective-permute-done.1.outer_ref
  13.6 0.0 collective-permute-done.2.inner_ref
  13.6 0.6 %shard_map.72 = (f32[104,128]{1,0:T(8,128)S(1)}, f32[104,128]{1,0:T(8,128)S(1)}, f32[2,1,8,128]{3,2,1,0:T(8,128)S(1)}, f32[2,8,8,128]{3,2,1,0:T(8,128)S(1)}, f32...) custom-call(s32[1]{0:T(128)} %bitcast.side_ref, f32[2,2,8,8,128]{4,3,2,1,0:T(8,128)S(1)} %get-tuple-element.44.rough_ref, ...), custom_call_target="tpu_custom_call" | custom-call | tf_op jit(solution)/shard_map/pallas_call | solution.py:710
  14.2 3.4 %collective-permute-start.3 = (f32[104,128]{1,0:T(8,128)S(1)}, f32[104,128]{1,0:T(8,128)S(1)}, u32[]{:S(2)}, u32[]{:S(2)}) collective-permute-start(f32[104,128]{1,0:T(8,128)S(1)} %get-tuple-element.59.sent_outer_ref), channel_id=1, source_target_pairs={{0,30},{2,4},{4,2},{6,8},{8,6},{10,12},{12,10},{14,16},{16,14},{18... | collective-permute-start | bytes 159752 | tf_op jit(solution)/shard_map/ppermute | solution.py:739
  17.6 0.0 collective-permute-start.7
  17.6 0.0 collective-permute-done.4.outer_ref
  17.6 0.0 collective-permute-done.5.inner_ref
  17.6 0.2 shard_map.73
  17.8 1.6 %collective-permute-start.6 = (f32[2,1,8,128]{3,2,1,0:T(8,128)S(1)}, f32[2,1,8,128]{3,2,1,0:T(8,128)S(1)}, u32[]{:S(2)}, u32[]{:S(2)}) collective-permute-start(f32[2,1,8,128]{3,2,1,0:T(8,128)S(1)} %get-tuple-element.65), channel_id=1, source_target_pairs={{0,1},{1,0},{2,3},{3,2},{4,5},{5,4},{6,7},{7,6},{8,9},{9,8},{10,11... | collective-permute-start | bytes 24584 | tf_op jit(solution)/shard_map/ppermute | solution.py:723
  19.4 0.0 collective-permute-start.8
  19.4 0.0 collective-permute-start.9
  19.4 2.1 %collective-permute-done.6.below_ref.above_ref = f32[2,1,8,128]{3,2,1,0:T(8,128)S(1)} collective-permute-done((f32[2,1,8,128]{3,2,1,0:T(8,128)S(1)}, f32[2,1,8,128]{3,2,1,0:T(8,128)S(1)}, u32[]{:S(2)}, u32[]{:S(2)}) %collective-permute-start.6) | collective-permute-done | bytes 8224 | tf_op jit(solution)/shard_map/ppermute | solution.py:723
  21.5 0.0 collective-permute-done.3.outer_ref
  21.5 0.0 collective-permute-done.7.inner_ref
  21.5 0.2 shard_map.75
  21.7 1.6 %collective-permute-start.10 = (f32[3,128]{1,0:T(4,128)S(1)}, f32[3,128]{1,0:T(4,128)S(1)}, u32[]{:S(2)}, u32[]{:S(2)}) collective-permute-start(f32[3,128]{1,0:T(4,128)S(1)} %get-tuple-element.73), channel_id=1, source_target_pairs={{0,1},{1,0},{2,3},{3,2},{4,5},{5,4},{6,7},{7,6},{8,9},{9,8},{10,11... | collective-permute-start | bytes 4616 | tf_op jit(solution)/shard_map/ppermute | solution.py:723
  23.3 0.8 %shard_map.74 = (f32[8,64,128]{2,1,0:T(8,128)}, f32[1,128]{1,0:T(1,128)S(1)}) custom-call(s32[1]{0:T(128)} %bitcast.side_ref, f32[8,8,8,128]{3,2,1,0:T(8,128)S(1)} %get-tuple-element.57.sofar_ref, f32[8,8,8,128]{3,2,1,0:T(8,128)S(1)} %get-tuple-element.49.gain_ref, f32[2,8,8,128]{3,2,1,0:T(8,128)S(1)} %get-tuple-element.58.gface_ref, ...), custom_call_target="tpu_custom_call" | custom-call | tf_op jit(solution)/shard_map/pallas_call | solution.py:710
  24.1 2.4 %collective-permute-done.9.top_ref = f32[1,128]{1,0:T(1,128)S(1)} collective-permute-done((f32[1,128]{1,0:T(1,128)S(1)}, f32[1,128]{1,0:T(1,128)S(1)}, u32[]{:S(2)}, u32[]{:S(2)}) %collective-permute-start.9) | collective-permute-done | bytes 544 | tf_op jit(solution)/shard_map/ppermute | solution.py:750
  26.5 0.0 collective-permute-done.8.next_ref
  26.5 0.0 collective-permute-done.10.below_ref.above_ref
  26.5 0.6 %shard_map.77 = f32[8,17]{1,0:T(8,128)} custom-call(f32[8,128]{1,0:T(8,128)S(1)} %get-tuple-element.69.plane_ref, f32[8,128]{1,0:T(8,128)S(1)} %shard_map.76.joined_ref, f32[3,128]{1,0:T(4,128)S(1)} %collective-permute-done.10.below_ref.above_ref, f32[3,128]{1,0:T(4,128)S(1)} %collective-permute-done.10.below_ref.above_ref), custom_call_target="tpu_custom_call" | custom-call | tf_op jit(solution)/shard_map/pallas_call | solution.py:710
  (2 shorter events, 0.0 us)
Async XLA Ops:
  2.0 5.0 %collective-permute-start = (f32[2,5,8,128]{3,2,1,0:T(8,128)S(1)}, f32[2,5,8,128]{3,2,1,0:T(8,128)S(1)}, u32[]{:S(2)}, u32[]{:S(2)}) collective-permute-start(f32[2,5,8,128]{3,2,1,0:T(8,128)S(1)} %get-tuple-element.43), channel_id=1, source_target_pairs={{0,1},{1,0},{2,3},{3,2},{4,5},{5,4},{6,7},{7,6},{8,9},{9,8},{10,11... | collective-permute-start | bytes 122888 | tf_op jit(solution)/shard_map/ppermute | solution.py:723
  7.1 6.5 %collective-permute-start.1 = (f32[144,128]{1,0:T(8,128)S(1)}, f32[144,128]{1,0:T(8,128)S(1)}, u32[]{:S(2)}, u32[]{:S(2)}) collective-permute-start(f32[144,128]{1,0:T(8,128)S(1)} %get-tuple-element.55), channel_id=1, source_target_pairs={{0,30},{2,4},{4,2},{6,8},{8,6},{10,12},{12,10},{14,16},{16,14},{18... | collective-permute-start | bytes 221192 | tf_op jit(solution)/shard_map/ppermute | solution.py:739
  10.4 3.2 %collective-permute-start.2 = (f32[144,128]{1,0:T(8,128)S(1)}, f32[144,128]{1,0:T(8,128)S(1)}, u32[]{:S(2)}, u32[]{:S(2)}) collective-permute-start(f32[144,128]{1,0:T(8,128)S(1)} %get-tuple-element.56), channel_id=1, source_target_pairs={{0,2},{2,0},{4,6},{6,4},{8,10},{10,8},{12,14},{14,12},{16,18},{18,... | collective-permute-start | bytes 221192 | tf_op jit(solution)/shard_map/ppermute | solution.py:740
  10.4 7.1 %collective-permute-start.4 = (f32[144,128]{1,0:T(8,128)S(1)}, f32[144,128]{1,0:T(8,128)S(1)}, u32[]{:S(2)}, u32[]{:S(2)}) collective-permute-start(f32[144,128]{1,0:T(8,128)S(1)} %get-tuple-element.62), channel_id=1, source_target_pairs={{0,30},{2,4},{4,2},{6,8},{8,6},{10,12},{12,10},{14,16},{16,14},{18... | collective-permute-start | bytes 221192 | tf_op jit(solution)/shard_map/ppermute | solution.py:739
  12.3 5.2 %collective-permute-start.5 = (f32[144,128]{1,0:T(8,128)S(1)}, f32[144,128]{1,0:T(8,128)S(1)}, u32[]{:S(2)}, u32[]{:S(2)}) collective-permute-start(f32[144,128]{1,0:T(8,128)S(1)} %get-tuple-element.63), channel_id=1, source_target_pairs={{0,2},{2,0},{4,6},{6,4},{8,10},{10,8},{12,14},{14,12},{16,18},{18,... | collective-permute-start | bytes 221192 | tf_op jit(solution)/shard_map/ppermute | solution.py:740
  14.2 7.3 %collective-permute-start.3 = (f32[104,128]{1,0:T(8,128)S(1)}, f32[104,128]{1,0:T(8,128)S(1)}, u32[]{:S(2)}, u32[]{:S(2)}) collective-permute-start(f32[104,128]{1,0:T(8,128)S(1)} %get-tuple-element.59.sent_outer_ref), channel_id=1, source_target_pairs={{0,30},{2,4},{4,2},{6,8},{8,6},{10,12},{12,10},{14,16},{16,14},{18... | collective-permute-start | bytes 159752 | tf_op jit(solution)/shard_map/ppermute | solution.py:739
  17.6 3.9 %collective-permute-start.7 = (f32[104,128]{1,0:T(8,128)S(1)}, f32[104,128]{1,0:T(8,128)S(1)}, u32[]{:S(2)}, u32[]{:S(2)}) collective-permute-start(f32[104,128]{1,0:T(8,128)S(1)} %get-tuple-element.60.sent_inner_ref), channel_id=1, source_target_pairs={{0,2},{2,0},{4,6},{6,4},{8,10},{10,8},{12,14},{14,12},{16,18},{18,... | collective-permute-start | bytes 159752 | tf_op jit(solution)/shard_map/ppermute | solution.py:740
  17.8 3.7 %collective-permute-start.6 = (f32[2,1,8,128]{3,2,1,0:T(8,128)S(1)}, f32[2,1,8,128]{3,2,1,0:T(8,128)S(1)}, u32[]{:S(2)}, u32[]{:S(2)}) collective-permute-start(f32[2,1,8,128]{3,2,1,0:T(8,128)S(1)} %get-tuple-element.65), channel_id=1, source_target_pairs={{0,1},{1,0},{2,3},{3,2},{4,5},{5,4},{6,7},{7,6},{8,9},{9,8},{10,11... | collective-permute-start | bytes 24584 | tf_op jit(solution)/shard_map/ppermute | solution.py:723
  19.4 7.1 %collective-permute-start.8 = (f32[8,128]{1,0:T(8,128)S(1)}, f32[8,128]{1,0:T(8,128)S(1)}, u32[]{:S(2)}, u32[]{:S(2)}) collective-permute-start(f32[8,128]{1,0:T(8,128)S(1)} %get-tuple-element.70), channel_id=1, source_target_pairs={{0,4},{2,6},{4,8},{6,10},{8,12},{10,14},{12,16},{14,18},{16,20},{1... | collective-permute-start | bytes 12296 | tf_op jit(solution)/shard_map/ppermute | solution.py:746
  19.4 7.1 %collective-permute-start.9 = (f32[1,128]{1,0:T(1,128)S(1)}, f32[1,128]{1,0:T(1,128)S(1)}, u32[]{:S(2)}, u32[]{:S(2)}) collective-permute-start(f32[1,128]{1,0:T(1,128)S(1)} %get-tuple-element.71), channel_id=1, source_target_pairs={{0,5},{1,4},{2,7},{3,6},{4,9},{5,8},{6,11},{7,10},{8,13},{9,12},{1... | collective-permute-start | bytes 1544 | tf_op jit(solution)/shard_map/ppermute | solution.py:750
  21.7 4.8 %collective-permute-start.10 = (f32[3,128]{1,0:T(4,128)S(1)}, f32[3,128]{1,0:T(4,128)S(1)}, u32[]{:S(2)}, u32[]{:S(2)}) collective-permute-start(f32[3,128]{1,0:T(4,128)S(1)} %get-tuple-element.73), channel_id=1, source_target_pairs={{0,1},{1,0},{2,3},{3,2},{4,5},{5,4},{6,7},{7,6},{8,9},{9,8},{10,11... | collective-permute-start | bytes 4616 | tf_op jit(solution)/shard_map/ppermute | solution.py:723

commit v6 on v5

--- a/solution.py
+++ b/solution.py
@@ -1,5 +1,6 @@
 import jax
 import jax.numpy as jnp
+import ml_dtypes
 import numpy as np
 from jax import lax
 from jax.experimental import pallas as pl
@@ -58,17 +59,54 @@
 SLOPE = (-0.125, 0.125)
 
 
-def small_tables(width):
-    cells = width // PTS
-    grad = np.tile(D.T, (1, cells))
-    back = np.tile(D, (1, cells))
-    square = np.tile(D * D, (1, cells))
-    weight = np.tile(W[None], (PTS, cells))
-    row_weight = np.tile(W[:, None], (1, width))
-    return jnp.asarray(np.stack([grad, back, square, weight, row_weight]), F32)
-
-
-def restrict_tables(width):
+def tiled(matrix, width):
+    column = lax.broadcasted_iota(jnp.int32, (PTS, width), 1) % PTS
+    row = lax.broadcasted_iota(jnp.int32, (PTS, width), 0)
+    total = jnp.zeros((PTS, width), F32)
+    for c in range(PTS):
+        lines = jnp.zeros((PTS, width), F32)
+        for r in range(PTS):
+            lines = jnp.where(row == r, float(matrix[r, c]), lines)
+        total = jnp.where(column == c, lines, total)
+    return total
+
+
+def by_row(values, width):
+    return tiled(np.tile(np.asarray(values)[:, None], (1, PTS)), width)
+
+
+def cell_blocks(rows):
+    width = rows.shape[1]
+    cell = lax.broadcasted_iota(jnp.int32, rows.shape, 1) // PTS
+    return jnp.concatenate(
+        [jnp.where(cell == g, rows, 0.0) for g in range(width // PTS)], axis=0
+    )
+
+
+def paired_here(b):
+    high, low = halves(b)
+    return jnp.concatenate(
+        [
+            jnp.concatenate([high, low], axis=1),
+            jnp.concatenate([high, jnp.zeros_like(low)], axis=1),
+        ],
+        axis=0,
+    )
+
+
+def paired(b):
+    b = np.asarray(b, np.float32)
+    high = b.astype(ml_dtypes.bfloat16)
+    low = (b - high.astype(np.float32)).astype(ml_dtypes.bfloat16)
+    return jnp.asarray(np.block([[high, low], [high, np.zeros_like(low)]]))
+
+
+def column_tables(width):
+    cells = np.eye(width // PTS)
+    return paired(np.kron(cells, D.T)), paired(np.kron(cells, D))
+
+
+def restrict_table(width):
     cells = width // PTS
     hat = np.zeros((width, 128))
     slope = np.zeros((width, 128))
@@ -76,7 +114,7 @@
         rows = slice(c * PTS, (c + 1) * PTS)
         hat[rows, c], hat[rows, c + 1] = HAT[:, 0], HAT[:, 1]
         slope[rows, c], slope[rows, c + 1] = SLOPE
-    return jnp.asarray(np.concatenate([hat, slope]), F32)
+    return paired(np.concatenate([hat, slope]))
 
 
 def dot(a, b):
@@ -88,31 +126,12 @@
     return high, (a - high.astype(F32)).astype(jnp.bfloat16)
 
 
-def paired(b):
-    high, low = halves(b)
-    return jnp.concatenate(
-        [
-            jnp.concatenate([high, low], axis=1),
-            jnp.concatenate([high, jnp.zeros_like(low)], axis=1),
-        ],
-        axis=0,
-    )
-
-
 def dot_split(a, b_pair):
     both = jnp.dot(
         jnp.concatenate(halves(a), axis=1), b_pair, preferred_element_type=F32
     )
     n = both.shape[1] // 2
     return both[:, :n] + both[:, n:]
-
-
-def cell_blocks(rows):
-    width = rows.shape[1]
-    cell = lax.broadcasted_iota(jnp.int32, rows.shape, 1) // PTS
-    return jnp.concatenate(
-        [jnp.where(cell == g, rows, 0.0) for g in range(width // PTS)], axis=0
-    )
 
 
 def contract(matrix, lines, parity):
@@ -130,12 +149,20 @@
 
 
 def spread_metric(metric, weight_row):
-    cells = metric.shape[2]
+    _, rows, cells = metric.shape
     width = weight_row.shape[1]
     cell = lax.broadcasted_iota(jnp.int32, (cells, width), 1) // PTS
     row = lax.broadcasted_iota(jnp.int32, (cells, width), 0)
-    pick = jnp.where(cell == row, 1.0, 0.0).astype(F32)
-    return [dot(metric[d], pick) * weight_row for d in range(3)]
+    pick = jnp.where(cell == row, 1.0, 0.0).astype(jnp.bfloat16)
+    flat = metric.reshape(3 * rows, cells)
+    high = flat.astype(jnp.bfloat16)
+    rest = flat - high.astype(F32)
+    parts = jnp.concatenate([high, *halves(rest)], axis=1)
+    spread = jnp.dot(
+        parts, jnp.concatenate([pick] * 3, axis=0), preferred_element_type=F32
+    )
+    spread = [spread[d * rows : (d + 1) * rows] for d in range(3)]
+    return [v * weight_row[:1] for v in spread], spread[2]
 
 
 def column_masks(shape):
@@ -171,80 +198,66 @@
     return lambda i, j: ref[i, pl.ds(j, ny, stride=PTS)]
 
 
-def edge_kernel(
-    load_in, mob_in, metric_in, tab_in, restrict_in,
-    load_ref, mob_ref, spread_ref, tab_ref, restrict_ref, yface_ref, metric_ref, sems,
-):
-    copies = [
-        pltpu.make_async_copy(source, target, sems.at[n])
-        for n, (source, target) in enumerate(
-            [
-                (tab_in, tab_ref),
-                (metric_in, metric_ref),
-                (mob_in, mob_ref),
-                (load_in, load_ref),
-                (restrict_in, restrict_ref),
-            ]
-        )
-    ]
+def edge_kernel(metric_in, mob_in, load_in, spread_ref, yface_ref, metric_ref, mob_ref, load_ref, sems):
+    ny, width = spread_ref.shape[1:]
+    ends = (0, PTS - 1)
+    copies = [pltpu.make_async_copy(metric_in, metric_ref, sems.at[0])]
+    for n, (source, target) in enumerate(((mob_in, mob_ref), (load_in, load_ref))):
+        for s, e in enumerate((0, ny - 1)):
+            copies.append(
+                pltpu.make_async_copy(
+                    source.at[:, pl.ds(e * PTS, PTS)], target.at[s], sems.at[1 + 2 * n + s]
+                )
+            )
     for copy in copies:
         copy.start()
-    copies[0].wait()
-    copies[1].wait()
-    ny, width = spread_ref.shape[1:]
-    tables = tab_ref[...]
-    spread = spread_metric(metric_ref[...], tables[3])
+    masks = column_masks((PTS, width))
+    weight_row = tiled(np.tile(W[None], (PTS, 1)), width)
+    row_weight = by_row(W, width)
+    squared = paired_here(cell_blocks(tiled(D * D, width)))
+    squares = [by_row(D[a] ** 2, width) for a in range(PTS)]
+    mob_rows, load_rows = (r.reshape(2 * PTS * PTS, width) for r in (mob_ref, load_ref))
+
+    def across(ref, s, j):
+        return ref[pl.ds(s * PTS * PTS + j, PTS, stride=PTS)]
+
+    for copy in copies:
+        copy.wait()
+    spread, cell_metric = spread_metric(metric_ref[...], weight_row)
     for d in range(3):
         spread_ref[d] = spread[d]
-    squared = paired(cell_blocks(tables[2]))
-    square = D * D
-    mob, load = plane(mob_ref, ny), plane(load_ref, ny)
-    masks = column_masks((PTS * ny, width))
-    copies[2].wait()
-    ends = (0, PTS - 1)
-    sums, weights = [[], []], [[], []]
-    for i in range(PTS):
-        factor = [mob(i, j) * (float(W[i]) * spread[1]) for j in range(PTS)]
-        for s in range(2):
-            e = 0 if s == 0 else ny - 1
-            sums[s].append(sum(float(square[j, ends[s]] * W[j]) * factor[j] for j in range(PTS)))
-            weights[s].append(
-                sum(float(D[j, ends[s]] * W[j]) * factor[j] for j in range(PTS))[e : e + 1]
-            )
+    points = [across(mob_rows, s, ends[s]) * (float(W[ends[s]]) * row_weight) for s in range(2)]
+    columns = dot_split(
+        jnp.concatenate([p * weight_row for p in points], axis=0), squared
+    )
+    for s, e in enumerate((0, ny - 1)):
+        j = ends[s]
+        scale = [spread[d][e : e + 1] for d in range(3)]
+        along = points[s] * scale[0]
+        total = sum(squares[a] * along[a : a + 1] for a in range(PTS))
+        sums = [
+            sum(float(D[b, j] ** power * W[b]) * across(mob_rows, s, b) for b in range(PTS))
+            * row_weight
+            * scale[1]
+            for power in (1, 2)
+        ]
+        yface_ref[s, 2] = along
+        yface_ref[s, 3] = points[s] * scale[2]
+        yface_ref[s, 4] = sums[0]
+        column = columns[s * PTS : (s + 1) * PTS] * cell_metric[e : e + 1]
+        yface_ref[s, 1] = sum_z(total + sums[1] + column, masks)
     for s in range(2):
-        j = ends[s]
-        points = [mob(i, j) * float(W[i] * W[j]) for i in range(PTS)]
-        along = contract(square.T, [p * spread[0] for p in points], 1)
-        column = dot_split(jnp.concatenate([p * spread[2] for p in points], axis=0), squared)
-        total = column + jnp.concatenate([along[i] + sums[s][i] for i in range(PTS)], axis=0)
-        total = sum_z(total, masks)
-        e = 0 if s == 0 else ny - 1
-        yface_ref[s, 1] = jnp.concatenate(
-            [total[i * ny + e : i * ny + e + 1] for i in range(PTS)], axis=0
-        )
-    copies[3].wait()
-    for s in range(2):
-        e = 0 if s == 0 else ny - 1
-        row = e * PTS + ends[s]
-        value = jnp.concatenate([load_ref[i, row : row + 1] for i in range(PTS)], axis=0)
-        yface_ref[s, 0] = sum_z(value, column_masks((PTS, width)))
-        points = jnp.concatenate([mob_ref[i, row : row + 1] for i in range(PTS)], axis=0)
-        points = points * (float(W[ends[s]]) * tables[4])
-        yface_ref[s, 2] = points * spread[0][e : e + 1]
-        yface_ref[s, 3] = points * spread[2][e : e + 1]
-        yface_ref[s, 4] = jnp.concatenate(weights[s], axis=0)
-    copies[4].wait()
+        yface_ref[s, 0] = sum_z(across(load_rows, s, ends[s]), masks)
 
 
 def diag_kernel(
-    side_ref, load_ref, mob_ref, spread_ref, tab_ref,
+    side_ref, load_ref, mob_ref, spread_ref,
     fields_ref, xface_ref, factor_ref, to_outer_ref, to_inner_ref,
 ):
-    tables = tab_ref[...]
     ny, width = fields_ref.shape[3:]
     spread = [spread_ref[d] for d in range(3)]
-    squared = paired(cell_blocks(tables[2]))
     square = D * D
+    squared = paired_here(cell_blocks(tiled(square, width)))
     mob, load = plane(mob_ref, ny), plane(load_ref, ny)
     diag_ref = fields_ref.at[1]
     even = side_ref[0] == 0
@@ -278,9 +291,10 @@
         sum_y_local(fields_ref.at[f], ny)
         xface_ref[f, 0] = fields_ref[f, 0]
         xface_ref[f, 1] = fields_ref[f, PTS - 1]
+    row_weight = by_row(W, width)
     for s, i in enumerate((0, PTS - 1)):
         for n, e in enumerate((0, ny - 1)):
-            points = mob_ref[i, e * PTS : (e + 1) * PTS] * (float(W[i]) * tables[4])
+            points = mob_ref[i, e * PTS : (e + 1) * PTS] * (float(W[i]) * row_weight)
             factor_ref[s, n] = points * spread[1][e : e + 1]
 
 
@@ -309,12 +323,11 @@
 
 
 def inside_kernel(
-    fields_ref, load_ref, mob_ref, spread_ref, tab_ref, below_ref, above_ref,
+    fields_ref, load_ref, mob_ref, spread_ref, grad_ref, back_ref, below_ref, above_ref,
     rough_ref, value_ref, partial_ref, gain_ref, out_ref, pair_ref, weights_ref, sums_ref, edge_weights_ref,
     work_ref,
 ):
     below_ref, above_ref = below_ref.at[1], above_ref.at[0]
-    tables = tab_ref[...]
     ny, width = out_ref.shape[2:]
     spread = [spread_ref[d] for d in range(3)]
     mob, load = plane(mob_ref, ny), plane(load_ref, ny)
@@ -334,12 +347,13 @@
                 value_ref[i, j] = partial_ref[i, j] = gain_ref[i, j] = zero
             else:
                 value_ref[i, j], partial_ref[i, j], gain_ref[i, j] = first_step(*sums)
-    grad = paired(cell_blocks(tables[0]))
-    back = paired(cell_blocks(tables[1]))
+    grad, back = grad_ref[...], back_ref[...]
     for j in range(PTS):
         factor = [mob(i, j) * (float(W[i] * W[j]) * spread[0]) for i in range(PTS)]
-        for n, (p, q) in enumerate(((0, 0), (0, PTS - 1), (PTS - 1, PTS - 1))):
-            pair_ref[n, j] = sum(float(D[a, p] * D[a, q]) * factor[a] for a in range(PTS))
+        for n, p in enumerate((0, PTS - 1)):
+            coupling = contract(D.T, [float(D[a, p]) * factor[a] for a in range(PTS)], -1)
+            for i in range(PTS):
+                pair_ref[n, i, j] = coupling[i]
         flux = contract(D, [value_ref[i, j] for i in range(PTS)], -1)
         flux = [flux[i] * factor[i] for i in range(PTS)]
         for i, value in enumerate(contract(D.T, flux, -1)):
@@ -373,7 +387,7 @@
     for n in range(4):
         sums_ref[n] = sums[n]
     for t, ref in enumerate((below_ref, above_ref)):
-        edge_weights_ref[t, 0] = dot(tables[0][:, :PTS], ref[2])
+        edge_weights_ref[t, 0] = sum(by_row(D[a], width) * ref[2, a : a + 1] for a in range(PTS))
         edge_weights_ref[t, 1] = ref[4]
         edge_weights_ref[t, 2] = dot_split(ref[3], back)
 
@@ -386,14 +400,13 @@
 
 
 def faces_kernel(
-    side_ref, rough_ref, value_ref, out_ref, pair_ref, mob_ref, spread_ref, tab_ref,
+    side_ref, rough_ref, value_ref, out_ref, pair_ref, mob_ref, spread_ref, grad_ref, back_ref,
     below_ref, above_ref, partial_ref, gain_ref, weights_ref, load_sums_ref, edge_weights_ref,
     outer_ref, inner_ref,
     to_outer_ref, to_inner_ref, yface_ref, gface_ref, sofar_ref, sums_ref, line_ref, work_ref,
 ):
     below_ref, above_ref = below_ref.at[1], above_ref.at[0]
     even = side_ref[0] == 0
-    tables = tab_ref[...]
     ny, width = out_ref.shape[2:]
     spread = [spread_ref[d] for d in range(3)]
     mob = plane(mob_ref, ny)
@@ -425,10 +438,8 @@
         for t, ref in enumerate((below_ref, above_ref)):
             lines.append(value[s][ends[t]])
             factors.append(jnp.broadcast_to(ref[3, ends[s] : ends[s] + 1], (ny, width)))
-    grad = paired(cell_blocks(tables[0]))
-    back = paired(cell_blocks(tables[1]))
-    flux = dot_split(jnp.concatenate(lines, axis=0), grad) * jnp.concatenate(factors, axis=0)
-    line_ref[...] = dot_split(flux, back)
+    flux = dot_split(jnp.concatenate(lines, axis=0), grad_ref[...]) * jnp.concatenate(factors, axis=0)
+    line_ref[...] = dot_split(flux, back_ref[...])
     edge_y = [[None, None], [None, None]]
     total = [[None] * PTS, [None] * PTS]
     for s in range(2):
@@ -443,22 +454,18 @@
                 float(D[j, ends[t]]) * (gradient[j] * factor[j : j + 1]) for j in range(PTS)
             )[rows[t] : rows[t] + 1]
     for j in range(PTS):
-        total[0][j] += out_ref[0, j] + pair_ref[0, j] * value[0][j] + pair_ref[1, j] * value[1][j]
-        total[1][j] += out_ref[PTS - 1, j] + pair_ref[1, j] * value[0][j] + pair_ref[2, j] * value[1][j]
+        across = [
+            out_ref[i, j] + (pair_ref[0, i, j] * value[0][j] + pair_ref[1, i, j] * value[1][j])
+            for i in range(PTS)
+        ]
+        total[0][j] += across[0]
+        total[1][j] += across[PTS - 1]
+        for i in range(1, PTS - 1):
+            work_ref[i, j] = across[i]
     for s in range(2):
         for j in range(PTS):
             at = (s * PTS + j) * ny
             total[s][j] += line_ref[at : at + ny]
-    for j in range(PTS):
-        flux = [
-            mob(a, j)
-            * (float(W[a] * W[j]) * spread[0])
-            * (float(D[a, 0]) * value[0][j] + float(D[a, PTS - 1]) * value[1][j])
-            for a in range(PTS)
-        ]
-        flux = contract(D.T, flux, -1)
-        for i in range(1, PTS - 1):
-            work_ref[i, j] = out_ref[i, j] + flux[i]
     ymessage = []
     for t in range(2):
         j = ends[t]
@@ -601,37 +608,51 @@
     return dot_split(jnp.concatenate([smooth, slope], axis=1), restrict)
 
 
+def pick(even, first, second, at, count):
+    return jnp.where(even, first[at : at + count], second[at : at + count])
+
+
 def ahead_kernel(
-    side_ref, sent_outer_ref, sent_inner_ref, gface_ref, tab_ref, restrict_ref, outer_ref, inner_ref, yface_ref,
-    own_ref, next_ref, top_ref, to_y_ref,
+    side_ref, sent_outer_ref, sent_inner_ref, gface_ref, restrict_ref, outer_ref, inner_ref,
+    next_ref, top_ref,
 ):
     ny, width = gface_ref.shape[2:]
-    to_y_ref[...] = yface_ref[...]
     even = side_ref[0] == 0
-    back = paired(cell_blocks(tab_ref[1]))
-
-    def rows(at, first, second):
-        return jnp.where(even, first[at : at + ny], second[at : at + ny])
-
-    change = [-(gface_ref[0, j] * rows(j * ny, sent_outer_ref, sent_inner_ref)) for j in range(PTS)]
-    spread = [rows((2 * PTS + d) * ny, outer_ref, inner_ref) for d in range(2)]
-    points = [rows((PTS + j) * ny, outer_ref, inner_ref) for j in range(PTS)]
-    column = dot_split(jnp.concatenate([p * spread[1] for p in points], axis=0), back)
-    weight = [
-        [rows(j * ny, outer_ref, inner_ref) for j in range(PTS)],
-        contract(D.T, [p * spread[0] for p in points], -1),
-        [column[j * ny : (j + 1) * ny] for j in range(PTS)],
-    ]
-    for q in range(2):
-        own_ref[q], own_ref[2 + q] = face_change(change, weight, PTS - 1, 1, q)
-    change = [-(gface_ref[1, j] * rows(j * ny, sent_inner_ref, sent_outer_ref)) for j in range(PTS)]
-    weight = [[rows(j * ny, inner_ref, outer_ref) for j in range(PTS)]]
+    change = [
+        -(gface_ref[1, j] * pick(even, sent_inner_ref, sent_outer_ref, j * ny, ny)) for j in range(PTS)
+    ]
+    weight = [[pick(even, inner_ref, outer_ref, j * ny, ny) for j in range(PTS)]]
     smooth = jnp.concatenate([face_change(change, weight, 0, 1, q)[0] for q in range(2)], axis=0)
-    corners = to_vertices(smooth, jnp.zeros_like(smooth), paired(restrict_ref[...]))
+    corners = to_vertices(smooth, jnp.zeros_like(smooth), restrict_ref[...])
     lower, upper = corners[:ny], corners[ny:]
     row = lax.broadcasted_iota(jnp.int32, lower.shape, 0)
     next_ref[...] = lower + jnp.where(row == 0, 0.0, pltpu.roll(upper, 1, 0))
-    top_ref[...] = upper[ny - 1 : ny]
+    top_ref[...] = jnp.broadcast_to(upper[ny - 1 : ny], top_ref.shape)
+
+
+def behind_kernel(
+    side_ref, sent_outer_ref, sent_inner_ref, gface_ref, back_ref, outer_ref, inner_ref,
+    own_ref,
+):
+    ny, width = gface_ref.shape[2:]
+    even = side_ref[0] == 0
+
+    def rows(at):
+        return pick(even, outer_ref, inner_ref, at, ny)
+
+    change = [
+        -(gface_ref[0, j] * pick(even, sent_outer_ref, sent_inner_ref, j * ny, ny)) for j in range(PTS)
+    ]
+    spread = [rows((2 * PTS + d) * ny) for d in range(2)]
+    points = [rows((PTS + j) * ny) for j in range(PTS)]
+    column = dot_split(jnp.concatenate([p * spread[1] for p in points], axis=0), back_ref[...])
+    weight = [
+        [rows(j * ny) for j in range(PTS)],
+        contract(D.T, [p * spread[0] for p in points], -1),
+        [column[j * ny : (j + 1) * ny] for j in range(PTS)],
+    ]
+    for q in range(2):
+        own_ref[q], own_ref[2 + q] = face_change(change, weight, PTS - 1, 1, q)
 
 
 def coarse_kernel(
@@ -660,7 +681,7 @@
     extra = before(base + 4 * ny, PTS)
     smooth = jnp.concatenate(total[:2] + [extra], axis=0)
     slope = jnp.concatenate(total[2:] + [pltpu.roll(extra, PTS - 2, 0)], axis=0)
-    corners = to_vertices(smooth, slope, paired(restrict_ref[...]))
+    corners = to_vertices(smooth, slope, restrict_ref[...])
     lower, upper = corners[:ny], corners[ny : 2 * ny]
     extra = corners[2 * ny :]
     row = lax.broadcasted_iota(jnp.int32, lower.shape, 0)
@@ -693,7 +714,7 @@
 
 def join_kernel(next_ref, top_ref, token_ref, joined_ref):
     row = lax.broadcasted_iota(jnp.int32, next_ref.shape, 0)
-    joined_ref[...] = next_ref[...] + jnp.where(row == 0, top_ref[...], 0.0) + token_ref[...]
+    joined_ref[...] = next_ref[...] + jnp.where(row == 0, top_ref[0:1], 0.0) + token_ref[...]
 
 
 def last_kernel(plane_ref, joined_ref, below_ref, above_ref, coarse_ref):
@@ -709,7 +730,7 @@
     spaces = spaces or [pltpu.SMEM if a.dtype == jnp.int32 else pltpu.VMEM for a in args]
     return pl.pallas_call(
         body,
-        out_shape=[jax.ShapeDtypeStruct(s, F32) for s in outs],
+        out_shape=[jax.ShapeDtypeStruct(s, F32) if isinstance(s, tuple) else s for s in outs],
         in_specs=[pl.BlockSpec(memory_space=m) for m in spaces],
         out_specs=[pl.BlockSpec(memory_space=m) for m in out_spaces or [pltpu.VMEM] * len(outs)],
         scratch_shapes=[pltpu.VMEM(s, F32) if isinstance(s, tuple) else s for s in scratch],
@@ -756,16 +777,20 @@
     mob = mobility.reshape(PTS, ny * PTS, width)
     metric = metric[:, 0]
     side = (lax.axis_index("dom") % 2).astype(jnp.int32).reshape(1)
-    tables = small_tables(width)
-    restrict = restrict_tables(width)
+    def in_hbm(*arrays):
+        return [pltpu.with_memory_space_constraint(a, pltpu.HBM) for a in arrays]
+
+    grad, back = column_tables(width)
+    restrict = restrict_table(width)
     field = (PTS, PTS, ny, width)
     face = (PTS, ny, width)
-    load, mob, spread, tables, restrict, yface = call(
+    ends = (2, PTS, PTS, width)
+    spread, yface = call(
         edge_kernel,
-        [load.shape, mob.shape, (3, ny, width), tables.shape, restrict.shape, (2, 5, PTS, width)],
-        [metric.shape, pltpu.SemaphoreType.DMA((5,))],
-        *(pltpu.with_memory_space_constraint(a, pltpu.HBM) for a in (load, mob, metric, tables, restrict)),
-        spaces=[pltpu.HBM] * 5,
+        [(3, ny, width), (2, 5, PTS, width)],
+        [metric.shape, ends, ends, pltpu.SemaphoreType.DMA((5,))],
+        *in_hbm(metric, mob, load),
+        spaces=[pltpu.HBM] * 3,
     )
     below, above = from_y(yface)
     still = (2 * (PTS + 1) * ny, width)
@@ -773,7 +798,7 @@
         diag_kernel,
         [(2,) + field, (2, 2) + face, (2, 2, PTS, width), still, still],
         [],
-        side, load, mob, spread, tables,
+        side, load, mob, spread,
     )
     rows = (2 * PTS * ny + 2 * PTS, width)
     outer, inner = to_x(*call(merge_kernel, [rows, rows], [], side, xface, factor, below, above))
@@ -782,30 +807,36 @@
     rough, value, partial, gain, out, pair, weights, load_sums, edge_weights = call(
         inside_kernel,
         [
-            (2,) + faces, field, field, field, field, (3,) + face,
+            (2,) + faces, field, field, field, field, (2,) + field,
             (3,) + field, (4, ny, width), (2, 3, PTS, width),
         ],
         [face],
-        fields, load, mob, spread, tables, below, above,
+        fields, load, mob, spread, grad, back, below, above,
     )
     rows = ((PTS + 4) * ny + PTS, width)
     sent_outer, sent_inner, yface, gface, sofar, sums = call(
         faces_kernel,
         [rows, rows, (2, 1, PTS, width), faces, field, (4, ny, width)],
         [((2 * PTS + 4) * ny, width), field],
-        side, rough, value, out, pair, mob, spread, tables, below, above,
+        side, rough, value, out, pair, mob, spread, grad, back, below, above,
         partial, gain, weights, load_sums, edge_weights, outer, inner,
     )
     outer, inner = to_x(sent_outer, sent_inner)
-    own, onward, top, yface = call(
+    onward, top = call(
         ahead_kernel,
-        [(4, ny, width), (ny, 128), (1, 128), yface.shape],
+        [(ny, 128), (3 * PTS, 128)],
         [],
-        side, sent_outer, sent_inner, gface, tables, restrict, still_outer, still_inner, yface,
+        side, sent_outer, sent_inner, gface, restrict, still_outer, still_inner,
+    )
+    (own,) = call(
+        behind_kernel,
+        [(4, ny, width)],
+        [],
+        side, sent_outer, sent_inner, gface, back, still_outer, still_inner,
     )
     onward, top = two_on(onward, top)
     below, above = from_y(yface)
-    plane, edge = call(
+    own_rows, tops = call(
         coarse_kernel,
         [(ny, 128), (3, 128)],
         [],
@@ -819,8 +850,8 @@
         out_spaces=[pltpu.HBM, pltpu.VMEM],
     )
     (onward,) = call(join_kernel, [(ny, 128)], [], onward, top, token, flops=FLOPS_JOIN)
-    below, above = from_y(edge)
-    (coarse,) = call(last_kernel, [(ny, width // PTS + 1)], [], plane, onward, below, above)
+    below, above = from_y(tops)
+    (coarse,) = call(last_kernel, [(ny, width // PTS + 1)], [], own_rows, onward, below, above)
     return pressure.reshape(element_load.shape), coarse[None]
 
 

time: 27.3 us -> 26.2 us (0.960)
  waiting for transfers between devices: 6.02 us -> 4.91 us
    ppermute x1, waiting for transfers between devices: 2.43 us -> 0.01 us  [two_on(): return (rows, lax.ppermute(top, ('dom', 'sub'), pairs))]
    ppermute x1, waiting for transfers between devices: 0.01 us -> 1.58 us  [two_on(): rows = lax.ppermute(rows, 'dom', [(i, (i + 2) % size) for i in range(size)])]
    pallas_call x10 -> x11, Pallas kernels: 5.5 us -> 5.55 us  [call(): pl.pallas_call(body, out_shape=[jax.ShapeDtypeStruct(s, F32) if isinstanc...]
  transfers between devices with their start and end apart: 11 -> 11, of which waited for: 4 -> 3; matrix products, arithmetic and copies ran while one was open for 0% -> 0% of each run, Pallas kernels for 13% -> 14%
where the time goes in v6:
time: 26.2 us; the launch traced here: 26.1 us
  starting transfers between devices  14.8 us (56%)
  Pallas kernels  5.55 us (21%)
  waiting for transfers between devices  4.91 us (19%)
  between operations  0.75 us (3%)
    ppermute x3, starting transfers between devices, to_x(): outer = lax.ppermute(outer, 'dom', outer_pairs(size))  8.61 us
    ppermute x3, starting transfers between devices, from_y(): up = lax.ppermute(faces, 'sub', [(i, (i + 1) % size) for i in range(size)])  6.2 us
    pallas_call x11, Pallas kernels, call(): pl.pallas_call(body, out_shape=[jax.ShapeDtypeStruct(s, F32) if isinstanc...  5.55 us
    ppermute x3, waiting for transfers between devices, from_y(): up = lax.ppermute(faces, 'sub', [(i, (i + 1) % size) for i in range(size)])  3.31 us
    ppermute x1, waiting for transfers between devices, two_on(): rows = lax.ppermute(rows, 'dom', [(i, (i + 2) % size) for i in range(size)])  1.58 us
  transfers between devices with their start and end apart: 11, of which 3 were waited for; matrix products, arithmetic and copies ran while one was open for 0% of the time, Pallas kernels for 14%

profile of v6, /device:TPU:0, one launch (start us, length us, event | category | flops | bytes accessed | tf_op | source)
XLA Modules:
  0.0 26.1 jit_solution(5454363510312926210)
XLA Ops:
  0.6 0.0 copy-start
  0.6 0.0 copy-start.1
  0.6 1.2 %shard_map.77 = (f32[3,8,128]{2,1,0:T(8,128)S(1)}, f32[2,5,8,128]{3,2,1,0:T(8,128)S(1)}) custom-call(f32[3,8,16]{2,1,0:T(8,128)} %bitcast.13, f32[8,64,128]{2,1,0:T(8,128)} %bitcast.6, f32[8,64,128]{2,1,0:T(8,128)} %bitcast.10), custom_call_target="tpu_custom_call" | custom-call | tf_op jit(solution)/shard_map/pallas_call | solution.py:731
  1.9 3.0 %collective-permute-start = (f32[2,5,8,128]{3,2,1,0:T(8,128)S(1)}, f32[2,5,8,128]{3,2,1,0:T(8,128)S(1)}, u32[]{:S(2)}, u32[]{:S(2)}) collective-permute-start(f32[2,5,8,128]{3,2,1,0:T(8,128)S(1)} %get-tuple-element.34), channel_id=1, source_target_pairs={{0,1},{1,0},{2,3},{3,2},{4,5},{5,4},{6,7},{7,6},{8,9},{9,8},{10,11... | collective-permute-start | bytes 122888 | tf_op jit(solution)/shard_map/ppermute | solution.py:744
  4.9 0.0 copy-done
  4.9 0.0 copy-done.1
  4.9 0.0 copy-start.4
  4.9 0.6 %shard_map.78 = (f32[2,8,8,8,128]{4,3,2,1,0:T(8,128)S(1)}, f32[2,2,8,8,128]{4,3,2,1,0:T(8,128)S(1)}, f32[2,2,8,128]{3,2,1,0:T(8,128)S(1)}, f32[144,128]{1,0:T(8,128)S(1)}, f32[144,128]{1,0:T(8,128)S(1)}) custom-call(s32[1]{0:T(128)} %bitcast.side_ref, f32[8,64,128]{2,1,0:T(8,128)S(1)} %bitcast.11, f32[8,64,128]{2,1,0:T(8,128)S(1)} %bitcast.7, ...), custom_call_target="tpu_custom_call" | custom-call | tf_op jit(solution)/shard_map/pallas_call | solution.py:731
  5.5 0.0 copy-start.2
  5.5 1.3 %collective-permute-done.below_ref.above_ref = f32[2,5,8,128]{3,2,1,0:T(8,128)S(1)} collective-permute-done((f32[2,5,8,128]{3,2,1,0:T(8,128)S(1)}, f32[2,5,8,128]{3,2,1,0:T(8,128)S(1)}, u32[]{:S(2)}, u32[]{:S(2)}) %collective-permute-start) | collective-permute-done | bytes 40992 | tf_op jit(solution)/shard_map/ppermute | solution.py:744
  6.9 3.4 %collective-permute-start.1 = (f32[144,128]{1,0:T(8,128)S(1)}, f32[144,128]{1,0:T(8,128)S(1)}, u32[]{:S(2)}, u32[]{:S(2)}) collective-permute-start(f32[144,128]{1,0:T(8,128)S(1)} %get-tuple-element.46), channel_id=1, source_target_pairs={{0,30},{2,4},{4,2},{6,8},{8,6},{10,12},{12,10},{14,16},{16,14},{18... | collective-permute-start | bytes 221192 | tf_op jit(solution)/shard_map/ppermute | solution.py:760
  10.3 0.0 collective-permute-start.2
  10.3 1.9 %collective-permute-start.6 = (f32[144,128]{1,0:T(8,128)S(1)}, f32[144,128]{1,0:T(8,128)S(1)}, u32[]{:S(2)}, u32[]{:S(2)}) collective-permute-start(f32[144,128]{1,0:T(8,128)S(1)} %get-tuple-element.55), channel_id=1, source_target_pairs={{0,30},{2,4},{4,2},{6,8},{8,6},{10,12},{12,10},{14,16},{16,14},{18... | collective-permute-start | bytes 221192 | tf_op jit(solution)/shard_map/ppermute | solution.py:760
  12.2 0.0 collective-permute-start.7
  12.2 0.0 copy-done.4
  12.2 0.0 copy-done.2
  12.2 1.3 %shard_map.79 = (f32[2,2,8,8,128]{4,3,2,1,0:T(8,128)S(1)}, f32[8,8,8,128]{3,2,1,0:T(8,128)S(1)}, f32[8,8,8,128]{3,2,1,0:T(8,128)S(1)}, f32[8,8,8,128]{3,2,1,0:T(...) custom-call(f32[2,8,8,8,128]{4,3,2,1,0:T(8,128)S(1)} %get-tuple-elem, ...), custom_call_target="tpu_custom_call" | custom-call | tf_op jit(solution)/shard_map/pallas_call | solution.py:731
  13.5 0.0 collective-permute-done.1.outer_ref
  13.5 0.0 collective-permute-done.2.inner_ref
  13.5 0.0 copy-start.3
  13.5 0.5 %shard_map.81 = (f32[104,128]{1,0:T(8,128)S(1)}, f32[104,128]{1,0:T(8,128)S(1)}, f32[2,1,8,128]{3,2,1,0:T(8,128)S(1)}, f32[2,8,8,128]{3,2,1,0:T(8,128)S(1)}, f32...) custom-call(s32[1]{0:T(128)} %bitcast.side_ref, f32[2,2,8,8,128]{4,3,2,1,0:T(8,128)S(1)} %get-tuple-element.35.rough_ref, ...), custom_call_target="tpu_custom_call" | custom-call | tf_op jit(solution)/shard_map/pallas_call | solution.py:731
  14.0 3.3 %collective-permute-start.3 = (f32[104,128]{1,0:T(8,128)S(1)}, f32[104,128]{1,0:T(8,128)S(1)}, u32[]{:S(2)}, u32[]{:S(2)}) collective-permute-start(f32[104,128]{1,0:T(8,128)S(1)} %get-tuple-element.50.sent_outer_ref), channel_id=1, source_target_pairs={{0,30},{2,4},{4,2},{6,8},{8,6},{10,12},{12,10},{14,16},{16,14},{18... | collective-permute-start | bytes 159752 | tf_op jit(solution)/shard_map/ppermute | solution.py:760
  17.4 0.0 collective-permute-start.5
  17.4 0.0 collective-permute-done.6.outer_ref
  17.4 0.0 collective-permute-done.7.inner_ref
  17.4 0.0 copy-done.3
  17.4 0.2 shard_map.85
  17.5 0.0 collective-permute-start.9
  17.5 1.6 %collective-permute-start.4 = (f32[2,1,8,128]{3,2,1,0:T(8,128)S(1)}, f32[2,1,8,128]{3,2,1,0:T(8,128)S(1)}, u32[]{:S(2)}, u32[]{:S(2)}) collective-permute-start(f32[2,1,8,128]{3,2,1,0:T(8,128)S(1)} %get-tuple-element.51), channel_id=1, source_target_pairs={{0,1},{1,0},{2,3},{3,2},{4,5},{5,4},{6,7},{7,6},{8,9},{9,8},{10,11... | collective-permute-start | bytes 24584 | tf_op jit(solution)/shard_map/ppermute | solution.py:744
  19.1 0.0 collective-permute-start.8
  19.1 0.2 shard_map.83.own_ref
  19.3 2.0 %collective-permute-done.4.below_ref.above_ref = f32[2,1,8,128]{3,2,1,0:T(8,128)S(1)} collective-permute-done((f32[2,1,8,128]{3,2,1,0:T(8,128)S(1)}, f32[2,1,8,128]{3,2,1,0:T(8,128)S(1)}, u32[]{:S(2)}, u32[]{:S(2)}) %collective-permute-start.4) | collective-permute-done | bytes 8224 | tf_op jit(solution)/shard_map/ppermute | solution.py:744
  21.3 0.0 collective-permute-done.3.outer_ref
  21.3 0.0 collective-permute-done.5.inner_ref
  21.3 0.2 shard_map.84
  21.5 1.6 %collective-permute-start.10 = (f32[3,128]{1,0:T(4,128)S(1)}, f32[3,128]{1,0:T(4,128)S(1)}, u32[]{:S(2)}, u32[]{:S(2)}) collective-permute-start(f32[3,128]{1,0:T(4,128)S(1)} %get-tuple-element.61), channel_id=1, source_target_pairs={{0,1},{1,0},{2,3},{3,2},{4,5},{5,4},{6,7},{7,6},{8,9},{9,8},{10,11... | collective-permute-start | bytes 4616 | tf_op jit(solution)/shard_map/ppermute | solution.py:744
  23.1 0.8 %shard_map.82 = (f32[8,64,128]{2,1,0:T(8,128)}, f32[1,128]{1,0:T(1,128)S(1)}) custom-call(s32[1]{0:T(128)} %bitcast.side_ref, f32[8,8,8,128]{3,2,1,0:T(8,128)S(1)} %get-tuple-element.48.sofar_ref, f32[8,8,8,128]{3,2,1,0:T(8,128)S(1)} %get-tuple-element.40.gain_ref, f32[2,8,8,128]{3,2,1,0:T(8,128)S(1)} %get-tuple-element.49.gface_ref, ...), custom_call_target="tpu_custom_call" | custom-call | tf_op jit(solution)/shard_map/pallas_call | solution.py:731
  23.9 1.6 %collective-permute-done.8.next_ref = f32[8,128]{1,0:T(8,128)S(1)} collective-permute-done((f32[8,128]{1,0:T(8,128)S(1)}, f32[8,128]{1,0:T(8,128)S(1)}, u32[]{:S(2)}, u32[]{:S(2)}) %collective-permute-start.8) | collective-permute-done | bytes 4128 | tf_op jit(solution)/shard_map/ppermute | solution.py:767
  25.4 0.0 collective-permute-done.9.top_ref
  25.5 0.0 collective-permute-done.10.below_ref.above_ref
  25.5 0.6 %shard_map.87 = f32[8,17]{1,0:T(8,128)} custom-call(f32[8,128]{1,0:T(8,128)S(1)} %get-tuple-element.57.plane_ref, f32[8,128]{1,0:T(8,128)S(1)} %shard_map.86.joined_ref, f32[3,128]{1,0:T(4,128)S(1)} %collective-permute-done.10.below_ref.above_ref, f32[3,128]{1,0:T(4,128)S(1)} %collective-permute-done.10.below_ref.above_ref), custom_call_target="tpu_custom_call" | custom-call | tf_op jit(solution)/shard_map/pallas_call | solution.py:731
  (2 shorter events, 0.0 us)
Async XLA Ops:
  0.6 4.3 %copy-start = (f32[1,8,8,8,128]{4,3,2,1,0:T(8,128)S(1)}, f32[1,8,8,8,128]{4,3,2,1,0:T(8,128)}, u32[]{:S(2)}) copy-start(f32[1,8,8,8,128]{4,3,2,1,0:T(8,128)} %param.7) | copy-start | bytes 786436
  0.6 4.3 %copy-start.1 = (f32[1,8,8,8,128]{4,3,2,1,0:T(8,128)S(1)}, f32[1,8,8,8,128]{4,3,2,1,0:T(8,128)}, u32[]{:S(2)}) copy-start(f32[1,8,8,8,128]{4,3,2,1,0:T(8,128)} %param.6) | copy-start | bytes 786436
  1.9 5.0 %collective-permute-start = (f32[2,5,8,128]{3,2,1,0:T(8,128)S(1)}, f32[2,5,8,128]{3,2,1,0:T(8,128)S(1)}, u32[]{:S(2)}, u32[]{:S(2)}) collective-permute-start(f32[2,5,8,128]{3,2,1,0:T(8,128)S(1)} %get-tuple-element.34), channel_id=1, source_target_pairs={{0,1},{1,0},{2,3},{3,2},{4,5},{5,4},{6,7},{7,6},{8,9},{9,8},{10,11... | collective-permute-start | bytes 122888 | tf_op jit(solution)/shard_map/ppermute | solution.py:744
  4.9 7.3 %copy-start.4 = (bf16[256,256]{1,0:T(8,128)(2,1)S(1)}, bf16[256,256]{1,0:T(8,128)(2,1)}, u32[]{:S(2)}) copy-start(bf16[256,256]{1,0:T(8,128)(2,1)} %constant.25.clone.grad_ref) | copy-start | bytes 393220
  5.5 6.7 %copy-start.2 = (bf16[256,256]{1,0:T(8,128)(2,1)S(1)}, bf16[256,256]{1,0:T(8,128)(2,1)}, u32[]{:S(2)}) copy-start(bf16[256,256]{1,0:T(8,128)(2,1)} %constant.26.clone.back_ref) | copy-start | bytes 393220
  6.9 6.6 %collective-permute-start.1 = (f32[144,128]{1,0:T(8,128)S(1)}, f32[144,128]{1,0:T(8,128)S(1)}, u32[]{:S(2)}, u32[]{:S(2)}) collective-permute-start(f32[144,128]{1,0:T(8,128)S(1)} %get-tuple-element.46), channel_id=1, source_target_pairs={{0,30},{2,4},{4,2},{6,8},{8,6},{10,12},{12,10},{14,16},{16,14},{18... | collective-permute-start | bytes 221192 | tf_op jit(solution)/shard_map/ppermute | solution.py:760
  10.3 3.2 %collective-permute-start.2 = (f32[144,128]{1,0:T(8,128)S(1)}, f32[144,128]{1,0:T(8,128)S(1)}, u32[]{:S(2)}, u32[]{:S(2)}) collective-permute-start(f32[144,128]{1,0:T(8,128)S(1)} %get-tuple-element.47), channel_id=1, source_target_pairs={{0,2},{2,0},{4,6},{6,4},{8,10},{10,8},{12,14},{14,12},{16,18},{18,... | collective-permute-start | bytes 221192 | tf_op jit(solution)/shard_map/ppermute | solution.py:761
  10.3 7.1 %collective-permute-start.6 = (f32[144,128]{1,0:T(8,128)S(1)}, f32[144,128]{1,0:T(8,128)S(1)}, u32[]{:S(2)}, u32[]{:S(2)}) collective-permute-start(f32[144,128]{1,0:T(8,128)S(1)} %get-tuple-element.55), channel_id=1, source_target_pairs={{0,30},{2,4},{4,2},{6,8},{8,6},{10,12},{12,10},{14,16},{16,14},{18... | collective-permute-start | bytes 221192 | tf_op jit(solution)/shard_map/ppermute | solution.py:760
  12.2 5.2 %collective-permute-start.7 = (f32[144,128]{1,0:T(8,128)S(1)}, f32[144,128]{1,0:T(8,128)S(1)}, u32[]{:S(2)}, u32[]{:S(2)}) collective-permute-start(f32[144,128]{1,0:T(8,128)S(1)} %get-tuple-element.56), channel_id=1, source_target_pairs={{0,2},{2,0},{4,6},{6,4},{8,10},{10,8},{12,14},{14,12},{16,18},{18,... | collective-permute-start | bytes 221192 | tf_op jit(solution)/shard_map/ppermute | solution.py:761
  13.5 3.9 %copy-start.3 = (bf16[512,256]{1,0:T(8,128)(2,1)S(1)}, bf16[512,256]{1,0:T(8,128)(2,1)}, u32[]{:S(2)}) copy-start(bf16[512,256]{1,0:T(8,128)(2,1)} %constant.27.clone.restrict_ref) | copy-start | bytes 786436
  14.0 7.2 %collective-permute-start.3 = (f32[104,128]{1,0:T(8,128)S(1)}, f32[104,128]{1,0:T(8,128)S(1)}, u32[]{:S(2)}, u32[]{:S(2)}) collective-permute-start(f32[104,128]{1,0:T(8,128)S(1)} %get-tuple-element.50.sent_outer_ref), channel_id=1, source_target_pairs={{0,30},{2,4},{4,2},{6,8},{8,6},{10,12},{12,10},{14,16},{16,14},{18... | collective-permute-start | bytes 159752 | tf_op jit(solution)/shard_map/ppermute | solution.py:760
  17.4 3.9 %collective-permute-start.5 = (f32[104,128]{1,0:T(8,128)S(1)}, f32[104,128]{1,0:T(8,128)S(1)}, u32[]{:S(2)}, u32[]{:S(2)}) collective-permute-start(f32[104,128]{1,0:T(8,128)S(1)} %get-tuple-element.52.sent_inner_ref), channel_id=1, source_target_pairs={{0,2},{2,0},{4,6},{6,4},{8,10},{10,8},{12,14},{14,12},{16,18},{18,... | collective-permute-start | bytes 159752 | tf_op jit(solution)/shard_map/ppermute | solution.py:761
  17.5 7.9 %collective-permute-start.9 = (f32[24,128]{1,0:T(8,128)S(1)}, f32[24,128]{1,0:T(8,128)S(1)}, u32[]{:S(2)}, u32[]{:S(2)}) collective-permute-start(f32[24,128]{1,0:T(8,128)S(1)} %get-tuple-element.59), channel_id=1, source_target_pairs={{0,5},{1,4},{2,7},{3,6},{4,9},{5,8},{6,11},{7,10},{8,13},{9,12},{1... | collective-permute-start | bytes 36872 | tf_op jit(solution)/shard_map/ppermute | solution.py:771
  17.5 3.7 %collective-permute-start.4 = (f32[2,1,8,128]{3,2,1,0:T(8,128)S(1)}, f32[2,1,8,128]{3,2,1,0:T(8,128)S(1)}, u32[]{:S(2)}, u32[]{:S(2)}) collective-permute-start(f32[2,1,8,128]{3,2,1,0:T(8,128)S(1)} %get-tuple-element.51), channel_id=1, source_target_pairs={{0,1},{1,0},{2,3},{3,2},{4,5},{5,4},{6,7},{7,6},{8,9},{9,8},{10,11... | collective-permute-start | bytes 24584 | tf_op jit(solution)/shard_map/ppermute | solution.py:744
  19.1 6.3 %collective-permute-start.8 = (f32[8,128]{1,0:T(8,128)S(1)}, f32[8,128]{1,0:T(8,128)S(1)}, u32[]{:S(2)}, u32[]{:S(2)}) collective-permute-start(f32[8,128]{1,0:T(8,128)S(1)} %get-tuple-element.58), channel_id=1, source_target_pairs={{0,4},{2,6},{4,8},{6,10},{8,12},{10,14},{12,16},{14,18},{16,20},{1... | collective-permute-start | bytes 12296 | tf_op jit(solution)/shard_map/ppermute | solution.py:767
  21.5 4.0 %collective-permute-start.10 = (f32[3,128]{1,0:T(4,128)S(1)}, f32[3,128]{1,0:T(4,128)S(1)}, u32[]{:S(2)}, u32[]{:S(2)}) collective-permute-start(f32[3,128]{1,0:T(4,128)S(1)} %get-tuple-element.61), channel_id=1, source_target_pairs={{0,1},{1,0},{2,3},{3,2},{4,5},{5,4},{6,7},{7,6},{8,9},{9,8},{10,11... | collective-permute-start | bytes 4616 | tf_op jit(solution)/shard_map/ppermute | solution.py:744

commit v7 on v6

--- a/solution.py
+++ b/solution.py
@@ -216,17 +216,12 @@
     row_weight = by_row(W, width)
     squared = paired_here(cell_blocks(tiled(D * D, width)))
     squares = [by_row(D[a] ** 2, width) for a in range(PTS)]
-    mob_rows, load_rows = (r.reshape(2 * PTS * PTS, width) for r in (mob_ref, load_ref))
-
-    def across(ref, s, j):
-        return ref[pl.ds(s * PTS * PTS + j, PTS, stride=PTS)]
-
     for copy in copies:
         copy.wait()
     spread, cell_metric = spread_metric(metric_ref[...], weight_row)
     for d in range(3):
         spread_ref[d] = spread[d]
-    points = [across(mob_rows, s, ends[s]) * (float(W[ends[s]]) * row_weight) for s in range(2)]
+    points = [mob_ref[s, :, ends[s]] * (float(W[ends[s]]) * row_weight) for s in range(2)]
     columns = dot_split(
         jnp.concatenate([p * weight_row for p in points], axis=0), squared
     )
@@ -236,7 +231,7 @@
         along = points[s] * scale[0]
         total = sum(squares[a] * along[a : a + 1] for a in range(PTS))
         sums = [
-            sum(float(D[b, j] ** power * W[b]) * across(mob_rows, s, b) for b in range(PTS))
+            sum(float(D[b, j] ** power * W[b]) * mob_ref[s, :, b] for b in range(PTS))
             * row_weight
             * scale[1]
             for power in (1, 2)
@@ -247,7 +242,7 @@
         column = columns[s * PTS : (s + 1) * PTS] * cell_metric[e : e + 1]
         yface_ref[s, 1] = sum_z(total + sums[1] + column, masks)
     for s in range(2):
-        yface_ref[s, 0] = sum_z(across(load_rows, s, ends[s]), masks)
+        yface_ref[s, 0] = sum_z(load_ref[s, :, ends[s]], masks)
 
 
 def diag_kernel(
@@ -403,7 +398,7 @@
     side_ref, rough_ref, value_ref, out_ref, pair_ref, mob_ref, spread_ref, grad_ref, back_ref,
     below_ref, above_ref, partial_ref, gain_ref, weights_ref, load_sums_ref, edge_weights_ref,
     outer_ref, inner_ref,
-    to_outer_ref, to_inner_ref, yface_ref, gface_ref, sofar_ref, sums_ref, line_ref, work_ref,
+    to_outer_ref, to_inner_ref, yface_ref, gface_ref, sofar_ref, sums_ref, edge_ref, line_ref, work_ref,
 ):
     below_ref, above_ref = below_ref.at[1], above_ref.at[0]
     even = side_ref[0] == 0
@@ -523,7 +518,12 @@
         j = ends[t]
         gain = [gface[0][j]] + [gain_ref[i, j] for i in range(1, PTS - 1)] + [gface[1][j]]
         gain = jnp.concatenate([g[rows[t] : rows[t] + 1] for g in gain], axis=0)
-        changes += edge_change(-(gain * ymessage[t]), edge_weights_ref.at[t], ends[1 - t])
+        change = -(gain * ymessage[t])
+        changes += edge_change(change, edge_weights_ref.at[t], ends[1 - t], 1)
+        if t == 0:
+            own = edge_change(change, edge_weights_ref.at[t], ends[1 - t], 0)
+            zero = jnp.zeros_like(own[1])
+            edge_ref[...] = jnp.concatenate([zero, own[1], zero, own[3]] + [zero] * 4, axis=0)
     changes = jnp.concatenate(changes, axis=0)
     for ref in (to_outer_ref, to_inner_ref):
         for n, k in enumerate((2, 3, 6, 7)):
@@ -531,16 +531,16 @@
         ref[base + 4 * ny : base + 4 * ny + PTS] = changes
 
 
-def edge_change(change, weight_ref, j):
+def edge_change(change, weight_ref, j, p):
     upper = lax.broadcasted_iota(jnp.int32, change.shape, 0)
     hat = jnp.zeros_like(change)
     for i in range(PTS):
-        hat = jnp.where(upper == i, float(HAT[i, 1]), hat)
+        hat = jnp.where(upper == i, float(HAT[i, p]), hat)
     along_x, along_y, along_z = (
         jnp.sum(v, axis=0, keepdims=True)
         for v in (weight_ref[0] * change, hat * weight_ref[1] * change, hat * weight_ref[2] * change)
     )
-    smooth = [-(SLOPE[1] * float(HAT[j, q]) * along_x + SLOPE[q] * along_y) for q in range(2)]
+    smooth = [-(SLOPE[p] * float(HAT[j, q]) * along_x + SLOPE[q] * along_y) for q in range(2)]
     return smooth + [-float(HAT[j, q]) * along_z for q in range(2)]
 
 
@@ -572,23 +572,26 @@
     return sums
 
 
-def corrections(even, gain_ref, gface_ref, outer_ref, below_ref, above_ref, inner_ref):
+def x_corrections(even, gface_ref, outer_ref, inner_ref):
+    ny = gface_ref.shape[2]
+    change = {}
+    for j in range(PTS):
+        low = pick(even, outer_ref, inner_ref, j * ny, ny)
+        high = pick(even, inner_ref, outer_ref, j * ny, ny)
+        change[0, j] = -(gface_ref[0, j] * low)
+        change[PTS - 1, j] = -(gface_ref[1, j] * high)
+    return change
+
+
+def y_corrections(gain_ref, gface_ref, below_ref, above_ref):
     ny, width = gain_ref.shape[2:]
     row = lax.broadcasted_iota(jnp.int32, (ny, width), 0)
+    faces = {0: 0, PTS - 1: 1}
     change = {}
-    for j in range(PTS):
-        inner, outer = inner_ref[j * ny : (j + 1) * ny], outer_ref[j * ny : (j + 1) * ny]
-        change[0, j] = jnp.where(even, outer, inner)
-        change[PTS - 1, j] = jnp.where(even, inner, outer)
     for i in range(PTS):
-        low = jnp.where(row == 0, below_ref[0, i : i + 1], 0.0)
-        high = jnp.where(row == ny - 1, above_ref[0, i : i + 1], 0.0)
-        change[i, 0] = change[i, 0] + low if (i, 0) in change else low
-        change[i, PTS - 1] = change[i, PTS - 1] + high if (i, PTS - 1) in change else high
-    faces = {0: 0, PTS - 1: 1}
-    for i, j in change:
-        gain = gface_ref[faces[i], j] if i in faces else gain_ref[i, j]
-        change[i, j] = -(gain * change[i, j])
+        for j, at, ref in ((0, 0, below_ref), (PTS - 1, ny - 1, above_ref)):
+            gain = gface_ref[faces[i], j] if i in faces else gain_ref[i, j]
+            change[i, j] = -(gain * jnp.where(row == at, ref[0, i : i + 1], 0.0))
     return change
 
 
@@ -626,7 +629,7 @@
     corners = to_vertices(smooth, jnp.zeros_like(smooth), restrict_ref[...])
     lower, upper = corners[:ny], corners[ny:]
     row = lax.broadcasted_iota(jnp.int32, lower.shape, 0)
-    next_ref[...] = lower + jnp.where(row == 0, 0.0, pltpu.roll(upper, 1, 0))
+    next_ref[:ny] = lower + jnp.where(row == 0, 0.0, pltpu.roll(upper, 1, 0))
     top_ref[...] = jnp.broadcast_to(upper[ny - 1 : ny], top_ref.shape)
 
 
@@ -656,14 +659,12 @@
 
 
 def coarse_kernel(
-    side_ref, gain_ref, gface_ref, sums_ref, own_ref, weights_ref, restrict_ref,
-    outer_ref, below_ref, above_ref, inner_ref,
+    side_ref, gface_ref, sums_ref, own_ref, edge_in_ref, weights_ref, restrict_ref, outer_ref, inner_ref,
     plane_ref, edge_ref,
 ):
-    below_ref, above_ref = below_ref.at[1], above_ref.at[0]
-    ny, width = gain_ref.shape[2:]
+    ny, width = gface_ref.shape[2:]
     even = side_ref[0] == 0
-    change = corrections(even, gain_ref, gface_ref, outer_ref, below_ref, above_ref, inner_ref)
+    change = x_corrections(even, gface_ref, outer_ref, inner_ref)
     sums = restricted(
         list(change),
         lambda i, j: change[i, j],
@@ -673,23 +674,43 @@
     base = PTS * ny
 
     def before(at, count):
-        return jnp.where(even, outer_ref[at : at + count], inner_ref[at : at + count])
+        return pick(even, outer_ref, inner_ref, at, count)
 
     total = [
         sums[(0, 1, 4, 5)[n]] + sums_ref[n] + own_ref[n] + before(base + n * ny, ny) for n in range(4)
     ]
-    extra = before(base + 4 * ny, PTS)
+    extra = before(base + 4 * ny, PTS) + edge_in_ref[...]
     smooth = jnp.concatenate(total[:2] + [extra], axis=0)
     slope = jnp.concatenate(total[2:] + [pltpu.roll(extra, PTS - 2, 0)], axis=0)
     corners = to_vertices(smooth, slope, restrict_ref[...])
     lower, upper = corners[:ny], corners[ny : 2 * ny]
     extra = corners[2 * ny :]
     row = lax.broadcasted_iota(jnp.int32, lower.shape, 0)
-    shifted = jnp.where(row == 0, extra[1:2], pltpu.roll(upper, 1, 0))
-    plane_ref[...] = lower + shifted
+    plane_ref[...] = lower + jnp.where(row == 0, extra[1:2], pltpu.roll(upper, 1, 0))
     edge_ref[0:1] = upper[ny - 1 : ny] + extra[4:5]
     edge_ref[1:2] = extra[5:6]
     edge_ref[2:3] = extra[0:1]
+
+
+def beside_kernel(
+    own_ref, gain_ref, gface_ref, weights_ref, restrict_ref, below_ref, above_ref,
+    plane_ref,
+):
+    below_ref, above_ref = below_ref.at[1], above_ref.at[0]
+    ny, width = gain_ref.shape[2:]
+    change = y_corrections(gain_ref, gface_ref, below_ref, above_ref)
+    sums = restricted(
+        list(change),
+        lambda i, j: change[i, j],
+        lambda d, i, j: weights_ref[d, i, j],
+        jnp.zeros((ny, width), F32),
+    )
+    smooth = jnp.concatenate([sums[0], sums[1]], axis=0)
+    slope = jnp.concatenate([sums[4], sums[5]], axis=0)
+    corners = to_vertices(smooth, slope, restrict_ref[...])
+    lower, upper = corners[:ny], corners[ny:]
+    row = lax.broadcasted_iota(jnp.int32, lower.shape, 0)
+    plane_ref[...] = own_ref[...] + lower + jnp.where(row == 0, 0.0, pltpu.roll(upper, 1, 0))
 
 
 def pressure_kernel(
@@ -700,25 +721,30 @@
     below_ref, above_ref = below_ref.at[1], above_ref.at[0]
     ny = sofar_ref.shape[2]
     even = side_ref[0] == 0
-    change = corrections(even, gain_ref, gface_ref, outer_ref, below_ref, above_ref, inner_ref)
+    changes = (
+        x_corrections(even, gface_ref, outer_ref, inner_ref),
+        y_corrections(gain_ref, gface_ref, below_ref, above_ref),
+    )
     for i in range(PTS):
         for j in range(PTS):
             value = sofar_ref[i, j]
-            if (i, j) in change:
-                value = value + change[i, j]
+            for change in changes:
+                if (i, j) in change:
+                    value = value + change[i, j]
             pressure_ref[i, pl.ds(j, ny, stride=PTS)] = value
     copy = pltpu.make_async_copy(pressure_ref, pressure_out, sem)
     copy.start()
     copy.wait()
 
 
-def join_kernel(next_ref, top_ref, token_ref, joined_ref):
-    row = lax.broadcasted_iota(jnp.int32, next_ref.shape, 0)
-    joined_ref[...] = next_ref[...] + jnp.where(row == 0, top_ref[0:1], 0.0) + token_ref[...]
-
-
-def last_kernel(plane_ref, joined_ref, below_ref, above_ref, coarse_ref):
-    total = plane_ref[...] + joined_ref[...]
+def join_kernel(own_ref, next_ref, top_ref, token_ref, joined_ref):
+    row = lax.broadcasted_iota(jnp.int32, joined_ref.shape, 0)
+    total = own_ref[...] + next_ref[: row.shape[0]] + token_ref[...]
+    joined_ref[...] = total + jnp.where(row == 0, top_ref[0:1], 0.0)
+
+
+def last_kernel(joined_ref, below_ref, above_ref, coarse_ref):
+    total = joined_ref[...]
     ny = total.shape[0]
     row = lax.broadcasted_iota(jnp.int32, total.shape, 0)
     total = total + jnp.where(row == 0, below_ref[0:1], jnp.where(row == 1, below_ref[1:2], 0.0))
@@ -814,9 +840,9 @@
         fields, load, mob, spread, grad, back, below, above,
     )
     rows = ((PTS + 4) * ny + PTS, width)
-    sent_outer, sent_inner, yface, gface, sofar, sums = call(
+    sent_outer, sent_inner, yface, gface, sofar, sums, edge = call(
         faces_kernel,
-        [rows, rows, (2, 1, PTS, width), faces, field, (4, ny, width)],
+        [rows, rows, (2, 1, PTS, width), faces, field, (4, ny, width), (PTS, width)],
         [((2 * PTS + 4) * ny, width), field],
         side, rough, value, out, pair, mob, spread, grad, back, below, above,
         partial, gain, weights, load_sums, edge_weights, outer, inner,
@@ -824,7 +850,7 @@
     outer, inner = to_x(sent_outer, sent_inner)
     onward, top = call(
         ahead_kernel,
-        [(ny, 128), (3 * PTS, 128)],
+        [(3 * ny, 128), (3 * PTS, 128)],
         [],
         side, sent_outer, sent_inner, gface, restrict, still_outer, still_inner,
     )
@@ -840,7 +866,10 @@
         coarse_kernel,
         [(ny, 128), (3, 128)],
         [],
-        side, gain, gface, sums, own, weights, restrict, outer, below, above, inner,
+        side, gface, sums, own, edge, weights, restrict, outer, inner,
+    )
+    (own_rows,) = call(
+        beside_kernel, [(ny, 128)], [], own_rows, gain, gface, weights, restrict, below, above
     )
     pressure, token = call(
         pressure_kernel,
@@ -849,9 +878,9 @@
         side, sofar, gain, gface, outer, below, above, inner,
         out_spaces=[pltpu.HBM, pltpu.VMEM],
     )
-    (onward,) = call(join_kernel, [(ny, 128)], [], onward, top, token, flops=FLOPS_JOIN)
-    below, above = from_y(tops)
-    (coarse,) = call(last_kernel, [(ny, width // PTS + 1)], [], own_rows, onward, below, above)
+    (onward,) = call(join_kernel, [(ny, 128)], [], own_rows, onward, top, token, flops=FLOPS_JOIN)
+    row_below, row_above = from_y(tops)
+    (coarse,) = call(last_kernel, [(ny, width // PTS + 1)], [], onward, row_below, row_above)
     return pressure.reshape(element_load.shape), coarse[None]
 
 

time: 26.2 us -> 25.8 us (0.985)
  waiting for transfers between devices: 4.91 us -> 3.86 us
  starting transfers between devices: 14.8 us -> 15.3 us
    ppermute x3, waiting for transfers between devices: 3.31 us -> 1.35 us  [from_y(): up = lax.ppermute(faces, 'sub', [(i, (i + 1) % size) for i in range(size)])]
    ppermute x1, waiting for transfers between devices: 1.58 us -> 0.43 us  [two_on(): rows = lax.ppermute(rows, 'dom', [(i, (i + 2) % size) for i in range(size)])]
    ppermute x1, waiting for transfers between devices: 0.01 us -> 1.09 us  [two_on(): return (rows, lax.ppermute(top, ('dom', 'sub'), pairs))]
    ppermute x3, waiting for transfers between devices: 0.01 us -> 0.98 us  [to_x(): outer = lax.ppermute(outer, 'dom', outer_pairs(size))]
    ppermute x1, starting transfers between devices: 0.01 us -> 0.96 us  [two_on(): return (rows, lax.ppermute(top, ('dom', 'sub'), pairs))]
    ppermute x3, starting transfers between devices: 6.2 us -> 5.73 us  [from_y(): up = lax.ppermute(faces, 'sub', [(i, (i + 1) % size) for i in range(size)])]
    pallas_call x11 -> x12, Pallas kernels: 5.55 us -> 5.7 us  [call(): pl.pallas_call(body, out_shape=[jax.ShapeDtypeStruct(s, F32) if isinstanc...]
  transfers between devices with their start and end apart: 11 -> 11, of which waited for: 3 -> 4; matrix products, arithmetic and copies ran while one was open for 0% -> 0% of each run, Pallas kernels for 14% -> 15%
where the time goes in v7:
time: 25.8 us; the launch traced here: 25.6 us
  starting transfers between devices  15.3 us (59%)
  Pallas kernels  5.7 us (22%)
  waiting for transfers between devices  3.86 us (15%)
  between operations  0.75 us (3%)
    ppermute x3, starting transfers between devices, to_x(): outer = lax.ppermute(outer, 'dom', outer_pairs(size))  8.61 us
    ppermute x3, starting transfers between devices, from_y(): up = lax.ppermute(faces, 'sub', [(i, (i + 1) % size) for i in range(size)])  5.73 us
    pallas_call x12, Pallas kernels, call(): pl.pallas_call(body, out_shape=[jax.ShapeDtypeStruct(s, F32) if isinstanc...  5.7 us
    ppermute x3, waiting for transfers between devices, from_y(): up = lax.ppermute(faces, 'sub', [(i, (i + 1) % size) for i in range(size)])  1.35 us
    ppermute x1, waiting for transfers between devices, two_on(): return (rows, lax.ppermute(top, ('dom', 'sub'), pairs))  1.09 us
    ppermute x3, waiting for transfers between devices, to_x(): outer = lax.ppermute(outer, 'dom', outer_pairs(size))  0.98 us
    ppermute x1, starting transfers between devices, two_on(): return (rows, lax.ppermute(top, ('dom', 'sub'), pairs))  0.96 us
  transfers between devices with their start and end apart: 11, of which 4 were waited for; matrix products, arithmetic and copies ran while one was open for 0% of the time, Pallas kernels for 15%

profile of v7, /device:TPU:0, one launch (start us, length us, event | category | flops | bytes accessed | tf_op | source)
XLA Modules:
  0.0 25.6 jit_solution(15564721079054115826)
XLA Ops:
  0.6 0.0 copy-start
  0.6 0.0 copy-start.1
  0.6 1.2 %shard_map.77 = (f32[3,8,128]{2,1,0:T(8,128)S(1)}, f32[2,5,8,128]{3,2,1,0:T(8,128)S(1)}) custom-call(f32[3,8,16]{2,1,0:T(8,128)} %bitcast.13, f32[8,64,128]{2,1,0:T(8,128)} %bitcast.6, f32[8,64,128]{2,1,0:T(8,128)} %bitcast.10), custom_call_target="tpu_custom_call" | custom-call | tf_op jit(solution)/shard_map/pallas_call | solution.py:757
  1.9 3.0 %collective-permute-start = (f32[2,5,8,128]{3,2,1,0:T(8,128)S(1)}, f32[2,5,8,128]{3,2,1,0:T(8,128)S(1)}, u32[]{:S(2)}, u32[]{:S(2)}) collective-permute-start(f32[2,5,8,128]{3,2,1,0:T(8,128)S(1)} %get-tuple-element.35), channel_id=1, source_target_pairs={{0,1},{1,0},{2,3},{3,2},{4,5},{5,4},{6,7},{7,6},{8,9},{9,8},{10,11... | collective-permute-start | bytes 122888 | tf_op jit(solution)/shard_map/ppermute | solution.py:770
  4.9 0.0 copy-done
  4.9 0.0 copy-done.1
  4.9 0.0 copy-start.4
  4.9 0.6 %shard_map.78 = (f32[2,8,8,8,128]{4,3,2,1,0:T(8,128)S(1)}, f32[2,2,8,8,128]{4,3,2,1,0:T(8,128)S(1)}, f32[2,2,8,128]{3,2,1,0:T(8,128)S(1)}, f32[144,128]{1,0:T(8,128)S(1)}, f32[144,128]{1,0:T(8,128)S(1)}) custom-call(s32[1]{0:T(128)} %bitcast.side_ref, f32[8,64,128]{2,1,0:T(8,128)S(1)} %bitcast.11, f32[8,64,128]{2,1,0:T(8,128)S(1)} %bitcast.7, ...), custom_call_target="tpu_custom_call" | custom-call | tf_op jit(solution)/shard_map/pallas_call | solution.py:757
  5.5 0.0 copy-start.3
  5.5 1.3 %collective-permute-done.below_ref.above_ref = f32[2,5,8,128]{3,2,1,0:T(8,128)S(1)} collective-permute-done((f32[2,5,8,128]{3,2,1,0:T(8,128)S(1)}, f32[2,5,8,128]{3,2,1,0:T(8,128)S(1)}, u32[]{:S(2)}, u32[]{:S(2)}) %collective-permute-start) | collective-permute-done | bytes 40992 | tf_op jit(solution)/shard_map/ppermute | solution.py:770
  6.9 3.4 %collective-permute-start.1 = (f32[144,128]{1,0:T(8,128)S(1)}, f32[144,128]{1,0:T(8,128)S(1)}, u32[]{:S(2)}, u32[]{:S(2)}) collective-permute-start(f32[144,128]{1,0:T(8,128)S(1)} %get-tuple-element.47), channel_id=1, source_target_pairs={{0,30},{2,4},{4,2},{6,8},{8,6},{10,12},{12,10},{14,16},{16,14},{18... | collective-permute-start | bytes 221192 | tf_op jit(solution)/shard_map/ppermute | solution.py:786
  10.3 0.0 collective-permute-start.2
  10.3 1.9 %collective-permute-start.6 = (f32[144,128]{1,0:T(8,128)S(1)}, f32[144,128]{1,0:T(8,128)S(1)}, u32[]{:S(2)}, u32[]{:S(2)}) collective-permute-start(f32[144,128]{1,0:T(8,128)S(1)} %get-tuple-element.56), channel_id=1, source_target_pairs={{0,30},{2,4},{4,2},{6,8},{8,6},{10,12},{12,10},{14,16},{16,14},{18... | collective-permute-start | bytes 221192 | tf_op jit(solution)/shard_map/ppermute | solution.py:786
  12.2 0.0 collective-permute-start.7
  12.2 0.0 copy-done.4
  12.2 0.0 copy-done.3
  12.2 1.3 %shard_map.79 = (f32[2,2,8,8,128]{4,3,2,1,0:T(8,128)S(1)}, f32[8,8,8,128]{3,2,1,0:T(8,128)S(1)}, f32[8,8,8,128]{3,2,1,0:T(8,128)S(1)}, f32[8,8,8,128]{3,2,1,0:T(...) custom-call(f32[2,8,8,8,128]{4,3,2,1,0:T(8,128)S(1)} %get-tuple-elem, ...), custom_call_target="tpu_custom_call" | custom-call | tf_op jit(solution)/shard_map/pallas_call | solution.py:757
  13.5 0.0 collective-permute-done.1.outer_ref
  13.5 0.0 collective-permute-done.2.inner_ref
  13.5 0.0 copy-start.2
  13.5 0.5 %shard_map.81 = (f32[104,128]{1,0:T(8,128)S(1)}, f32[104,128]{1,0:T(8,128)S(1)}, f32[2,1,8,128]{3,2,1,0:T(8,128)S(1)}, f32[2,8,8,128]{3,2,1,0:T(8,128)S(1)}, f32...) custom-call(s32[1]{0:T(128)} %bitcast.side_ref, ...), custom_call_target="tpu_custom_call" | custom-call | tf_op jit(solution)/shard_map/pallas_call | solution.py:757
  14.0 3.3 %collective-permute-start.3 = (f32[104,128]{1,0:T(8,128)S(1)}, f32[104,128]{1,0:T(8,128)S(1)}, u32[]{:S(2)}, u32[]{:S(2)}) collective-permute-start(f32[104,128]{1,0:T(8,128)S(1)} %get-tuple-element.51.sent_outer_ref), channel_id=1, source_target_pairs={{0,30},{2,4},{4,2},{6,8},{8,6},{10,12},{12,10},{14,16},{16,14},{18... | collective-permute-start | bytes 159752 | tf_op jit(solution)/shard_map/ppermute | solution.py:786
  17.4 0.0 collective-permute-start.5
  17.4 0.0 collective-permute-done.6.outer_ref
  17.4 0.0 collective-permute-done.7.inner_ref
  17.4 0.0 copy-done.2
  17.4 0.2 shard_map.86
  17.6 0.0 collective-permute-start.8
  17.6 1.0 %collective-permute-start.9 = (f32[24,128]{1,0:T(8,128)S(1)}, f32[24,128]{1,0:T(8,128)S(1)}, u32[]{:S(2)}, u32[]{:S(2)}) collective-permute-start(f32[24,128]{1,0:T(8,128)S(1)} %get-tuple-element.61), channel_id=1, source_target_pairs={{0,5},{1,4},{2,7},{3,6},{4,9},{5,8},{6,11},{7,10},{8,13},{9,12},{1... | collective-permute-start | bytes 36872 | tf_op jit(solution)/shard_map/ppermute | solution.py:797
  18.5 0.7 %collective-permute-start.4 = (f32[2,1,8,128]{3,2,1,0:T(8,128)S(1)}, f32[2,1,8,128]{3,2,1,0:T(8,128)S(1)}, u32[]{:S(2)}, u32[]{:S(2)}) collective-permute-start(f32[2,1,8,128]{3,2,1,0:T(8,128)S(1)} %get-tuple-element.52), channel_id=1, source_target_pairs={{0,1},{1,0},{2,3},{3,2},{4,5},{5,4},{6,7},{7,6},{8,9},{9,8},{10,11... | collective-permute-start | bytes 24584 | tf_op jit(solution)/shard_map/ppermute | solution.py:770
  19.2 0.2 shard_map.83.own_ref
  19.4 1.0 %collective-permute-done.3.outer_ref = f32[104,128]{1,0:T(8,128)S(1)} collective-permute-done((f32[104,128]{1,0:T(8,128)S(1)}, f32[104,128]{1,0:T(8,128)S(1)}, u32[]{:S(2)}, u32[]{:S(2)}) %collective-permute-start.3) | collective-permute-done | bytes 53280 | tf_op jit(solution)/shard_map/ppermute | solution.py:786
  20.4 0.0 collective-permute-done.5.inner_ref
  20.4 0.2 shard_map.84
  20.5 2.0 %collective-permute-start.10 = (f32[3,128]{1,0:T(4,128)S(1)}, f32[3,128]{1,0:T(4,128)S(1)}, u32[]{:S(2)}, u32[]{:S(2)}) collective-permute-start(f32[3,128]{1,0:T(4,128)S(1)} %get-tuple-element.63), channel_id=1, source_target_pairs={{0,1},{1,0},{2,3},{3,2},{4,5},{5,4},{6,7},{7,6},{8,9},{9,8},{10,11... | collective-permute-start | bytes 4616 | tf_op jit(solution)/shard_map/ppermute | solution.py:770
  22.6 0.0 collective-permute-done.4.below_ref.above_ref
  22.6 0.8 %shard_map.82 = (f32[8,64,128]{2,1,0:T(8,128)}, f32[1,128]{1,0:T(1,128)S(1)}) custom-call(s32[1]{0:T(128)} %bitcast.side_ref, f32[8,8,8,128]{3,2,1,0:T(8,128)S(1)} %get-tuple-element.49.sofar_ref, f32[8,8,8,128]{3,2,1,0:T(8,128)S(1)} %get-tuple-element.41.gain_ref, f32[2,8,8,128]{3,2,1,0:T(8,128)S(1)} %get-tuple-element.50.gface_ref, ...), custom_call_target="tpu_custom_call" | custom-call | tf_op jit(solution)/shard_map/pallas_call | solution.py:757
  23.3 0.2 shard_map.85.own_ref
  23.5 0.4 %collective-permute-done.8.next_ref = f32[24,128]{1,0:T(8,128)S(1)} collective-permute-done((f32[24,128]{1,0:T(8,128)S(1)}, f32[24,128]{1,0:T(8,128)S(1)}, u32[]{:S(2)}, u32[]{:S(2)}) %collective-permute-start.8) | collective-permute-done | bytes 12320 | tf_op jit(solution)/shard_map/ppermute | solution.py:793
  23.9 1.1 %collective-permute-done.9.top_ref = f32[24,128]{1,0:T(8,128)S(1)} collective-permute-done((f32[24,128]{1,0:T(8,128)S(1)}, f32[24,128]{1,0:T(8,128)S(1)}, u32[]{:S(2)}, u32[]{:S(2)}) %collective-permute-start.9) | collective-permute-done | bytes 12320 | tf_op jit(solution)/shard_map/ppermute | solution.py:797
  25.0 0.0 collective-permute-done.10.below_ref.above_ref
  25.0 0.6 %shard_map.88 = f32[8,17]{1,0:T(8,128)} custom-call(f32[8,128]{1,0:T(8,128)S(1)} %shard_map.87.joined_ref, f32[3,128]{1,0:T(4,128)S(1)} %collective-permute-done.10.below_ref.above_ref, f32[3,128]{1,0:T(4,128)S(1)} %collective-permute-done.10.below_ref.above_ref), custom_call_target="tpu_custom_call" | custom-call | tf_op jit(solution)/shard_map/pallas_call | solution.py:757
  (2 shorter events, 0.0 us)
Async XLA Ops:
  0.6 4.3 %copy-start = (f32[1,8,8,8,128]{4,3,2,1,0:T(8,128)S(1)}, f32[1,8,8,8,128]{4,3,2,1,0:T(8,128)}, u32[]{:S(2)}) copy-start(f32[1,8,8,8,128]{4,3,2,1,0:T(8,128)} %param.7) | copy-start | bytes 786436
  0.6 4.3 %copy-start.1 = (f32[1,8,8,8,128]{4,3,2,1,0:T(8,128)S(1)}, f32[1,8,8,8,128]{4,3,2,1,0:T(8,128)}, u32[]{:S(2)}) copy-start(f32[1,8,8,8,128]{4,3,2,1,0:T(8,128)} %param.6) | copy-start | bytes 786436
  1.9 5.0 %collective-permute-start = (f32[2,5,8,128]{3,2,1,0:T(8,128)S(1)}, f32[2,5,8,128]{3,2,1,0:T(8,128)S(1)}, u32[]{:S(2)}, u32[]{:S(2)}) collective-permute-start(f32[2,5,8,128]{3,2,1,0:T(8,128)S(1)} %get-tuple-element.35), channel_id=1, source_target_pairs={{0,1},{1,0},{2,3},{3,2},{4,5},{5,4},{6,7},{7,6},{8,9},{9,8},{10,11... | collective-permute-start | bytes 122888 | tf_op jit(solution)/shard_map/ppermute | solution.py:770
  4.9 7.3 %copy-start.4 = (bf16[256,256]{1,0:T(8,128)(2,1)S(1)}, bf16[256,256]{1,0:T(8,128)(2,1)}, u32[]{:S(2)}) copy-start(bf16[256,256]{1,0:T(8,128)(2,1)} %constant.25.clone.grad_ref) | copy-start | bytes 393220
  5.5 6.7 %copy-start.3 = (bf16[256,256]{1,0:T(8,128)(2,1)S(1)}, bf16[256,256]{1,0:T(8,128)(2,1)}, u32[]{:S(2)}) copy-start(bf16[256,256]{1,0:T(8,128)(2,1)} %constant.26.clone.back_ref) | copy-start | bytes 393220
  6.9 6.6 %collective-permute-start.1 = (f32[144,128]{1,0:T(8,128)S(1)}, f32[144,128]{1,0:T(8,128)S(1)}, u32[]{:S(2)}, u32[]{:S(2)}) collective-permute-start(f32[144,128]{1,0:T(8,128)S(1)} %get-tuple-element.47), channel_id=1, source_target_pairs={{0,30},{2,4},{4,2},{6,8},{8,6},{10,12},{12,10},{14,16},{16,14},{18... | collective-permute-start | bytes 221192 | tf_op jit(solution)/shard_map/ppermute | solution.py:786
  10.3 3.2 %collective-permute-start.2 = (f32[144,128]{1,0:T(8,128)S(1)}, f32[144,128]{1,0:T(8,128)S(1)}, u32[]{:S(2)}, u32[]{:S(2)}) collective-permute-start(f32[144,128]{1,0:T(8,128)S(1)} %get-tuple-element.48), channel_id=1, source_target_pairs={{0,2},{2,0},{4,6},{6,4},{8,10},{10,8},{12,14},{14,12},{16,18},{18,... | collective-permute-start | bytes 221192 | tf_op jit(solution)/shard_map/ppermute | solution.py:787
  10.3 7.1 %collective-permute-start.6 = (f32[144,128]{1,0:T(8,128)S(1)}, f32[144,128]{1,0:T(8,128)S(1)}, u32[]{:S(2)}, u32[]{:S(2)}) collective-permute-start(f32[144,128]{1,0:T(8,128)S(1)} %get-tuple-element.56), channel_id=1, source_target_pairs={{0,30},{2,4},{4,2},{6,8},{8,6},{10,12},{12,10},{14,16},{16,14},{18... | collective-permute-start | bytes 221192 | tf_op jit(solution)/shard_map/ppermute | solution.py:786
  12.2 5.2 %collective-permute-start.7 = (f32[144,128]{1,0:T(8,128)S(1)}, f32[144,128]{1,0:T(8,128)S(1)}, u32[]{:S(2)}, u32[]{:S(2)}) collective-permute-start(f32[144,128]{1,0:T(8,128)S(1)} %get-tuple-element.57), channel_id=1, source_target_pairs={{0,2},{2,0},{4,6},{6,4},{8,10},{10,8},{12,14},{14,12},{16,18},{18,... | collective-permute-start | bytes 221192 | tf_op jit(solution)/shard_map/ppermute | solution.py:787
  13.5 3.9 %copy-start.2 = (bf16[512,256]{1,0:T(8,128)(2,1)S(1)}, bf16[512,256]{1,0:T(8,128)(2,1)}, u32[]{:S(2)}) copy-start(bf16[512,256]{1,0:T(8,128)(2,1)} %constant.27.clone.restrict_ref) | copy-start | bytes 786436
  14.0 6.3 %collective-permute-start.3 = (f32[104,128]{1,0:T(8,128)S(1)}, f32[104,128]{1,0:T(8,128)S(1)}, u32[]{:S(2)}, u32[]{:S(2)}) collective-permute-start(f32[104,128]{1,0:T(8,128)S(1)} %get-tuple-element.51.sent_outer_ref), channel_id=1, source_target_pairs={{0,30},{2,4},{4,2},{6,8},{8,6},{10,12},{12,10},{14,16},{16,14},{18... | collective-permute-start | bytes 159752 | tf_op jit(solution)/shard_map/ppermute | solution.py:786
  17.4 3.0 %collective-permute-start.5 = (f32[104,128]{1,0:T(8,128)S(1)}, f32[104,128]{1,0:T(8,128)S(1)}, u32[]{:S(2)}, u32[]{:S(2)}) collective-permute-start(f32[104,128]{1,0:T(8,128)S(1)} %get-tuple-element.53.sent_inner_ref), channel_id=1, source_target_pairs={{0,2},{2,0},{4,6},{6,4},{8,10},{10,8},{12,14},{14,12},{16,18},{18,... | collective-permute-start | bytes 159752 | tf_op jit(solution)/shard_map/ppermute | solution.py:787
  17.6 6.4 %collective-permute-start.8 = (f32[24,128]{1,0:T(8,128)S(1)}, f32[24,128]{1,0:T(8,128)S(1)}, u32[]{:S(2)}, u32[]{:S(2)}) collective-permute-start(f32[24,128]{1,0:T(8,128)S(1)} %get-tuple-element.60), channel_id=1, source_target_pairs={{0,4},{2,6},{4,8},{6,10},{8,12},{10,14},{12,16},{14,18},{16,20},{1... | collective-permute-start | bytes 36872 | tf_op jit(solution)/shard_map/ppermute | solution.py:793
  17.6 7.5 %collective-permute-start.9 = (f32[24,128]{1,0:T(8,128)S(1)}, f32[24,128]{1,0:T(8,128)S(1)}, u32[]{:S(2)}, u32[]{:S(2)}) collective-permute-start(f32[24,128]{1,0:T(8,128)S(1)} %get-tuple-element.61), channel_id=1, source_target_pairs={{0,5},{1,4},{2,7},{3,6},{4,9},{5,8},{6,11},{7,10},{8,13},{9,12},{1... | collective-permute-start | bytes 36872 | tf_op jit(solution)/shard_map/ppermute | solution.py:797
  18.5 4.0 %collective-permute-start.4 = (f32[2,1,8,128]{3,2,1,0:T(8,128)S(1)}, f32[2,1,8,128]{3,2,1,0:T(8,128)S(1)}, u32[]{:S(2)}, u32[]{:S(2)}) collective-permute-start(f32[2,1,8,128]{3,2,1,0:T(8,128)S(1)} %get-tuple-element.52), channel_id=1, source_target_pairs={{0,1},{1,0},{2,3},{3,2},{4,5},{5,4},{6,7},{7,6},{8,9},{9,8},{10,11... | collective-permute-start | bytes 24584 | tf_op jit(solution)/shard_map/ppermute | solution.py:770
  20.5 4.5 %collective-permute-start.10 = (f32[3,128]{1,0:T(4,128)S(1)}, f32[3,128]{1,0:T(4,128)S(1)}, u32[]{:S(2)}, u32[]{:S(2)}) collective-permute-start(f32[3,128]{1,0:T(4,128)S(1)} %get-tuple-element.63), channel_id=1, source_target_pairs={{0,1},{1,0},{2,3},{3,2},{4,5},{5,4},{6,7},{7,6},{8,9},{9,8},{10,11... | collective-permute-start | bytes 4616 | tf_op jit(solution)/shard_map/ppermute | solution.py:770

commit v8 on v7

--- a/solution.py
+++ b/solution.py
@@ -37,10 +37,8 @@
 RHO_SECOND = 1.0 / (2.0 * THETA / DELTA - RHO_FIRST)
 KEEP = 1.0 + RHO_SECOND * RHO_FIRST
 GAIN = 2.0 * RHO_SECOND / DELTA
-EXACT = lax.Precision.HIGHEST
 PTS = 8
 F32 = jnp.float32
-FLOPS_JOIN = 5_000_000_000
 
 
 def derivative_table():
@@ -115,10 +113,6 @@
         hat[rows, c], hat[rows, c + 1] = HAT[:, 0], HAT[:, 1]
         slope[rows, c], slope[rows, c + 1] = SLOPE
     return paired(np.concatenate([hat, slope]))
-
-
-def dot(a, b):
-    return jnp.dot(a, b, precision=EXACT, preferred_element_type=F32)
 
 
 def halves(a):
@@ -228,15 +222,15 @@
     for s, e in enumerate((0, ny - 1)):
         j = ends[s]
         scale = [spread[d][e : e + 1] for d in range(3)]
-        along = points[s] * scale[0]
-        total = sum(squares[a] * along[a : a + 1] for a in range(PTS))
+        along = sum(squares[a] * points[s][a : a + 1] for a in range(PTS))
+        total = along * scale[0]
         sums = [
             sum(float(D[b, j] ** power * W[b]) * mob_ref[s, :, b] for b in range(PTS))
             * row_weight
             * scale[1]
             for power in (1, 2)
         ]
-        yface_ref[s, 2] = along
+        yface_ref[s, 2] = points[s] * scale[0]
         yface_ref[s, 3] = points[s] * scale[2]
         yface_ref[s, 4] = sums[0]
         column = columns[s * PTS : (s + 1) * PTS] * cell_metric[e : e + 1]
@@ -626,10 +620,12 @@
     ]
     weight = [[pick(even, inner_ref, outer_ref, j * ny, ny) for j in range(PTS)]]
     smooth = jnp.concatenate([face_change(change, weight, 0, 1, q)[0] for q in range(2)], axis=0)
-    corners = to_vertices(smooth, jnp.zeros_like(smooth), restrict_ref[...])
+    hats = jnp.concatenate([restrict_ref[:width], restrict_ref[2 * width : 3 * width]], axis=0)
+    corners = dot_split(smooth, hats)
     lower, upper = corners[:ny], corners[ny:]
     row = lax.broadcasted_iota(jnp.int32, lower.shape, 0)
-    next_ref[:ny] = lower + jnp.where(row == 0, 0.0, pltpu.roll(upper, 1, 0))
+    rows = lower + jnp.where(row == 0, 0.0, pltpu.roll(upper, 1, 0))
+    next_ref[...] = jnp.concatenate([rows] * (next_ref.shape[0] // ny), axis=0)
     top_ref[...] = jnp.broadcast_to(upper[ny - 1 : ny], top_ref.shape)
 
 
@@ -752,7 +748,7 @@
     coarse_ref[...] = total[:, : coarse_ref.shape[1]]
 
 
-def call(body, outs, scratch, *args, spaces=None, out_spaces=None, flops=None):
+def call(body, outs, scratch, *args, spaces=None, out_spaces=None):
     spaces = spaces or [pltpu.SMEM if a.dtype == jnp.int32 else pltpu.VMEM for a in args]
     return pl.pallas_call(
         body,
@@ -761,7 +757,6 @@
         out_specs=[pl.BlockSpec(memory_space=m) for m in out_spaces or [pltpu.VMEM] * len(outs)],
         scratch_shapes=[pltpu.VMEM(s, F32) if isinstance(s, tuple) else s for s in scratch],
         compiler_params=pltpu.CompilerParams(vmem_limit_bytes=16 * 1024 * 1024),
-        cost_estimate=flops and pl.CostEstimate(flops=flops, bytes_accessed=0, transcendentals=0),
     )(*args)
 
 
@@ -878,7 +873,7 @@
         side, sofar, gain, gface, outer, below, above, inner,
         out_spaces=[pltpu.HBM, pltpu.VMEM],
     )
-    (onward,) = call(join_kernel, [(ny, 128)], [], own_rows, onward, top, token, flops=FLOPS_JOIN)
+    (onward,) = call(join_kernel, [(ny, 128)], [], own_rows, onward, top, token)
     row_below, row_above = from_y(tops)
     (coarse,) = call(last_kernel, [(ny, width // PTS + 1)], [], onward, row_below, row_above)
     return pressure.reshape(element_load.shape), coarse[None]

time: 25.8 us -> 25.8 us (level)
  no operation moved by 1% of the time
where the time goes in v8:
time: 25.8 us; the launch traced here: 25.6 us
  starting transfers between devices  15.3 us (59%)
  Pallas kernels  5.69 us (22%)
  waiting for transfers between devices  3.89 us (15%)
  between operations  0.74 us (3%)
    ppermute x3, starting transfers between devices, to_x(): outer = lax.ppermute(outer, 'dom', outer_pairs(size))  8.61 us
    ppermute x3, starting transfers between devices, from_y(): up = lax.ppermute(faces, 'sub', [(i, (i + 1) % size) for i in range(size)])  5.7 us
    pallas_call x12, Pallas kernels, call(): pl.pallas_call(body, out_shape=[jax.ShapeDtypeStruct(s, F32) if isinstanc...  5.69 us
    ppermute x3, waiting for transfers between devices, from_y(): up = lax.ppermute(faces, 'sub', [(i, (i + 1) % size) for i in range(size)])  1.35 us
    ppermute x1, waiting for transfers between devices, two_on(): return (rows, lax.ppermute(top, ('dom', 'sub'), pairs))  1.09 us
    ppermute x3, waiting for transfers between devices, to_x(): outer = lax.ppermute(outer, 'dom', outer_pairs(size))  1.02 us
    ppermute x1, starting transfers between devices, two_on(): return (rows, lax.ppermute(top, ('dom', 'sub'), pairs))  0.96 us
  transfers between devices with their start and end apart: 11, of which 4 were waited for; matrix products, arithmetic and copies ran while one was open for 0% of the time, Pallas kernels for 15%

profile of v8, /device:TPU:0, one launch (start us, length us, event | category | flops | bytes accessed | tf_op | source)
XLA Modules:
  0.0 25.6 jit_solution(8587641699978879990)
XLA Ops:
  0.6 0.0 copy-start
  0.6 0.0 copy-start.1
  0.6 1.2 %shard_map.77 = (f32[3,8,128]{2,1,0:T(8,128)S(1)}, f32[2,5,8,128]{3,2,1,0:T(8,128)S(1)}) custom-call(f32[3,8,16]{2,1,0:T(8,128)} %bitcast.13, f32[8,64,128]{2,1,0:T(8,128)} %bitcast.6, f32[8,64,128]{2,1,0:T(8,128)} %bitcast.10), custom_call_target="tpu_custom_call" | custom-call | tf_op jit(solution)/shard_map/pallas_call | solution.py:753
  1.9 3.0 %collective-permute-start = (f32[2,5,8,128]{3,2,1,0:T(8,128)S(1)}, f32[2,5,8,128]{3,2,1,0:T(8,128)S(1)}, u32[]{:S(2)}, u32[]{:S(2)}) collective-permute-start(f32[2,5,8,128]{3,2,1,0:T(8,128)S(1)} %get-tuple-element.35), channel_id=1, source_target_pairs={{0,1},{1,0},{2,3},{3,2},{4,5},{5,4},{6,7},{7,6},{8,9},{9,8},{10,11... | collective-permute-start | bytes 122888 | tf_op jit(solution)/shard_map/ppermute | solution.py:765
  4.9 0.0 copy-done
  4.9 0.0 copy-done.1
  4.9 0.0 copy-start.4
  4.9 0.6 %shard_map.78 = (f32[2,8,8,8,128]{4,3,2,1,0:T(8,128)S(1)}, f32[2,2,8,8,128]{4,3,2,1,0:T(8,128)S(1)}, f32[2,2,8,128]{3,2,1,0:T(8,128)S(1)}, f32[144,128]{1,0:T(8,128)S(1)}, f32[144,128]{1,0:T(8,128)S(1)}) custom-call(s32[1]{0:T(128)} %bitcast.side_ref, f32[8,64,128]{2,1,0:T(8,128)S(1)} %bitcast.11, f32[8,64,128]{2,1,0:T(8,128)S(1)} %bitcast.7, ...), custom_call_target="tpu_custom_call" | custom-call | tf_op jit(solution)/shard_map/pallas_call | solution.py:753
  5.5 0.0 copy-start.3
  5.5 1.3 %collective-permute-done.below_ref.above_ref = f32[2,5,8,128]{3,2,1,0:T(8,128)S(1)} collective-permute-done((f32[2,5,8,128]{3,2,1,0:T(8,128)S(1)}, f32[2,5,8,128]{3,2,1,0:T(8,128)S(1)}, u32[]{:S(2)}, u32[]{:S(2)}) %collective-permute-start) | collective-permute-done | bytes 40992 | tf_op jit(solution)/shard_map/ppermute | solution.py:765
  6.9 3.4 %collective-permute-start.1 = (f32[144,128]{1,0:T(8,128)S(1)}, f32[144,128]{1,0:T(8,128)S(1)}, u32[]{:S(2)}, u32[]{:S(2)}) collective-permute-start(f32[144,128]{1,0:T(8,128)S(1)} %get-tuple-element.47), channel_id=1, source_target_pairs={{0,30},{2,4},{4,2},{6,8},{8,6},{10,12},{12,10},{14,16},{16,14},{18... | collective-permute-start | bytes 221192 | tf_op jit(solution)/shard_map/ppermute | solution.py:781
  10.3 0.0 collective-permute-start.2
  10.3 1.9 %collective-permute-start.6 = (f32[144,128]{1,0:T(8,128)S(1)}, f32[144,128]{1,0:T(8,128)S(1)}, u32[]{:S(2)}, u32[]{:S(2)}) collective-permute-start(f32[144,128]{1,0:T(8,128)S(1)} %get-tuple-element.56), channel_id=1, source_target_pairs={{0,30},{2,4},{4,2},{6,8},{8,6},{10,12},{12,10},{14,16},{16,14},{18... | collective-permute-start | bytes 221192 | tf_op jit(solution)/shard_map/ppermute | solution.py:781
  12.2 0.0 collective-permute-start.7
  12.2 0.0 copy-done.4
  12.2 0.0 copy-done.3
  12.2 1.3 %shard_map.79 = (f32[2,2,8,8,128]{4,3,2,1,0:T(8,128)S(1)}, f32[8,8,8,128]{3,2,1,0:T(8,128)S(1)}, f32[8,8,8,128]{3,2,1,0:T(8,128)S(1)}, f32[8,8,8,128]{3,2,1,0:T(...) custom-call(f32[2,8,8,8,128]{4,3,2,1,0:T(8,128)S(1)} %get-tuple-elem, ...), custom_call_target="tpu_custom_call" | custom-call | tf_op jit(solution)/shard_map/pallas_call | solution.py:753
  13.5 0.0 collective-permute-done.1.outer_ref
  13.5 0.0 collective-permute-done.2.inner_ref
  13.5 0.0 copy-start.2
  13.5 0.5 %shard_map.81 = (f32[104,128]{1,0:T(8,128)S(1)}, f32[104,128]{1,0:T(8,128)S(1)}, f32[2,1,8,128]{3,2,1,0:T(8,128)S(1)}, f32[2,8,8,128]{3,2,1,0:T(8,128)S(1)}, f32...) custom-call(s32[1]{0:T(128)} %bitcast.side_ref, ...), custom_call_target="tpu_custom_call" | custom-call | tf_op jit(solution)/shard_map/pallas_call | solution.py:753
  14.0 3.3 %collective-permute-start.3 = (f32[104,128]{1,0:T(8,128)S(1)}, f32[104,128]{1,0:T(8,128)S(1)}, u32[]{:S(2)}, u32[]{:S(2)}) collective-permute-start(f32[104,128]{1,0:T(8,128)S(1)} %get-tuple-element.51.sent_outer_ref), channel_id=1, source_target_pairs={{0,30},{2,4},{4,2},{6,8},{8,6},{10,12},{12,10},{14,16},{16,14},{18... | collective-permute-start | bytes 159752 | tf_op jit(solution)/shard_map/ppermute | solution.py:781
  17.4 0.0 collective-permute-start.5
  17.4 0.0 collective-permute-done.6.outer_ref
  17.4 0.0 collective-permute-done.7.inner_ref
  17.4 0.0 copy-done.2
  17.4 0.2 shard_map.86
  17.5 0.0 collective-permute-start.8
  17.5 1.0 %collective-permute-start.9 = (f32[24,128]{1,0:T(8,128)S(1)}, f32[24,128]{1,0:T(8,128)S(1)}, u32[]{:S(2)}, u32[]{:S(2)}) collective-permute-start(f32[24,128]{1,0:T(8,128)S(1)} %get-tuple-element.61), channel_id=1, source_target_pairs={{0,5},{1,4},{2,7},{3,6},{4,9},{5,8},{6,11},{7,10},{8,13},{9,12},{1... | collective-permute-start | bytes 36872 | tf_op jit(solution)/shard_map/ppermute | solution.py:792
  18.5 0.7 %collective-permute-start.4 = (f32[2,1,8,128]{3,2,1,0:T(8,128)S(1)}, f32[2,1,8,128]{3,2,1,0:T(8,128)S(1)}, u32[]{:S(2)}, u32[]{:S(2)}) collective-permute-start(f32[2,1,8,128]{3,2,1,0:T(8,128)S(1)} %get-tuple-element.52), channel_id=1, source_target_pairs={{0,1},{1,0},{2,3},{3,2},{4,5},{5,4},{6,7},{7,6},{8,9},{9,8},{10,11... | collective-permute-start | bytes 24584 | tf_op jit(solution)/shard_map/ppermute | solution.py:765
  19.2 0.2 shard_map.83.own_ref
  19.3 1.0 %collective-permute-done.3.outer_ref = f32[104,128]{1,0:T(8,128)S(1)} collective-permute-done((f32[104,128]{1,0:T(8,128)S(1)}, f32[104,128]{1,0:T(8,128)S(1)}, u32[]{:S(2)}, u32[]{:S(2)}) %collective-permute-start.3) | collective-permute-done | bytes 53280 | tf_op jit(solution)/shard_map/ppermute | solution.py:781
  20.4 0.0 collective-permute-done.5.inner_ref
  20.4 0.2 shard_map.84
  20.5 2.0 %collective-permute-start.10 = (f32[3,128]{1,0:T(4,128)S(1)}, f32[3,128]{1,0:T(4,128)S(1)}, u32[]{:S(2)}, u32[]{:S(2)}) collective-permute-start(f32[3,128]{1,0:T(4,128)S(1)} %get-tuple-element.63), channel_id=1, source_target_pairs={{0,1},{1,0},{2,3},{3,2},{4,5},{5,4},{6,7},{7,6},{8,9},{9,8},{10,11... | collective-permute-start | bytes 4616 | tf_op jit(solution)/shard_map/ppermute | solution.py:765
  22.6 0.0 collective-permute-done.4.below_ref.above_ref
  22.6 0.8 %shard_map.82 = (f32[8,64,128]{2,1,0:T(8,128)}, f32[1,128]{1,0:T(1,128)S(1)}) custom-call(s32[1]{0:T(128)} %bitcast.side_ref, f32[8,8,8,128]{3,2,1,0:T(8,128)S(1)} %get-tuple-element.49.sofar_ref, f32[8,8,8,128]{3,2,1,0:T(8,128)S(1)} %get-tuple-element.41.gain_ref, f32[2,8,8,128]{3,2,1,0:T(8,128)S(1)} %get-tuple-element.50.gface_ref, ...), custom_call_target="tpu_custom_call" | custom-call | tf_op jit(solution)/shard_map/pallas_call | solution.py:753
  23.3 0.2 shard_map.85.own_ref
  23.5 0.4 %collective-permute-done.8.next_ref = f32[24,128]{1,0:T(8,128)S(1)} collective-permute-done((f32[24,128]{1,0:T(8,128)S(1)}, f32[24,128]{1,0:T(8,128)S(1)}, u32[]{:S(2)}, u32[]{:S(2)}) %collective-permute-start.8) | collective-permute-done | bytes 12320 | tf_op jit(solution)/shard_map/ppermute | solution.py:788
  23.9 1.1 %collective-permute-done.9.top_ref = f32[24,128]{1,0:T(8,128)S(1)} collective-permute-done((f32[24,128]{1,0:T(8,128)S(1)}, f32[24,128]{1,0:T(8,128)S(1)}, u32[]{:S(2)}, u32[]{:S(2)}) %collective-permute-start.9) | collective-permute-done | bytes 12320 | tf_op jit(solution)/shard_map/ppermute | solution.py:792
  25.0 0.0 collective-permute-done.10.below_ref.above_ref
  25.0 0.6 %shard_map.88 = f32[8,17]{1,0:T(8,128)} custom-call(f32[8,128]{1,0:T(8,128)S(1)} %shard_map.87.joined_ref, f32[3,128]{1,0:T(4,128)S(1)} %collective-permute-done.10.below_ref.above_ref, f32[3,128]{1,0:T(4,128)S(1)} %collective-permute-done.10.below_ref.above_ref), custom_call_target="tpu_custom_call" | custom-call | tf_op jit(solution)/shard_map/pallas_call | solution.py:753
  (2 shorter events, 0.0 us)
Async XLA Ops:
  0.6 4.3 %copy-start = (f32[1,8,8,8,128]{4,3,2,1,0:T(8,128)S(1)}, f32[1,8,8,8,128]{4,3,2,1,0:T(8,128)}, u32[]{:S(2)}) copy-start(f32[1,8,8,8,128]{4,3,2,1,0:T(8,128)} %param.7) | copy-start | bytes 786436
  0.6 4.3 %copy-start.1 = (f32[1,8,8,8,128]{4,3,2,1,0:T(8,128)S(1)}, f32[1,8,8,8,128]{4,3,2,1,0:T(8,128)}, u32[]{:S(2)}) copy-start(f32[1,8,8,8,128]{4,3,2,1,0:T(8,128)} %param.6) | copy-start | bytes 786436
  1.9 5.0 %collective-permute-start = (f32[2,5,8,128]{3,2,1,0:T(8,128)S(1)}, f32[2,5,8,128]{3,2,1,0:T(8,128)S(1)}, u32[]{:S(2)}, u32[]{:S(2)}) collective-permute-start(f32[2,5,8,128]{3,2,1,0:T(8,128)S(1)} %get-tuple-element.35), channel_id=1, source_target_pairs={{0,1},{1,0},{2,3},{3,2},{4,5},{5,4},{6,7},{7,6},{8,9},{9,8},{10,11... | collective-permute-start | bytes 122888 | tf_op jit(solution)/shard_map/ppermute | solution.py:765
  4.9 7.3 %copy-start.4 = (bf16[256,256]{1,0:T(8,128)(2,1)S(1)}, bf16[256,256]{1,0:T(8,128)(2,1)}, u32[]{:S(2)}) copy-start(bf16[256,256]{1,0:T(8,128)(2,1)} %constant.25.clone.grad_ref) | copy-start | bytes 393220
  5.5 6.7 %copy-start.3 = (bf16[256,256]{1,0:T(8,128)(2,1)S(1)}, bf16[256,256]{1,0:T(8,128)(2,1)}, u32[]{:S(2)}) copy-start(bf16[256,256]{1,0:T(8,128)(2,1)} %constant.26.clone.back_ref) | copy-start | bytes 393220
  6.9 6.6 %collective-permute-start.1 = (f32[144,128]{1,0:T(8,128)S(1)}, f32[144,128]{1,0:T(8,128)S(1)}, u32[]{:S(2)}, u32[]{:S(2)}) collective-permute-start(f32[144,128]{1,0:T(8,128)S(1)} %get-tuple-element.47), channel_id=1, source_target_pairs={{0,30},{2,4},{4,2},{6,8},{8,6},{10,12},{12,10},{14,16},{16,14},{18... | collective-permute-start | bytes 221192 | tf_op jit(solution)/shard_map/ppermute | solution.py:781
  10.3 3.2 %collective-permute-start.2 = (f32[144,128]{1,0:T(8,128)S(1)}, f32[144,128]{1,0:T(8,128)S(1)}, u32[]{:S(2)}, u32[]{:S(2)}) collective-permute-start(f32[144,128]{1,0:T(8,128)S(1)} %get-tuple-element.48), channel_id=1, source_target_pairs={{0,2},{2,0},{4,6},{6,4},{8,10},{10,8},{12,14},{14,12},{16,18},{18,... | collective-permute-start | bytes 221192 | tf_op jit(solution)/shard_map/ppermute | solution.py:782
  10.3 7.1 %collective-permute-start.6 = (f32[144,128]{1,0:T(8,128)S(1)}, f32[144,128]{1,0:T(8,128)S(1)}, u32[]{:S(2)}, u32[]{:S(2)}) collective-permute-start(f32[144,128]{1,0:T(8,128)S(1)} %get-tuple-element.56), channel_id=1, source_target_pairs={{0,30},{2,4},{4,2},{6,8},{8,6},{10,12},{12,10},{14,16},{16,14},{18... | collective-permute-start | bytes 221192 | tf_op jit(solution)/shard_map/ppermute | solution.py:781
  12.2 5.2 %collective-permute-start.7 = (f32[144,128]{1,0:T(8,128)S(1)}, f32[144,128]{1,0:T(8,128)S(1)}, u32[]{:S(2)}, u32[]{:S(2)}) collective-permute-start(f32[144,128]{1,0:T(8,128)S(1)} %get-tuple-element.57), channel_id=1, source_target_pairs={{0,2},{2,0},{4,6},{6,4},{8,10},{10,8},{12,14},{14,12},{16,18},{18,... | collective-permute-start | bytes 221192 | tf_op jit(solution)/shard_map/ppermute | solution.py:782
  13.5 3.9 %copy-start.2 = (bf16[512,256]{1,0:T(8,128)(2,1)S(1)}, bf16[512,256]{1,0:T(8,128)(2,1)}, u32[]{:S(2)}) copy-start(bf16[512,256]{1,0:T(8,128)(2,1)} %constant.27.clone.restrict_ref) | copy-start | bytes 786436
  14.0 6.3 %collective-permute-start.3 = (f32[104,128]{1,0:T(8,128)S(1)}, f32[104,128]{1,0:T(8,128)S(1)}, u32[]{:S(2)}, u32[]{:S(2)}) collective-permute-start(f32[104,128]{1,0:T(8,128)S(1)} %get-tuple-element.51.sent_outer_ref), channel_id=1, source_target_pairs={{0,30},{2,4},{4,2},{6,8},{8,6},{10,12},{12,10},{14,16},{16,14},{18... | collective-permute-start | bytes 159752 | tf_op jit(solution)/shard_map/ppermute | solution.py:781
  17.4 3.0 %collective-permute-start.5 = (f32[104,128]{1,0:T(8,128)S(1)}, f32[104,128]{1,0:T(8,128)S(1)}, u32[]{:S(2)}, u32[]{:S(2)}) collective-permute-start(f32[104,128]{1,0:T(8,128)S(1)} %get-tuple-element.53.sent_inner_ref), channel_id=1, source_target_pairs={{0,2},{2,0},{4,6},{6,4},{8,10},{10,8},{12,14},{14,12},{16,18},{18,... | collective-permute-start | bytes 159752 | tf_op jit(solution)/shard_map/ppermute | solution.py:782
  17.5 6.4 %collective-permute-start.8 = (f32[24,128]{1,0:T(8,128)S(1)}, f32[24,128]{1,0:T(8,128)S(1)}, u32[]{:S(2)}, u32[]{:S(2)}) collective-permute-start(f32[24,128]{1,0:T(8,128)S(1)} %get-tuple-element.60), channel_id=1, source_target_pairs={{0,4},{2,6},{4,8},{6,10},{8,12},{10,14},{12,16},{14,18},{16,20},{1... | collective-permute-start | bytes 36872 | tf_op jit(solution)/shard_map/ppermute | solution.py:788
  17.5 7.5 %collective-permute-start.9 = (f32[24,128]{1,0:T(8,128)S(1)}, f32[24,128]{1,0:T(8,128)S(1)}, u32[]{:S(2)}, u32[]{:S(2)}) collective-permute-start(f32[24,128]{1,0:T(8,128)S(1)} %get-tuple-element.61), channel_id=1, source_target_pairs={{0,5},{1,4},{2,7},{3,6},{4,9},{5,8},{6,11},{7,10},{8,13},{9,12},{1... | collective-permute-start | bytes 36872 | tf_op jit(solution)/shard_map/ppermute | solution.py:792
  18.5 4.1 %collective-permute-start.4 = (f32[2,1,8,128]{3,2,1,0:T(8,128)S(1)}, f32[2,1,8,128]{3,2,1,0:T(8,128)S(1)}, u32[]{:S(2)}, u32[]{:S(2)}) collective-permute-start(f32[2,1,8,128]{3,2,1,0:T(8,128)S(1)} %get-tuple-element.52), channel_id=1, source_target_pairs={{0,1},{1,0},{2,3},{3,2},{4,5},{5,4},{6,7},{7,6},{8,9},{9,8},{10,11... | collective-permute-start | bytes 24584 | tf_op jit(solution)/shard_map/ppermute | solution.py:765
  20.5 4.5 %collective-permute-start.10 = (f32[3,128]{1,0:T(4,128)S(1)}, f32[3,128]{1,0:T(4,128)S(1)}, u32[]{:S(2)}, u32[]{:S(2)}) collective-permute-start(f32[3,128]{1,0:T(4,128)S(1)} %get-tuple-element.63), channel_id=1, source_target_pairs={{0,1},{1,0},{2,3},{3,2},{4,5},{5,4},{6,7},{7,6},{8,9},{9,8},{10,11... | collective-permute-start | bytes 4616 | tf_op jit(solution)/shard_map/ppermute | solution.py:765

commit v9 on v8

--- a/solution.py
+++ b/solution.py
@@ -145,17 +145,12 @@
 def spread_metric(metric, weight_row):
     _, rows, cells = metric.shape
     width = weight_row.shape[1]
-    cell = lax.broadcasted_iota(jnp.int32, (cells, width), 1) // PTS
-    row = lax.broadcasted_iota(jnp.int32, (cells, width), 0)
-    pick = jnp.where(cell == row, 1.0, 0.0).astype(jnp.bfloat16)
-    flat = metric.reshape(3 * rows, cells)
-    high = flat.astype(jnp.bfloat16)
-    rest = flat - high.astype(F32)
-    parts = jnp.concatenate([high, *halves(rest)], axis=1)
-    spread = jnp.dot(
-        parts, jnp.concatenate([pick] * 3, axis=0), preferred_element_type=F32
-    )
-    spread = [spread[d * rows : (d + 1) * rows] for d in range(3)]
+    cell = lax.broadcasted_iota(jnp.int32, (rows, width), 1) // PTS
+    fill = jnp.zeros((rows, width - cells), F32)
+    spread = [
+        jnp.take_along_axis(jnp.concatenate([metric[d], fill], axis=1), cell, axis=1, mode="promise_in_bounds")
+        for d in range(3)
+    ]
     return [v * weight_row[:1] for v in spread], spread[2]
 
 
@@ -241,12 +236,13 @@
 
 def diag_kernel(
     side_ref, load_ref, mob_ref, spread_ref,
-    fields_ref, xface_ref, factor_ref, to_outer_ref, to_inner_ref,
+    fields_ref, xface_ref, factor_ref, to_outer_ref, to_inner_ref, weights_ref, sums_ref,
 ):
     ny, width = fields_ref.shape[3:]
     spread = [spread_ref[d] for d in range(3)]
     square = D * D
     squared = paired_here(cell_blocks(tiled(square, width)))
+    back = paired_here(cell_blocks(tiled(D, width)))
     mob, load = plane(mob_ref, ny), plane(load_ref, ny)
     diag_ref = fields_ref.at[1]
     even = side_ref[0] == 0
@@ -263,15 +259,20 @@
         post((PTS + j) * ny, *(float(W[i] * W[j]) * mob(i, j) for i in (0, PTS - 1)))
         for i, value in enumerate(contract(square.T, factor, 1)):
             diag_ref[i, j] = value
+        for i, value in enumerate(contract(D.T, factor, -1)):
+            weights_ref[0, i, j] = value
     for i in range(PTS):
         factor = [mob(i, j) * (float(W[i] * W[j]) * spread[1]) for j in range(PTS)]
         for j, value in enumerate(contract(square.T, factor, 1)):
             diag_ref[i, j] += value
+        for j, value in enumerate(contract(D.T, factor, -1)):
+            weights_ref[1, i, j] = value
     for i in range(PTS):
         factor = jnp.concatenate(
             [mob(i, j) * (float(W[i] * W[j]) * spread[2]) for j in range(PTS)], axis=0
         )
         diag_ref[i] += dot_split(factor, squared).reshape(PTS, ny, width)
+        weights_ref[2, i] = dot_split(factor, back).reshape(PTS, ny, width)
         fields_ref[0, i] = jnp.stack([load(i, j) for j in range(PTS)], axis=0)
     masks = column_masks((PTS, ny, width))
     for f in range(2):
@@ -285,6 +286,16 @@
         for n, e in enumerate((0, ny - 1)):
             points = mob_ref[i, e * PTS : (e + 1) * PTS] * (float(W[i]) * row_weight)
             factor_ref[s, n] = points * spread[1][e : e + 1]
+    zero = jnp.zeros((ny, width), F32)
+    sums = [zero] * 4
+    for i in range(PTS):
+        for q in range(2):
+            from_load = sum(float(HAT[j, q]) * load(i, j) for j in range(PTS))
+            for p in range(2):
+                if HAT[i, p]:
+                    sums[2 * p + q] = sums[2 * p + q] + float(HAT[i, p]) * from_load
+    for n in range(4):
+        sums_ref[n] = sums[n]
 
 
 def merge_kernel(side_ref, xface_ref, factor_ref, below_ref, above_ref, outer_ref, inner_ref):
@@ -312,14 +323,14 @@
 
 
 def inside_kernel(
-    fields_ref, load_ref, mob_ref, spread_ref, grad_ref, back_ref, below_ref, above_ref,
-    rough_ref, value_ref, partial_ref, gain_ref, out_ref, pair_ref, weights_ref, sums_ref, edge_weights_ref,
+    fields_ref, mob_ref, spread_ref, grad_ref, back_ref, below_ref, above_ref,
+    rough_ref, value_ref, partial_ref, gain_ref, out_ref, pair_ref, edge_weights_ref,
     work_ref,
 ):
     below_ref, above_ref = below_ref.at[1], above_ref.at[0]
     ny, width = out_ref.shape[2:]
     spread = [spread_ref[d] for d in range(3)]
-    mob, load = plane(mob_ref, ny), plane(load_ref, ny)
+    mob = plane(mob_ref, ny)
     row = lax.broadcasted_iota(jnp.int32, (ny, width), 0)
     zero = jnp.zeros((ny, width), F32)
     for i in range(PTS):
@@ -347,8 +358,6 @@
         flux = [flux[i] * factor[i] for i in range(PTS)]
         for i, value in enumerate(contract(D.T, flux, -1)):
             out_ref[i, j] = value
-        for i, value in enumerate(contract(D.T, factor, -1)):
-            weights_ref[0, i, j] = value
     for i in range(1, PTS - 1):
         flux = contract(D, [value_ref[i, j] for j in range(PTS)], -1)
         flux = [flux[j] * (mob(i, j) * (float(W[i] * W[j]) * spread[1])) for j in range(PTS)]
@@ -358,23 +367,6 @@
         for j in range(PTS):
             work_ref[j] *= mob(i, j) * (float(W[i] * W[j]) * spread[2])
         out_ref[i] += dot_split(work_ref[...].reshape(PTS * ny, width), back).reshape(PTS, ny, width)
-    for i in range(PTS):
-        factor = [mob(i, j) * (float(W[i] * W[j]) * spread[1]) for j in range(PTS)]
-        for j, value in enumerate(contract(D.T, factor, -1)):
-            weights_ref[1, i, j] = value
-        factor = jnp.concatenate(
-            [mob(i, j) * (float(W[i] * W[j]) * spread[2]) for j in range(PTS)], axis=0
-        )
-        weights_ref[2, i] = dot_split(factor, back).reshape(PTS, ny, width)
-    sums = [zero] * 4
-    for i in range(PTS):
-        for q in range(2):
-            from_load = sum(float(HAT[j, q]) * load(i, j) for j in range(PTS))
-            for p in range(2):
-                if HAT[i, p]:
-                    sums[2 * p + q] = sums[2 * p + q] + float(HAT[i, p]) * from_load
-    for n in range(4):
-        sums_ref[n] = sums[n]
     for t, ref in enumerate((below_ref, above_ref)):
         edge_weights_ref[t, 0] = sum(by_row(D[a], width) * ref[2, a : a + 1] for a in range(PTS))
         edge_weights_ref[t, 1] = ref[4]
@@ -815,9 +807,12 @@
     )
     below, above = from_y(yface)
     still = (2 * (PTS + 1) * ny, width)
-    fields, xface, factor, still_outer, still_inner = call(
+    fields, xface, factor, still_outer, still_inner, weights, load_sums = call(
         diag_kernel,
-        [(2,) + field, (2, 2) + face, (2, 2, PTS, width), still, still],
+        [
+            (2,) + field, (2, 2) + face, (2, 2, PTS, width), still, still,
+            (3,) + field, (4, ny, width),
+        ],
         [],
         side, load, mob, spread,
     )
@@ -825,14 +820,14 @@
     outer, inner = to_x(*call(merge_kernel, [rows, rows], [], side, xface, factor, below, above))
     still_outer, still_inner = to_x(still_outer, still_inner)
     faces = (2,) + face
-    rough, value, partial, gain, out, pair, weights, load_sums, edge_weights = call(
+    rough, value, partial, gain, out, pair, edge_weights = call(
         inside_kernel,
         [
             (2,) + faces, field, field, field, field, (2,) + field,
-            (3,) + field, (4, ny, width), (2, 3, PTS, width),
+            (2, 3, PTS, width),
         ],
         [face],
-        fields, load, mob, spread, grad, back, below, above,
+        fields, mob, spread, grad, back, below, above,
     )
     rows = ((PTS + 4) * ny + PTS, width)
     sent_outer, sent_inner, yface, gface, sofar, sums, edge = call(

time: 25.8 us -> 25.7 us (level)
  Pallas kernels: 5.69 us -> 5.4 us
    ppermute x3, waiting for transfers between devices: 1.02 us -> 1.33 us  [to_x(): outer = lax.ppermute(outer, 'dom', outer_pairs(size))]
    pallas_call x12, Pallas kernels: 5.69 us -> 5.4 us  [call(): pl.pallas_call(body, out_shape=[jax.ShapeDtypeStruct(s, F32) if isinstanc...]
  transfers between devices with their start and end apart: 11 -> 11, of which waited for: 4 -> 5; matrix products, arithmetic and copies ran while one was open for 0% -> 0% of each run, Pallas kernels for 15% -> 14%
where the time goes in v9:
time: 25.7 us; the launch traced here: 25.6 us
  starting transfers between devices  15.4 us (60%)
  Pallas kernels  5.4 us (21%)
  waiting for transfers between devices  3.97 us (15%)
  between operations  0.74 us (3%)
    ppermute x3, starting transfers between devices, to_x(): outer = lax.ppermute(outer, 'dom', outer_pairs(size))  8.69 us
    ppermute x3, starting transfers between devices, from_y(): up = lax.ppermute(faces, 'sub', [(i, (i + 1) % size) for i in range(size)])  5.89 us
    pallas_call x12, Pallas kernels, call(): pl.pallas_call(body, out_shape=[jax.ShapeDtypeStruct(s, F32) if isinstanc...  5.4 us
    ppermute x3, waiting for transfers between devices, to_x(): outer = lax.ppermute(outer, 'dom', outer_pairs(size))  1.33 us
    ppermute x3, waiting for transfers between devices, from_y(): up = lax.ppermute(faces, 'sub', [(i, (i + 1) % size) for i in range(size)])  1.12 us
    ppermute x1, waiting for transfers between devices, two_on(): return (rows, lax.ppermute(top, ('dom', 'sub'), pairs))  1.09 us
    ppermute x1, starting transfers between devices, two_on(): return (rows, lax.ppermute(top, ('dom', 'sub'), pairs))  0.85 us
  transfers between devices with their start and end apart: 11, of which 5 were waited for; matrix products, arithmetic and copies ran while one was open for 0% of the time, Pallas kernels for 14%

profile of v9, /device:TPU:0, one launch (start us, length us, event | category | flops | bytes accessed | tf_op | source)
XLA Modules:
  0.0 25.6 jit_solution(2784841407856080266)
XLA Ops:
  0.6 0.0 copy-start
  0.6 0.0 copy-start.3
  0.6 1.1 %shard_map.77 = (f32[3,8,128]{2,1,0:T(8,128)S(1)}, f32[2,5,8,128]{3,2,1,0:T(8,128)S(1)}) custom-call(f32[3,8,16]{2,1,0:T(8,128)} %bitcast.12, f32[8,64,128]{2,1,0:T(8,128)} %bitcast.6, f32[8,64,128]{2,1,0:T(8,128)} %bitcast.10), custom_call_target="tpu_custom_call" | custom-call | tf_op jit(solution)/shard_map/pallas_call | solution.py:745
  1.8 3.0 %collective-permute-start = (f32[2,5,8,128]{3,2,1,0:T(8,128)S(1)}, f32[2,5,8,128]{3,2,1,0:T(8,128)S(1)}, u32[]{:S(2)}, u32[]{:S(2)}) collective-permute-start(f32[2,5,8,128]{3,2,1,0:T(8,128)S(1)} %get-tuple-element.35), channel_id=1, source_target_pairs={{0,1},{1,0},{2,3},{3,2},{4,5},{5,4},{6,7},{7,6},{8,9},{9,8},{10,11... | collective-permute-start | bytes 122888 | tf_op jit(solution)/shard_map/ppermute | solution.py:757
  4.8 0.0 copy-done
  4.8 0.0 copy-done.3
  4.8 0.0 copy-start.4
  4.8 0.8 %shard_map.78 = (f32[2,8,8,8,128]{4,3,2,1,0:T(8,128)S(1)}, f32[2,2,8,8,128]{4,3,2,1,0:T(8,128)S(1)}, f32[2,2,8,128]{3,2,1,0:T(8,128)S(1)}, f32[144,128]{1,0:T(8,...) custom-call(s32[1]{0:T(128)} %bitcast.side_ref, ...), custom_call_target="tpu_custom_call" | custom-call | tf_op jit(solution)/shard_map/pallas_call | solution.py:745
  5.7 0.0 copy-start.2
  5.7 1.1 %collective-permute-done.below_ref.above_ref = f32[2,5,8,128]{3,2,1,0:T(8,128)S(1)} collective-permute-done((f32[2,5,8,128]{3,2,1,0:T(8,128)S(1)}, f32[2,5,8,128]{3,2,1,0:T(8,128)S(1)}, u32[]{:S(2)}, u32[]{:S(2)}) %collective-permute-start) | collective-permute-done | bytes 40992 | tf_op jit(solution)/shard_map/ppermute | solution.py:757
  6.8 3.4 %collective-permute-start.1 = (f32[144,128]{1,0:T(8,128)S(1)}, f32[144,128]{1,0:T(8,128)S(1)}, u32[]{:S(2)}, u32[]{:S(2)}) collective-permute-start(f32[144,128]{1,0:T(8,128)S(1)} %get-tuple-element.47), channel_id=1, source_target_pairs={{0,30},{2,4},{4,2},{6,8},{8,6},{10,12},{12,10},{14,16},{16,14},{18... | collective-permute-start | bytes 221192 | tf_op jit(solution)/shard_map/ppermute | solution.py:773
  10.2 0.0 collective-permute-start.2
  10.2 1.9 %collective-permute-start.6 = (f32[144,128]{1,0:T(8,128)S(1)}, f32[144,128]{1,0:T(8,128)S(1)}, u32[]{:S(2)}, u32[]{:S(2)}) collective-permute-start(f32[144,128]{1,0:T(8,128)S(1)} %get-tuple-element.56), channel_id=1, source_target_pairs={{0,30},{2,4},{4,2},{6,8},{8,6},{10,12},{12,10},{14,16},{16,14},{18... | collective-permute-start | bytes 221192 | tf_op jit(solution)/shard_map/ppermute | solution.py:773
  12.1 0.0 collective-permute-start.7
  12.1 0.0 copy-done.4
  12.1 0.0 copy-done.2
  12.1 0.9 %shard_map.79 = (f32[2,2,8,8,128]{4,3,2,1,0:T(8,128)S(1)}, f32[8,8,8,128]{3,2,1,0:T(8,128)S(1)}, f32[8,8,8,128]{3,2,1,0:T(8,128)S(1)}, f32[8,8,8,128]{3,2,1,0:T(...) custom-call(f32[2,8,8,8,128]{4,3,2,1,0:T(8,128)S(1)} %get-tuple-element.34., ...), custom_call_target="tpu_custom_call" | custom-call | tf_op jit(solution)/shard_map/pallas_call | solution.py:745
  13.0 0.4 %collective-permute-done.1.outer_ref = f32[144,128]{1,0:T(8,128)S(1)} collective-permute-done((f32[144,128]{1,0:T(8,128)S(1)}, f32[144,128]{1,0:T(8,128)S(1)}, u32[]{:S(2)}, u32[]{:S(2)}) %collective-permute-start.1) | collective-permute-done | bytes 73760 | tf_op jit(solution)/shard_map/ppermute | solution.py:773
  13.4 0.0 collective-permute-done.2.inner_ref
  13.4 0.0 copy-start.1
  13.4 0.5 %shard_map.81 = (f32[104,128]{1,0:T(8,128)S(1)}, f32[104,128]{1,0:T(8,128)S(1)}, f32[2,1,8,128]{3,2,1,0:T(8,128)S(1)}, f32[2,8,8,128]{3,2,1,0:T(8,128)S(1)}, f32...) custom-call(s32[1]{0:T(128)} %bitcast.side_ref, ...), custom_call_target="tpu_custom_call" | custom-call | tf_op jit(solution)/shard_map/pallas_call | solution.py:745
  13.9 3.4 %collective-permute-start.3 = (f32[104,128]{1,0:T(8,128)S(1)}, f32[104,128]{1,0:T(8,128)S(1)}, u32[]{:S(2)}, u32[]{:S(2)}) collective-permute-start(f32[104,128]{1,0:T(8,128)S(1)} %get-tuple-element.51.sent_outer_ref), channel_id=1, source_target_pairs={{0,30},{2,4},{4,2},{6,8},{8,6},{10,12},{12,10},{14,16},{16,14},{18... | collective-permute-start | bytes 159752 | tf_op jit(solution)/shard_map/ppermute | solution.py:773
  17.3 0.0 collective-permute-start.5
  17.3 0.0 collective-permute-done.6.outer_ref
  17.3 0.0 collective-permute-done.7.inner_ref
  17.3 0.0 copy-done.1
  17.3 0.2 shard_map.86
  17.5 0.0 collective-permute-start.8
  17.5 0.8 %collective-permute-start.9 = (f32[24,128]{1,0:T(8,128)S(1)}, f32[24,128]{1,0:T(8,128)S(1)}, u32[]{:S(2)}, u32[]{:S(2)}) collective-permute-start(f32[24,128]{1,0:T(8,128)S(1)} %get-tuple-element.61), channel_id=1, source_target_pairs={{0,5},{1,4},{2,7},{3,6},{4,9},{5,8},{6,11},{7,10},{8,13},{9,12},{1... | collective-permute-start | bytes 36872 | tf_op jit(solution)/shard_map/ppermute | solution.py:784
  18.3 0.8 %collective-permute-start.4 = (f32[2,1,8,128]{3,2,1,0:T(8,128)S(1)}, f32[2,1,8,128]{3,2,1,0:T(8,128)S(1)}, u32[]{:S(2)}, u32[]{:S(2)}) collective-permute-start(f32[2,1,8,128]{3,2,1,0:T(8,128)S(1)} %get-tuple-element.52), channel_id=1, source_target_pairs={{0,1},{1,0},{2,3},{3,2},{4,5},{5,4},{6,7},{7,6},{8,9},{9,8},{10,11... | collective-permute-start | bytes 24584 | tf_op jit(solution)/shard_map/ppermute | solution.py:757
  19.1 0.2 shard_map.83.own_ref
  19.3 0.9 %collective-permute-done.3.outer_ref = f32[104,128]{1,0:T(8,128)S(1)} collective-permute-done((f32[104,128]{1,0:T(8,128)S(1)}, f32[104,128]{1,0:T(8,128)S(1)}, u32[]{:S(2)}, u32[]{:S(2)}) %collective-permute-start.3) | collective-permute-done | bytes 53280 | tf_op jit(solution)/shard_map/ppermute | solution.py:773
  20.2 0.0 collective-permute-done.5.inner_ref
  20.2 0.2 shard_map.84
  20.4 2.1 %collective-permute-start.10 = (f32[3,128]{1,0:T(4,128)S(1)}, f32[3,128]{1,0:T(4,128)S(1)}, u32[]{:S(2)}, u32[]{:S(2)}) collective-permute-start(f32[3,128]{1,0:T(4,128)S(1)} %get-tuple-element.63), channel_id=1, source_target_pairs={{0,1},{1,0},{2,3},{3,2},{4,5},{5,4},{6,7},{7,6},{8,9},{9,8},{10,11... | collective-permute-start | bytes 4616 | tf_op jit(solution)/shard_map/ppermute | solution.py:757
  22.5 0.0 collective-permute-done.4.below_ref.above_ref
  22.5 0.8 %shard_map.82 = (f32[8,64,128]{2,1,0:T(8,128)}, f32[1,128]{1,0:T(1,128)S(1)}) custom-call(s32[1]{0:T(128)} %bitcast.side_ref, f32[8,8,8,128]{3,2,1,0:T(8,128)S(1)} %get-tuple-element.49.sofar_ref, f32[8,8,8,128]{3,2,1,0:T(8,128)S(1)} %get-tuple-element.41.gain_ref, f32[2,8,8,128]{3,2,1,0:T(8,128)S(1)} %get-tuple-element.50.gface_ref, ...), custom_call_target="tpu_custom_call" | custom-call | tf_op jit(solution)/shard_map/pallas_call | solution.py:745
  23.3 0.2 shard_map.85.own_ref
  23.5 0.4 %collective-permute-done.8.next_ref = f32[24,128]{1,0:T(8,128)S(1)} collective-permute-done((f32[24,128]{1,0:T(8,128)S(1)}, f32[24,128]{1,0:T(8,128)S(1)}, u32[]{:S(2)}, u32[]{:S(2)}) %collective-permute-start.8) | collective-permute-done | bytes 12320 | tf_op jit(solution)/shard_map/ppermute | solution.py:780
  23.9 1.1 %collective-permute-done.9.top_ref = f32[24,128]{1,0:T(8,128)S(1)} collective-permute-done((f32[24,128]{1,0:T(8,128)S(1)}, f32[24,128]{1,0:T(8,128)S(1)}, u32[]{:S(2)}, u32[]{:S(2)}) %collective-permute-start.9) | collective-permute-done | bytes 12320 | tf_op jit(solution)/shard_map/ppermute | solution.py:784
  25.0 0.0 collective-permute-done.10.below_ref.above_ref
  25.0 0.6 %shard_map.88 = f32[8,17]{1,0:T(8,128)} custom-call(f32[8,128]{1,0:T(8,128)S(1)} %shard_map.87.joined_ref, f32[3,128]{1,0:T(4,128)S(1)} %collective-permute-done.10.below_ref.above_ref, f32[3,128]{1,0:T(4,128)S(1)} %collective-permute-done.10.below_ref.above_ref), custom_call_target="tpu_custom_call" | custom-call | tf_op jit(solution)/shard_map/pallas_call | solution.py:745
  (2 shorter events, 0.0 us)
Async XLA Ops:
  0.6 4.2 %copy-start = (f32[1,8,8,8,128]{4,3,2,1,0:T(8,128)S(1)}, f32[1,8,8,8,128]{4,3,2,1,0:T(8,128)}, u32[]{:S(2)}) copy-start(f32[1,8,8,8,128]{4,3,2,1,0:T(8,128)} %param.7) | copy-start | bytes 786436
  0.6 4.2 %copy-start.3 = (f32[1,8,8,8,128]{4,3,2,1,0:T(8,128)S(1)}, f32[1,8,8,8,128]{4,3,2,1,0:T(8,128)}, u32[]{:S(2)}) copy-start(f32[1,8,8,8,128]{4,3,2,1,0:T(8,128)} %param.6) | copy-start | bytes 786436
  1.8 5.0 %collective-permute-start = (f32[2,5,8,128]{3,2,1,0:T(8,128)S(1)}, f32[2,5,8,128]{3,2,1,0:T(8,128)S(1)}, u32[]{:S(2)}, u32[]{:S(2)}) collective-permute-start(f32[2,5,8,128]{3,2,1,0:T(8,128)S(1)} %get-tuple-element.35), channel_id=1, source_target_pairs={{0,1},{1,0},{2,3},{3,2},{4,5},{5,4},{6,7},{7,6},{8,9},{9,8},{10,11... | collective-permute-start | bytes 122888 | tf_op jit(solution)/shard_map/ppermute | solution.py:757
  4.8 7.3 %copy-start.4 = (bf16[256,256]{1,0:T(8,128)(2,1)S(1)}, bf16[256,256]{1,0:T(8,128)(2,1)}, u32[]{:S(2)}) copy-start(bf16[256,256]{1,0:T(8,128)(2,1)} %constant.25.clone.grad_ref) | copy-start | bytes 393220
  5.7 6.4 %copy-start.2 = (bf16[256,256]{1,0:T(8,128)(2,1)S(1)}, bf16[256,256]{1,0:T(8,128)(2,1)}, u32[]{:S(2)}) copy-start(bf16[256,256]{1,0:T(8,128)(2,1)} %constant.26.clone.back_ref) | copy-start | bytes 393220
  6.8 6.5 %collective-permute-start.1 = (f32[144,128]{1,0:T(8,128)S(1)}, f32[144,128]{1,0:T(8,128)S(1)}, u32[]{:S(2)}, u32[]{:S(2)}) collective-permute-start(f32[144,128]{1,0:T(8,128)S(1)} %get-tuple-element.47), channel_id=1, source_target_pairs={{0,30},{2,4},{4,2},{6,8},{8,6},{10,12},{12,10},{14,16},{16,14},{18... | collective-permute-start | bytes 221192 | tf_op jit(solution)/shard_map/ppermute | solution.py:773
  10.2 3.2 %collective-permute-start.2 = (f32[144,128]{1,0:T(8,128)S(1)}, f32[144,128]{1,0:T(8,128)S(1)}, u32[]{:S(2)}, u32[]{:S(2)}) collective-permute-start(f32[144,128]{1,0:T(8,128)S(1)} %get-tuple-element.48), channel_id=1, source_target_pairs={{0,2},{2,0},{4,6},{6,4},{8,10},{10,8},{12,14},{14,12},{16,18},{18,... | collective-permute-start | bytes 221192 | tf_op jit(solution)/shard_map/ppermute | solution.py:774
  10.2 7.1 %collective-permute-start.6 = (f32[144,128]{1,0:T(8,128)S(1)}, f32[144,128]{1,0:T(8,128)S(1)}, u32[]{:S(2)}, u32[]{:S(2)}) collective-permute-start(f32[144,128]{1,0:T(8,128)S(1)} %get-tuple-element.56), channel_id=1, source_target_pairs={{0,30},{2,4},{4,2},{6,8},{8,6},{10,12},{12,10},{14,16},{16,14},{18... | collective-permute-start | bytes 221192 | tf_op jit(solution)/shard_map/ppermute | solution.py:773
  12.1 5.2 %collective-permute-start.7 = (f32[144,128]{1,0:T(8,128)S(1)}, f32[144,128]{1,0:T(8,128)S(1)}, u32[]{:S(2)}, u32[]{:S(2)}) collective-permute-start(f32[144,128]{1,0:T(8,128)S(1)} %get-tuple-element.57), channel_id=1, source_target_pairs={{0,2},{2,0},{4,6},{6,4},{8,10},{10,8},{12,14},{14,12},{16,18},{18,... | collective-permute-start | bytes 221192 | tf_op jit(solution)/shard_map/ppermute | solution.py:774
  13.4 3.9 %copy-start.1 = (bf16[512,256]{1,0:T(8,128)(2,1)S(1)}, bf16[512,256]{1,0:T(8,128)(2,1)}, u32[]{:S(2)}) copy-start(bf16[512,256]{1,0:T(8,128)(2,1)} %constant.27.clone.restrict_ref) | copy-start | bytes 786436
  13.9 6.3 %collective-permute-start.3 = (f32[104,128]{1,0:T(8,128)S(1)}, f32[104,128]{1,0:T(8,128)S(1)}, u32[]{:S(2)}, u32[]{:S(2)}) collective-permute-start(f32[104,128]{1,0:T(8,128)S(1)} %get-tuple-element.51.sent_outer_ref), channel_id=1, source_target_pairs={{0,30},{2,4},{4,2},{6,8},{8,6},{10,12},{12,10},{14,16},{16,14},{18... | collective-permute-start | bytes 159752 | tf_op jit(solution)/shard_map/ppermute | solution.py:773
  17.3 2.9 %collective-permute-start.5 = (f32[104,128]{1,0:T(8,128)S(1)}, f32[104,128]{1,0:T(8,128)S(1)}, u32[]{:S(2)}, u32[]{:S(2)}) collective-permute-start(f32[104,128]{1,0:T(8,128)S(1)} %get-tuple-element.53.sent_inner_ref), channel_id=1, source_target_pairs={{0,2},{2,0},{4,6},{6,4},{8,10},{10,8},{12,14},{14,12},{16,18},{18,... | collective-permute-start | bytes 159752 | tf_op jit(solution)/shard_map/ppermute | solution.py:774
  17.5 6.4 %collective-permute-start.8 = (f32[24,128]{1,0:T(8,128)S(1)}, f32[24,128]{1,0:T(8,128)S(1)}, u32[]{:S(2)}, u32[]{:S(2)}) collective-permute-start(f32[24,128]{1,0:T(8,128)S(1)} %get-tuple-element.60), channel_id=1, source_target_pairs={{0,4},{2,6},{4,8},{6,10},{8,12},{10,14},{12,16},{14,18},{16,20},{1... | collective-permute-start | bytes 36872 | tf_op jit(solution)/shard_map/ppermute | solution.py:780
  17.5 7.5 %collective-permute-start.9 = (f32[24,128]{1,0:T(8,128)S(1)}, f32[24,128]{1,0:T(8,128)S(1)}, u32[]{:S(2)}, u32[]{:S(2)}) collective-permute-start(f32[24,128]{1,0:T(8,128)S(1)} %get-tuple-element.61), channel_id=1, source_target_pairs={{0,5},{1,4},{2,7},{3,6},{4,9},{5,8},{6,11},{7,10},{8,13},{9,12},{1... | collective-permute-start | bytes 36872 | tf_op jit(solution)/shard_map/ppermute | solution.py:784
  18.3 4.2 %collective-permute-start.4 = (f32[2,1,8,128]{3,2,1,0:T(8,128)S(1)}, f32[2,1,8,128]{3,2,1,0:T(8,128)S(1)}, u32[]{:S(2)}, u32[]{:S(2)}) collective-permute-start(f32[2,1,8,128]{3,2,1,0:T(8,128)S(1)} %get-tuple-element.52), channel_id=1, source_target_pairs={{0,1},{1,0},{2,3},{3,2},{4,5},{5,4},{6,7},{7,6},{8,9},{9,8},{10,11... | collective-permute-start | bytes 24584 | tf_op jit(solution)/shard_map/ppermute | solution.py:757
  20.4 4.6 %collective-permute-start.10 = (f32[3,128]{1,0:T(4,128)S(1)}, f32[3,128]{1,0:T(4,128)S(1)}, u32[]{:S(2)}, u32[]{:S(2)}) collective-permute-start(f32[3,128]{1,0:T(4,128)S(1)} %get-tuple-element.63), channel_id=1, source_target_pairs={{0,1},{1,0},{2,3},{3,2},{4,5},{5,4},{6,7},{7,6},{8,9},{9,8},{10,11... | collective-permute-start | bytes 4616 | tf_op jit(solution)/shard_map/ppermute | solution.py:757

commit v10 on v9

--- a/solution.py
+++ b/solution.py
@@ -384,7 +384,7 @@
     side_ref, rough_ref, value_ref, out_ref, pair_ref, mob_ref, spread_ref, grad_ref, back_ref,
     below_ref, above_ref, partial_ref, gain_ref, weights_ref, load_sums_ref, edge_weights_ref,
     outer_ref, inner_ref,
-    to_outer_ref, to_inner_ref, yface_ref, gface_ref, sofar_ref, sums_ref, edge_ref, line_ref, work_ref,
+    to_outer_ref, to_inner_ref, yface_ref, gface_ref, sofar_ref, edge_ref, line_ref, work_ref,
 ):
     below_ref, above_ref = below_ref.at[1], above_ref.at[0]
     even = side_ref[0] == 0
@@ -492,12 +492,10 @@
         [(i, j) for i in range(PTS) for j in range(PTS)],
         lambda i, j: sofar_ref[i, j],
         lambda d, i, j: weights_ref[d, i, j],
-        jnp.zeros((ny, width), F32),
+        1,
     )
     for q in range(2):
-        sums_ref[q] = sums[q] + load_sums_ref[q]
-        sums_ref[2 + q] = sums[4 + q]
-        sums[2 + q] = sums[2 + q] + load_sums_ref[2 + q]
+        sums[q] = sums[q] + load_sums_ref[2 + q]
     base = PTS * ny
     changes = []
     for t in range(2):
@@ -512,8 +510,8 @@
             edge_ref[...] = jnp.concatenate([zero, own[1], zero, own[3]] + [zero] * 4, axis=0)
     changes = jnp.concatenate(changes, axis=0)
     for ref in (to_outer_ref, to_inner_ref):
-        for n, k in enumerate((2, 3, 6, 7)):
-            ref[base + n * ny : base + (n + 1) * ny] = sums[k]
+        for n in range(4):
+            ref[base + n * ny : base + (n + 1) * ny] = sums[n]
         ref[base + 4 * ny : base + 4 * ny + PTS] = changes
 
 
@@ -530,32 +528,21 @@
     return smooth + [-float(HAT[j, q]) * along_z for q in range(2)]
 
 
-def restricted(points, value, weight, zero):
-    sums = [zero] * 8
-    along_x = {}
-    along_y = {}
-    along_z = {}
+def restricted(points, value, weight, p):
+    along_x, along_z, along_y = {}, {}, {}
     for i, j in points:
         v = value(i, j)
         along_x[j] = along_x.get(j, 0.0) + weight(0, i, j) * v
-        along_y[i] = along_y.get(i, 0.0) + weight(1, i, j) * v
-        product = weight(2, i, j) * v
-        for q in range(2):
-            if HAT[j, q]:
-                along_z[i, q] = along_z.get((i, q), 0.0) + float(HAT[j, q]) * product
-    x_sums = [
-        sum(float(HAT[j, q]) * total for j, total in along_x.items() if HAT[j, q]) for q in range(2)
-    ]
-    y_sums = [
-        sum(float(HAT[i, p]) * total for i, total in along_y.items() if HAT[i, p]) for p in range(2)
-    ]
-    for p in range(2):
-        for q in range(2):
-            sums[2 * p + q] = -(SLOPE[p] * x_sums[q] + SLOPE[q] * y_sums[p])
-            sums[4 + 2 * p + q] = -sum(
-                float(HAT[i, p]) * total for (i, r), total in along_z.items() if r == q and HAT[i, p]
-            )
-    return sums
+        if HAT[i, p]:
+            along_y[i] = along_y.get(i, 0.0) + weight(1, i, j) * v
+            along_z[j] = along_z.get(j, 0.0) + float(HAT[i, p]) * (weight(2, i, j) * v)
+    y_sum = sum(float(HAT[i, p]) * total for i, total in along_y.items())
+    smooth, slope = [], []
+    for q in range(2):
+        x_sum = sum(float(HAT[j, q]) * total for j, total in along_x.items() if HAT[j, q])
+        smooth.append(-(SLOPE[p] * x_sum + SLOPE[q] * y_sum))
+        slope.append(-sum(float(HAT[j, q]) * total for j, total in along_z.items() if HAT[j, q]))
+    return smooth + slope
 
 
 def x_corrections(even, gface_ref, outer_ref, inner_ref):
@@ -622,7 +609,8 @@
 
 
 def behind_kernel(
-    side_ref, sent_outer_ref, sent_inner_ref, gface_ref, back_ref, outer_ref, inner_ref,
+    side_ref, sent_outer_ref, sent_inner_ref, gface_ref, back_ref, sofar_ref, weights_ref, load_sums_ref,
+    outer_ref, inner_ref,
     own_ref,
 ):
     ny, width = gface_ref.shape[2:]
@@ -642,12 +630,20 @@
         contract(D.T, [p * spread[0] for p in points], -1),
         [column[j * ny : (j + 1) * ny] for j in range(PTS)],
     ]
+    sums = restricted(
+        [(i, j) for i in range(PTS) for j in range(PTS)],
+        lambda i, j: sofar_ref[i, j],
+        lambda d, i, j: weights_ref[d, i, j],
+        0,
+    )
     for q in range(2):
-        own_ref[q], own_ref[2 + q] = face_change(change, weight, PTS - 1, 1, q)
+        smooth, slope = face_change(change, weight, PTS - 1, 1, q)
+        own_ref[q] = sums[q] + load_sums_ref[q] + smooth
+        own_ref[2 + q] = sums[2 + q] + slope
 
 
 def coarse_kernel(
-    side_ref, gface_ref, sums_ref, own_ref, edge_in_ref, weights_ref, restrict_ref, outer_ref, inner_ref,
+    side_ref, gface_ref, own_ref, edge_in_ref, weights_ref, restrict_ref, outer_ref, inner_ref,
     plane_ref, edge_ref,
 ):
     ny, width = gface_ref.shape[2:]
@@ -657,16 +653,14 @@
         list(change),
         lambda i, j: change[i, j],
         lambda d, i, j: weights_ref[d, i, j],
-        jnp.zeros((ny, width), F32),
+        0,
     )
     base = PTS * ny
 
     def before(at, count):
         return pick(even, outer_ref, inner_ref, at, count)
 
-    total = [
-        sums[(0, 1, 4, 5)[n]] + sums_ref[n] + own_ref[n] + before(base + n * ny, ny) for n in range(4)
-    ]
+    total = [sums[n] + own_ref[n] + before(base + n * ny, ny) for n in range(4)]
     extra = before(base + 4 * ny, PTS) + edge_in_ref[...]
     smooth = jnp.concatenate(total[:2] + [extra], axis=0)
     slope = jnp.concatenate(total[2:] + [pltpu.roll(extra, PTS - 2, 0)], axis=0)
@@ -691,10 +685,10 @@
         list(change),
         lambda i, j: change[i, j],
         lambda d, i, j: weights_ref[d, i, j],
-        jnp.zeros((ny, width), F32),
-    )
-    smooth = jnp.concatenate([sums[0], sums[1]], axis=0)
-    slope = jnp.concatenate([sums[4], sums[5]], axis=0)
+        0,
+    )
+    smooth = jnp.concatenate(sums[:2], axis=0)
+    slope = jnp.concatenate(sums[2:], axis=0)
     corners = to_vertices(smooth, slope, restrict_ref[...])
     lower, upper = corners[:ny], corners[ny:]
     row = lax.broadcasted_iota(jnp.int32, lower.shape, 0)
@@ -830,9 +824,9 @@
         fields, mob, spread, grad, back, below, above,
     )
     rows = ((PTS + 4) * ny + PTS, width)
-    sent_outer, sent_inner, yface, gface, sofar, sums, edge = call(
+    sent_outer, sent_inner, yface, gface, sofar, edge = call(
         faces_kernel,
-        [rows, rows, (2, 1, PTS, width), faces, field, (4, ny, width), (PTS, width)],
+        [rows, rows, (2, 1, PTS, width), faces, field, (PTS, width)],
         [((2 * PTS + 4) * ny, width), field],
         side, rough, value, out, pair, mob, spread, grad, back, below, above,
         partial, gain, weights, load_sums, edge_weights, outer, inner,
@@ -848,7 +842,7 @@
         behind_kernel,
         [(4, ny, width)],
         [],
-        side, sent_outer, sent_inner, gface, back, still_outer, still_inner,
+        side, sent_outer, sent_inner, gface, back, sofar, weights, load_sums, still_outer, still_inner,
     )
     onward, top = two_on(onward, top)
     below, above = from_y(yface)
@@ -856,7 +850,7 @@
         coarse_kernel,
         [(ny, 128), (3, 128)],
         [],
-        side, gface, sums, own, edge, weights, restrict, outer, inner,
+        side, gface, own, edge, weights, restrict, outer, inner,
     )
     (own_rows,) = call(
         beside_kernel, [(ny, 128)], [], own_rows, gain, gface, weights, restrict, below, above

time: 25.7 us -> 25.7 us (level)
  no operation moved by 1% of the time
where the time goes in v10:
time: 25.7 us; the launch traced here: 25.5 us
  starting transfers between devices  15.4 us (60%)
  Pallas kernels  5.37 us (21%)
  waiting for transfers between devices  3.97 us (15%)
  between operations  0.74 us (3%)
    ppermute x3, starting transfers between devices, to_x(): outer = lax.ppermute(outer, 'dom', outer_pairs(size))  8.69 us
    ppermute x3, starting transfers between devices, from_y(): up = lax.ppermute(faces, 'sub', [(i, (i + 1) % size) for i in range(size)])  5.89 us
    pallas_call x12, Pallas kernels, call(): pl.pallas_call(body, out_shape=[jax.ShapeDtypeStruct(s, F32) if isinstanc...  5.37 us
    ppermute x3, waiting for transfers between devices, to_x(): outer = lax.ppermute(outer, 'dom', outer_pairs(size))  1.33 us
    ppermute x3, waiting for transfers between devices, from_y(): up = lax.ppermute(faces, 'sub', [(i, (i + 1) % size) for i in range(size)])  1.13 us
    ppermute x1, waiting for transfers between devices, two_on(): return (rows, lax.ppermute(top, ('dom', 'sub'), pairs))  1.09 us
    ppermute x1, starting transfers between devices, two_on(): return (rows, lax.ppermute(top, ('dom', 'sub'), pairs))  0.85 us
  transfers between devices with their start and end apart: 11, of which 5 were waited for; matrix products, arithmetic and copies ran while one was open for 0% of the time, Pallas kernels for 14%

profile of v10, /device:TPU:0, one launch (start us, length us, event | category | flops | bytes accessed | tf_op | source)
XLA Modules:
  0.0 25.5 jit_solution(9452042406986612964)
XLA Ops:
  0.6 0.0 copy-start
  0.6 0.0 copy-start.3
  0.6 1.1 %shard_map.77 = (f32[3,8,128]{2,1,0:T(8,128)S(1)}, f32[2,5,8,128]{3,2,1,0:T(8,128)S(1)}) custom-call(f32[3,8,16]{2,1,0:T(8,128)} %bitcast.12, f32[8,64,128]{2,1,0:T(8,128)} %bitcast.6, f32[8,64,128]{2,1,0:T(8,128)} %bitcast.10), custom_call_target="tpu_custom_call" | custom-call | tf_op jit(solution)/shard_map/pallas_call | solution.py:739
  1.8 3.0 %collective-permute-start = (f32[2,5,8,128]{3,2,1,0:T(8,128)S(1)}, f32[2,5,8,128]{3,2,1,0:T(8,128)S(1)}, u32[]{:S(2)}, u32[]{:S(2)}) collective-permute-start(f32[2,5,8,128]{3,2,1,0:T(8,128)S(1)} %get-tuple-element.34), channel_id=1, source_target_pairs={{0,1},{1,0},{2,3},{3,2},{4,5},{5,4},{6,7},{7,6},{8,9},{9,8},{10,11... | collective-permute-start | bytes 122888 | tf_op jit(solution)/shard_map/ppermute | solution.py:751
  4.8 0.0 copy-done
  4.8 0.0 copy-done.3
  4.8 0.0 copy-start.4
  4.8 0.8 %shard_map.78 = (f32[2,8,8,8,128]{4,3,2,1,0:T(8,128)S(1)}, f32[2,2,8,8,128]{4,3,2,1,0:T(8,128)S(1)}, f32[2,2,8,128]{3,2,1,0:T(8,128)S(1)}, f32[144,128]{1,0:T(8,...) custom-call(s32[1]{0:T(128)} %bitcast.side_ref, ...), custom_call_target="tpu_custom_call" | custom-call | tf_op jit(solution)/shard_map/pallas_call | solution.py:739
  5.7 0.0 copy-start.2
  5.7 1.1 %collective-permute-done.below_ref.above_ref = f32[2,5,8,128]{3,2,1,0:T(8,128)S(1)} collective-permute-done((f32[2,5,8,128]{3,2,1,0:T(8,128)S(1)}, f32[2,5,8,128]{3,2,1,0:T(8,128)S(1)}, u32[]{:S(2)}, u32[]{:S(2)}) %collective-permute-start) | collective-permute-done | bytes 40992 | tf_op jit(solution)/shard_map/ppermute | solution.py:751
  6.8 3.4 %collective-permute-start.1 = (f32[144,128]{1,0:T(8,128)S(1)}, f32[144,128]{1,0:T(8,128)S(1)}, u32[]{:S(2)}, u32[]{:S(2)}) collective-permute-start(f32[144,128]{1,0:T(8,128)S(1)} %get-tuple-element.46), channel_id=1, source_target_pairs={{0,30},{2,4},{4,2},{6,8},{8,6},{10,12},{12,10},{14,16},{16,14},{18... | collective-permute-start | bytes 221192 | tf_op jit(solution)/shard_map/ppermute | solution.py:767
  10.2 0.0 collective-permute-start.2
  10.2 1.9 %collective-permute-start.6 = (f32[144,128]{1,0:T(8,128)S(1)}, f32[144,128]{1,0:T(8,128)S(1)}, u32[]{:S(2)}, u32[]{:S(2)}) collective-permute-start(f32[144,128]{1,0:T(8,128)S(1)} %get-tuple-element.54), channel_id=1, source_target_pairs={{0,30},{2,4},{4,2},{6,8},{8,6},{10,12},{12,10},{14,16},{16,14},{18... | collective-permute-start | bytes 221192 | tf_op jit(solution)/shard_map/ppermute | solution.py:767
  12.1 0.0 collective-permute-start.7
  12.1 0.0 copy-done.4
  12.1 0.0 copy-done.2
  12.1 0.8 %shard_map.79 = (f32[2,2,8,8,128]{4,3,2,1,0:T(8,128)S(1)}, f32[8,8,8,128]{3,2,1,0:T(8,128)S(1)}, f32[8,8,8,128]{3,2,1,0:T(8,128)S(1)}, f32[8,8,8,128]{3,2,1,0:T(...) custom-call(f32[2,8,8,8,128]{4,3,2,1,0:T(8,128)S(1)} %get-tuple-element.33., ...), custom_call_target="tpu_custom_call" | custom-call | tf_op jit(solution)/shard_map/pallas_call | solution.py:739
  13.0 0.4 %collective-permute-done.1.outer_ref = f32[144,128]{1,0:T(8,128)S(1)} collective-permute-done((f32[144,128]{1,0:T(8,128)S(1)}, f32[144,128]{1,0:T(8,128)S(1)}, u32[]{:S(2)}, u32[]{:S(2)}) %collective-permute-start.1) | collective-permute-done | bytes 73760 | tf_op jit(solution)/shard_map/ppermute | solution.py:767
  13.4 0.0 collective-permute-done.2.inner_ref
  13.4 0.0 copy-start.1
  13.4 0.5 %shard_map.81 = (f32[104,128]{1,0:T(8,128)S(1)}, f32[104,128]{1,0:T(8,128)S(1)}, f32[2,1,8,128]{3,2,1,0:T(8,128)S(1)}, f32[2,8,8,128]{3,2,1,0:T(8,128)S(1)}, f32...) custom-call(s32[1]{0:T(128)} %bitcast.side_ref, f32[2,2,8,8,128]{4,3,2,1,0:T(8,128)S(1)} %get-tuple-element.35.rough_ref, ...), custom_call_target="tpu_custom_call" | custom-call | tf_op jit(solution)/shard_map/pallas_call | solution.py:739
  13.9 3.4 %collective-permute-start.3 = (f32[104,128]{1,0:T(8,128)S(1)}, f32[104,128]{1,0:T(8,128)S(1)}, u32[]{:S(2)}, u32[]{:S(2)}) collective-permute-start(f32[104,128]{1,0:T(8,128)S(1)} %get-tuple-element.50.sent_outer_ref), channel_id=1, source_target_pairs={{0,30},{2,4},{4,2},{6,8},{8,6},{10,12},{12,10},{14,16},{16,14},{18... | collective-permute-start | bytes 159752 | tf_op jit(solution)/shard_map/ppermute | solution.py:767
  17.3 0.0 collective-permute-start.5
  17.3 0.0 collective-permute-done.6.outer_ref
  17.3 0.0 collective-permute-done.7.inner_ref
  17.3 0.0 copy-done.1
  17.3 0.2 shard_map.86
  17.4 0.0 collective-permute-start.8
  17.4 0.8 %collective-permute-start.9 = (f32[24,128]{1,0:T(8,128)S(1)}, f32[24,128]{1,0:T(8,128)S(1)}, u32[]{:S(2)}, u32[]{:S(2)}) collective-permute-start(f32[24,128]{1,0:T(8,128)S(1)} %get-tuple-element.59), channel_id=1, source_target_pairs={{0,5},{1,4},{2,7},{3,6},{4,9},{5,8},{6,11},{7,10},{8,13},{9,12},{1... | collective-permute-start | bytes 36872 | tf_op jit(solution)/shard_map/ppermute | solution.py:778
  18.3 0.8 %collective-permute-start.4 = (f32[2,1,8,128]{3,2,1,0:T(8,128)S(1)}, f32[2,1,8,128]{3,2,1,0:T(8,128)S(1)}, u32[]{:S(2)}, u32[]{:S(2)}) collective-permute-start(f32[2,1,8,128]{3,2,1,0:T(8,128)S(1)} %get-tuple-element.51), channel_id=1, source_target_pairs={{0,1},{1,0},{2,3},{3,2},{4,5},{5,4},{6,7},{7,6},{8,9},{9,8},{10,11... | collective-permute-start | bytes 24584 | tf_op jit(solution)/shard_map/ppermute | solution.py:751
  19.1 0.2 shard_map.83.own_ref
  19.2 0.9 %collective-permute-done.3.outer_ref = f32[104,128]{1,0:T(8,128)S(1)} collective-permute-done((f32[104,128]{1,0:T(8,128)S(1)}, f32[104,128]{1,0:T(8,128)S(1)}, u32[]{:S(2)}, u32[]{:S(2)}) %collective-permute-start.3) | collective-permute-done | bytes 53280 | tf_op jit(solution)/shard_map/ppermute | solution.py:767
  20.2 0.0 collective-permute-done.5.inner_ref
  20.2 0.2 shard_map.84
  20.4 2.1 %collective-permute-start.10 = (f32[3,128]{1,0:T(4,128)S(1)}, f32[3,128]{1,0:T(4,128)S(1)}, u32[]{:S(2)}, u32[]{:S(2)}) collective-permute-start(f32[3,128]{1,0:T(4,128)S(1)} %get-tuple-element.61), channel_id=1, source_target_pairs={{0,1},{1,0},{2,3},{3,2},{4,5},{5,4},{6,7},{7,6},{8,9},{9,8},{10,11... | collective-permute-start | bytes 4616 | tf_op jit(solution)/shard_map/ppermute | solution.py:751
  22.5 0.0 collective-permute-done.4.below_ref.above_ref
  22.5 0.8 %shard_map.82 = (f32[8,64,128]{2,1,0:T(8,128)}, f32[1,128]{1,0:T(1,128)S(1)}) custom-call(s32[1]{0:T(128)} %bitcast.side_ref, f32[8,8,8,128]{3,2,1,0:T(8,128)S(1)} %get-tuple-element.48.sofar_ref, f32[8,8,8,128]{3,2,1,0:T(8,128)S(1)} %get-tuple-element.40.gain_ref, f32[2,8,8,128]{3,2,1,0:T(8,128)S(1)} %get-tuple-element.49.gface_ref, ...), custom_call_target="tpu_custom_call" | custom-call | tf_op jit(solution)/shard_map/pallas_call | solution.py:739
  23.2 0.2 shard_map.85.own_ref
  23.4 0.4 %collective-permute-done.8.next_ref = f32[24,128]{1,0:T(8,128)S(1)} collective-permute-done((f32[24,128]{1,0:T(8,128)S(1)}, f32[24,128]{1,0:T(8,128)S(1)}, u32[]{:S(2)}, u32[]{:S(2)}) %collective-permute-start.8) | collective-permute-done | bytes 12320 | tf_op jit(solution)/shard_map/ppermute | solution.py:774
  23.8 1.1 %collective-permute-done.9.top_ref = f32[24,128]{1,0:T(8,128)S(1)} collective-permute-done((f32[24,128]{1,0:T(8,128)S(1)}, f32[24,128]{1,0:T(8,128)S(1)}, u32[]{:S(2)}, u32[]{:S(2)}) %collective-permute-start.9) | collective-permute-done | bytes 12320 | tf_op jit(solution)/shard_map/ppermute | solution.py:778
  24.9 0.0 collective-permute-done.10.below_ref.above_ref
  24.9 0.6 %shard_map.88 = f32[8,17]{1,0:T(8,128)} custom-call(f32[8,128]{1,0:T(8,128)S(1)} %shard_map.87.joined_ref, f32[3,128]{1,0:T(4,128)S(1)} %collective-permute-done.10.below_ref.above_ref, f32[3,128]{1,0:T(4,128)S(1)} %collective-permute-done.10.below_ref.above_ref), custom_call_target="tpu_custom_call" | custom-call | tf_op jit(solution)/shard_map/pallas_call | solution.py:739
  (2 shorter events, 0.0 us)
Async XLA Ops:
  0.6 4.2 %copy-start = (f32[1,8,8,8,128]{4,3,2,1,0:T(8,128)S(1)}, f32[1,8,8,8,128]{4,3,2,1,0:T(8,128)}, u32[]{:S(2)}) copy-start(f32[1,8,8,8,128]{4,3,2,1,0:T(8,128)} %param.7) | copy-start | bytes 786436
  0.6 4.2 %copy-start.3 = (f32[1,8,8,8,128]{4,3,2,1,0:T(8,128)S(1)}, f32[1,8,8,8,128]{4,3,2,1,0:T(8,128)}, u32[]{:S(2)}) copy-start(f32[1,8,8,8,128]{4,3,2,1,0:T(8,128)} %param.6) | copy-start | bytes 786436
  1.8 5.0 %collective-permute-start = (f32[2,5,8,128]{3,2,1,0:T(8,128)S(1)}, f32[2,5,8,128]{3,2,1,0:T(8,128)S(1)}, u32[]{:S(2)}, u32[]{:S(2)}) collective-permute-start(f32[2,5,8,128]{3,2,1,0:T(8,128)S(1)} %get-tuple-element.34), channel_id=1, source_target_pairs={{0,1},{1,0},{2,3},{3,2},{4,5},{5,4},{6,7},{7,6},{8,9},{9,8},{10,11... | collective-permute-start | bytes 122888 | tf_op jit(solution)/shard_map/ppermute | solution.py:751
  4.8 7.3 %copy-start.4 = (bf16[256,256]{1,0:T(8,128)(2,1)S(1)}, bf16[256,256]{1,0:T(8,128)(2,1)}, u32[]{:S(2)}) copy-start(bf16[256,256]{1,0:T(8,128)(2,1)} %constant.25.clone.grad_ref) | copy-start | bytes 393220
  5.7 6.5 %copy-start.2 = (bf16[256,256]{1,0:T(8,128)(2,1)S(1)}, bf16[256,256]{1,0:T(8,128)(2,1)}, u32[]{:S(2)}) copy-start(bf16[256,256]{1,0:T(8,128)(2,1)} %constant.26.clone.back_ref) | copy-start | bytes 393220
  6.8 6.5 %collective-permute-start.1 = (f32[144,128]{1,0:T(8,128)S(1)}, f32[144,128]{1,0:T(8,128)S(1)}, u32[]{:S(2)}, u32[]{:S(2)}) collective-permute-start(f32[144,128]{1,0:T(8,128)S(1)} %get-tuple-element.46), channel_id=1, source_target_pairs={{0,30},{2,4},{4,2},{6,8},{8,6},{10,12},{12,10},{14,16},{16,14},{18... | collective-permute-start | bytes 221192 | tf_op jit(solution)/shard_map/ppermute | solution.py:767
  10.2 3.2 %collective-permute-start.2 = (f32[144,128]{1,0:T(8,128)S(1)}, f32[144,128]{1,0:T(8,128)S(1)}, u32[]{:S(2)}, u32[]{:S(2)}) collective-permute-start(f32[144,128]{1,0:T(8,128)S(1)} %get-tuple-element.47), channel_id=1, source_target_pairs={{0,2},{2,0},{4,6},{6,4},{8,10},{10,8},{12,14},{14,12},{16,18},{18,... | collective-permute-start | bytes 221192 | tf_op jit(solution)/shard_map/ppermute | solution.py:768
  10.2 7.0 %collective-permute-start.6 = (f32[144,128]{1,0:T(8,128)S(1)}, f32[144,128]{1,0:T(8,128)S(1)}, u32[]{:S(2)}, u32[]{:S(2)}) collective-permute-start(f32[144,128]{1,0:T(8,128)S(1)} %get-tuple-element.54), channel_id=1, source_target_pairs={{0,30},{2,4},{4,2},{6,8},{8,6},{10,12},{12,10},{14,16},{16,14},{18... | collective-permute-start | bytes 221192 | tf_op jit(solution)/shard_map/ppermute | solution.py:767
  12.1 5.1 %collective-permute-start.7 = (f32[144,128]{1,0:T(8,128)S(1)}, f32[144,128]{1,0:T(8,128)S(1)}, u32[]{:S(2)}, u32[]{:S(2)}) collective-permute-start(f32[144,128]{1,0:T(8,128)S(1)} %get-tuple-element.55), channel_id=1, source_target_pairs={{0,2},{2,0},{4,6},{6,4},{8,10},{10,8},{12,14},{14,12},{16,18},{18,... | collective-permute-start | bytes 221192 | tf_op jit(solution)/shard_map/ppermute | solution.py:768
  13.4 3.9 %copy-start.1 = (bf16[512,256]{1,0:T(8,128)(2,1)S(1)}, bf16[512,256]{1,0:T(8,128)(2,1)}, u32[]{:S(2)}) copy-start(bf16[512,256]{1,0:T(8,128)(2,1)} %constant.27.clone.restrict_ref) | copy-start | bytes 786436
  13.9 6.3 %collective-permute-start.3 = (f32[104,128]{1,0:T(8,128)S(1)}, f32[104,128]{1,0:T(8,128)S(1)}, u32[]{:S(2)}, u32[]{:S(2)}) collective-permute-start(f32[104,128]{1,0:T(8,128)S(1)} %get-tuple-element.50.sent_outer_ref), channel_id=1, source_target_pairs={{0,30},{2,4},{4,2},{6,8},{8,6},{10,12},{12,10},{14,16},{16,14},{18... | collective-permute-start | bytes 159752 | tf_op jit(solution)/shard_map/ppermute | solution.py:767
  17.3 2.9 %collective-permute-start.5 = (f32[104,128]{1,0:T(8,128)S(1)}, f32[104,128]{1,0:T(8,128)S(1)}, u32[]{:S(2)}, u32[]{:S(2)}) collective-permute-start(f32[104,128]{1,0:T(8,128)S(1)} %get-tuple-element.52.sent_inner_ref), channel_id=1, source_target_pairs={{0,2},{2,0},{4,6},{6,4},{8,10},{10,8},{12,14},{14,12},{16,18},{18,... | collective-permute-start | bytes 159752 | tf_op jit(solution)/shard_map/ppermute | solution.py:768
  17.4 6.4 %collective-permute-start.8 = (f32[24,128]{1,0:T(8,128)S(1)}, f32[24,128]{1,0:T(8,128)S(1)}, u32[]{:S(2)}, u32[]{:S(2)}) collective-permute-start(f32[24,128]{1,0:T(8,128)S(1)} %get-tuple-element.58), channel_id=1, source_target_pairs={{0,4},{2,6},{4,8},{6,10},{8,12},{10,14},{12,16},{14,18},{16,20},{1... | collective-permute-start | bytes 36872 | tf_op jit(solution)/shard_map/ppermute | solution.py:774
  17.4 7.5 %collective-permute-start.9 = (f32[24,128]{1,0:T(8,128)S(1)}, f32[24,128]{1,0:T(8,128)S(1)}, u32[]{:S(2)}, u32[]{:S(2)}) collective-permute-start(f32[24,128]{1,0:T(8,128)S(1)} %get-tuple-element.59), channel_id=1, source_target_pairs={{0,5},{1,4},{2,7},{3,6},{4,9},{5,8},{6,11},{7,10},{8,13},{9,12},{1... | collective-permute-start | bytes 36872 | tf_op jit(solution)/shard_map/ppermute | solution.py:778
  18.3 4.2 %collective-permute-start.4 = (f32[2,1,8,128]{3,2,1,0:T(8,128)S(1)}, f32[2,1,8,128]{3,2,1,0:T(8,128)S(1)}, u32[]{:S(2)}, u32[]{:S(2)}) collective-permute-start(f32[2,1,8,128]{3,2,1,0:T(8,128)S(1)} %get-tuple-element.51), channel_id=1, source_target_pairs={{0,1},{1,0},{2,3},{3,2},{4,5},{5,4},{6,7},{7,6},{8,9},{9,8},{10,11... | collective-permute-start | bytes 24584 | tf_op jit(solution)/shard_map/ppermute | solution.py:751
  20.4 4.6 %collective-permute-start.10 = (f32[3,128]{1,0:T(4,128)S(1)}, f32[3,128]{1,0:T(4,128)S(1)}, u32[]{:S(2)}, u32[]{:S(2)}) collective-permute-start(f32[3,128]{1,0:T(4,128)S(1)} %get-tuple-element.61), channel_id=1, source_target_pairs={{0,1},{1,0},{2,3},{3,2},{4,5},{5,4},{6,7},{7,6},{8,9},{9,8},{10,11... | collective-permute-start | bytes 4616 | tf_op jit(solution)/shard_map/ppermute | solution.py:751

commit v11 on v10

--- a/solution.py
+++ b/solution.py
@@ -605,7 +605,7 @@
     row = lax.broadcasted_iota(jnp.int32, lower.shape, 0)
     rows = lower + jnp.where(row == 0, 0.0, pltpu.roll(upper, 1, 0))
     next_ref[...] = jnp.concatenate([rows] * (next_ref.shape[0] // ny), axis=0)
-    top_ref[...] = jnp.broadcast_to(upper[ny - 1 : ny], top_ref.shape)
+    top_ref[...] = jnp.concatenate([upper[ny - 1 : ny]] * (top_ref.shape[1] // 128), axis=1)
 
 
 def behind_kernel(
@@ -719,16 +719,11 @@
     copy.wait()
 
 
-def join_kernel(own_ref, next_ref, top_ref, token_ref, joined_ref):
-    row = lax.broadcasted_iota(jnp.int32, joined_ref.shape, 0)
-    total = own_ref[...] + next_ref[: row.shape[0]] + token_ref[...]
-    joined_ref[...] = total + jnp.where(row == 0, top_ref[0:1], 0.0)
-
-
-def last_kernel(joined_ref, below_ref, above_ref, coarse_ref):
-    total = joined_ref[...]
-    ny = total.shape[0]
-    row = lax.broadcasted_iota(jnp.int32, total.shape, 0)
+def last_kernel(own_ref, next_ref, top_ref, token_ref, below_ref, above_ref, coarse_ref):
+    ny = own_ref.shape[0]
+    row = lax.broadcasted_iota(jnp.int32, own_ref.shape, 0)
+    total = own_ref[...] + next_ref[:ny] + token_ref[...]
+    total = total + jnp.where(row == 0, top_ref[:, :128], 0.0)
     total = total + jnp.where(row == 0, below_ref[0:1], jnp.where(row == 1, below_ref[1:2], 0.0))
     total = total + jnp.where(row == ny - 1, above_ref[2:3], 0.0)
     coarse_ref[...] = total[:, : coarse_ref.shape[1]]
@@ -834,7 +829,7 @@
     outer, inner = to_x(sent_outer, sent_inner)
     onward, top = call(
         ahead_kernel,
-        [(3 * ny, 128), (3 * PTS, 128)],
+        [(3 * ny, 128), (1, (2 * PTS + 1) * 128)],
         [],
         side, sent_outer, sent_inner, gface, restrict, still_outer, still_inner,
     )
@@ -862,9 +857,8 @@
         side, sofar, gain, gface, outer, below, above, inner,
         out_spaces=[pltpu.HBM, pltpu.VMEM],
     )
-    (onward,) = call(join_kernel, [(ny, 128)], [], own_rows, onward, top, token)
     row_below, row_above = from_y(tops)
-    (coarse,) = call(last_kernel, [(ny, width // PTS + 1)], [], onward, row_below, row_above)
+    (coarse,) = call(last_kernel, [(ny, width // PTS + 1)], [], own_rows, onward, top, token, row_below, row_above)
     return pressure.reshape(element_load.shape), coarse[None]
 
 

time: 25.7 us -> 25.6 us (level)
    ppermute x1, waiting for transfers between devices: 0.42 us -> 0.01 us  [two_on(): rows = lax.ppermute(rows, 'dom', [(i, (i + 2) % size) for i in range(size)])]
    ppermute x1, waiting for transfers between devices: 1.09 us -> 1.47 us  [two_on(): return (rows, lax.ppermute(top, ('dom', 'sub'), pairs))]
    pallas_call x12 -> x11, Pallas kernels: 5.37 us -> 5.37 us  [call(): pl.pallas_call(body, out_shape=[jax.ShapeDtypeStruct(s, F32) if isinstanc...]
  transfers between devices with their start and end apart: 11 -> 11, of which waited for: 5 -> 4; matrix products, arithmetic and copies ran while one was open for 0% -> 0% of each run, Pallas kernels for 14% -> 14%
where the time goes in v11:
time: 25.6 us; the launch traced here: 25.5 us
  starting transfers between devices  15.5 us (61%)
  Pallas kernels  5.37 us (21%)
  waiting for transfers between devices  3.91 us (15%)
  between operations  0.74 us (3%)
    ppermute x3, starting transfers between devices, to_x(): outer = lax.ppermute(outer, 'dom', outer_pairs(size))  8.69 us
    ppermute x3, starting transfers between devices, from_y(): up = lax.ppermute(faces, 'sub', [(i, (i + 1) % size) for i in range(size)])  5.92 us
    pallas_call x11, Pallas kernels, call(): pl.pallas_call(body, out_shape=[jax.ShapeDtypeStruct(s, F32) if isinstanc...  5.37 us
    ppermute x1, waiting for transfers between devices, two_on(): return (rows, lax.ppermute(top, ('dom', 'sub'), pairs))  1.47 us
    ppermute x3, waiting for transfers between devices, to_x(): outer = lax.ppermute(outer, 'dom', outer_pairs(size))  1.3 us
    ppermute x3, waiting for transfers between devices, from_y(): up = lax.ppermute(faces, 'sub', [(i, (i + 1) % size) for i in range(size)])  1.13 us
    ppermute x1, starting transfers between devices, two_on(): return (rows, lax.ppermute(top, ('dom', 'sub'), pairs))  0.85 us
  transfers between devices with their start and end apart: 11, of which 4 were waited for; matrix products, arithmetic and copies ran while one was open for 0% of the time, Pallas kernels for 14%

profile of v11, /device:TPU:0, one launch (start us, length us, event | category | flops | bytes accessed | tf_op | source)
XLA Modules:
  0.0 25.5 jit_solution(307871279801383713)
XLA Ops:
  0.6 0.0 copy-start
  0.6 0.0 copy-start.3
  0.6 1.1 %shard_map.77 = (f32[3,8,128]{2,1,0:T(8,128)S(1)}, f32[2,5,8,128]{3,2,1,0:T(8,128)S(1)}) custom-call(f32[3,8,16]{2,1,0:T(8,128)} %bitcast.12, f32[8,64,128]{2,1,0:T(8,128)} %bitcast.6, f32[8,64,128]{2,1,0:T(8,128)} %bitcast.10), custom_call_target="tpu_custom_call" | custom-call | tf_op jit(solution)/shard_map/pallas_call | solution.py:734
  1.8 3.0 %collective-permute-start = (f32[2,5,8,128]{3,2,1,0:T(8,128)S(1)}, f32[2,5,8,128]{3,2,1,0:T(8,128)S(1)}, u32[]{:S(2)}, u32[]{:S(2)}) collective-permute-start(f32[2,5,8,128]{3,2,1,0:T(8,128)S(1)} %get-tuple-element.34), channel_id=1, source_target_pairs={{0,1},{1,0},{2,3},{3,2},{4,5},{5,4},{6,7},{7,6},{8,9},{9,8},{10,11... | collective-permute-start | bytes 122888 | tf_op jit(solution)/shard_map/ppermute | solution.py:746
  4.8 0.0 copy-done
  4.8 0.0 copy-done.3
  4.8 0.0 copy-start.4
  4.8 0.8 %shard_map.78 = (f32[2,8,8,8,128]{4,3,2,1,0:T(8,128)S(1)}, f32[2,2,8,8,128]{4,3,2,1,0:T(8,128)S(1)}, f32[2,2,8,128]{3,2,1,0:T(8,128)S(1)}, f32[144,128]{1,0:T(8,...) custom-call(s32[1]{0:T(128)} %bitcast.side_ref, ...), custom_call_target="tpu_custom_call" | custom-call | tf_op jit(solution)/shard_map/pallas_call | solution.py:734
  5.7 0.0 copy-start.2
  5.7 1.1 %collective-permute-done.below_ref.above_ref = f32[2,5,8,128]{3,2,1,0:T(8,128)S(1)} collective-permute-done((f32[2,5,8,128]{3,2,1,0:T(8,128)S(1)}, f32[2,5,8,128]{3,2,1,0:T(8,128)S(1)}, u32[]{:S(2)}, u32[]{:S(2)}) %collective-permute-start) | collective-permute-done | bytes 40992 | tf_op jit(solution)/shard_map/ppermute | solution.py:746
  6.8 3.4 %collective-permute-start.1 = (f32[144,128]{1,0:T(8,128)S(1)}, f32[144,128]{1,0:T(8,128)S(1)}, u32[]{:S(2)}, u32[]{:S(2)}) collective-permute-start(f32[144,128]{1,0:T(8,128)S(1)} %get-tuple-element.46), channel_id=1, source_target_pairs={{0,30},{2,4},{4,2},{6,8},{8,6},{10,12},{12,10},{14,16},{16,14},{18... | collective-permute-start | bytes 221192 | tf_op jit(solution)/shard_map/ppermute | solution.py:762
  10.2 0.0 collective-permute-start.2
  10.2 1.9 %collective-permute-start.6 = (f32[144,128]{1,0:T(8,128)S(1)}, f32[144,128]{1,0:T(8,128)S(1)}, u32[]{:S(2)}, u32[]{:S(2)}) collective-permute-start(f32[144,128]{1,0:T(8,128)S(1)} %get-tuple-element.54), channel_id=1, source_target_pairs={{0,30},{2,4},{4,2},{6,8},{8,6},{10,12},{12,10},{14,16},{16,14},{18... | collective-permute-start | bytes 221192 | tf_op jit(solution)/shard_map/ppermute | solution.py:762
  12.1 0.0 collective-permute-start.7
  12.1 0.0 copy-done.4
  12.1 0.0 copy-done.2
  12.1 0.8 %shard_map.79 = (f32[2,2,8,8,128]{4,3,2,1,0:T(8,128)S(1)}, f32[8,8,8,128]{3,2,1,0:T(8,128)S(1)}, f32[8,8,8,128]{3,2,1,0:T(8,128)S(1)}, f32[8,8,8,128]{3,2,1,0:T(...) custom-call(f32[2,8,8,8,128]{4,3,2,1,0:T(8,128)S(1)} %get-tuple-element.33., ...), custom_call_target="tpu_custom_call" | custom-call | tf_op jit(solution)/shard_map/pallas_call | solution.py:734
  13.0 0.4 %collective-permute-done.1.outer_ref = f32[144,128]{1,0:T(8,128)S(1)} collective-permute-done((f32[144,128]{1,0:T(8,128)S(1)}, f32[144,128]{1,0:T(8,128)S(1)}, u32[]{:S(2)}, u32[]{:S(2)}) %collective-permute-start.1) | collective-permute-done | bytes 73760 | tf_op jit(solution)/shard_map/ppermute | solution.py:762
  13.4 0.0 collective-permute-done.2.inner_ref
  13.4 0.0 copy-start.1
  13.4 0.5 %shard_map.81 = (f32[104,128]{1,0:T(8,128)S(1)}, f32[104,128]{1,0:T(8,128)S(1)}, f32[2,1,8,128]{3,2,1,0:T(8,128)S(1)}, f32[2,8,8,128]{3,2,1,0:T(8,128)S(1)}, f32...) custom-call(s32[1]{0:T(128)} %bitcast.side_ref, f32[2,2,8,8,128]{4,3,2,1,0:T(8,128)S(1)} %get-tuple-element.35.rough_ref, ...), custom_call_target="tpu_custom_call" | custom-call | tf_op jit(solution)/shard_map/pallas_call | solution.py:734
  13.9 3.4 %collective-permute-start.3 = (f32[104,128]{1,0:T(8,128)S(1)}, f32[104,128]{1,0:T(8,128)S(1)}, u32[]{:S(2)}, u32[]{:S(2)}) collective-permute-start(f32[104,128]{1,0:T(8,128)S(1)} %get-tuple-element.50.sent_outer_ref), channel_id=1, source_target_pairs={{0,30},{2,4},{4,2},{6,8},{8,6},{10,12},{12,10},{14,16},{16,14},{18... | collective-permute-start | bytes 159752 | tf_op jit(solution)/shard_map/ppermute | solution.py:762
  17.3 0.0 collective-permute-start.5
  17.3 0.0 collective-permute-done.6.outer_ref
  17.3 0.0 collective-permute-done.7.inner_ref
  17.3 0.0 copy-done.1
  17.3 0.2 shard_map.86
  17.4 0.0 collective-permute-start.8
  17.5 0.8 %collective-permute-start.9 = (f32[1,2176]{1,0:T(1,128)S(1)}, f32[1,2176]{1,0:T(1,128)S(1)}, u32[]{:S(2)}, u32[]{:S(2)}) collective-permute-start(f32[1,2176]{1,0:T(1,128)S(1)} %get-tuple-element.59), channel_id=1, source_target_pairs={{0,5},{1,4},{2,7},{3,6},{4,9},{5,8},{6,11},{7,10},{8,13},{9,12},{1... | collective-permute-start | bytes 26120 | tf_op jit(solution)/shard_map/ppermute | solution.py:773
  18.3 0.8 %collective-permute-start.4 = (f32[2,1,8,128]{3,2,1,0:T(8,128)S(1)}, f32[2,1,8,128]{3,2,1,0:T(8,128)S(1)}, u32[]{:S(2)}, u32[]{:S(2)}) collective-permute-start(f32[2,1,8,128]{3,2,1,0:T(8,128)S(1)} %get-tuple-element.51), channel_id=1, source_target_pairs={{0,1},{1,0},{2,3},{3,2},{4,5},{5,4},{6,7},{7,6},{8,9},{9,8},{10,11... | collective-permute-start | bytes 24584 | tf_op jit(solution)/shard_map/ppermute | solution.py:746
  19.1 0.2 shard_map.83.own_ref
  19.3 0.9 %collective-permute-done.3.outer_ref = f32[104,128]{1,0:T(8,128)S(1)} collective-permute-done((f32[104,128]{1,0:T(8,128)S(1)}, f32[104,128]{1,0:T(8,128)S(1)}, u32[]{:S(2)}, u32[]{:S(2)}) %collective-permute-start.3) | collective-permute-done | bytes 53280 | tf_op jit(solution)/shard_map/ppermute | solution.py:762
  20.2 0.0 collective-permute-done.5.inner_ref
  20.2 0.2 shard_map.84
  20.4 2.1 %collective-permute-start.10 = (f32[3,128]{1,0:T(4,128)S(1)}, f32[3,128]{1,0:T(4,128)S(1)}, u32[]{:S(2)}, u32[]{:S(2)}) collective-permute-start(f32[3,128]{1,0:T(4,128)S(1)} %get-tuple-element.61), channel_id=1, source_target_pairs={{0,1},{1,0},{2,3},{3,2},{4,5},{5,4},{6,7},{7,6},{8,9},{9,8},{10,11... | collective-permute-start | bytes 4616 | tf_op jit(solution)/shard_map/ppermute | solution.py:746
  22.5 0.0 collective-permute-done.4.below_ref.above_ref
  22.5 0.8 %shard_map.82 = (f32[8,64,128]{2,1,0:T(8,128)}, f32[1,128]{1,0:T(1,128)S(1)}) custom-call(s32[1]{0:T(128)} %bitcast.side_ref, f32[8,8,8,128]{3,2,1,0:T(8,128)S(1)} %get-tuple-element.48.sofar_ref, f32[8,8,8,128]{3,2,1,0:T(8,128)S(1)} %get-tuple-element.40.gain_ref, f32[2,8,8,128]{3,2,1,0:T(8,128)S(1)} %get-tuple-element.49.gface_ref, ...), custom_call_target="tpu_custom_call" | custom-call | tf_op jit(solution)/shard_map/pallas_call | solution.py:734
  23.2 0.2 shard_map.85.own_ref
  23.4 1.5 %collective-permute-done.9.top_ref = f32[1,2176]{1,0:T(1,128)S(1)} collective-permute-done((f32[1,2176]{1,0:T(1,128)S(1)}, f32[1,2176]{1,0:T(1,128)S(1)}, u32[]{:S(2)}, u32[]{:S(2)}) %collective-permute-start.9) | collective-permute-done | bytes 8736 | tf_op jit(solution)/shard_map/ppermute | solution.py:773
  24.9 0.0 collective-permute-done.8.next_ref
  24.9 0.0 collective-permute-done.10.below_ref.above_ref
  24.9 0.6 %shard_map.87 = f32[8,17]{1,0:T(8,128)} custom-call(f32[8,128]{1,0:T(8,128)S(1)} %shard_map.85.own_ref, f32[24,128]{1,0:T(8,128)S(1)} %collective-permute-done.8.next_ref, f32[1,2176]{1,0:T(1,128)S(1)} %collective-permute-done.9.top_ref, f32[1,128]{1,0:T(1,128)S(1)} %get-tuple-element.60.token_ref, f32[3,128]{1,0:T(4,128)S(1)} %collective-permute-done.10.below_ref.above_ref, ...), custom_call_target="tpu_custom_call" | custom-call | tf_op jit(solution)/shard_map/pallas_call | solution.py:734
  (1 shorter events, 0.0 us)
Async XLA Ops:
  0.6 4.2 %copy-start = (f32[1,8,8,8,128]{4,3,2,1,0:T(8,128)S(1)}, f32[1,8,8,8,128]{4,3,2,1,0:T(8,128)}, u32[]{:S(2)}) copy-start(f32[1,8,8,8,128]{4,3,2,1,0:T(8,128)} %param.7) | copy-start | bytes 786436
  0.6 4.2 %copy-start.3 = (f32[1,8,8,8,128]{4,3,2,1,0:T(8,128)S(1)}, f32[1,8,8,8,128]{4,3,2,1,0:T(8,128)}, u32[]{:S(2)}) copy-start(f32[1,8,8,8,128]{4,3,2,1,0:T(8,128)} %param.6) | copy-start | bytes 786436
  1.8 5.0 %collective-permute-start = (f32[2,5,8,128]{3,2,1,0:T(8,128)S(1)}, f32[2,5,8,128]{3,2,1,0:T(8,128)S(1)}, u32[]{:S(2)}, u32[]{:S(2)}) collective-permute-start(f32[2,5,8,128]{3,2,1,0:T(8,128)S(1)} %get-tuple-element.34), channel_id=1, source_target_pairs={{0,1},{1,0},{2,3},{3,2},{4,5},{5,4},{6,7},{7,6},{8,9},{9,8},{10,11... | collective-permute-start | bytes 122888 | tf_op jit(solution)/shard_map/ppermute | solution.py:746
  4.8 7.3 %copy-start.4 = (bf16[256,256]{1,0:T(8,128)(2,1)S(1)}, bf16[256,256]{1,0:T(8,128)(2,1)}, u32[]{:S(2)}) copy-start(bf16[256,256]{1,0:T(8,128)(2,1)} %constant.25.clone.grad_ref) | copy-start | bytes 393220
  5.7 6.5 %copy-start.2 = (bf16[256,256]{1,0:T(8,128)(2,1)S(1)}, bf16[256,256]{1,0:T(8,128)(2,1)}, u32[]{:S(2)}) copy-start(bf16[256,256]{1,0:T(8,128)(2,1)} %constant.26.clone.back_ref) | copy-start | bytes 393220
  6.8 6.5 %collective-permute-start.1 = (f32[144,128]{1,0:T(8,128)S(1)}, f32[144,128]{1,0:T(8,128)S(1)}, u32[]{:S(2)}, u32[]{:S(2)}) collective-permute-start(f32[144,128]{1,0:T(8,128)S(1)} %get-tuple-element.46), channel_id=1, source_target_pairs={{0,30},{2,4},{4,2},{6,8},{8,6},{10,12},{12,10},{14,16},{16,14},{18... | collective-permute-start | bytes 221192 | tf_op jit(solution)/shard_map/ppermute | solution.py:762
  10.2 3.2 %collective-permute-start.2 = (f32[144,128]{1,0:T(8,128)S(1)}, f32[144,128]{1,0:T(8,128)S(1)}, u32[]{:S(2)}, u32[]{:S(2)}) collective-permute-start(f32[144,128]{1,0:T(8,128)S(1)} %get-tuple-element.47), channel_id=1, source_target_pairs={{0,2},{2,0},{4,6},{6,4},{8,10},{10,8},{12,14},{14,12},{16,18},{18,... | collective-permute-start | bytes 221192 | tf_op jit(solution)/shard_map/ppermute | solution.py:763
  10.2 7.0 %collective-permute-start.6 = (f32[144,128]{1,0:T(8,128)S(1)}, f32[144,128]{1,0:T(8,128)S(1)}, u32[]{:S(2)}, u32[]{:S(2)}) collective-permute-start(f32[144,128]{1,0:T(8,128)S(1)} %get-tuple-element.54), channel_id=1, source_target_pairs={{0,30},{2,4},{4,2},{6,8},{8,6},{10,12},{12,10},{14,16},{16,14},{18... | collective-permute-start | bytes 221192 | tf_op jit(solution)/shard_map/ppermute | solution.py:762
  12.1 5.1 %collective-permute-start.7 = (f32[144,128]{1,0:T(8,128)S(1)}, f32[144,128]{1,0:T(8,128)S(1)}, u32[]{:S(2)}, u32[]{:S(2)}) collective-permute-start(f32[144,128]{1,0:T(8,128)S(1)} %get-tuple-element.55), channel_id=1, source_target_pairs={{0,2},{2,0},{4,6},{6,4},{8,10},{10,8},{12,14},{14,12},{16,18},{18,... | collective-permute-start | bytes 221192 | tf_op jit(solution)/shard_map/ppermute | solution.py:763
  13.4 3.9 %copy-start.1 = (bf16[512,256]{1,0:T(8,128)(2,1)S(1)}, bf16[512,256]{1,0:T(8,128)(2,1)}, u32[]{:S(2)}) copy-start(bf16[512,256]{1,0:T(8,128)(2,1)} %constant.27.clone.restrict_ref) | copy-start | bytes 786436
  13.9 6.3 %collective-permute-start.3 = (f32[104,128]{1,0:T(8,128)S(1)}, f32[104,128]{1,0:T(8,128)S(1)}, u32[]{:S(2)}, u32[]{:S(2)}) collective-permute-start(f32[104,128]{1,0:T(8,128)S(1)} %get-tuple-element.50.sent_outer_ref), channel_id=1, source_target_pairs={{0,30},{2,4},{4,2},{6,8},{8,6},{10,12},{12,10},{14,16},{16,14},{18... | collective-permute-start | bytes 159752 | tf_op jit(solution)/shard_map/ppermute | solution.py:762
  17.3 2.9 %collective-permute-start.5 = (f32[104,128]{1,0:T(8,128)S(1)}, f32[104,128]{1,0:T(8,128)S(1)}, u32[]{:S(2)}, u32[]{:S(2)}) collective-permute-start(f32[104,128]{1,0:T(8,128)S(1)} %get-tuple-element.52.sent_inner_ref), channel_id=1, source_target_pairs={{0,2},{2,0},{4,6},{6,4},{8,10},{10,8},{12,14},{14,12},{16,18},{18,... | collective-permute-start | bytes 159752 | tf_op jit(solution)/shard_map/ppermute | solution.py:763
  17.4 7.4 %collective-permute-start.8 = (f32[24,128]{1,0:T(8,128)S(1)}, f32[24,128]{1,0:T(8,128)S(1)}, u32[]{:S(2)}, u32[]{:S(2)}) collective-permute-start(f32[24,128]{1,0:T(8,128)S(1)} %get-tuple-element.58), channel_id=1, source_target_pairs={{0,4},{2,6},{4,8},{6,10},{8,12},{10,14},{12,16},{14,18},{16,20},{1... | collective-permute-start | bytes 36872 | tf_op jit(solution)/shard_map/ppermute | solution.py:769
  17.5 7.4 %collective-permute-start.9 = (f32[1,2176]{1,0:T(1,128)S(1)}, f32[1,2176]{1,0:T(1,128)S(1)}, u32[]{:S(2)}, u32[]{:S(2)}) collective-permute-start(f32[1,2176]{1,0:T(1,128)S(1)} %get-tuple-element.59), channel_id=1, source_target_pairs={{0,5},{1,4},{2,7},{3,6},{4,9},{5,8},{6,11},{7,10},{8,13},{9,12},{1... | collective-permute-start | bytes 26120 | tf_op jit(solution)/shard_map/ppermute | solution.py:773
  18.3 4.2 %collective-permute-start.4 = (f32[2,1,8,128]{3,2,1,0:T(8,128)S(1)}, f32[2,1,8,128]{3,2,1,0:T(8,128)S(1)}, u32[]{:S(2)}, u32[]{:S(2)}) collective-permute-start(f32[2,1,8,128]{3,2,1,0:T(8,128)S(1)} %get-tuple-element.51), channel_id=1, source_target_pairs={{0,1},{1,0},{2,3},{3,2},{4,5},{5,4},{6,7},{7,6},{8,9},{9,8},{10,11... | collective-permute-start | bytes 24584 | tf_op jit(solution)/shard_map/ppermute | solution.py:746
  20.4 4.5 %collective-permute-start.10 = (f32[3,128]{1,0:T(4,128)S(1)}, f32[3,128]{1,0:T(4,128)S(1)}, u32[]{:S(2)}, u32[]{:S(2)}) collective-permute-start(f32[3,128]{1,0:T(4,128)S(1)} %get-tuple-element.61), channel_id=1, source_target_pairs={{0,1},{1,0},{2,3},{3,2},{4,5},{5,4},{6,7},{7,6},{8,9},{9,8},{10,11... | collective-permute-start | bytes 4616 | tf_op jit(solution)/shard_map/ppermute | solution.py:746

commit v12 on v11

--- a/solution.py
+++ b/solution.py
@@ -374,7 +374,7 @@
 
 
 def first_step(right, diagonal):
-    inverse = 1.0 / diagonal
+    inverse = pl.reciprocal(diagonal)
     scaled = inverse * right
     value = scaled * (1.0 / THETA)
     return value, KEEP * value + GAIN * scaled, GAIN * inverse
@@ -509,10 +509,9 @@
             zero = jnp.zeros_like(own[1])
             edge_ref[...] = jnp.concatenate([zero, own[1], zero, own[3]] + [zero] * 4, axis=0)
     changes = jnp.concatenate(changes, axis=0)
-    for ref in (to_outer_ref, to_inner_ref):
-        for n in range(4):
-            ref[base + n * ny : base + (n + 1) * ny] = sums[n]
-        ref[base + 4 * ny : base + 4 * ny + PTS] = changes
+    rest = jnp.concatenate(sums + [changes], axis=0)
+    to_outer_ref[base:] = rest
+    to_inner_ref[base:] = rest
 
 
 def edge_change(change, weight_ref, j, p):

time: 25.6 us -> 25.6 us (level)
  no operation moved by 1% of the time
where the time goes in v12:
time: 25.6 us; the launch traced here: 25.5 us
  starting transfers between devices  15.5 us (61%)
  Pallas kernels  5.37 us (21%)
  waiting for transfers between devices  3.91 us (15%)
  between operations  0.74 us (3%)
    ppermute x3, starting transfers between devices, to_x(): outer = lax.ppermute(outer, 'dom', outer_pairs(size))  8.69 us
    ppermute x3, starting transfers between devices, from_y(): up = lax.ppermute(faces, 'sub', [(i, (i + 1) % size) for i in range(size)])  5.92 us
    pallas_call x11, Pallas kernels, call(): pl.pallas_call(body, out_shape=[jax.ShapeDtypeStruct(s, F32) if isinstanc...  5.37 us
    ppermute x1, waiting for transfers between devices, two_on(): return (rows, lax.ppermute(top, ('dom', 'sub'), pairs))  1.47 us
    ppermute x3, waiting for transfers between devices, to_x(): outer = lax.ppermute(outer, 'dom', outer_pairs(size))  1.3 us
    ppermute x3, waiting for transfers between devices, from_y(): up = lax.ppermute(faces, 'sub', [(i, (i + 1) % size) for i in range(size)])  1.13 us
    ppermute x1, starting transfers between devices, two_on(): return (rows, lax.ppermute(top, ('dom', 'sub'), pairs))  0.85 us
  transfers between devices with their start and end apart: 11, of which 4 were waited for; matrix products, arithmetic and copies ran while one was open for 0% of the time, Pallas kernels for 14%

profile of v12, /device:TPU:0, one launch (start us, length us, event | category | flops | bytes accessed | tf_op | source)
XLA Modules:
  0.0 25.5 jit_solution(307871279801383713)
XLA Ops:
  0.6 0.0 copy-start
  0.6 0.0 copy-start.3
  0.6 1.1 %shard_map.77 = (f32[3,8,128]{2,1,0:T(8,128)S(1)}, f32[2,5,8,128]{3,2,1,0:T(8,128)S(1)}) custom-call(f32[3,8,16]{2,1,0:T(8,128)} %bitcast.12, f32[8,64,128]{2,1,0:T(8,128)} %bitcast.6, f32[8,64,128]{2,1,0:T(8,128)} %bitcast.10), custom_call_target="tpu_custom_call" | custom-call | tf_op jit(solution)/shard_map/pallas_call | solution.py:733
  1.8 3.0 %collective-permute-start = (f32[2,5,8,128]{3,2,1,0:T(8,128)S(1)}, f32[2,5,8,128]{3,2,1,0:T(8,128)S(1)}, u32[]{:S(2)}, u32[]{:S(2)}) collective-permute-start(f32[2,5,8,128]{3,2,1,0:T(8,128)S(1)} %get-tuple-element.34), channel_id=1, source_target_pairs={{0,1},{1,0},{2,3},{3,2},{4,5},{5,4},{6,7},{7,6},{8,9},{9,8},{10,11... | collective-permute-start | bytes 122888 | tf_op jit(solution)/shard_map/ppermute | solution.py:745
  4.8 0.0 copy-done
  4.8 0.0 copy-done.3
  4.8 0.0 copy-start.4
  4.8 0.8 %shard_map.78 = (f32[2,8,8,8,128]{4,3,2,1,0:T(8,128)S(1)}, f32[2,2,8,8,128]{4,3,2,1,0:T(8,128)S(1)}, f32[2,2,8,128]{3,2,1,0:T(8,128)S(1)}, f32[144,128]{1,0:T(8,...) custom-call(s32[1]{0:T(128)} %bitcast.side_ref, ...), custom_call_target="tpu_custom_call" | custom-call | tf_op jit(solution)/shard_map/pallas_call | solution.py:733
  5.7 0.0 copy-start.2
  5.7 1.1 %collective-permute-done.below_ref.above_ref = f32[2,5,8,128]{3,2,1,0:T(8,128)S(1)} collective-permute-done((f32[2,5,8,128]{3,2,1,0:T(8,128)S(1)}, f32[2,5,8,128]{3,2,1,0:T(8,128)S(1)}, u32[]{:S(2)}, u32[]{:S(2)}) %collective-permute-start) | collective-permute-done | bytes 40992 | tf_op jit(solution)/shard_map/ppermute | solution.py:745
  6.8 3.4 %collective-permute-start.1 = (f32[144,128]{1,0:T(8,128)S(1)}, f32[144,128]{1,0:T(8,128)S(1)}, u32[]{:S(2)}, u32[]{:S(2)}) collective-permute-start(f32[144,128]{1,0:T(8,128)S(1)} %get-tuple-element.46), channel_id=1, source_target_pairs={{0,30},{2,4},{4,2},{6,8},{8,6},{10,12},{12,10},{14,16},{16,14},{18... | collective-permute-start | bytes 221192 | tf_op jit(solution)/shard_map/ppermute | solution.py:761
  10.2 0.0 collective-permute-start.2
  10.2 1.9 %collective-permute-start.6 = (f32[144,128]{1,0:T(8,128)S(1)}, f32[144,128]{1,0:T(8,128)S(1)}, u32[]{:S(2)}, u32[]{:S(2)}) collective-permute-start(f32[144,128]{1,0:T(8,128)S(1)} %get-tuple-element.54), channel_id=1, source_target_pairs={{0,30},{2,4},{4,2},{6,8},{8,6},{10,12},{12,10},{14,16},{16,14},{18... | collective-permute-start | bytes 221192 | tf_op jit(solution)/shard_map/ppermute | solution.py:761
  12.1 0.0 collective-permute-start.7
  12.1 0.0 copy-done.4
  12.1 0.0 copy-done.2
  12.1 0.8 %shard_map.79 = (f32[2,2,8,8,128]{4,3,2,1,0:T(8,128)S(1)}, f32[8,8,8,128]{3,2,1,0:T(8,128)S(1)}, f32[8,8,8,128]{3,2,1,0:T(8,128)S(1)}, f32[8,8,8,128]{3,2,1,0:T(...) custom-call(f32[2,8,8,8,128]{4,3,2,1,0:T(8,128)S(1)} %get-tuple-element.33., ...), custom_call_target="tpu_custom_call" | custom-call | tf_op jit(solution)/shard_map/pallas_call | solution.py:733
  13.0 0.4 %collective-permute-done.1.outer_ref = f32[144,128]{1,0:T(8,128)S(1)} collective-permute-done((f32[144,128]{1,0:T(8,128)S(1)}, f32[144,128]{1,0:T(8,128)S(1)}, u32[]{:S(2)}, u32[]{:S(2)}) %collective-permute-start.1) | collective-permute-done | bytes 73760 | tf_op jit(solution)/shard_map/ppermute | solution.py:761
  13.4 0.0 collective-permute-done.2.inner_ref
  13.4 0.0 copy-start.1
  13.4 0.5 %shard_map.81 = (f32[104,128]{1,0:T(8,128)S(1)}, f32[104,128]{1,0:T(8,128)S(1)}, f32[2,1,8,128]{3,2,1,0:T(8,128)S(1)}, f32[2,8,8,128]{3,2,1,0:T(8,128)S(1)}, f32...) custom-call(s32[1]{0:T(128)} %bitcast.side_ref, f32[2,2,8,8,128]{4,3,2,1,0:T(8,128)S(1)} %get-tuple-element.35.rough_ref, ...), custom_call_target="tpu_custom_call" | custom-call | tf_op jit(solution)/shard_map/pallas_call | solution.py:733
  13.9 3.4 %collective-permute-start.3 = (f32[104,128]{1,0:T(8,128)S(1)}, f32[104,128]{1,0:T(8,128)S(1)}, u32[]{:S(2)}, u32[]{:S(2)}) collective-permute-start(f32[104,128]{1,0:T(8,128)S(1)} %get-tuple-element.50.sent_outer_ref), channel_id=1, source_target_pairs={{0,30},{2,4},{4,2},{6,8},{8,6},{10,12},{12,10},{14,16},{16,14},{18... | collective-permute-start | bytes 159752 | tf_op jit(solution)/shard_map/ppermute | solution.py:761
  17.3 0.0 collective-permute-start.5
  17.3 0.0 collective-permute-done.6.outer_ref
  17.3 0.0 collective-permute-done.7.inner_ref
  17.3 0.0 copy-done.1
  17.3 0.2 shard_map.86
  17.4 0.0 collective-permute-start.8
  17.5 0.8 %collective-permute-start.9 = (f32[1,2176]{1,0:T(1,128)S(1)}, f32[1,2176]{1,0:T(1,128)S(1)}, u32[]{:S(2)}, u32[]{:S(2)}) collective-permute-start(f32[1,2176]{1,0:T(1,128)S(1)} %get-tuple-element.59), channel_id=1, source_target_pairs={{0,5},{1,4},{2,7},{3,6},{4,9},{5,8},{6,11},{7,10},{8,13},{9,12},{1... | collective-permute-start | bytes 26120 | tf_op jit(solution)/shard_map/ppermute | solution.py:772
  18.3 0.8 %collective-permute-start.4 = (f32[2,1,8,128]{3,2,1,0:T(8,128)S(1)}, f32[2,1,8,128]{3,2,1,0:T(8,128)S(1)}, u32[]{:S(2)}, u32[]{:S(2)}) collective-permute-start(f32[2,1,8,128]{3,2,1,0:T(8,128)S(1)} %get-tuple-element.51), channel_id=1, source_target_pairs={{0,1},{1,0},{2,3},{3,2},{4,5},{5,4},{6,7},{7,6},{8,9},{9,8},{10,11... | collective-permute-start | bytes 24584 | tf_op jit(solution)/shard_map/ppermute | solution.py:745
  19.1 0.2 shard_map.83.own_ref
  19.3 0.9 %collective-permute-done.3.outer_ref = f32[104,128]{1,0:T(8,128)S(1)} collective-permute-done((f32[104,128]{1,0:T(8,128)S(1)}, f32[104,128]{1,0:T(8,128)S(1)}, u32[]{:S(2)}, u32[]{:S(2)}) %collective-permute-start.3) | collective-permute-done | bytes 53280 | tf_op jit(solution)/shard_map/ppermute | solution.py:761
  20.2 0.0 collective-permute-done.5.inner_ref
  20.2 0.2 shard_map.84
  20.4 2.1 %collective-permute-start.10 = (f32[3,128]{1,0:T(4,128)S(1)}, f32[3,128]{1,0:T(4,128)S(1)}, u32[]{:S(2)}, u32[]{:S(2)}) collective-permute-start(f32[3,128]{1,0:T(4,128)S(1)} %get-tuple-element.61), channel_id=1, source_target_pairs={{0,1},{1,0},{2,3},{3,2},{4,5},{5,4},{6,7},{7,6},{8,9},{9,8},{10,11... | collective-permute-start | bytes 4616 | tf_op jit(solution)/shard_map/ppermute | solution.py:745
  22.5 0.0 collective-permute-done.4.below_ref.above_ref
  22.5 0.8 %shard_map.82 = (f32[8,64,128]{2,1,0:T(8,128)}, f32[1,128]{1,0:T(1,128)S(1)}) custom-call(s32[1]{0:T(128)} %bitcast.side_ref, f32[8,8,8,128]{3,2,1,0:T(8,128)S(1)} %get-tuple-element.48.sofar_ref, f32[8,8,8,128]{3,2,1,0:T(8,128)S(1)} %get-tuple-element.40.gain_ref, f32[2,8,8,128]{3,2,1,0:T(8,128)S(1)} %get-tuple-element.49.gface_ref, ...), custom_call_target="tpu_custom_call" | custom-call | tf_op jit(solution)/shard_map/pallas_call | solution.py:733
  23.2 0.2 shard_map.85.own_ref
  23.4 1.5 %collective-permute-done.9.top_ref = f32[1,2176]{1,0:T(1,128)S(1)} collective-permute-done((f32[1,2176]{1,0:T(1,128)S(1)}, f32[1,2176]{1,0:T(1,128)S(1)}, u32[]{:S(2)}, u32[]{:S(2)}) %collective-permute-start.9) | collective-permute-done | bytes 8736 | tf_op jit(solution)/shard_map/ppermute | solution.py:772
  24.9 0.0 collective-permute-done.8.next_ref
  24.9 0.0 collective-permute-done.10.below_ref.above_ref
  24.9 0.6 %shard_map.87 = f32[8,17]{1,0:T(8,128)} custom-call(f32[8,128]{1,0:T(8,128)S(1)} %shard_map.85.own_ref, f32[24,128]{1,0:T(8,128)S(1)} %collective-permute-done.8.next_ref, f32[1,2176]{1,0:T(1,128)S(1)} %collective-permute-done.9.top_ref, f32[1,128]{1,0:T(1,128)S(1)} %get-tuple-element.60.token_ref, f32[3,128]{1,0:T(4,128)S(1)} %collective-permute-done.10.below_ref.above_ref, ...), custom_call_target="tpu_custom_call" | custom-call | tf_op jit(solution)/shard_map/pallas_call | solution.py:733
  (1 shorter events, 0.0 us)
Async XLA Ops:
  0.6 4.2 %copy-start = (f32[1,8,8,8,128]{4,3,2,1,0:T(8,128)S(1)}, f32[1,8,8,8,128]{4,3,2,1,0:T(8,128)}, u32[]{:S(2)}) copy-start(f32[1,8,8,8,128]{4,3,2,1,0:T(8,128)} %param.7) | copy-start | bytes 786436
  0.6 4.2 %copy-start.3 = (f32[1,8,8,8,128]{4,3,2,1,0:T(8,128)S(1)}, f32[1,8,8,8,128]{4,3,2,1,0:T(8,128)}, u32[]{:S(2)}) copy-start(f32[1,8,8,8,128]{4,3,2,1,0:T(8,128)} %param.6) | copy-start | bytes 786436
  1.8 5.0 %collective-permute-start = (f32[2,5,8,128]{3,2,1,0:T(8,128)S(1)}, f32[2,5,8,128]{3,2,1,0:T(8,128)S(1)}, u32[]{:S(2)}, u32[]{:S(2)}) collective-permute-start(f32[2,5,8,128]{3,2,1,0:T(8,128)S(1)} %get-tuple-element.34), channel_id=1, source_target_pairs={{0,1},{1,0},{2,3},{3,2},{4,5},{5,4},{6,7},{7,6},{8,9},{9,8},{10,11... | collective-permute-start | bytes 122888 | tf_op jit(solution)/shard_map/ppermute | solution.py:745
  4.8 7.3 %copy-start.4 = (bf16[256,256]{1,0:T(8,128)(2,1)S(1)}, bf16[256,256]{1,0:T(8,128)(2,1)}, u32[]{:S(2)}) copy-start(bf16[256,256]{1,0:T(8,128)(2,1)} %constant.25.clone.grad_ref) | copy-start | bytes 393220
  5.7 6.5 %copy-start.2 = (bf16[256,256]{1,0:T(8,128)(2,1)S(1)}, bf16[256,256]{1,0:T(8,128)(2,1)}, u32[]{:S(2)}) copy-start(bf16[256,256]{1,0:T(8,128)(2,1)} %constant.26.clone.back_ref) | copy-start | bytes 393220
  6.8 6.5 %collective-permute-start.1 = (f32[144,128]{1,0:T(8,128)S(1)}, f32[144,128]{1,0:T(8,128)S(1)}, u32[]{:S(2)}, u32[]{:S(2)}) collective-permute-start(f32[144,128]{1,0:T(8,128)S(1)} %get-tuple-element.46), channel_id=1, source_target_pairs={{0,30},{2,4},{4,2},{6,8},{8,6},{10,12},{12,10},{14,16},{16,14},{18... | collective-permute-start | bytes 221192 | tf_op jit(solution)/shard_map/ppermute | solution.py:761
  10.2 3.2 %collective-permute-start.2 = (f32[144,128]{1,0:T(8,128)S(1)}, f32[144,128]{1,0:T(8,128)S(1)}, u32[]{:S(2)}, u32[]{:S(2)}) collective-permute-start(f32[144,128]{1,0:T(8,128)S(1)} %get-tuple-element.47), channel_id=1, source_target_pairs={{0,2},{2,0},{4,6},{6,4},{8,10},{10,8},{12,14},{14,12},{16,18},{18,... | collective-permute-start | bytes 221192 | tf_op jit(solution)/shard_map/ppermute | solution.py:762
  10.2 7.0 %collective-permute-start.6 = (f32[144,128]{1,0:T(8,128)S(1)}, f32[144,128]{1,0:T(8,128)S(1)}, u32[]{:S(2)}, u32[]{:S(2)}) collective-permute-start(f32[144,128]{1,0:T(8,128)S(1)} %get-tuple-element.54), channel_id=1, source_target_pairs={{0,30},{2,4},{4,2},{6,8},{8,6},{10,12},{12,10},{14,16},{16,14},{18... | collective-permute-start | bytes 221192 | tf_op jit(solution)/shard_map/ppermute | solution.py:761
  12.1 5.1 %collective-permute-start.7 = (f32[144,128]{1,0:T(8,128)S(1)}, f32[144,128]{1,0:T(8,128)S(1)}, u32[]{:S(2)}, u32[]{:S(2)}) collective-permute-start(f32[144,128]{1,0:T(8,128)S(1)} %get-tuple-element.55), channel_id=1, source_target_pairs={{0,2},{2,0},{4,6},{6,4},{8,10},{10,8},{12,14},{14,12},{16,18},{18,... | collective-permute-start | bytes 221192 | tf_op jit(solution)/shard_map/ppermute | solution.py:762
  13.4 3.9 %copy-start.1 = (bf16[512,256]{1,0:T(8,128)(2,1)S(1)}, bf16[512,256]{1,0:T(8,128)(2,1)}, u32[]{:S(2)}) copy-start(bf16[512,256]{1,0:T(8,128)(2,1)} %constant.27.clone.restrict_ref) | copy-start | bytes 786436
  13.9 6.3 %collective-permute-start.3 = (f32[104,128]{1,0:T(8,128)S(1)}, f32[104,128]{1,0:T(8,128)S(1)}, u32[]{:S(2)}, u32[]{:S(2)}) collective-permute-start(f32[104,128]{1,0:T(8,128)S(1)} %get-tuple-element.50.sent_outer_ref), channel_id=1, source_target_pairs={{0,30},{2,4},{4,2},{6,8},{8,6},{10,12},{12,10},{14,16},{16,14},{18... | collective-permute-start | bytes 159752 | tf_op jit(solution)/shard_map/ppermute | solution.py:761
  17.3 2.9 %collective-permute-start.5 = (f32[104,128]{1,0:T(8,128)S(1)}, f32[104,128]{1,0:T(8,128)S(1)}, u32[]{:S(2)}, u32[]{:S(2)}) collective-permute-start(f32[104,128]{1,0:T(8,128)S(1)} %get-tuple-element.52.sent_inner_ref), channel_id=1, source_target_pairs={{0,2},{2,0},{4,6},{6,4},{8,10},{10,8},{12,14},{14,12},{16,18},{18,... | collective-permute-start | bytes 159752 | tf_op jit(solution)/shard_map/ppermute | solution.py:762
  17.4 7.4 %collective-permute-start.8 = (f32[24,128]{1,0:T(8,128)S(1)}, f32[24,128]{1,0:T(8,128)S(1)}, u32[]{:S(2)}, u32[]{:S(2)}) collective-permute-start(f32[24,128]{1,0:T(8,128)S(1)} %get-tuple-element.58), channel_id=1, source_target_pairs={{0,4},{2,6},{4,8},{6,10},{8,12},{10,14},{12,16},{14,18},{16,20},{1... | collective-permute-start | bytes 36872 | tf_op jit(solution)/shard_map/ppermute | solution.py:768
  17.5 7.4 %collective-permute-start.9 = (f32[1,2176]{1,0:T(1,128)S(1)}, f32[1,2176]{1,0:T(1,128)S(1)}, u32[]{:S(2)}, u32[]{:S(2)}) collective-permute-start(f32[1,2176]{1,0:T(1,128)S(1)} %get-tuple-element.59), channel_id=1, source_target_pairs={{0,5},{1,4},{2,7},{3,6},{4,9},{5,8},{6,11},{7,10},{8,13},{9,12},{1... | collective-permute-start | bytes 26120 | tf_op jit(solution)/shard_map/ppermute | solution.py:772
  18.3 4.2 %collective-permute-start.4 = (f32[2,1,8,128]{3,2,1,0:T(8,128)S(1)}, f32[2,1,8,128]{3,2,1,0:T(8,128)S(1)}, u32[]{:S(2)}, u32[]{:S(2)}) collective-permute-start(f32[2,1,8,128]{3,2,1,0:T(8,128)S(1)} %get-tuple-element.51), channel_id=1, source_target_pairs={{0,1},{1,0},{2,3},{3,2},{4,5},{5,4},{6,7},{7,6},{8,9},{9,8},{10,11... | collective-permute-start | bytes 24584 | tf_op jit(solution)/shard_map/ppermute | solution.py:745
  20.4 4.5 %collective-permute-start.10 = (f32[3,128]{1,0:T(4,128)S(1)}, f32[3,128]{1,0:T(4,128)S(1)}, u32[]{:S(2)}, u32[]{:S(2)}) collective-permute-start(f32[3,128]{1,0:T(4,128)S(1)} %get-tuple-element.61), channel_id=1, source_target_pairs={{0,1},{1,0},{2,3},{3,2},{4,5},{5,4},{6,7},{7,6},{8,9},{9,8},{10,11... | collective-permute-start | bytes 4616 | tf_op jit(solution)/shard_map/ppermute | solution.py:745

commit v13 on v11

--- a/solution.py
+++ b/solution.py
@@ -829,7 +829,7 @@
     outer, inner = to_x(sent_outer, sent_inner)
     onward, top = call(
         ahead_kernel,
-        [(3 * ny, 128), (1, (2 * PTS + 1) * 128)],
+        [(3 * ny, 128), (1, (3 * PTS + 1) * 128)],
         [],
         side, sent_outer, sent_inner, gface, restrict, still_outer, still_inner,
     )

time: 25.6 us -> 25.7 us (level)
    ppermute x1, waiting for transfers between devices: 0.01 us -> 1.51 us  [two_on(): rows = lax.ppermute(rows, 'dom', [(i, (i + 2) % size) for i in range(size)])]
    ppermute x1, waiting for transfers between devices: 1.47 us -> 0.01 us  [two_on(): return (rows, lax.ppermute(top, ('dom', 'sub'), pairs))]
    ppermute x1, starting transfers between devices: 0.85 us -> 0.01 us  [two_on(): return (rows, lax.ppermute(top, ('dom', 'sub'), pairs))]
    ppermute x1, starting transfers between devices: 0.01 us -> 0.85 us  [two_on(): rows = lax.ppermute(rows, 'dom', [(i, (i + 2) % size) for i in range(size)])]
where the time goes in v13:
time: 25.7 us; the launch traced here: 25.5 us
  starting transfers between devices  15.5 us (60%)
  Pallas kernels  5.37 us (21%)
  waiting for transfers between devices  3.95 us (15%)
  between operations  0.74 us (3%)
    ppermute x3, starting transfers between devices, to_x(): outer = lax.ppermute(outer, 'dom', outer_pairs(size))  8.69 us
    ppermute x3, starting transfers between devices, from_y(): up = lax.ppermute(faces, 'sub', [(i, (i + 1) % size) for i in range(size)])  5.92 us
    pallas_call x11, Pallas kernels, call(): pl.pallas_call(body, out_shape=[jax.ShapeDtypeStruct(s, F32) if isinstanc...  5.37 us
    ppermute x1, waiting for transfers between devices, two_on(): rows = lax.ppermute(rows, 'dom', [(i, (i + 2) % size) for i in range(size)])  1.51 us
    ppermute x3, waiting for transfers between devices, to_x(): outer = lax.ppermute(outer, 'dom', outer_pairs(size))  1.3 us
    ppermute x3, waiting for transfers between devices, from_y(): up = lax.ppermute(faces, 'sub', [(i, (i + 1) % size) for i in range(size)])  1.13 us
    ppermute x1, starting transfers between devices, two_on(): rows = lax.ppermute(rows, 'dom', [(i, (i + 2) % size) for i in range(size)])  0.85 us
  transfers between devices with their start and end apart: 11, of which 4 were waited for; matrix products, arithmetic and copies ran while one was open for 0% of the time, Pallas kernels for 14%

profile of v13, /device:TPU:0, one launch (start us, length us, event | category | flops | bytes accessed | tf_op | source)
XLA Modules:
  0.0 25.5 jit_solution(15112771373390213649)
XLA Ops:
  0.6 0.0 copy-start
  0.6 0.0 copy-start.3
  0.6 1.1 %shard_map.77 = (f32[3,8,128]{2,1,0:T(8,128)S(1)}, f32[2,5,8,128]{3,2,1,0:T(8,128)S(1)}) custom-call(f32[3,8,16]{2,1,0:T(8,128)} %bitcast.12, f32[8,64,128]{2,1,0:T(8,128)} %bitcast.6, f32[8,64,128]{2,1,0:T(8,128)} %bitcast.10), custom_call_target="tpu_custom_call" | custom-call | tf_op jit(solution)/shard_map/pallas_call | solution.py:734
  1.8 3.0 %collective-permute-start = (f32[2,5,8,128]{3,2,1,0:T(8,128)S(1)}, f32[2,5,8,128]{3,2,1,0:T(8,128)S(1)}, u32[]{:S(2)}, u32[]{:S(2)}) collective-permute-start(f32[2,5,8,128]{3,2,1,0:T(8,128)S(1)} %get-tuple-element.34), channel_id=1, source_target_pairs={{0,1},{1,0},{2,3},{3,2},{4,5},{5,4},{6,7},{7,6},{8,9},{9,8},{10,11... | collective-permute-start | bytes 122888 | tf_op jit(solution)/shard_map/ppermute | solution.py:746
  4.8 0.0 copy-done
  4.8 0.0 copy-done.3
  4.8 0.0 copy-start.4
  4.8 0.8 %shard_map.78 = (f32[2,8,8,8,128]{4,3,2,1,0:T(8,128)S(1)}, f32[2,2,8,8,128]{4,3,2,1,0:T(8,128)S(1)}, f32[2,2,8,128]{3,2,1,0:T(8,128)S(1)}, f32[144,128]{1,0:T(8,...) custom-call(s32[1]{0:T(128)} %bitcast.side_ref, ...), custom_call_target="tpu_custom_call" | custom-call | tf_op jit(solution)/shard_map/pallas_call | solution.py:734
  5.7 0.0 copy-start.2
  5.7 1.1 %collective-permute-done.below_ref.above_ref = f32[2,5,8,128]{3,2,1,0:T(8,128)S(1)} collective-permute-done((f32[2,5,8,128]{3,2,1,0:T(8,128)S(1)}, f32[2,5,8,128]{3,2,1,0:T(8,128)S(1)}, u32[]{:S(2)}, u32[]{:S(2)}) %collective-permute-start) | collective-permute-done | bytes 40992 | tf_op jit(solution)/shard_map/ppermute | solution.py:746
  6.8 3.4 %collective-permute-start.1 = (f32[144,128]{1,0:T(8,128)S(1)}, f32[144,128]{1,0:T(8,128)S(1)}, u32[]{:S(2)}, u32[]{:S(2)}) collective-permute-start(f32[144,128]{1,0:T(8,128)S(1)} %get-tuple-element.46), channel_id=1, source_target_pairs={{0,30},{2,4},{4,2},{6,8},{8,6},{10,12},{12,10},{14,16},{16,14},{18... | collective-permute-start | bytes 221192 | tf_op jit(solution)/shard_map/ppermute | solution.py:762
  10.2 0.0 collective-permute-start.2
  10.2 1.9 %collective-permute-start.6 = (f32[144,128]{1,0:T(8,128)S(1)}, f32[144,128]{1,0:T(8,128)S(1)}, u32[]{:S(2)}, u32[]{:S(2)}) collective-permute-start(f32[144,128]{1,0:T(8,128)S(1)} %get-tuple-element.54), channel_id=1, source_target_pairs={{0,30},{2,4},{4,2},{6,8},{8,6},{10,12},{12,10},{14,16},{16,14},{18... | collective-permute-start | bytes 221192 | tf_op jit(solution)/shard_map/ppermute | solution.py:762
  12.1 0.0 collective-permute-start.7
  12.1 0.0 copy-done.4
  12.1 0.0 copy-done.2
  12.1 0.8 %shard_map.79 = (f32[2,2,8,8,128]{4,3,2,1,0:T(8,128)S(1)}, f32[8,8,8,128]{3,2,1,0:T(8,128)S(1)}, f32[8,8,8,128]{3,2,1,0:T(8,128)S(1)}, f32[8,8,8,128]{3,2,1,0:T(...) custom-call(f32[2,8,8,8,128]{4,3,2,1,0:T(8,128)S(1)} %get-tuple-element.33., ...), custom_call_target="tpu_custom_call" | custom-call | tf_op jit(solution)/shard_map/pallas_call | solution.py:734
  13.0 0.4 %collective-permute-done.1.outer_ref = f32[144,128]{1,0:T(8,128)S(1)} collective-permute-done((f32[144,128]{1,0:T(8,128)S(1)}, f32[144,128]{1,0:T(8,128)S(1)}, u32[]{:S(2)}, u32[]{:S(2)}) %collective-permute-start.1) | collective-permute-done | bytes 73760 | tf_op jit(solution)/shard_map/ppermute | solution.py:762
  13.4 0.0 collective-permute-done.2.inner_ref
  13.4 0.0 copy-start.1
  13.4 0.5 %shard_map.81 = (f32[104,128]{1,0:T(8,128)S(1)}, f32[104,128]{1,0:T(8,128)S(1)}, f32[2,1,8,128]{3,2,1,0:T(8,128)S(1)}, f32[2,8,8,128]{3,2,1,0:T(8,128)S(1)}, f32...) custom-call(s32[1]{0:T(128)} %bitcast.side_ref, f32[2,2,8,8,128]{4,3,2,1,0:T(8,128)S(1)} %get-tuple-element.35.rough_ref, ...), custom_call_target="tpu_custom_call" | custom-call | tf_op jit(solution)/shard_map/pallas_call | solution.py:734
  13.9 3.4 %collective-permute-start.3 = (f32[104,128]{1,0:T(8,128)S(1)}, f32[104,128]{1,0:T(8,128)S(1)}, u32[]{:S(2)}, u32[]{:S(2)}) collective-permute-start(f32[104,128]{1,0:T(8,128)S(1)} %get-tuple-element.50.sent_outer_ref), channel_id=1, source_target_pairs={{0,30},{2,4},{4,2},{6,8},{8,6},{10,12},{12,10},{14,16},{16,14},{18... | collective-permute-start | bytes 159752 | tf_op jit(solution)/shard_map/ppermute | solution.py:762
  17.3 0.0 collective-permute-start.5
  17.3 0.0 collective-permute-done.6.outer_ref
  17.3 0.0 collective-permute-done.7.inner_ref
  17.3 0.0 copy-done.1
  17.3 0.2 shard_map.86
  17.4 0.0 collective-permute-start.9
  17.5 0.8 %collective-permute-start.8 = (f32[24,128]{1,0:T(8,128)S(1)}, f32[24,128]{1,0:T(8,128)S(1)}, u32[]{:S(2)}, u32[]{:S(2)}) collective-permute-start(f32[24,128]{1,0:T(8,128)S(1)} %get-tuple-element.58), channel_id=1, source_target_pairs={{0,4},{2,6},{4,8},{6,10},{8,12},{10,14},{12,16},{14,18},{16,20},{1... | collective-permute-start | bytes 36872 | tf_op jit(solution)/shard_map/ppermute | solution.py:769
  18.3 0.8 %collective-permute-start.4 = (f32[2,1,8,128]{3,2,1,0:T(8,128)S(1)}, f32[2,1,8,128]{3,2,1,0:T(8,128)S(1)}, u32[]{:S(2)}, u32[]{:S(2)}) collective-permute-start(f32[2,1,8,128]{3,2,1,0:T(8,128)S(1)} %get-tuple-element.51), channel_id=1, source_target_pairs={{0,1},{1,0},{2,3},{3,2},{4,5},{5,4},{6,7},{7,6},{8,9},{9,8},{10,11... | collective-permute-start | bytes 24584 | tf_op jit(solution)/shard_map/ppermute | solution.py:746
  19.1 0.2 shard_map.83.own_ref
  19.3 0.9 %collective-permute-done.3.outer_ref = f32[104,128]{1,0:T(8,128)S(1)} collective-permute-done((f32[104,128]{1,0:T(8,128)S(1)}, f32[104,128]{1,0:T(8,128)S(1)}, u32[]{:S(2)}, u32[]{:S(2)}) %collective-permute-start.3) | collective-permute-done | bytes 53280 | tf_op jit(solution)/shard_map/ppermute | solution.py:762
  20.2 0.0 collective-permute-done.5.inner_ref
  20.2 0.2 shard_map.84
  20.4 2.1 %collective-permute-start.10 = (f32[3,128]{1,0:T(4,128)S(1)}, f32[3,128]{1,0:T(4,128)S(1)}, u32[]{:S(2)}, u32[]{:S(2)}) collective-permute-start(f32[3,128]{1,0:T(4,128)S(1)} %get-tuple-element.61), channel_id=1, source_target_pairs={{0,1},{1,0},{2,3},{3,2},{4,5},{5,4},{6,7},{7,6},{8,9},{9,8},{10,11... | collective-permute-start | bytes 4616 | tf_op jit(solution)/shard_map/ppermute | solution.py:746
  22.5 0.0 collective-permute-done.4.below_ref.above_ref
  22.5 0.8 %shard_map.82 = (f32[8,64,128]{2,1,0:T(8,128)}, f32[1,128]{1,0:T(1,128)S(1)}) custom-call(s32[1]{0:T(128)} %bitcast.side_ref, f32[8,8,8,128]{3,2,1,0:T(8,128)S(1)} %get-tuple-element.48.sofar_ref, f32[8,8,8,128]{3,2,1,0:T(8,128)S(1)} %get-tuple-element.40.gain_ref, f32[2,8,8,128]{3,2,1,0:T(8,128)S(1)} %get-tuple-element.49.gface_ref, ...), custom_call_target="tpu_custom_call" | custom-call | tf_op jit(solution)/shard_map/pallas_call | solution.py:734
  23.2 0.2 shard_map.85.own_ref
  23.4 1.5 %collective-permute-done.8.next_ref = f32[24,128]{1,0:T(8,128)S(1)} collective-permute-done((f32[24,128]{1,0:T(8,128)S(1)}, f32[24,128]{1,0:T(8,128)S(1)}, u32[]{:S(2)}, u32[]{:S(2)}) %collective-permute-start.8) | collective-permute-done | bytes 12320 | tf_op jit(solution)/shard_map/ppermute | solution.py:769
  24.9 0.0 collective-permute-done.9.top_ref
  24.9 0.0 collective-permute-done.10.below_ref.above_ref
  24.9 0.6 %shard_map.87 = f32[8,17]{1,0:T(8,128)} custom-call(f32[8,128]{1,0:T(8,128)S(1)} %shard_map.85.own_ref, f32[24,128]{1,0:T(8,128)S(1)} %collective-permute-done.8.next_ref, f32[1,3200]{1,0:T(1,128)S(1)} %collective-permute-done.9.top_ref, f32[1,128]{1,0:T(1,128)S(1)} %get-tuple-element.60.token_ref, f32[3,128]{1,0:T(4,128)S(1)} %collective-permute-done.10.below_ref.above_ref, ...), custom_call_target="tpu_custom_call" | custom-call | tf_op jit(solution)/shard_map/pallas_call | solution.py:734
  (1 shorter events, 0.0 us)
Async XLA Ops:
  0.6 4.2 %copy-start = (f32[1,8,8,8,128]{4,3,2,1,0:T(8,128)S(1)}, f32[1,8,8,8,128]{4,3,2,1,0:T(8,128)}, u32[]{:S(2)}) copy-start(f32[1,8,8,8,128]{4,3,2,1,0:T(8,128)} %param.7) | copy-start | bytes 786436
  0.6 4.2 %copy-start.3 = (f32[1,8,8,8,128]{4,3,2,1,0:T(8,128)S(1)}, f32[1,8,8,8,128]{4,3,2,1,0:T(8,128)}, u32[]{:S(2)}) copy-start(f32[1,8,8,8,128]{4,3,2,1,0:T(8,128)} %param.6) | copy-start | bytes 786436
  1.8 5.0 %collective-permute-start = (f32[2,5,8,128]{3,2,1,0:T(8,128)S(1)}, f32[2,5,8,128]{3,2,1,0:T(8,128)S(1)}, u32[]{:S(2)}, u32[]{:S(2)}) collective-permute-start(f32[2,5,8,128]{3,2,1,0:T(8,128)S(1)} %get-tuple-element.34), channel_id=1, source_target_pairs={{0,1},{1,0},{2,3},{3,2},{4,5},{5,4},{6,7},{7,6},{8,9},{9,8},{10,11... | collective-permute-start | bytes 122888 | tf_op jit(solution)/shard_map/ppermute | solution.py:746
  4.8 7.3 %copy-start.4 = (bf16[256,256]{1,0:T(8,128)(2,1)S(1)}, bf16[256,256]{1,0:T(8,128)(2,1)}, u32[]{:S(2)}) copy-start(bf16[256,256]{1,0:T(8,128)(2,1)} %constant.25.clone.grad_ref) | copy-start | bytes 393220
  5.7 6.5 %copy-start.2 = (bf16[256,256]{1,0:T(8,128)(2,1)S(1)}, bf16[256,256]{1,0:T(8,128)(2,1)}, u32[]{:S(2)}) copy-start(bf16[256,256]{1,0:T(8,128)(2,1)} %constant.26.clone.back_ref) | copy-start | bytes 393220
  6.8 6.5 %collective-permute-start.1 = (f32[144,128]{1,0:T(8,128)S(1)}, f32[144,128]{1,0:T(8,128)S(1)}, u32[]{:S(2)}, u32[]{:S(2)}) collective-permute-start(f32[144,128]{1,0:T(8,128)S(1)} %get-tuple-element.46), channel_id=1, source_target_pairs={{0,30},{2,4},{4,2},{6,8},{8,6},{10,12},{12,10},{14,16},{16,14},{18... | collective-permute-start | bytes 221192 | tf_op jit(solution)/shard_map/ppermute | solution.py:762
  10.2 3.2 %collective-permute-start.2 = (f32[144,128]{1,0:T(8,128)S(1)}, f32[144,128]{1,0:T(8,128)S(1)}, u32[]{:S(2)}, u32[]{:S(2)}) collective-permute-start(f32[144,128]{1,0:T(8,128)S(1)} %get-tuple-element.47), channel_id=1, source_target_pairs={{0,2},{2,0},{4,6},{6,4},{8,10},{10,8},{12,14},{14,12},{16,18},{18,... | collective-permute-start | bytes 221192 | tf_op jit(solution)/shard_map/ppermute | solution.py:763
  10.2 7.0 %collective-permute-start.6 = (f32[144,128]{1,0:T(8,128)S(1)}, f32[144,128]{1,0:T(8,128)S(1)}, u32[]{:S(2)}, u32[]{:S(2)}) collective-permute-start(f32[144,128]{1,0:T(8,128)S(1)} %get-tuple-element.54), channel_id=1, source_target_pairs={{0,30},{2,4},{4,2},{6,8},{8,6},{10,12},{12,10},{14,16},{16,14},{18... | collective-permute-start | bytes 221192 | tf_op jit(solution)/shard_map/ppermute | solution.py:762
  12.1 5.1 %collective-permute-start.7 = (f32[144,128]{1,0:T(8,128)S(1)}, f32[144,128]{1,0:T(8,128)S(1)}, u32[]{:S(2)}, u32[]{:S(2)}) collective-permute-start(f32[144,128]{1,0:T(8,128)S(1)} %get-tuple-element.55), channel_id=1, source_target_pairs={{0,2},{2,0},{4,6},{6,4},{8,10},{10,8},{12,14},{14,12},{16,18},{18,... | collective-permute-start | bytes 221192 | tf_op jit(solution)/shard_map/ppermute | solution.py:763
  13.4 3.9 %copy-start.1 = (bf16[512,256]{1,0:T(8,128)(2,1)S(1)}, bf16[512,256]{1,0:T(8,128)(2,1)}, u32[]{:S(2)}) copy-start(bf16[512,256]{1,0:T(8,128)(2,1)} %constant.27.clone.restrict_ref) | copy-start | bytes 786436
  13.9 6.3 %collective-permute-start.3 = (f32[104,128]{1,0:T(8,128)S(1)}, f32[104,128]{1,0:T(8,128)S(1)}, u32[]{:S(2)}, u32[]{:S(2)}) collective-permute-start(f32[104,128]{1,0:T(8,128)S(1)} %get-tuple-element.50.sent_outer_ref), channel_id=1, source_target_pairs={{0,30},{2,4},{4,2},{6,8},{8,6},{10,12},{12,10},{14,16},{16,14},{18... | collective-permute-start | bytes 159752 | tf_op jit(solution)/shard_map/ppermute | solution.py:762
  17.3 2.9 %collective-permute-start.5 = (f32[104,128]{1,0:T(8,128)S(1)}, f32[104,128]{1,0:T(8,128)S(1)}, u32[]{:S(2)}, u32[]{:S(2)}) collective-permute-start(f32[104,128]{1,0:T(8,128)S(1)} %get-tuple-element.52.sent_inner_ref), channel_id=1, source_target_pairs={{0,2},{2,0},{4,6},{6,4},{8,10},{10,8},{12,14},{14,12},{16,18},{18,... | collective-permute-start | bytes 159752 | tf_op jit(solution)/shard_map/ppermute | solution.py:763
  17.4 7.5 %collective-permute-start.9 = (f32[1,3200]{1,0:T(1,128)S(1)}, f32[1,3200]{1,0:T(1,128)S(1)}, u32[]{:S(2)}, u32[]{:S(2)}) collective-permute-start(f32[1,3200]{1,0:T(1,128)S(1)} %get-tuple-element.59), channel_id=1, source_target_pairs={{0,5},{1,4},{2,7},{3,6},{4,9},{5,8},{6,11},{7,10},{8,13},{9,12},{1... | collective-permute-start | bytes 38408 | tf_op jit(solution)/shard_map/ppermute | solution.py:773
  17.5 7.5 %collective-permute-start.8 = (f32[24,128]{1,0:T(8,128)S(1)}, f32[24,128]{1,0:T(8,128)S(1)}, u32[]{:S(2)}, u32[]{:S(2)}) collective-permute-start(f32[24,128]{1,0:T(8,128)S(1)} %get-tuple-element.58), channel_id=1, source_target_pairs={{0,4},{2,6},{4,8},{6,10},{8,12},{10,14},{12,16},{14,18},{16,20},{1... | collective-permute-start | bytes 36872 | tf_op jit(solution)/shard_map/ppermute | solution.py:769
  18.3 4.2 %collective-permute-start.4 = (f32[2,1,8,128]{3,2,1,0:T(8,128)S(1)}, f32[2,1,8,128]{3,2,1,0:T(8,128)S(1)}, u32[]{:S(2)}, u32[]{:S(2)}) collective-permute-start(f32[2,1,8,128]{3,2,1,0:T(8,128)S(1)} %get-tuple-element.51), channel_id=1, source_target_pairs={{0,1},{1,0},{2,3},{3,2},{4,5},{5,4},{6,7},{7,6},{8,9},{9,8},{10,11... | collective-permute-start | bytes 24584 | tf_op jit(solution)/shard_map/ppermute | solution.py:746
  20.4 4.6 %collective-permute-start.10 = (f32[3,128]{1,0:T(4,128)S(1)}, f32[3,128]{1,0:T(4,128)S(1)}, u32[]{:S(2)}, u32[]{:S(2)}) collective-permute-start(f32[3,128]{1,0:T(4,128)S(1)} %get-tuple-element.61), channel_id=1, source_target_pairs={{0,1},{1,0},{2,3},{3,2},{4,5},{5,4},{6,7},{7,6},{8,9},{9,8},{10,11... | collective-permute-start | bytes 4616 | tf_op jit(solution)/shard_map/ppermute | solution.py:746
